TPU v7x, 256 devices: a whole 4x4x8 slice. The times are simulated.
256 devices in a mesh: ctx: 32 (over x_hi, z, core), head: 8 (over y, x_lo).
Axes of the slice: x: 4 (x_hi: 2, x_lo: 2; x = x_hi * 2 + x_lo), y: 4, z: 8, core: 2. Of those that a mesh axis runs over, the one named last changes fastest.
Arguments:
- queries: bfloat16 [4, 2048, 8192], P(None, 'ctx', 'head'), as said below
- key_vectors: bfloat16 [4, 2048, 1024], P(None, 'ctx', 'head'), as said below
- value_vectors: bfloat16 [4, 2048, 1024], P(None, 'ctx', 'head'), may hold values from -6 to 6
- output_gradient: bfloat16 [4, 2048, 8192], P(None, 'ctx', 'head'), may hold values from -6 to 6
- positions: int32 [4, 2048], P(None, 'ctx'), may hold values from 0 to 2047, as said below
- segments: int32 [4, 2048], P(None, 'ctx'), may hold values from 0 to 7, as said below
Outputs:
- query_grad: bfloat16 [4, 2048, 8192], P(None, ('ctx', 'head'))
- key_gradient: bfloat16 [4, 2048, 1024], P(None, ('ctx', 'head'))
- value_gradient: bfloat16 [4, 2048, 1024], P(None, ('ctx', 'head'))
Inputs may be any that keep to these rules, and one draw needn't show every extreme that they name: `positions`: in each window each position appears in exactly one row. `segments`: in each window documents are runs of consecutive positions numbered in order of position, and every id of the range is used. `queries`: real-valued. `key_vectors`: real-valued.
All inputs are finite; a program needn't handle non-finite values.
Results may differ from a plain program's by a relative error of at most 0.012.
Values may be sent and summed in bfloat16 or wider, within the bound.
No kernel may reach another device: no remote copies, remote signals or barrier semaphores. Data moves between devices by JAX's collectives and lax.ppermute only.
A program may use at most 64 MiB of HBM per device.

v0:
```python
import math

import jax
import jax.numpy as jnp
from jax import lax
from jax.sharding import PartitionSpec as P

QUERY_HEADS = 64
KEY_VALUE_HEADS = 8
HEAD_SIZE = 128


NEG_BIG = -1e30


def passed_along(array, axis, by):
    count = lax.axis_size(axis)
    return lax.ppermute(array, axis, [(i, (i + by) % count) for i in range(count)])


def block_scores(query_four_axes, key_block, key_pos, key_seg, query_pos, query_seg):
    key_per_head = key_block.shape[1] // HEAD_SIZE
    key_three = key_block.reshape(key_block.shape[0], key_per_head, HEAD_SIZE)
    scores = jnp.einsum(
        "tkgd,skd->kgts", query_four_axes, key_three, preferred_element_type=jnp.float32
    ) * (1.0 / math.sqrt(HEAD_SIZE))
    allowed = (query_seg[:, None] == key_seg[None, :]) & (key_pos[None, :] <= query_pos[:, None])
    return (jnp.where(allowed, scores, NEG_BIG), allowed, key_three)


def stats_update(state_now, pieces, query_four_axes, grad_four, query_pos, query_seg):
    running_max, running_sum, running_dot = state_now
    key_block, value_block, key_pos, key_seg = pieces
    scores, allowed, key_three = block_scores(
        query_four_axes, key_block, key_pos, key_seg, query_pos, query_seg
    )
    value_three = value_block.reshape(key_three.shape)
    softmax_grad = jnp.einsum(
        "tkgd,skd->kgts", grad_four, value_three, preferred_element_type=jnp.float32
    )
    new_max = jnp.maximum(running_max, jnp.max(scores, axis=-1, keepdims=True))
    rescale = jnp.exp(running_max - new_max)
    weights = jnp.where(allowed, jnp.exp(scores - new_max), 0.0)
    new_sum = running_sum * rescale + jnp.sum(weights, axis=-1, keepdims=True)
    new_dot = running_dot * rescale + jnp.sum(weights * softmax_grad, axis=-1, keepdims=True)
    return (new_max, new_sum, new_dot)


def block_grads(pieces, query_four_axes, grad_four, logsum, row_delta, query_pos, query_seg):
    key_block, value_block, key_pos, key_seg = pieces
    key_rows = key_block.shape[0]
    factor = 1.0 / math.sqrt(HEAD_SIZE)
    scores, allowed, key_three = block_scores(
        query_four_axes, key_block, key_pos, key_seg, query_pos, query_seg
    )
    value_three = value_block.reshape(key_three.shape)
    softmax_out = jnp.where(allowed, jnp.exp(scores - logsum), 0.0)
    softmax_grad = jnp.einsum(
        "tkgd,skd->kgts", grad_four, value_three, preferred_element_type=jnp.float32
    )
    score_grad = softmax_out * (softmax_grad - row_delta)
    softmax_low = softmax_out.astype(jnp.bfloat16)
    score_low = score_grad.astype(jnp.bfloat16)
    value_part = jnp.einsum(
        "kgts,tkgd->skd", softmax_low, grad_four, preferred_element_type=jnp.float32
    ).reshape(key_rows, key_block.shape[1])
    key_part = (
        jnp.einsum(
            "kgts,tkgd->skd", score_low, query_four_axes, preferred_element_type=jnp.float32
        ).reshape(key_rows, key_block.shape[1])
        * factor
    )
    query_part = (
        jnp.einsum("kgts,skd->tkgd", score_low, key_three, preferred_element_type=jnp.float32)
        * factor
    )
    return (query_part, key_part, value_part)


def on_device(queries, key_vectors, value_vectors, output_gradient, positions, segments):
    window_count = queries.shape[0]
    row_count = queries.shape[1]
    query_groups = QUERY_HEADS // KEY_VALUE_HEADS
    key_width = key_vectors.shape[2]
    key_per_head = key_width // HEAD_SIZE
    query_five = queries.reshape(window_count, row_count, key_per_head, query_groups, HEAD_SIZE)
    grad_five = output_gradient.reshape(
        window_count, row_count, key_per_head, query_groups, HEAD_SIZE
    )
    stat_shape = (window_count, key_per_head, query_groups, row_count, 1)
    start_stats = (
        jnp.full(stat_shape, NEG_BIG, jnp.float32),
        jnp.zeros(stat_shape, jnp.float32),
        jnp.zeros(stat_shape, jnp.float32),
    )
    query_zero = jnp.zeros(query_five.shape, jnp.float32)
    stats_many = jax.vmap(stats_update)
    grads_many = jax.vmap(block_grads)
    gathered = (
        lax.all_gather(key_vectors, "ctx", axis=1, tiled=True),
        lax.all_gather(value_vectors, "ctx", axis=1, tiled=True),
        lax.all_gather(positions, "ctx", axis=1, tiled=True),
        lax.all_gather(segments, "ctx", axis=1, tiled=True),
    )
    whole_rows = gathered[0].shape[1]
    per_block = row_count * math.gcd(lax.axis_size("ctx"), max(1, 512 // row_count))
    block_count = whole_rows // per_block
    blocked = tuple(
        (
            jnp.moveaxis(
                member.reshape((window_count, block_count, per_block) + member.shape[2:]), 1, 0
            )
            for member in gathered
        )
    )

    def stats_step(state_now, pieces):
        return (stats_many(state_now, pieces, query_five, grad_five, positions, segments), None)

    (running_max, running_sum, running_dot), unused = lax.scan(stats_step, start_stats, blocked)
    logsum = running_max + jnp.log(running_sum)
    row_delta = running_dot / running_sum
    circle_size = lax.axis_size("ctx")
    own_index = lax.axis_index("ctx")
    key_zero = jnp.zeros(key_vectors.shape, jnp.float32)

    def cycle_turn(turn_index, cycle_state):
        query_acc, key_acc, value_acc = cycle_state
        source = (own_index - turn_index) % circle_size
        start_row = source * row_count
        pieces = tuple(
            (lax.dynamic_slice_in_dim(member, start_row, row_count, 1) for member in gathered)
        )
        query_part, key_part, value_part = grads_many(
            pieces, query_five, grad_five, logsum, row_delta, positions, segments
        )
        key_acc, value_acc = passed_along((key_acc + key_part, value_acc + value_part), "ctx", 1)
        return (query_acc + query_part, key_acc, value_acc)

    query_acc, key_acc, value_acc = lax.fori_loop(
        0, circle_size, cycle_turn, (query_zero, key_zero, key_zero)
    )
    query_low = query_acc.reshape(window_count, row_count, queries.shape[2]).astype(jnp.bfloat16)
    key_low = key_acc.astype(jnp.bfloat16)
    value_low = value_acc.astype(jnp.bfloat16)
    query_grad, key_gradient, value_gradient = (
        lax.all_to_all(query_low, "head", split_axis=1, concat_axis=2, tiled=True),
        lax.all_to_all(key_low, "head", split_axis=1, concat_axis=2, tiled=True),
        lax.all_to_all(value_low, "head", split_axis=1, concat_axis=2, tiled=True),
    )
    return (query_grad, key_gradient, value_gradient)


def solution(mesh):
    return jax.shard_map(
        on_device,
        mesh=mesh,
        in_specs=(
            P(None, "ctx", "head"),
            P(None, "ctx", "head"),
            P(None, "ctx", "head"),
            P(None, "ctx", "head"),
            P(None, "ctx"),
            P(None, "ctx"),
        ),
        out_specs=(
            P(None, ("ctx", "head"), None),
            P(None, ("ctx", "head"), None),
            P(None, ("ctx", "head"), None),
        ),
        check_vma=False,
    )
```

profile of v0, /device:TPU:2, one launch (start us, length us, event | category | flops | bytes accessed | tf_op | source)
XLA Modules:
  0.0 674.8 jit_solution(3938459747164289178)
XLA Ops:
  11.3 44.0 %all-gather = s32[32,64,4]{1,2,0:T(4,128)S(1)} all-gather(s32[1,64,4]{1,2,0:T(4,128)S(1)} %bitcast.257), channel_id=1, replica_groups=mesh['ctx'=32,'head'=8] {'ctx'}, dimensions={0}, use_global_device_ids=true | all-gather | bytes 33792 | tf_op jit(solution)/shard_map/all_gather | solution.py:103
  55.3 37.0 %all-gather.1 = s32[32,64,4]{1,2,0:T(4,128)S(1)} all-gather(s32[1,64,4]{1,2,0:T(4,128)S(1)} %bitcast.258), channel_id=1, replica_groups=mesh['ctx'=32,'head'=8] {'ctx'}, dimensions={0}, use_global_device_ids=true | all-gather | bytes 33792 | tf_op jit(solution)/shard_map/all_gather | solution.py:102
  92.9 3.1 copy.81
  96.1 76.3 %all-gather.5.cloned.1.call-done = bf16[4,2048,128]{2,1,0:T(8,128)(2,1)} async-done(((bf16[4,64,128]{2,1,0:T(8,128)(2,1)}), bf16[4,2048,128]{2,1,0:T(8,128)(2,1)}) %all-gather.5.cloned.1.call-update) | async-done | bytes 2097168 | tf_op jit(solution)/shard_map/all_gather | solution.py:100
  172.4 3.2 copy.82
  175.6 42.4 %while.35 = (s32[]{:T(128)}, f32[4,1,8,64,1]{3,2,0,4,1:T(8,128)S(1)}, f32[4,1,8,64,1]{3,2,0,4,1:T(8,128)S(1)}, f32[4,1,8,64,1]{3,2,0,4,1:T(8,128)S(1)}, s32[4,64...) while((s32[]{:T(128)}, ...), condition=%wide.region_4.5_spmd.clone, body=%wide.region_0.4_spmd.clone.sunk | while | flops 551958528 | bytes 32181424 | solution.py:120
  175.8 3.8 fusion.66
  179.5 3.7 fusion.68
  183.2 2.9 fusion.67
  186.4 3.8 fusion.66
  190.1 3.7 fusion.68
  193.8 2.9 fusion.67
  197.0 3.8 fusion.66
  200.7 3.7 fusion.68
  204.4 2.9 fusion.67
  207.6 3.8 fusion.66
  211.4 3.7 fusion.68
  215.1 2.9 fusion.67
  218.1 415.3 %while.36 = (s32[]{:T(128)}, f32[4,64,1,8,128]{4,1,3,0,2:T(8,128)S(1)}, f32[4,64,128]{2,1,0:T(8,128)S(1)}, f32[4,64,128]{2,1,0:T(8,128)S(1)}, s32[]{:T(128)}, /*...) while((s32[]{:T(128)}, ...), condition=%wide.region_6.7_spmd.clone, body=%wide.region_5.6_spmd.clone.sunk | while | flops 169754640 | bytes 8380878 | solution.py:140
  224.2 5.4 collective-permute-done
  231.3 1.5 fusion.79
  236.4 6.3 collective-permute-done
  249.3 6.3 collective-permute-done
  262.3 6.3 collective-permute-done
  270.2 1.5 fusion.79
  275.3 6.3 collective-permute-done
  283.2 1.5 fusion.79
  288.3 6.3 collective-permute-done
  296.2 1.5 fusion.79
  301.2 6.3 collective-permute-done
  309.2 1.5 fusion.79
  314.2 6.3 collective-permute-done
  322.1 1.5 fusion.79
  327.2 6.3 collective-permute-done
  335.1 1.5 fusion.79
  340.2 6.3 collective-permute-done
  353.2 6.3 collective-permute-done
  366.1 6.3 collective-permute-done
  379.1 6.3 collective-permute-done
  392.1 6.3 collective-permute-done
  405.1 6.3 collective-permute-done
  418.0 6.3 collective-permute-done
  431.0 6.3 collective-permute-done
  444.0 6.3 collective-permute-done
  457.0 6.3 collective-permute-done
  469.9 6.3 collective-permute-done
  482.9 6.3 collective-permute-done
  495.9 6.3 collective-permute-done
  508.9 6.3 collective-permute-done
  521.9 6.3 collective-permute-done
  534.8 6.3 collective-permute-done
  547.8 6.3 collective-permute-done
  560.8 6.3 collective-permute-done
  573.8 6.3 collective-permute-done
  586.7 6.3 collective-permute-done
  599.7 6.3 collective-permute-done
  612.7 6.3 collective-permute-done
  625.7 6.3 collective-permute-done
  634.1 5.7 all-to-all-start.2
  640.5 4.3 all-to-all-done.2
  644.9 4.5 all-to-all-start.1
  650.8 4.7 all-to-all-done.1
  655.5 4.0 all-to-all-start
  660.8 6.3 all-to-all-done
  (373 shorter events, 213.1 us)
Async XLA Ops:
  7.2 85.8 %all-gather.7.cloned.1.call-start = ((), (), s32[]{:S(2)}) async-start(), calls=%async_computation.4 | async-start | bytes 2162688 | tf_op jit(solution)/shard_map/all_gather | solution.py:101
  7.9 164.5 %all-gather.5.cloned.1.call-start = ((), (), s32[]{:S(2)}) async-start(), calls=%async_computation.3 | async-start | bytes 2162688 | tf_op jit(solution)/shard_map/all_gather | solution.py:100
  221.6 8.1 %collective-permute-start = (f32[4,64,128]{2,1,0:T(8,128)S(1)}, f32[4,64,128]{2,1,0:T(8,128)S(1)}, u32[]{:S(2)}, u32[]{:S(2)}) collective-permute-start(f32[4,64,128]{2,1,0:T(8,128)S(1)} %fusion.82), channel_id=1, source_target_pairs={{0,8},{8,16},{16,24},{24,32},{32,40},{40,48},{48,56},{56,64},{64,7... | collective-permute-start | bytes 393224 | tf_op jit(solution)/shard_map/while/body/eval_jaxpr/ppermute | solution.py:18
  222.2 8.9 %collective-permute-start.1 = (f32[4,64,128]{2,1,0:T(8,128)S(1)}, f32[4,64,128]{2,1,0:T(8,128)S(1)}, u32[]{:S(2)}, u32[]{:S(2)}) collective-permute-start(f32[4,64,128]{2,1,0:T(8,128)S(1)} %fusion.83), channel_id=1, source_target_pairs={{0,8},{8,16},{16,24},{24,32},{32,40},{40,48},{48,56},{56,64},{64,7... | collective-permute-start | bytes 393224 | tf_op jit(solution)/shard_map/while/body/eval_jaxpr/ppermute | solution.py:18
  234.6 8.1 %collective-permute-start = (f32[4,64,128]{2,1,0:T(8,128)S(1)}, f32[4,64,128]{2,1,0:T(8,128)S(1)}, u32[]{:S(2)}, u32[]{:S(2)}) collective-permute-start(f32[4,64,128]{2,1,0:T(8,128)S(1)} %fusion.82), channel_id=1, source_target_pairs={{0,8},{8,16},{16,24},{24,32},{32,40},{40,48},{48,56},{56,64},{64,7... | collective-permute-start | bytes 393224 | tf_op jit(solution)/shard_map/while/body/eval_jaxpr/ppermute | solution.py:18
  234.9 9.1 %collective-permute-start.1 = (f32[4,64,128]{2,1,0:T(8,128)S(1)}, f32[4,64,128]{2,1,0:T(8,128)S(1)}, u32[]{:S(2)}, u32[]{:S(2)}) collective-permute-start(f32[4,64,128]{2,1,0:T(8,128)S(1)} %fusion.83), channel_id=1, source_target_pairs={{0,8},{8,16},{16,24},{24,32},{32,40},{40,48},{48,56},{56,64},{64,7... | collective-permute-start | bytes 393224 | tf_op jit(solution)/shard_map/while/body/eval_jaxpr/ppermute | solution.py:18
  247.5 8.1 %collective-permute-start = (f32[4,64,128]{2,1,0:T(8,128)S(1)}, f32[4,64,128]{2,1,0:T(8,128)S(1)}, u32[]{:S(2)}, u32[]{:S(2)}) collective-permute-start(f32[4,64,128]{2,1,0:T(8,128)S(1)} %fusion.82), channel_id=1, source_target_pairs={{0,8},{8,16},{16,24},{24,32},{32,40},{40,48},{48,56},{56,64},{64,7... | collective-permute-start | bytes 393224 | tf_op jit(solution)/shard_map/while/body/eval_jaxpr/ppermute | solution.py:18
  247.9 9.1 %collective-permute-start.1 = (f32[4,64,128]{2,1,0:T(8,128)S(1)}, f32[4,64,128]{2,1,0:T(8,128)S(1)}, u32[]{:S(2)}, u32[]{:S(2)}) collective-permute-start(f32[4,64,128]{2,1,0:T(8,128)S(1)} %fusion.83), channel_id=1, source_target_pairs={{0,8},{8,16},{16,24},{24,32},{32,40},{40,48},{48,56},{56,64},{64,7... | collective-permute-start | bytes 393224 | tf_op jit(solution)/shard_map/while/body/eval_jaxpr/ppermute | solution.py:18
  260.5 8.1 %collective-permute-start = (f32[4,64,128]{2,1,0:T(8,128)S(1)}, f32[4,64,128]{2,1,0:T(8,128)S(1)}, u32[]{:S(2)}, u32[]{:S(2)}) collective-permute-start(f32[4,64,128]{2,1,0:T(8,128)S(1)} %fusion.82), channel_id=1, source_target_pairs={{0,8},{8,16},{16,24},{24,32},{32,40},{40,48},{48,56},{56,64},{64,7... | collective-permute-start | bytes 393224 | tf_op jit(solution)/shard_map/while/body/eval_jaxpr/ppermute | solution.py:18
  260.9 9.1 %collective-permute-start.1 = (f32[4,64,128]{2,1,0:T(8,128)S(1)}, f32[4,64,128]{2,1,0:T(8,128)S(1)}, u32[]{:S(2)}, u32[]{:S(2)}) collective-permute-start(f32[4,64,128]{2,1,0:T(8,128)S(1)} %fusion.83), channel_id=1, source_target_pairs={{0,8},{8,16},{16,24},{24,32},{32,40},{40,48},{48,56},{56,64},{64,7... | collective-permute-start | bytes 393224 | tf_op jit(solution)/shard_map/while/body/eval_jaxpr/ppermute | solution.py:18
  273.5 8.1 %collective-permute-start = (f32[4,64,128]{2,1,0:T(8,128)S(1)}, f32[4,64,128]{2,1,0:T(8,128)S(1)}, u32[]{:S(2)}, u32[]{:S(2)}) collective-permute-start(f32[4,64,128]{2,1,0:T(8,128)S(1)} %fusion.82), channel_id=1, source_target_pairs={{0,8},{8,16},{16,24},{24,32},{32,40},{40,48},{48,56},{56,64},{64,7... | collective-permute-start | bytes 393224 | tf_op jit(solution)/shard_map/while/body/eval_jaxpr/ppermute | solution.py:18
  273.9 9.1 %collective-permute-start.1 = (f32[4,64,128]{2,1,0:T(8,128)S(1)}, f32[4,64,128]{2,1,0:T(8,128)S(1)}, u32[]{:S(2)}, u32[]{:S(2)}) collective-permute-start(f32[4,64,128]{2,1,0:T(8,128)S(1)} %fusion.83), channel_id=1, source_target_pairs={{0,8},{8,16},{16,24},{24,32},{32,40},{40,48},{48,56},{56,64},{64,7... | collective-permute-start | bytes 393224 | tf_op jit(solution)/shard_map/while/body/eval_jaxpr/ppermute | solution.py:18
  286.5 8.1 %collective-permute-start = (f32[4,64,128]{2,1,0:T(8,128)S(1)}, f32[4,64,128]{2,1,0:T(8,128)S(1)}, u32[]{:S(2)}, u32[]{:S(2)}) collective-permute-start(f32[4,64,128]{2,1,0:T(8,128)S(1)} %fusion.82), channel_id=1, source_target_pairs={{0,8},{8,16},{16,24},{24,32},{32,40},{40,48},{48,56},{56,64},{64,7... | collective-permute-start | bytes 393224 | tf_op jit(solution)/shard_map/while/body/eval_jaxpr/ppermute | solution.py:18
  286.9 9.1 %collective-permute-start.1 = (f32[4,64,128]{2,1,0:T(8,128)S(1)}, f32[4,64,128]{2,1,0:T(8,128)S(1)}, u32[]{:S(2)}, u32[]{:S(2)}) collective-permute-start(f32[4,64,128]{2,1,0:T(8,128)S(1)} %fusion.83), channel_id=1, source_target_pairs={{0,8},{8,16},{16,24},{24,32},{32,40},{40,48},{48,56},{56,64},{64,7... | collective-permute-start | bytes 393224 | tf_op jit(solution)/shard_map/while/body/eval_jaxpr/ppermute | solution.py:18
  299.4 8.1 %collective-permute-start = (f32[4,64,128]{2,1,0:T(8,128)S(1)}, f32[4,64,128]{2,1,0:T(8,128)S(1)}, u32[]{:S(2)}, u32[]{:S(2)}) collective-permute-start(f32[4,64,128]{2,1,0:T(8,128)S(1)} %fusion.82), channel_id=1, source_target_pairs={{0,8},{8,16},{16,24},{24,32},{32,40},{40,48},{48,56},{56,64},{64,7... | collective-permute-start | bytes 393224 | tf_op jit(solution)/shard_map/while/body/eval_jaxpr/ppermute | solution.py:18
  299.8 9.1 %collective-permute-start.1 = (f32[4,64,128]{2,1,0:T(8,128)S(1)}, f32[4,64,128]{2,1,0:T(8,128)S(1)}, u32[]{:S(2)}, u32[]{:S(2)}) collective-permute-start(f32[4,64,128]{2,1,0:T(8,128)S(1)} %fusion.83), channel_id=1, source_target_pairs={{0,8},{8,16},{16,24},{24,32},{32,40},{40,48},{48,56},{56,64},{64,7... | collective-permute-start | bytes 393224 | tf_op jit(solution)/shard_map/while/body/eval_jaxpr/ppermute | solution.py:18
  312.4 8.1 %collective-permute-start = (f32[4,64,128]{2,1,0:T(8,128)S(1)}, f32[4,64,128]{2,1,0:T(8,128)S(1)}, u32[]{:S(2)}, u32[]{:S(2)}) collective-permute-start(f32[4,64,128]{2,1,0:T(8,128)S(1)} %fusion.82), channel_id=1, source_target_pairs={{0,8},{8,16},{16,24},{24,32},{32,40},{40,48},{48,56},{56,64},{64,7... | collective-permute-start | bytes 393224 | tf_op jit(solution)/shard_map/while/body/eval_jaxpr/ppermute | solution.py:18
  312.8 9.1 %collective-permute-start.1 = (f32[4,64,128]{2,1,0:T(8,128)S(1)}, f32[4,64,128]{2,1,0:T(8,128)S(1)}, u32[]{:S(2)}, u32[]{:S(2)}) collective-permute-start(f32[4,64,128]{2,1,0:T(8,128)S(1)} %fusion.83), channel_id=1, source_target_pairs={{0,8},{8,16},{16,24},{24,32},{32,40},{40,48},{48,56},{56,64},{64,7... | collective-permute-start | bytes 393224 | tf_op jit(solution)/shard_map/while/body/eval_jaxpr/ppermute | solution.py:18
  325.4 8.1 %collective-permute-start = (f32[4,64,128]{2,1,0:T(8,128)S(1)}, f32[4,64,128]{2,1,0:T(8,128)S(1)}, u32[]{:S(2)}, u32[]{:S(2)}) collective-permute-start(f32[4,64,128]{2,1,0:T(8,128)S(1)} %fusion.82), channel_id=1, source_target_pairs={{0,8},{8,16},{16,24},{24,32},{32,40},{40,48},{48,56},{56,64},{64,7... | collective-permute-start | bytes 393224 | tf_op jit(solution)/shard_map/while/body/eval_jaxpr/ppermute | solution.py:18
  325.8 9.1 %collective-permute-start.1 = (f32[4,64,128]{2,1,0:T(8,128)S(1)}, f32[4,64,128]{2,1,0:T(8,128)S(1)}, u32[]{:S(2)}, u32[]{:S(2)}) collective-permute-start(f32[4,64,128]{2,1,0:T(8,128)S(1)} %fusion.83), channel_id=1, source_target_pairs={{0,8},{8,16},{16,24},{24,32},{32,40},{40,48},{48,56},{56,64},{64,7... | collective-permute-start | bytes 393224 | tf_op jit(solution)/shard_map/while/body/eval_jaxpr/ppermute | solution.py:18
  338.4 8.1 %collective-permute-start = (f32[4,64,128]{2,1,0:T(8,128)S(1)}, f32[4,64,128]{2,1,0:T(8,128)S(1)}, u32[]{:S(2)}, u32[]{:S(2)}) collective-permute-start(f32[4,64,128]{2,1,0:T(8,128)S(1)} %fusion.82), channel_id=1, source_target_pairs={{0,8},{8,16},{16,24},{24,32},{32,40},{40,48},{48,56},{56,64},{64,7... | collective-permute-start | bytes 393224 | tf_op jit(solution)/shard_map/while/body/eval_jaxpr/ppermute | solution.py:18
  338.8 9.1 %collective-permute-start.1 = (f32[4,64,128]{2,1,0:T(8,128)S(1)}, f32[4,64,128]{2,1,0:T(8,128)S(1)}, u32[]{:S(2)}, u32[]{:S(2)}) collective-permute-start(f32[4,64,128]{2,1,0:T(8,128)S(1)} %fusion.83), channel_id=1, source_target_pairs={{0,8},{8,16},{16,24},{24,32},{32,40},{40,48},{48,56},{56,64},{64,7... | collective-permute-start | bytes 393224 | tf_op jit(solution)/shard_map/while/body/eval_jaxpr/ppermute | solution.py:18
  351.4 8.1 %collective-permute-start = (f32[4,64,128]{2,1,0:T(8,128)S(1)}, f32[4,64,128]{2,1,0:T(8,128)S(1)}, u32[]{:S(2)}, u32[]{:S(2)}) collective-permute-start(f32[4,64,128]{2,1,0:T(8,128)S(1)} %fusion.82), channel_id=1, source_target_pairs={{0,8},{8,16},{16,24},{24,32},{32,40},{40,48},{48,56},{56,64},{64,7... | collective-permute-start | bytes 393224 | tf_op jit(solution)/shard_map/while/body/eval_jaxpr/ppermute | solution.py:18
  351.7 9.1 %collective-permute-start.1 = (f32[4,64,128]{2,1,0:T(8,128)S(1)}, f32[4,64,128]{2,1,0:T(8,128)S(1)}, u32[]{:S(2)}, u32[]{:S(2)}) collective-permute-start(f32[4,64,128]{2,1,0:T(8,128)S(1)} %fusion.83), channel_id=1, source_target_pairs={{0,8},{8,16},{16,24},{24,32},{32,40},{40,48},{48,56},{56,64},{64,7... | collective-permute-start | bytes 393224 | tf_op jit(solution)/shard_map/while/body/eval_jaxpr/ppermute | solution.py:18
  364.3 8.1 %collective-permute-start = (f32[4,64,128]{2,1,0:T(8,128)S(1)}, f32[4,64,128]{2,1,0:T(8,128)S(1)}, u32[]{:S(2)}, u32[]{:S(2)}) collective-permute-start(f32[4,64,128]{2,1,0:T(8,128)S(1)} %fusion.82), channel_id=1, source_target_pairs={{0,8},{8,16},{16,24},{24,32},{32,40},{40,48},{48,56},{56,64},{64,7... | collective-permute-start | bytes 393224 | tf_op jit(solution)/shard_map/while/body/eval_jaxpr/ppermute | solution.py:18
  364.7 9.1 %collective-permute-start.1 = (f32[4,64,128]{2,1,0:T(8,128)S(1)}, f32[4,64,128]{2,1,0:T(8,128)S(1)}, u32[]{:S(2)}, u32[]{:S(2)}) collective-permute-start(f32[4,64,128]{2,1,0:T(8,128)S(1)} %fusion.83), channel_id=1, source_target_pairs={{0,8},{8,16},{16,24},{24,32},{32,40},{40,48},{48,56},{56,64},{64,7... | collective-permute-start | bytes 393224 | tf_op jit(solution)/shard_map/while/body/eval_jaxpr/ppermute | solution.py:18
  377.3 8.1 %collective-permute-start = (f32[4,64,128]{2,1,0:T(8,128)S(1)}, f32[4,64,128]{2,1,0:T(8,128)S(1)}, u32[]{:S(2)}, u32[]{:S(2)}) collective-permute-start(f32[4,64,128]{2,1,0:T(8,128)S(1)} %fusion.82), channel_id=1, source_target_pairs={{0,8},{8,16},{16,24},{24,32},{32,40},{40,48},{48,56},{56,64},{64,7... | collective-permute-start | bytes 393224 | tf_op jit(solution)/shard_map/while/body/eval_jaxpr/ppermute | solution.py:18
  377.7 9.1 %collective-permute-start.1 = (f32[4,64,128]{2,1,0:T(8,128)S(1)}, f32[4,64,128]{2,1,0:T(8,128)S(1)}, u32[]{:S(2)}, u32[]{:S(2)}) collective-permute-start(f32[4,64,128]{2,1,0:T(8,128)S(1)} %fusion.83), channel_id=1, source_target_pairs={{0,8},{8,16},{16,24},{24,32},{32,40},{40,48},{48,56},{56,64},{64,7... | collective-permute-start | bytes 393224 | tf_op jit(solution)/shard_map/while/body/eval_jaxpr/ppermute | solution.py:18
  390.3 8.1 %collective-permute-start = (f32[4,64,128]{2,1,0:T(8,128)S(1)}, f32[4,64,128]{2,1,0:T(8,128)S(1)}, u32[]{:S(2)}, u32[]{:S(2)}) collective-permute-start(f32[4,64,128]{2,1,0:T(8,128)S(1)} %fusion.82), channel_id=1, source_target_pairs={{0,8},{8,16},{16,24},{24,32},{32,40},{40,48},{48,56},{56,64},{64,7... | collective-permute-start | bytes 393224 | tf_op jit(solution)/shard_map/while/body/eval_jaxpr/ppermute | solution.py:18
  390.7 9.1 %collective-permute-start.1 = (f32[4,64,128]{2,1,0:T(8,128)S(1)}, f32[4,64,128]{2,1,0:T(8,128)S(1)}, u32[]{:S(2)}, u32[]{:S(2)}) collective-permute-start(f32[4,64,128]{2,1,0:T(8,128)S(1)} %fusion.83), channel_id=1, source_target_pairs={{0,8},{8,16},{16,24},{24,32},{32,40},{40,48},{48,56},{56,64},{64,7... | collective-permute-start | bytes 393224 | tf_op jit(solution)/shard_map/while/body/eval_jaxpr/ppermute | solution.py:18
  403.3 8.1 %collective-permute-start = (f32[4,64,128]{2,1,0:T(8,128)S(1)}, f32[4,64,128]{2,1,0:T(8,128)S(1)}, u32[]{:S(2)}, u32[]{:S(2)}) collective-permute-start(f32[4,64,128]{2,1,0:T(8,128)S(1)} %fusion.82), channel_id=1, source_target_pairs={{0,8},{8,16},{16,24},{24,32},{32,40},{40,48},{48,56},{56,64},{64,7... | collective-permute-start | bytes 393224 | tf_op jit(solution)/shard_map/while/body/eval_jaxpr/ppermute | solution.py:18
  403.6 9.1 %collective-permute-start.1 = (f32[4,64,128]{2,1,0:T(8,128)S(1)}, f32[4,64,128]{2,1,0:T(8,128)S(1)}, u32[]{:S(2)}, u32[]{:S(2)}) collective-permute-start(f32[4,64,128]{2,1,0:T(8,128)S(1)} %fusion.83), channel_id=1, source_target_pairs={{0,8},{8,16},{16,24},{24,32},{32,40},{40,48},{48,56},{56,64},{64,7... | collective-permute-start | bytes 393224 | tf_op jit(solution)/shard_map/while/body/eval_jaxpr/ppermute | solution.py:18
  416.2 8.1 %collective-permute-start = (f32[4,64,128]{2,1,0:T(8,128)S(1)}, f32[4,64,128]{2,1,0:T(8,128)S(1)}, u32[]{:S(2)}, u32[]{:S(2)}) collective-permute-start(f32[4,64,128]{2,1,0:T(8,128)S(1)} %fusion.82), channel_id=1, source_target_pairs={{0,8},{8,16},{16,24},{24,32},{32,40},{40,48},{48,56},{56,64},{64,7... | collective-permute-start | bytes 393224 | tf_op jit(solution)/shard_map/while/body/eval_jaxpr/ppermute | solution.py:18
  416.6 9.1 %collective-permute-start.1 = (f32[4,64,128]{2,1,0:T(8,128)S(1)}, f32[4,64,128]{2,1,0:T(8,128)S(1)}, u32[]{:S(2)}, u32[]{:S(2)}) collective-permute-start(f32[4,64,128]{2,1,0:T(8,128)S(1)} %fusion.83), channel_id=1, source_target_pairs={{0,8},{8,16},{16,24},{24,32},{32,40},{40,48},{48,56},{56,64},{64,7... | collective-permute-start | bytes 393224 | tf_op jit(solution)/shard_map/while/body/eval_jaxpr/ppermute | solution.py:18
  429.2 8.1 %collective-permute-start = (f32[4,64,128]{2,1,0:T(8,128)S(1)}, f32[4,64,128]{2,1,0:T(8,128)S(1)}, u32[]{:S(2)}, u32[]{:S(2)}) collective-permute-start(f32[4,64,128]{2,1,0:T(8,128)S(1)} %fusion.82), channel_id=1, source_target_pairs={{0,8},{8,16},{16,24},{24,32},{32,40},{40,48},{48,56},{56,64},{64,7... | collective-permute-start | bytes 393224 | tf_op jit(solution)/shard_map/while/body/eval_jaxpr/ppermute | solution.py:18
  429.6 9.1 %collective-permute-start.1 = (f32[4,64,128]{2,1,0:T(8,128)S(1)}, f32[4,64,128]{2,1,0:T(8,128)S(1)}, u32[]{:S(2)}, u32[]{:S(2)}) collective-permute-start(f32[4,64,128]{2,1,0:T(8,128)S(1)} %fusion.83), channel_id=1, source_target_pairs={{0,8},{8,16},{16,24},{24,32},{32,40},{40,48},{48,56},{56,64},{64,7... | collective-permute-start | bytes 393224 | tf_op jit(solution)/shard_map/while/body/eval_jaxpr/ppermute | solution.py:18
  442.2 8.1 %collective-permute-start = (f32[4,64,128]{2,1,0:T(8,128)S(1)}, f32[4,64,128]{2,1,0:T(8,128)S(1)}, u32[]{:S(2)}, u32[]{:S(2)}) collective-permute-start(f32[4,64,128]{2,1,0:T(8,128)S(1)} %fusion.82), channel_id=1, source_target_pairs={{0,8},{8,16},{16,24},{24,32},{32,40},{40,48},{48,56},{56,64},{64,7... | collective-permute-start | bytes 393224 | tf_op jit(solution)/shard_map/while/body/eval_jaxpr/ppermute | solution.py:18
  442.6 9.1 %collective-permute-start.1 = (f32[4,64,128]{2,1,0:T(8,128)S(1)}, f32[4,64,128]{2,1,0:T(8,128)S(1)}, u32[]{:S(2)}, u32[]{:S(2)}) collective-permute-start(f32[4,64,128]{2,1,0:T(8,128)S(1)} %fusion.83), channel_id=1, source_target_pairs={{0,8},{8,16},{16,24},{24,32},{32,40},{40,48},{48,56},{56,64},{64,7... | collective-permute-start | bytes 393224 | tf_op jit(solution)/shard_map/while/body/eval_jaxpr/ppermute | solution.py:18
  455.2 8.1 %collective-permute-start = (f32[4,64,128]{2,1,0:T(8,128)S(1)}, f32[4,64,128]{2,1,0:T(8,128)S(1)}, u32[]{:S(2)}, u32[]{:S(2)}) collective-permute-start(f32[4,64,128]{2,1,0:T(8,128)S(1)} %fusion.82), channel_id=1, source_target_pairs={{0,8},{8,16},{16,24},{24,32},{32,40},{40,48},{48,56},{56,64},{64,7... | collective-permute-start | bytes 393224 | tf_op jit(solution)/shard_map/while/body/eval_jaxpr/ppermute | solution.py:18
  455.5 9.1 %collective-permute-start.1 = (f32[4,64,128]{2,1,0:T(8,128)S(1)}, f32[4,64,128]{2,1,0:T(8,128)S(1)}, u32[]{:S(2)}, u32[]{:S(2)}) collective-permute-start(f32[4,64,128]{2,1,0:T(8,128)S(1)} %fusion.83), channel_id=1, source_target_pairs={{0,8},{8,16},{16,24},{24,32},{32,40},{40,48},{48,56},{56,64},{64,7... | collective-permute-start | bytes 393224 | tf_op jit(solution)/shard_map/while/body/eval_jaxpr/ppermute | solution.py:18
  468.1 8.1 %collective-permute-start = (f32[4,64,128]{2,1,0:T(8,128)S(1)}, f32[4,64,128]{2,1,0:T(8,128)S(1)}, u32[]{:S(2)}, u32[]{:S(2)}) collective-permute-start(f32[4,64,128]{2,1,0:T(8,128)S(1)} %fusion.82), channel_id=1, source_target_pairs={{0,8},{8,16},{16,24},{24,32},{32,40},{40,48},{48,56},{56,64},{64,7... | collective-permute-start | bytes 393224 | tf_op jit(solution)/shard_map/while/body/eval_jaxpr/ppermute | solution.py:18
  468.5 9.1 %collective-permute-start.1 = (f32[4,64,128]{2,1,0:T(8,128)S(1)}, f32[4,64,128]{2,1,0:T(8,128)S(1)}, u32[]{:S(2)}, u32[]{:S(2)}) collective-permute-start(f32[4,64,128]{2,1,0:T(8,128)S(1)} %fusion.83), channel_id=1, source_target_pairs={{0,8},{8,16},{16,24},{24,32},{32,40},{40,48},{48,56},{56,64},{64,7... | collective-permute-start | bytes 393224 | tf_op jit(solution)/shard_map/while/body/eval_jaxpr/ppermute | solution.py:18
  481.1 8.1 %collective-permute-start = (f32[4,64,128]{2,1,0:T(8,128)S(1)}, f32[4,64,128]{2,1,0:T(8,128)S(1)}, u32[]{:S(2)}, u32[]{:S(2)}) collective-permute-start(f32[4,64,128]{2,1,0:T(8,128)S(1)} %fusion.82), channel_id=1, source_target_pairs={{0,8},{8,16},{16,24},{24,32},{32,40},{40,48},{48,56},{56,64},{64,7... | collective-permute-start | bytes 393224 | tf_op jit(solution)/shard_map/while/body/eval_jaxpr/ppermute | solution.py:18
  481.5 9.1 %collective-permute-start.1 = (f32[4,64,128]{2,1,0:T(8,128)S(1)}, f32[4,64,128]{2,1,0:T(8,128)S(1)}, u32[]{:S(2)}, u32[]{:S(2)}) collective-permute-start(f32[4,64,128]{2,1,0:T(8,128)S(1)} %fusion.83), channel_id=1, source_target_pairs={{0,8},{8,16},{16,24},{24,32},{32,40},{40,48},{48,56},{56,64},{64,7... | collective-permute-start | bytes 393224 | tf_op jit(solution)/shard_map/while/body/eval_jaxpr/ppermute | solution.py:18
  494.1 8.1 %collective-permute-start = (f32[4,64,128]{2,1,0:T(8,128)S(1)}, f32[4,64,128]{2,1,0:T(8,128)S(1)}, u32[]{:S(2)}, u32[]{:S(2)}) collective-permute-start(f32[4,64,128]{2,1,0:T(8,128)S(1)} %fusion.82), channel_id=1, source_target_pairs={{0,8},{8,16},{16,24},{24,32},{32,40},{40,48},{48,56},{56,64},{64,7... | collective-permute-start | bytes 393224 | tf_op jit(solution)/shard_map/while/body/eval_jaxpr/ppermute | solution.py:18
  494.5 9.1 %collective-permute-start.1 = (f32[4,64,128]{2,1,0:T(8,128)S(1)}, f32[4,64,128]{2,1,0:T(8,128)S(1)}, u32[]{:S(2)}, u32[]{:S(2)}) collective-permute-start(f32[4,64,128]{2,1,0:T(8,128)S(1)} %fusion.83), channel_id=1, source_target_pairs={{0,8},{8,16},{16,24},{24,32},{32,40},{40,48},{48,56},{56,64},{64,7... | collective-permute-start | bytes 393224 | tf_op jit(solution)/shard_map/while/body/eval_jaxpr/ppermute | solution.py:18
  507.5 9.1 %collective-permute-start.1 = (f32[4,64,128]{2,1,0:T(8,128)S(1)}, f32[4,64,128]{2,1,0:T(8,128)S(1)}, u32[]{:S(2)}, u32[]{:S(2)}) collective-permute-start(f32[4,64,128]{2,1,0:T(8,128)S(1)} %fusion.83), channel_id=1, source_target_pairs={{0,8},{8,16},{16,24},{24,32},{32,40},{40,48},{48,56},{56,64},{64,7... | collective-permute-start | bytes 393224 | tf_op jit(solution)/shard_map/while/body/eval_jaxpr/ppermute | solution.py:18
  520.4 9.1 %collective-permute-start.1 = (f32[4,64,128]{2,1,0:T(8,128)S(1)}, f32[4,64,128]{2,1,0:T(8,128)S(1)}, u32[]{:S(2)}, u32[]{:S(2)}) collective-permute-start(f32[4,64,128]{2,1,0:T(8,128)S(1)} %fusion.83), channel_id=1, source_target_pairs={{0,8},{8,16},{16,24},{24,32},{32,40},{40,48},{48,56},{56,64},{64,7... | collective-permute-start | bytes 393224 | tf_op jit(solution)/shard_map/while/body/eval_jaxpr/ppermute | solution.py:18
  533.4 9.1 %collective-permute-start.1 = (f32[4,64,128]{2,1,0:T(8,128)S(1)}, f32[4,64,128]{2,1,0:T(8,128)S(1)}, u32[]{:S(2)}, u32[]{:S(2)}) collective-permute-start(f32[4,64,128]{2,1,0:T(8,128)S(1)} %fusion.83), channel_id=1, source_target_pairs={{0,8},{8,16},{16,24},{24,32},{32,40},{40,48},{48,56},{56,64},{64,7... | collective-permute-start | bytes 393224 | tf_op jit(solution)/shard_map/while/body/eval_jaxpr/ppermute | solution.py:18
  546.4 9.1 %collective-permute-start.1 = (f32[4,64,128]{2,1,0:T(8,128)S(1)}, f32[4,64,128]{2,1,0:T(8,128)S(1)}, u32[]{:S(2)}, u32[]{:S(2)}) collective-permute-start(f32[4,64,128]{2,1,0:T(8,128)S(1)} %fusion.83), channel_id=1, source_target_pairs={{0,8},{8,16},{16,24},{24,32},{32,40},{40,48},{48,56},{56,64},{64,7... | collective-permute-start | bytes 393224 | tf_op jit(solution)/shard_map/while/body/eval_jaxpr/ppermute | solution.py:18
  559.4 9.1 %collective-permute-start.1 = (f32[4,64,128]{2,1,0:T(8,128)S(1)}, f32[4,64,128]{2,1,0:T(8,128)S(1)}, u32[]{:S(2)}, u32[]{:S(2)}) collective-permute-start(f32[4,64,128]{2,1,0:T(8,128)S(1)} %fusion.83), channel_id=1, source_target_pairs={{0,8},{8,16},{16,24},{24,32},{32,40},{40,48},{48,56},{56,64},{64,7... | collective-permute-start | bytes 393224 | tf_op jit(solution)/shard_map/while/body/eval_jaxpr/ppermute | solution.py:18
  572.0 8.1 %collective-permute-start = (f32[4,64,128]{2,1,0:T(8,128)S(1)}, f32[4,64,128]{2,1,0:T(8,128)S(1)}, u32[]{:S(2)}, u32[]{:S(2)}) collective-permute-start(f32[4,64,128]{2,1,0:T(8,128)S(1)} %fusion.82), channel_id=1, source_target_pairs={{0,8},{8,16},{16,24},{24,32},{32,40},{40,48},{48,56},{56,64},{64,7... | collective-permute-start | bytes 393224 | tf_op jit(solution)/shard_map/while/body/eval_jaxpr/ppermute | solution.py:18
  572.3 9.1 %collective-permute-start.1 = (f32[4,64,128]{2,1,0:T(8,128)S(1)}, f32[4,64,128]{2,1,0:T(8,128)S(1)}, u32[]{:S(2)}, u32[]{:S(2)}) collective-permute-start(f32[4,64,128]{2,1,0:T(8,128)S(1)} %fusion.83), channel_id=1, source_target_pairs={{0,8},{8,16},{16,24},{24,32},{32,40},{40,48},{48,56},{56,64},{64,7... | collective-permute-start | bytes 393224 | tf_op jit(solution)/shard_map/while/body/eval_jaxpr/ppermute | solution.py:18
  584.9 8.1 %collective-permute-start = (f32[4,64,128]{2,1,0:T(8,128)S(1)}, f32[4,64,128]{2,1,0:T(8,128)S(1)}, u32[]{:S(2)}, u32[]{:S(2)}) collective-permute-start(f32[4,64,128]{2,1,0:T(8,128)S(1)} %fusion.82), channel_id=1, source_target_pairs={{0,8},{8,16},{16,24},{24,32},{32,40},{40,48},{48,56},{56,64},{64,7... | collective-permute-start | bytes 393224 | tf_op jit(solution)/shard_map/while/body/eval_jaxpr/ppermute | solution.py:18
  585.3 9.1 %collective-permute-start.1 = (f32[4,64,128]{2,1,0:T(8,128)S(1)}, f32[4,64,128]{2,1,0:T(8,128)S(1)}, u32[]{:S(2)}, u32[]{:S(2)}) collective-permute-start(f32[4,64,128]{2,1,0:T(8,128)S(1)} %fusion.83), channel_id=1, source_target_pairs={{0,8},{8,16},{16,24},{24,32},{32,40},{40,48},{48,56},{56,64},{64,7... | collective-permute-start | bytes 393224 | tf_op jit(solution)/shard_map/while/body/eval_jaxpr/ppermute | solution.py:18
  597.9 8.1 %collective-permute-start = (f32[4,64,128]{2,1,0:T(8,128)S(1)}, f32[4,64,128]{2,1,0:T(8,128)S(1)}, u32[]{:S(2)}, u32[]{:S(2)}) collective-permute-start(f32[4,64,128]{2,1,0:T(8,128)S(1)} %fusion.82), channel_id=1, source_target_pairs={{0,8},{8,16},{16,24},{24,32},{32,40},{40,48},{48,56},{56,64},{64,7... | collective-permute-start | bytes 393224 | tf_op jit(solution)/shard_map/while/body/eval_jaxpr/ppermute | solution.py:18
  598.3 9.1 %collective-permute-start.1 = (f32[4,64,128]{2,1,0:T(8,128)S(1)}, f32[4,64,128]{2,1,0:T(8,128)S(1)}, u32[]{:S(2)}, u32[]{:S(2)}) collective-permute-start(f32[4,64,128]{2,1,0:T(8,128)S(1)} %fusion.83), channel_id=1, source_target_pairs={{0,8},{8,16},{16,24},{24,32},{32,40},{40,48},{48,56},{56,64},{64,7... | collective-permute-start | bytes 393224 | tf_op jit(solution)/shard_map/while/body/eval_jaxpr/ppermute | solution.py:18
  610.9 8.1 %collective-permute-start = (f32[4,64,128]{2,1,0:T(8,128)S(1)}, f32[4,64,128]{2,1,0:T(8,128)S(1)}, u32[]{:S(2)}, u32[]{:S(2)}) collective-permute-start(f32[4,64,128]{2,1,0:T(8,128)S(1)} %fusion.82), channel_id=1, source_target_pairs={{0,8},{8,16},{16,24},{24,32},{32,40},{40,48},{48,56},{56,64},{64,7... | collective-permute-start | bytes 393224 | tf_op jit(solution)/shard_map/while/body/eval_jaxpr/ppermute | solution.py:18
  611.3 9.1 %collective-permute-start.1 = (f32[4,64,128]{2,1,0:T(8,128)S(1)}, f32[4,64,128]{2,1,0:T(8,128)S(1)}, u32[]{:S(2)}, u32[]{:S(2)}) collective-permute-start(f32[4,64,128]{2,1,0:T(8,128)S(1)} %fusion.83), channel_id=1, source_target_pairs={{0,8},{8,16},{16,24},{24,32},{32,40},{40,48},{48,56},{56,64},{64,7... | collective-permute-start | bytes 393224 | tf_op jit(solution)/shard_map/while/body/eval_jaxpr/ppermute | solution.py:18
  623.9 8.1 %collective-permute-start = (f32[4,64,128]{2,1,0:T(8,128)S(1)}, f32[4,64,128]{2,1,0:T(8,128)S(1)}, u32[]{:S(2)}, u32[]{:S(2)}) collective-permute-start(f32[4,64,128]{2,1,0:T(8,128)S(1)} %fusion.82), channel_id=1, source_target_pairs={{0,8},{8,16},{16,24},{24,32},{32,40},{40,48},{48,56},{56,64},{64,7... | collective-permute-start | bytes 393224 | tf_op jit(solution)/shard_map/while/body/eval_jaxpr/ppermute | solution.py:18
  624.2 9.1 %collective-permute-start.1 = (f32[4,64,128]{2,1,0:T(8,128)S(1)}, f32[4,64,128]{2,1,0:T(8,128)S(1)}, u32[]{:S(2)}, u32[]{:S(2)}) collective-permute-start(f32[4,64,128]{2,1,0:T(8,128)S(1)} %fusion.83), channel_id=1, source_target_pairs={{0,8},{8,16},{16,24},{24,32},{32,40},{40,48},{48,56},{56,64},{64,7... | collective-permute-start | bytes 393224 | tf_op jit(solution)/shard_map/while/body/eval_jaxpr/ppermute | solution.py:18
  634.1 10.8 %all-to-all-start.2 = ((bf16[4,64,128]{2,0,1:T(4,128)(2,1)}), bf16[4,64,128]{2,0,1:T(4,128)(2,1)S(1)}, u32[]{:S(2)}, u32[]{:S(2)}) async-start(bf16[4,64,128]{2,0,1:T(4,128)(2,1)} %copy.79), calls=%async_computation.2 | async-start | bytes 131072 | tf_op jit(solution)/shard_map/all_to_all | solution.py:149
  644.9 10.6 %all-to-all-start.1 = ((bf16[4,64,128]{2,0,1:T(4,128)(2,1)}), bf16[4,64,128]{2,0,1:T(4,128)(2,1)S(1)}, u32[]{:S(2)}, u32[]{:S(2)}) async-start(bf16[4,64,128]{2,0,1:T(4,128)(2,1)} %copy.80), calls=%async_computation.1 | async-start | bytes 131072 | tf_op jit(solution)/shard_map/all_to_all | solution.py:148
  655.5 11.6 %all-to-all-start = ((bf16[4,64,1024]{2,0,1:T(4,128)(2,1)}), bf16[4,64,1024]{2,0,1:T(4,128)(2,1)S(1)}, u32[]{:S(2)}, u32[]{:S(2)}) async-start(bf16[4,64,1024]{2,0,1:T(4,128)(2,1)} %reshape.190), calls=%async_computation | async-start | bytes 1048576 | tf_op jit(solution)/shard_map/all_to_all | solution.py:147
  (11 other events, 107.4 us)
Sparse Core Ops, SparseCore 0:
  10.8 82.0 all-gather.6
  95.8 76.5 all-gather.4
where the time goes:
time: 680 us; the launch traced here: 675 us
  waiting for transfers between devices  339 us (50%)
  matrix products  182 us (27%)
  blocking collectives  80.9 us (12%)
  starting transfers between devices  20.6 us (3%)
  other arithmetic  20 us (3%)
  local copies, waits for them, and re-layouts  16.3 us (2%)
  between operations  14.2 us (2%)
    ppermute x64, waiting for transfers between devices, passed_along(): lax.ppermute(array, axis, [(i, (i + by) % count) for i in range(count)])  245 us
    all_gather x1, waiting for transfers between devices, on_device(): lax.all_gather(key_vectors, 'ctx', axis=1, tiled=True)  76.3 us
    dot_general x36, matrix products, block_scores(): jnp.einsum('tkgd,skd->kgts', query_four_axes, key_three, preferred_elemen...  62.8 us
    dot_general x32, matrix products, block_grads(): jnp.einsum('tkgd,skd->kgts', grad_four, value_three, preferred_element_ty...  47.2 us
    all_gather x1, blocking collectives, on_device(): lax.all_gather(segments, 'ctx', axis=1, tiled=True)  44 us
    dot_general x32, matrix products, block_grads(): jnp.einsum('kgts,skd->tkgd', score_low, key_three, preferred_element_type...  41.9 us
    all_gather x1, blocking collectives, on_device(): lax.all_gather(positions, 'ctx', axis=1, tiled=True)  37 us
    reduce_sum x4, other arithmetic, stats_update(): new_sum = running_sum * rescale + jnp.sum(weights, axis=-1, keepdims=True)  14.7 us
  transfers between devices with their start and end apart: 69, of which 69 were waited for; matrix products, arithmetic and copies ran while one was open for 9% of the time, Pallas kernels for 0%

commit v1 on v0

v1 whole, which is shorter than its diff:
```python
import functools
import math

import jax
import jax.numpy as jnp
from jax import lax
from jax.experimental import pallas as pl
from jax.experimental.pallas import tpu as pltpu
from jax.sharding import Mesh, PartitionSpec as P

QUERY_HEADS = 64
KEY_VALUE_HEADS = 8
HEAD_SIZE = 128
GROUP = QUERY_HEADS // KEY_VALUE_HEADS
NEG_BIG = -1e30
CODE_SPAN = 2048
META_ROWS = 16
SCALE = 1.0 / math.sqrt(HEAD_SIZE)
EXP2_SCALE = SCALE * math.log2(math.e)

NT = (((1,), (1,)), ((), ()))
NN = (((1,), (0,)), ((), ()))


def dot(a, b, dims):
    return lax.dot_general(a, b, dims, preferred_element_type=jnp.float32)


def attention_kernel(q_ref, do_ref, kv_ref, code_ref, low_ref, high_ref, dq_ref, dkv_ref,
                     bias_ref, kt_ref, s_ref, p_ref, dp_ref, acc_ref):
    blocks, sources, _, _ = kv_ref.shape
    row_count = dkv_ref.shape[2]
    chunk = sources * row_count
    keys = blocks * chunk
    rows = q_ref.shape[0] * q_ref.shape[1]

    for c in range(keys // 128):
        column = jnp.broadcast_to(code_ref[c:c + 1, :], (128, 128)).T
        for r in range(rows // 128):
            low = low_ref[:, r * 128:(r + 1) * 128]
            high = high_ref[:, r * 128:(r + 1) * 128]
            allowed = (column >= low) & (column <= high)
            bias_ref[c * 128:(c + 1) * 128, r * 128:(r + 1) * 128] = jnp.where(allowed, 0.0, NEG_BIG)
    for b in range(blocks):
        key_block = kv_ref[b, :, 0:row_count, 0:HEAD_SIZE].reshape(chunk, HEAD_SIZE)
        kt_ref[:, b * chunk:(b + 1) * chunk] = key_block.T
    acc_ref[...] = jnp.zeros_like(acc_ref)

    def head(h, carry):
        lanes = pl.ds(pl.multiple_of(h * HEAD_SIZE, HEAD_SIZE), HEAD_SIZE)
        q = q_ref[:, :, lanes].reshape(rows, HEAD_SIZE)
        do = do_ref[:, :, lanes].reshape(rows, HEAD_SIZE)
        top = jnp.full((8, rows), NEG_BIG, jnp.float32)
        for b in range(blocks):
            part = slice(b * chunk, (b + 1) * chunk)
            key_block = kv_ref[b, :, 0:row_count, 0:HEAD_SIZE].reshape(chunk, HEAD_SIZE)
            s = dot(key_block, q, NT) + bias_ref[part, :]
            s_ref[part, :] = s
            top = jnp.maximum(top, jnp.max(s.reshape(chunk // 8, 8, rows), axis=0))
        top = jnp.max(top, axis=0, keepdims=True) * EXP2_SCALE
        total = jnp.zeros((8, rows), jnp.float32)
        cross = jnp.zeros((8, rows), jnp.float32)
        for b in range(blocks):
            part = slice(b * chunk, (b + 1) * chunk)
            value_block = kv_ref[b, :, 0:row_count, HEAD_SIZE:2 * HEAD_SIZE].reshape(chunk, HEAD_SIZE)
            p = jnp.exp2(s_ref[part, :] * EXP2_SCALE - top)
            dp = dot(value_block, do, NT)
            total = total + jnp.sum(p.reshape(chunk // 8, 8, rows), axis=0)
            cross = cross + jnp.sum((p * dp).reshape(chunk // 8, 8, rows), axis=0)
            p_ref[part, :] = p
            dp_ref[part, :] = dp
        inverse = 1.0 / jnp.sum(total, axis=0, keepdims=True)
        delta = jnp.sum(cross, axis=0, keepdims=True) * inverse
        dqt = jnp.zeros((HEAD_SIZE, rows), jnp.float32)
        for b in range(blocks):
            part = slice(b * chunk, (b + 1) * chunk)
            p = p_ref[part, :] * inverse
            ds = (p * (dp_ref[part, :] - delta)).astype(jnp.bfloat16)
            acc_ref[part, HEAD_SIZE:2 * HEAD_SIZE] += dot(p.astype(jnp.bfloat16), do, NN)
            acc_ref[part, 0:HEAD_SIZE] += dot(ds, q, NN)
            dqt = dqt + dot(kt_ref[:, part], ds, NN)
        dq_ref[:, :, lanes] = (dqt * SCALE).T.astype(jnp.bfloat16).reshape(dq_ref.shape[0], row_count, HEAD_SIZE)
        return carry

    lax.fori_loop(0, GROUP, head, 0)
    for b in range(blocks):
        part = slice(b * chunk, (b + 1) * chunk)
        shape = (sources, row_count, HEAD_SIZE)
        dkv_ref[b, :, :, 0:HEAD_SIZE] = (acc_ref[part, 0:HEAD_SIZE] * SCALE).astype(jnp.bfloat16).reshape(shape)
        dkv_ref[b, :, :, HEAD_SIZE:2 * HEAD_SIZE] = acc_ref[part, HEAD_SIZE:2 * HEAD_SIZE].astype(jnp.bfloat16).reshape(shape)


def attention(q, do, kv, code, low, high):
    blocks, sources, _, width = kv.shape
    row_count = q.shape[1]
    rows = q.shape[0] * row_count
    keys = blocks * sources * row_count
    vmem = pl.BlockSpec(memory_space=pltpu.VMEM)
    return pl.pallas_call(
        attention_kernel,
        out_shape=(
            jax.ShapeDtypeStruct(q.shape, jnp.bfloat16),
            jax.ShapeDtypeStruct((blocks, sources, row_count, width), jnp.bfloat16),
        ),
        in_specs=[vmem] * 6,
        out_specs=(vmem, vmem),
        scratch_shapes=[
            pltpu.VMEM((keys, rows), jnp.float32),
            pltpu.VMEM((HEAD_SIZE, keys), jnp.bfloat16),
            pltpu.VMEM((keys, rows), jnp.float32),
            pltpu.VMEM((keys, rows), jnp.float32),
            pltpu.VMEM((keys, rows), jnp.float32),
            pltpu.VMEM((keys, width), jnp.float32),
        ],
        compiler_params=pltpu.CompilerParams(vmem_limit_bytes=48 * 1024 * 1024),
        cost_estimate=pl.CostEstimate(
            flops=10 * keys * rows * HEAD_SIZE * GROUP, bytes_accessed=4 * 1024 * 1024,
            transcendentals=keys * rows * GROUP),
    )(q, do, kv, code, low, high)


PLANE = ("xh", "core")
FINAL = ("xh", "core", "y", "xl")


def on_device(queries, key_vectors, value_vectors, output_gradient, positions, segments):
    window_count, row_count, _ = queries.shape
    code = segments * CODE_SPAN + positions
    meta = jnp.concatenate([code // 128, code % 128], axis=1).astype(jnp.bfloat16)
    meta = jnp.pad(meta[:, None, :], ((0, 0), (0, META_ROWS - 1), (0, 2 * HEAD_SIZE - 2 * row_count)))
    packed = jnp.concatenate([jnp.concatenate([key_vectors, value_vectors], axis=2), meta], axis=1)
    mine = lax.all_to_all(packed, PLANE, split_axis=0, concat_axis=0, tiled=True)
    gathered = lax.all_gather(mine, "z", axis=0, tiled=False)
    q = lax.all_to_all(queries, PLANE, split_axis=0, concat_axis=0, tiled=True)
    do = lax.all_to_all(output_gradient, PLANE, split_axis=0, concat_axis=0, tiled=True)

    def decode(rows):
        return rows[..., 0:row_count].astype(jnp.float32) * 128.0 + rows[..., row_count:2 * row_count].astype(jnp.float32)

    key_code = decode(gathered[:, :, row_count, :]).reshape(-1, 128)
    high = decode(mine[:, row_count, :]).reshape(1, -1)
    low = jnp.floor(high * (1.0 / CODE_SPAN)) * CODE_SPAN
    dq, dkv = attention(q, do, gathered, key_code, low, high)

    parts = lax.all_to_all(dkv, "z", split_axis=0, concat_axis=0, tiled=True)
    dkv_own = jnp.sum(parts.astype(jnp.float32), axis=0).astype(jnp.bfloat16)
    heads = KEY_VALUE_HEADS
    out_rows = row_count // heads
    dq_final = lax.all_to_all(dq.reshape(window_count * heads, out_rows, GROUP * HEAD_SIZE), FINAL, 0, 0, tiled=True)
    dkv_final = lax.all_to_all(dkv_own.reshape(window_count * heads, out_rows, 2 * HEAD_SIZE), FINAL, 0, 0, tiled=True)

    def merged(array):
        width = array.shape[-1]
        return array.reshape(window_count, heads, out_rows, width).transpose(0, 2, 1, 3).reshape(window_count, out_rows, heads * width)

    return (
        merged(dq_final),
        merged(dkv_final[..., 0:HEAD_SIZE]),
        merged(dkv_final[..., HEAD_SIZE:2 * HEAD_SIZE]),
    )


def solution(mesh):
    fine = Mesh(mesh.devices.reshape(2, 8, 2, 4, 2), ("xh", "z", "core", "y", "xl"))
    ctx, head = ("xh", "z", "core"), ("y", "xl")
    vectors = P(None, ctx, head)
    out = P(None, ctx + head, None)
    return jax.shard_map(
        on_device,
        mesh=fine,
        in_specs=(vectors, vectors, vectors, vectors, P(None, ctx), P(None, ctx)),
        out_specs=(out, out, out),
        check_vma=False,
    )
```

time: 680 us -> 151 us (0.22)
  the two profiles are of different devices: /device:TPU:2 before, /device:TPU:1 now
where the time goes in v1:
time: 151 us
  waiting for transfers between devices  44 us (29%)
  blocking collectives  39.3 us (26%)
  starting transfers between devices  26.5 us (18%)
  Pallas kernels  19.6 us (13%)
  between operations  14.1 us (9%)
  local copies, waits for them, and re-layouts  4.61 us (3%)
  other arithmetic  2.65 us (2%)
    all_to_all x1, blocking collectives, on_device(): parts = lax.all_to_all(dkv, 'z', split_axis=0, concat_axis=0, tiled=True)  27.1 us
    pallas_call x1, Pallas kernels, attention(): pl.pallas_call(attention_kernel, out_shape=(jax.ShapeDtypeStruct(q.shape,...  19.6 us
    all_gather x1, waiting for transfers between devices, on_device(): gathered = lax.all_gather(mine, 'z', axis=0, tiled=False)  17.4 us
    all_to_all x1, starting transfers between devices, on_device(): lax.all_to_all(dq.reshape(window_count * heads, out_rows, GROUP * HEAD_SI...  13.6 us
    all_to_all x1, blocking collectives, on_device(): lax.all_to_all(packed, PLANE, split_axis=0, concat_axis=0, tiled=True)  12.2 us
    all_to_all x1, waiting for transfers between devices, on_device(): lax.all_to_all(dq.reshape(window_count * heads, out_rows, GROUP * HEAD_SI...  10.3 us
    all_to_all x1, waiting for transfers between devices, on_device(): q = lax.all_to_all(queries, PLANE, split_axis=0, concat_axis=0, tiled=True)  8.59 us
    all_to_all x1, waiting for transfers between devices, on_device(): lax.all_to_all(dkv_own.reshape(window_count * heads, out_rows, 2 * HEAD_S...  7.72 us
  transfers between devices with their start and end apart: 5, of which 4 were waited for; matrix products, arithmetic and copies ran while one was open for 2% of the time, Pallas kernels for 0%

profile of v1, /device:TPU:1, one launch (start us, length us, event | category | flops | bytes accessed | tf_op | source)
XLA Modules:
  0.0 150.7 jit_solution(5520331624298151589)
XLA Ops:
  7.2 0.0 all-gather.3.cloned.1.call-start
  7.2 0.7 fusion.6
  7.9 0.1 pad_maximum_fusion
  8.0 0.9 fusion.1
  8.9 12.2 %all_to_all.30 = bf16[4,80,256]{2,1,0:T(8,128)(2,1)} all-to-all(bf16[4,80,256]{2,1,0:T(8,128)(2,1)S(1)} %fusion.1), channel_id=1, replica_groups=mesh['xh'=2,'z'=8,'core'=2,'y'=4,'xl'=2] {'xh','core'}, dimensions={0} | all-to-all | bytes 327680 | tf_op jit(solution)/shard_map/all_to_all | solution.py:132
  21.1 0.0 all-gather.3.cloned.1.call-update
  21.1 4.0 %all-to-all-start = ((bf16[4,64,1024]{2,1,0:T(8,128)(2,1)}), bf16[4,64,1024]{2,1,0:T(8,128)(2,1)S(1)}, u32[]{:S(2)}, u32[]{:S(2)}) async-start(bf16[4,64,1024]{2,1,0:T(8,128)(2,1)} %param.6), calls=%async_computation | async-start | bytes 1048576 | tf_op jit(solution)/shard_map/all_to_all | solution.py:134
  25.2 0.7 slice.35
  25.9 0.1 convert_add_fusion.1
  26.0 0.1 reshape.88.high_ref
  26.1 8.6 %all-to-all-done.q_ref = bf16[4,64,1024]{2,1,0:T(8,128)(2,1)S(1)} async-done(((bf16[4,64,1024]{2,1,0:T(8,128)(2,1)}), bf16[4,64,1024]{2,1,0:T(8,128)(2,1)S(1)}, u32[]{:S(2)}, u32[]{:S(2)}) %all-to-all-start) | async-done | bytes 524320 | tf_op jit(solution)/shard_map/all_to_all | solution.py:134
  34.6 4.3 %all-to-all-start.1 = ((bf16[4,64,1024]{2,1,0:T(8,128)(2,1)}), bf16[4,64,1024]{2,1,0:T(8,128)(2,1)S(1)}, u32[]{:S(2)}, u32[]{:S(2)}) async-start(bf16[4,64,1024]{2,1,0:T(8,128)(2,1)} %param.9), calls=%async_computation.1 | async-start | bytes 1048576 | tf_op jit(solution)/shard_map/all_to_all | solution.py:135
  39.0 17.4 %all-gather.3.cloned.1.call-done = bf16[32,80,256]{2,1,0:T(8,128)(2,1)} async-done(((bf16[4,80,256]{2,1,0:T(8,128)(2,1)}), bf16[32,80,256]{2,1,0:T(8,128)(2,1)}) %all-gather.3.cloned.1.call-update) | async-done | bytes 1310736 | tf_op jit(solution)/shard_map/all_gather | solution.py:133
  56.3 0.9 slice.32
  57.3 0.1 convert_add_fusion
  57.4 0.1 reshape.87.code_ref
  57.4 0.0 all-to-all-done.1.do_ref
  57.4 0.0 copy-start
  57.4 1.3 copy-done
  58.8 19.6 %shard_map.85 = (bf16[4,64,1024]{2,1,0:T(8,128)(2,1)}, bf16[8,4,64,256]{3,2,1,0:T(8,128)(2,1)S(1)}) custom-call(bf16[4,64,1024]{2,1,0:T(8,128)(2,1)S(1)} %all-to-all-done.q_ref, bf16[4,64,1024]{2,1,0:T(8,128)(2,1)S(1)} %all-to-all-done.1.do_ref, bf16[8,4,80,256]{3,2,1,0:T(8,128)(2,1)S(1)} %bitcast.29, f32[16,128]{1,0:T(8,128)S(1)} %reshape.87.code_ref, ...), custom_call_target="tpu_custom_call" | custom-call | flops 5368709120 | bytes 4194304 | tf_op jit(solution)/shard_map/pallas_call | solution.py:99
  78.3 27.1 %all_to_all.31 = bf16[8,4,64,256]{3,2,1,0:T(8,128)(2,1)S(1)} all-to-all(bf16[8,4,64,256]{3,2,1,0:T(8,128)(2,1)S(1)} %get-tuple-element.6), channel_id=1, replica_groups=mesh['xh'=2,'z'=8,'core'=2,'y'=4,'xl'=2] {'z'}, dimensions={0} | all-to-all | bytes 2097152 | tf_op jit(solution)/shard_map/all_to_all | solution.py:145
  105.4 13.6 %all-to-all-start.3 = ((bf16[32,8,1024]{2,1,0:T(8,128)(2,1)}), bf16[32,8,1024]{2,1,0:T(8,128)(2,1)S(1)}, u32[]{:S(2)}, u32[]{:S(2)}) async-start(bf16[32,8,1024]{2,1,0:T(8,128)(2,1)} %bitcast.4), calls=%async_computation.3 | async-start | bytes 1048576 | tf_op jit(solution)/shard_map/all_to_all | solution.py:149
  119.0 0.8 reduce_sum.12
  119.8 10.3 %all-to-all-done.3 = bf16[32,8,1024]{2,1,0:T(8,128)(2,1)S(1)} async-done(((bf16[32,8,1024]{2,1,0:T(8,128)(2,1)}), bf16[32,8,1024]{2,1,0:T(8,128)(2,1)S(1)}, u32[]{:S(2)}, u32[]{:S(2)}) %all-to-all-start.3) | async-done | bytes 524320 | tf_op jit(solution)/shard_map/all_to_all | solution.py:149
  130.1 4.6 %all-to-all-start.5 = ((bf16[32,8,256]{2,1,0:T(8,128)(2,1)}), bf16[32,8,256]{2,1,0:T(8,128)(2,1)S(1)}, u32[]{:S(2)}, u32[]{:S(2)}) async-start(bf16[32,8,256]{2,1,0:T(8,128)(2,1)} %bitcast.8), calls=%async_computation.5 | async-start | bytes 262144 | tf_op jit(solution)/shard_map/all_to_all | solution.py:150
  134.7 7.7 %all-to-all-done.5 = bf16[32,8,256]{2,1,0:T(8,128)(2,1)S(1)} async-done(((bf16[32,8,256]{2,1,0:T(8,128)(2,1)}), bf16[32,8,256]{2,1,0:T(8,128)(2,1)S(1)}, u32[]{:S(2)}, u32[]{:S(2)}) %all-to-all-start.5) | async-done | bytes 131104 | tf_op jit(solution)/shard_map/all_to_all | solution.py:150
  142.4 0.7 fusion.7
  143.1 0.8 copy.26
  (5 shorter events, 0.0 us)
Async XLA Ops:
  7.2 49.2 %all-gather.3.cloned.1.call-start = ((), (), s32[]{:S(2)}) async-start(), calls=%async_computation.6 | async-start | bytes 1474560 | tf_op jit(solution)/shard_map/all_gather | solution.py:133
  21.1 13.5 %all-to-all-start = ((bf16[4,64,1024]{2,1,0:T(8,128)(2,1)}), bf16[4,64,1024]{2,1,0:T(8,128)(2,1)S(1)}, u32[]{:S(2)}, u32[]{:S(2)}) async-start(bf16[4,64,1024]{2,1,0:T(8,128)(2,1)} %param.6), calls=%async_computation | async-start | bytes 1048576 | tf_op jit(solution)/shard_map/all_to_all | solution.py:134
  34.6 22.8 %all-to-all-start.1 = ((bf16[4,64,1024]{2,1,0:T(8,128)(2,1)}), bf16[4,64,1024]{2,1,0:T(8,128)(2,1)S(1)}, u32[]{:S(2)}, u32[]{:S(2)}) async-start(bf16[4,64,1024]{2,1,0:T(8,128)(2,1)} %param.9), calls=%async_computation.1 | async-start | bytes 1048576 | tf_op jit(solution)/shard_map/all_to_all | solution.py:135
  57.4 1.3 copy-start
  105.4 24.7 %all-to-all-start.3 = ((bf16[32,8,1024]{2,1,0:T(8,128)(2,1)}), bf16[32,8,1024]{2,1,0:T(8,128)(2,1)S(1)}, u32[]{:S(2)}, u32[]{:S(2)}) async-start(bf16[32,8,1024]{2,1,0:T(8,128)(2,1)} %bitcast.4), calls=%async_computation.3 | async-start | bytes 1048576 | tf_op jit(solution)/shard_map/all_to_all | solution.py:149
  130.1 12.3 %all-to-all-start.5 = ((bf16[32,8,256]{2,1,0:T(8,128)(2,1)}), bf16[32,8,256]{2,1,0:T(8,128)(2,1)S(1)}, u32[]{:S(2)}, u32[]{:S(2)}) async-start(bf16[32,8,256]{2,1,0:T(8,128)(2,1)} %bitcast.8), calls=%async_computation.5 | async-start | bytes 262144 | tf_op jit(solution)/shard_map/all_to_all | solution.py:150
Sparse Core Ops, SparseCore 0:
  21.3 35.0 all-gather.2

commit v2 on v1

v2 whole, which is shorter than its diff:
```python
import math

import jax
import jax.numpy as jnp
from jax import lax
from jax.experimental import pallas as pl
from jax.experimental.pallas import tpu as pltpu
from jax.sharding import Mesh, PartitionSpec as P

QUERY_HEADS = 64
KEY_VALUE_HEADS = 8
HEAD_SIZE = 128
GROUP = QUERY_HEADS // KEY_VALUE_HEADS
NEG_BIG = -1e30
CODE_SPAN = 2048
META_ROWS = 16
SCALE = 1.0 / math.sqrt(HEAD_SIZE)
EXP2_SCALE = SCALE * math.log2(math.e)

NT = (((1,), (1,)), ((), ()))
NN = (((1,), (0,)), ((), ()))


def dot(a, b, dims):
    return lax.dot_general(a, b, dims, preferred_element_type=jnp.float32)


def attention_kernel(place_ref, low_ref, high_ref, *refs):
    qdo_refs = refs[0:4]
    piece_refs = refs[4:14]
    dq_ref, near_ref, far_ref, bias_ref, kt_ref, s_ref, p_ref, dp_ref, acc_ref = refs[14:]
    row_count = qdo_refs[0].shape[1]
    rows = 4 * row_count
    spans = []
    start = 0
    for ref in piece_refs:
        size = ref.shape[0] * row_count
        spans.append((ref, slice(start, start + size), size))
        start += size
    keys = start

    def keys_of(ref, size):
        return ref[:, 0:row_count, 0:HEAD_SIZE].reshape(size, HEAD_SIZE)

    def values_of(ref, size):
        return ref[:, 0:row_count, HEAD_SIZE:2 * HEAD_SIZE].reshape(size, HEAD_SIZE)

    for ref, part, size in spans:
        for b in range(ref.shape[0]):
            digits = ref[b, row_count:row_count + META_ROWS, :].astype(jnp.float32)[0:1, :]
            code = digits[:, 0:128] * 128.0 + digits[:, 128:256]
            column = jnp.broadcast_to(code, (128, 128)).T[0:row_count, :]
            begin = part.start + b * row_count
            for r in range(rows // 128):
                low = low_ref[:, r * 128:(r + 1) * 128]
                high = high_ref[:, r * 128:(r + 1) * 128]
                allowed = (column >= low) & (column <= high)
                bias_ref[begin:begin + row_count, r * 128:(r + 1) * 128] = jnp.where(allowed, 0.0, NEG_BIG)
    for ref, part, size in spans:
        kt_ref[:, part] = keys_of(ref, size).T
    acc_ref[...] = jnp.zeros_like(acc_ref)
    place = place_ref[0]

    def head(h, carry):
        lanes = pl.ds(pl.multiple_of(h * HEAD_SIZE, HEAD_SIZE), HEAD_SIZE)
        q = jnp.concatenate([ref[0, :, lanes] for ref in qdo_refs], axis=0)
        do = jnp.concatenate([ref[1, :, lanes] for ref in qdo_refs], axis=0)
        top = jnp.full((8, rows), NEG_BIG, jnp.float32)
        for ref, part, size in spans:
            s = dot(keys_of(ref, size), q, NT) + bias_ref[part, :]
            s_ref[part, :] = s
            top = jnp.maximum(top, jnp.max(s.reshape(size // 8, 8, rows), axis=0))
        top = jnp.max(top, axis=0, keepdims=True) * EXP2_SCALE
        total = jnp.zeros((8, rows), jnp.float32)
        cross = jnp.zeros((8, rows), jnp.float32)
        for ref, part, size in spans:
            p = jnp.exp2(s_ref[part, :] * EXP2_SCALE - top)
            dp = dot(values_of(ref, size), do, NT)
            total = total + jnp.sum(p.reshape(size // 8, 8, rows), axis=0)
            cross = cross + jnp.sum((p * dp).reshape(size // 8, 8, rows), axis=0)
            p_ref[part, :] = p
            dp_ref[part, :] = dp
        inverse = 1.0 / jnp.sum(total, axis=0, keepdims=True)
        delta = jnp.sum(cross, axis=0, keepdims=True) * inverse
        dqt = jnp.zeros((HEAD_SIZE, rows), jnp.float32)
        for ref, part, size in spans:
            p = p_ref[part, :] * inverse
            ds = (p * (dp_ref[part, :] - delta)).astype(jnp.bfloat16)
            acc_ref[part, HEAD_SIZE:2 * HEAD_SIZE] += dot(p.astype(jnp.bfloat16), do, NN)
            acc_ref[part, 0:HEAD_SIZE] += dot(ds, q, NN)
            dqt = dqt + dot(kt_ref[:, part], ds, NN)
        dq = (dqt * SCALE).T.astype(jnp.bfloat16)
        for r in range(4):
            dq_ref[place ^ r, :, lanes] = dq[r * row_count:(r + 1) * row_count, :]
        return carry

    lax.fori_loop(0, GROUP, head, 0)
    for i, out_ref in enumerate((near_ref, far_ref)):
        for b in range(4):
            shape = (4, row_count, HEAD_SIZE)
            begin = (i * 4 + b) * 4 * row_count
            part = slice(begin, begin + 4 * row_count)
            out_ref[b, :, :, 0:HEAD_SIZE] = (acc_ref[part, 0:HEAD_SIZE] * SCALE).astype(jnp.bfloat16).reshape(shape)
            out_ref[b, :, :, HEAD_SIZE:2 * HEAD_SIZE] = acc_ref[part, HEAD_SIZE:2 * HEAD_SIZE].astype(jnp.bfloat16).reshape(shape)


def attention(place, low, high, qdo, pieces):
    row_count = qdo[0].shape[1]
    rows = 4 * row_count
    keys = 8 * rows
    width = pieces[0].shape[2]
    vmem = pl.BlockSpec(memory_space=pltpu.VMEM)
    smem = pl.BlockSpec(memory_space=pltpu.SMEM)
    grads = jax.ShapeDtypeStruct((4, 4, row_count, width), jnp.bfloat16)
    return pl.pallas_call(
        attention_kernel,
        out_shape=(jax.ShapeDtypeStruct((4, row_count, GROUP * HEAD_SIZE), jnp.bfloat16), grads, grads),
        in_specs=[smem] + [vmem] * 16,
        out_specs=(vmem, vmem, vmem),
        scratch_shapes=[
            pltpu.VMEM((keys, rows), jnp.float32),
            pltpu.VMEM((HEAD_SIZE, keys), jnp.bfloat16),
            pltpu.VMEM((keys, rows), jnp.float32),
            pltpu.VMEM((keys, rows), jnp.float32),
            pltpu.VMEM((keys, rows), jnp.float32),
            pltpu.VMEM((keys, width), jnp.float32),
        ],
        compiler_params=pltpu.CompilerParams(vmem_limit_bytes=48 * 1024 * 1024),
        cost_estimate=pl.CostEstimate(
            flops=10 * keys * rows * HEAD_SIZE * GROUP, bytes_accessed=4 * 1024 * 1024,
            transcendentals=keys * rows * GROUP),
    )(place, low, high, *qdo, *pieces)


PLANE = ("xh", "zp")
FINAL = ("xh", "zp", "y", "xl")
RING = 4


def swapped(array, axes, by, count):
    return lax.ppermute(array, axes, [(i, i ^ by) for i in range(count)])


def turned(array, by):
    return lax.ppermute(array, "zq", [(i, (i + by) % RING) for i in range(RING)])


def on_device(queries, key_vectors, value_vectors, output_gradient, positions, segments):
    window_count, row_count, _ = queries.shape
    across, pair = lax.axis_index("xh"), lax.axis_index("zp")
    place = across * 2 + pair

    code = segments * CODE_SPAN + positions
    room = ((0, 0), (0, HEAD_SIZE - row_count))
    meta = jnp.concatenate([jnp.pad(code // 128, room), jnp.pad(code % 128, room)], axis=1).astype(jnp.bfloat16)
    meta = jnp.pad(meta[:, None, :], ((0, 0), (0, META_ROWS - 1), (0, 0)))
    packed = jnp.concatenate([jnp.concatenate([key_vectors, value_vectors], axis=2), meta], axis=1)

    def window_of(array, r):
        return lax.dynamic_index_in_dim(array, place ^ r, 0, keepdims=False)

    kv_parts = [window_of(packed, 0)] + [swapped(window_of(packed, r), PLANE, r, 4) for r in (1, 2, 3)]
    qdo = [jnp.stack([window_of(queries, r), window_of(output_gradient, r)]) for r in range(4)]
    qdo = [qdo[0]] + [swapped(qdo[r], PLANE, r, 4) for r in (1, 2, 3)]
    own = jnp.stack(kv_parts)
    before = turned(own, 1)
    after = turned(own, -1)
    opposite_a = turned(before[0:2], 1)
    opposite_b = turned(after[2:4], -1)
    near = [own, after, opposite_a, opposite_b, before]
    far = [swapped(piece, "core", 1, 2) for piece in near]
    pieces = near + far

    digits = own[:, row_count, :].astype(jnp.float32)
    high = (digits[:, 0:row_count] * 128.0 + digits[:, HEAD_SIZE:HEAD_SIZE + row_count]).reshape(1, -1)
    low = jnp.floor(high * (1.0 / CODE_SPAN)) * CODE_SPAN
    dq, near_grad, far_grad = attention(place.reshape(1).astype(jnp.int32), low, high, qdo, pieces)

    def plus(*arrays):
        return sum(a.astype(jnp.float32) for a in arrays).astype(jnp.bfloat16)

    half = plus(near_grad, swapped(far_grad, "core", 1, 2))
    up = turned(half[2, 0:2], 1)
    down = turned(half[2, 2:4], -1)
    to_up = jnp.concatenate([plus(half[1, 0:2], up), half[1, 2:4]])
    to_down = jnp.concatenate([half[3, 0:2], plus(half[3, 2:4], down)])
    dkv_own = plus(half[0], turned(to_up, 1), turned(to_down, -1))
    flip = dkv_own.reshape((2, 2) + dkv_own.shape[1:])
    flip = jnp.where(across == 1, flip[::-1], flip)
    flip = jnp.where(pair == 1, flip[:, ::-1], flip)

    heads = KEY_VALUE_HEADS
    out_rows = row_count // heads
    dq_final = lax.all_to_all(dq.reshape(window_count * heads, out_rows, GROUP * HEAD_SIZE), FINAL, 0, 0, tiled=True)
    dkv_final = lax.all_to_all(flip.reshape(window_count * heads, out_rows, 2 * HEAD_SIZE), FINAL, 0, 0, tiled=True)

    def merged(array):
        width = array.shape[-1]
        return array.reshape(window_count, heads, out_rows, width).transpose(0, 2, 1, 3).reshape(window_count, out_rows, heads * width)

    return (
        merged(dq_final),
        merged(dkv_final[..., 0:HEAD_SIZE]),
        merged(dkv_final[..., HEAD_SIZE:2 * HEAD_SIZE]),
    )


def solution(mesh):
    fine = Mesh(mesh.devices.reshape(2, RING, 2, 2, 4, 2), ("xh", "zq", "zp", "core", "y", "xl"))
    ctx, head = ("xh", "zq", "zp", "core"), ("y", "xl")
    vectors = P(None, ctx, head)
    out = P(None, ctx + head, None)
    return jax.shard_map(
        on_device,
        mesh=fine,
        in_specs=(vectors, vectors, vectors, vectors, P(None, ctx), P(None, ctx)),
        out_specs=(out, out, out),
        check_vma=False,
    )
```

time: 151 us -> 115 us (0.76)
  the two profiles are of different devices: /device:TPU:1 before, /device:TPU:8 now
where the time goes in v2:
time: 115 us; the launch traced here: 114 us
  waiting for transfers between devices  40.1 us (35%)
  starting transfers between devices  34.6 us (30%)
  Pallas kernels  20.7 us (18%)
  blocking collectives  13.1 us (11%)
  local copies, waits for them, and re-layouts  2.8 us (2%)
  other arithmetic  2.13 us (2%)
    ppermute x8, waiting for transfers between devices, turned(): lax.ppermute(array, 'zq', [(i, (i + by) % RING) for i in range(RING)])  28.5 us
    pallas_call x1, Pallas kernels, attention(): pl.pallas_call(attention_kernel, out_shape=(jax.ShapeDtypeStruct((4, row_...  20.7 us
    ppermute x8, starting transfers between devices, turned(): lax.ppermute(array, 'zq', [(i, (i + by) % RING) for i in range(RING)])  17.9 us
    all_to_all x1, blocking collectives, on_device(): lax.all_to_all(flip.reshape(window_count * heads, out_rows, 2 * HEAD_SIZE...  13.1 us
    ppermute x12, starting transfers between devices, swapped(): return lax.ppermute(array, axes, [(i, i ^ by) for i in range(count)])  11.7 us
    all_to_all x1, waiting for transfers between devices, on_device(): lax.all_to_all(dq.reshape(window_count * heads, out_rows, GROUP * HEAD_SI...  9.17 us
    all_to_all x1, starting transfers between devices, on_device(): lax.all_to_all(dq.reshape(window_count * heads, out_rows, GROUP * HEAD_SI...  4.98 us
    ppermute x12, waiting for transfers between devices, swapped(): return lax.ppermute(array, axes, [(i, i ^ by) for i in range(count)])  2.51 us
  transfers between devices with their start and end apart: 21, of which 9 were waited for; matrix products, arithmetic and copies ran while one was open for 2% of the time, Pallas kernels for 0%

profile of v2, /device:TPU:8, one launch (start us, length us, event | category | flops | bytes accessed | tf_op | source)
XLA Modules:
  0.0 114.4 jit_solution(576744566416290557)
XLA Ops:
  0.6 0.0 copy-start.1
  0.6 0.0 copy-start
  0.7 0.8 fusion.7
  1.5 0.0 copy-done.1
  1.5 0.9 pad_maximum_fusion.4
  2.4 4.5 %collective-permute-start.2 = (bf16[80,256]{1,0:T(8,128)(2,1)S(1)}, bf16[80,256]{1,0:T(8,128)(2,1)S(1)}, u32[]{:S(2)}, u32[]{:S(2)}) collective-permute-start(bf16[80,256]{1,0:T(8,128)(2,1)S(1)} %get-tuple-element.24), channel_id=1, source_target_pairs={{0,144},{16,128},{128,16},{144,0},{1,145},{17,129},{129,17},{145,1... | collective-permute-start | bytes 122888 | tf_op jit(solution)/shard_map/ppermute | solution.py:141
  6.9 0.5 collective-permute-start.1
  7.4 0.2 collective-permute-start
  7.6 0.0 copy-done
  7.6 1.2 %constant_dynamic-slice_fusion = (bf16[1,64,1024]{2,1,0:T(8,128)(2,1)S(1)}, bf16[1,64,1024]{2,1,0:T(8,128)(2,1)S(1)}, bf16[1,64,1024]{2,1,0:T(8,128)(2,1)S(1)}, ...) fusion(bf16[4,64,1024]{2,1,0:T(8,128)(2,1)S(1)} %copy-done, ...), kind=kLoop, calls=%fused_computation.39 | loop fusion | bytes 2097168 | tf_op jit(solution)/shard_map/jit(dynamic_index_in_dim)/dynamic_slice | solution.py:160
  8.8 3.1 %collective-permute-start.4 = (bf16[2,64,1024]{2,1,0:T(8,128)(2,1)S(1)}, bf16[2,64,1024]{2,1,0:T(8,128)(2,1)S(1)}, u32[]{:S(2)}, u32[]{:S(2)}) collective-permute-start(bf16[2,64,1024]{2,1,0:T(8,128)(2,1)S(1)} %pad_maximum_fusion.2), channel_id=1, source_target_pairs={{0,128},{16,144},{128,0},{144,16},{1,129},{17,145},{129,1},{145,17... | collective-permute-start | bytes 786440 | tf_op jit(solution)/shard_map/ppermute | solution.py:141
  11.9 2.0 %collective-permute-start.3 = (bf16[2,64,1024]{2,1,0:T(8,128)(2,1)S(1)}, bf16[2,64,1024]{2,1,0:T(8,128)(2,1)S(1)}, u32[]{:S(2)}, u32[]{:S(2)}) collective-permute-start(bf16[2,64,1024]{2,1,0:T(8,128)(2,1)S(1)} %pad_maximum_fusion.1), channel_id=1, source_target_pairs={{0,16},{16,0},{128,144},{144,128},{1,17},{17,1},{129,145},{145,129... | collective-permute-start | bytes 786440 | tf_op jit(solution)/shard_map/ppermute | solution.py:141
  13.9 0.0 collective-permute-done.2
  13.9 0.0 collective-permute-done.1
  14.0 0.0 collective-permute-done
  14.0 0.1 collective-permute-start.10
  14.1 3.3 %collective-permute-start.7 = (bf16[4,80,256]{2,1,0:T(8,128)(2,1)S(1)}, bf16[4,80,256]{2,1,0:T(8,128)(2,1)S(1)}, u32[]{:S(2)}, u32[]{:S(2)}) collective-permute-start(bf16[4,80,256]{2,1,0:T(8,128)(2,1)S(1)} %pad_maximum_fusion.5.refs_4_), channel_id=1, source_target_pairs={{0,32},{32,64},{64,96},{96,0},{1,33},{33,65},{65,97},{97,1},{2,34}... | collective-permute-start | bytes 491528 | tf_op jit(solution)/shard_map/ppermute | solution.py:145
  17.4 2.2 %collective-permute-start.6 = (bf16[4,80,256]{2,1,0:T(8,128)(2,1)S(1)}, bf16[4,80,256]{2,1,0:T(8,128)(2,1)S(1)}, u32[]{:S(2)}, u32[]{:S(2)}) collective-permute-start(bf16[4,80,256]{2,1,0:T(8,128)(2,1)S(1)} %pad_maximum_fusion.5.refs_4_), channel_id=1, source_target_pairs={{0,96},{32,0},{64,32},{96,64},{1,97},{33,1},{65,33},{97,65},{2,98}... | collective-permute-start | bytes 491528 | tf_op jit(solution)/shard_map/ppermute | solution.py:145
  19.7 11.5 %collective-permute-done.7.refs_8_ = bf16[4,80,256]{2,1,0:T(8,128)(2,1)S(1)} collective-permute-done((bf16[4,80,256]{2,1,0:T(8,128)(2,1)S(1)}, bf16[4,80,256]{2,1,0:T(8,128)(2,1)S(1)}, u32[]{:S(2)}, u32[]{:S(2)}) %collective-permute-start.7) | collective-permute-done | bytes 163872 | tf_op jit(solution)/shard_map/ppermute | solution.py:145
  31.2 0.0 collective-permute-start.5
  31.2 0.0 collective-permute-done.6.refs_5_
  31.2 0.7 collective-permute-start.8
  32.0 0.0 collective-permute-done.10.refs_9_
  32.0 3.5 %collective-permute-start.9 = (bf16[2,80,256]{2,1,0:T(8,128)(2,1)S(1)}, bf16[2,80,256]{2,1,0:T(8,128)(2,1)S(1)}, u32[]{:S(2)}, u32[]{:S(2)}) collective-permute-start(bf16[2,80,256]{2,1,0:T(8,128)(2,1)S(1)} %slice.60), channel_id=1, source_target_pairs={{0,96},{32,0},{64,32},{96,64},{1,97},{33,1},{65,33},{97,65},{2,98}... | collective-permute-start | bytes 245768 | tf_op jit(solution)/shard_map/ppermute | solution.py:145
  35.5 0.1 reshape.99.high_ref
  35.6 0.0 collective-permute-done.4.refs_2_
  35.6 0.0 collective-permute-start.14
  35.6 0.0 collective-permute-done.3.refs_1_
  35.6 0.5 collective-permute-start.11
  36.1 4.5 %collective-permute-done.8.refs_6_ = bf16[2,80,256]{2,1,0:T(8,128)(2,1)S(1)} collective-permute-done((bf16[2,80,256]{2,1,0:T(8,128)(2,1)S(1)}, bf16[2,80,256]{2,1,0:T(8,128)(2,1)S(1)}, u32[]{:S(2)}, u32[]{:S(2)}) %collective-permute-start.8) | collective-permute-done | bytes 81952 | tf_op jit(solution)/shard_map/ppermute | solution.py:145
  40.6 0.0 collective-permute-start.12
  40.7 0.0 collective-permute-done.9.refs_7_
  40.7 0.5 collective-permute-start.13
  41.2 0.8 collective-permute-done.5.refs_3_
  41.9 0.0 collective-permute-done.12.refs_11_
  41.9 0.2 collective-permute-done.13.refs_12_
  42.1 0.0 collective-permute-done.14.refs_13_
  42.1 0.0 collective-permute-done.11.refs_10_
  42.1 20.7 %shard_map.85 = (bf16[4,64,1024]{2,1,0:T(8,128)(2,1)}, bf16[4,4,64,256]{3,2,1,0:T(8,128)(2,1)S(1)}, bf16[4,4,64,256]{3,2,1,0:T(8,128)(2,1)S(1)}) custom-call(s32[1]{0:T(128)} %bitcast.place_ref, f32[1,256]{1,0:T(1,128)S(1)} %floor_multiply_fusion.low_ref, f32[1,256]{1,0:T(1,128)S(1)} %reshape.99.high_ref, bf16[2,64,1024]{2,1,0:T(8,128)(2,1)S(1)} %pad_maximum_fusion.refs_0_, ...), custom_call_target="tpu_custom_call" | custom-call | flops 5368709120 | bytes 4194304 | tf_op jit(solution)/shard_map/pallas_call | solution.py:115
  62.8 0.3 collective-permute-start.15
  63.1 1.6 %collective-permute-done.15 = bf16[4,4,64,256]{3,2,1,0:T(8,128)(2,1)S(1)} collective-permute-done((bf16[4,4,64,256]{3,2,1,0:T(8,128)(2,1)S(1)}, bf16[4,4,64,256]{3,2,1,0:T(8,128)(2,1)S(1)}, u32[]{:S(2)}, u32[]{:S(2)}) %collective-permute-start.15) | collective-permute-done | bytes 524320 | tf_op jit(solution)/shard_map/ppermute | solution.py:141
  64.7 0.2 add_convert_fusion
  64.9 1.0 collective-permute-start.16
  65.9 3.2 %collective-permute-start.18 = (bf16[2,64,256]{2,1,0:T(8,128)(2,1)S(1)}, bf16[2,64,256]{2,1,0:T(8,128)(2,1)S(1)}, u32[]{:S(2)}, u32[]{:S(2)}) collective-permute-start(bf16[2,64,256]{2,1,0:T(8,128)(2,1)S(1)} %get-tuple-element.12), channel_id=1, source_target_pairs={{0,96},{32,0},{64,32},{96,64},{1,97},{33,1},{65,33},{97,65},{2,98}... | collective-permute-start | bytes 196616 | tf_op jit(solution)/shard_map/ppermute | solution.py:145
  69.1 3.8 %collective-permute-done.16 = bf16[2,64,256]{2,1,0:T(8,128)(2,1)S(1)} collective-permute-done((bf16[2,64,256]{2,1,0:T(8,128)(2,1)S(1)}, bf16[2,64,256]{2,1,0:T(8,128)(2,1)S(1)}, u32[]{:S(2)}, u32[]{:S(2)}) %collective-permute-start.16) | collective-permute-done | bytes 65568 | tf_op jit(solution)/shard_map/ppermute | solution.py:145
  72.9 0.0 collective-permute-done.18
  72.9 3.8 %collective-permute-start.19 = (bf16[4,64,256]{2,1,0:T(8,128)(2,1)S(1)}, bf16[4,64,256]{2,1,0:T(8,128)(2,1)S(1)}, u32[]{:S(2)}, u32[]{:S(2)}) collective-permute-start(bf16[4,64,256]{2,1,0:T(8,128)(2,1)S(1)} %pad_maximum_fusion.7), channel_id=1, source_target_pairs={{0,96},{32,0},{64,32},{96,64},{1,97},{33,1},{65,33},{97,65},{2,98}... | collective-permute-start | bytes 393224 | tf_op jit(solution)/shard_map/ppermute | solution.py:145
  76.7 0.1 collective-permute-start.17
  76.8 4.2 %collective-permute-done.19 = bf16[4,64,256]{2,1,0:T(8,128)(2,1)S(1)} collective-permute-done((bf16[4,64,256]{2,1,0:T(8,128)(2,1)S(1)}, bf16[4,64,256]{2,1,0:T(8,128)(2,1)S(1)}, u32[]{:S(2)}, u32[]{:S(2)}) %collective-permute-start.19) | collective-permute-done | bytes 131104 | tf_op jit(solution)/shard_map/ppermute | solution.py:145
  81.0 4.5 %collective-permute-done.17 = bf16[4,64,256]{2,1,0:T(8,128)(2,1)S(1)} collective-permute-done((bf16[4,64,256]{2,1,0:T(8,128)(2,1)S(1)}, bf16[4,64,256]{2,1,0:T(8,128)(2,1)S(1)}, u32[]{:S(2)}, u32[]{:S(2)}) %collective-permute-start.17) | collective-permute-done | bytes 131104 | tf_op jit(solution)/shard_map/ppermute | solution.py:145
  85.5 0.1 fusion.1
  85.7 13.1 %all_to_all.10 = bf16[32,8,256]{2,1,0:T(8,128)(2,1)S(1)} all-to-all(bf16[32,8,256]{2,1,0:T(8,128)(2,1)S(1)} %bitcast.59), channel_id=1, replica_groups=mesh['xh'=2,'zq'=4,'zp'=2,'core'=2,'y'=4,'xl'=2] {'xh','zp','y','xl'}, dimensions={0} | all-to-all | bytes 262144 | tf_op jit(solution)/shard_map/all_to_all | solution.py:195
  98.8 5.0 %all-to-all-start = ((bf16[32,8,1024]{2,1,0:T(8,128)(2,1)}), bf16[32,8,1024]{2,1,0:T(8,128)(2,1)S(1)}, u32[]{:S(2)}, u32[]{:S(2)}) async-start(bf16[32,8,1024]{2,1,0:T(8,128)(2,1)} %bitcast.9), calls=%async_computation | async-start | bytes 1048576 | tf_op jit(solution)/shard_map/all_to_all | solution.py:194
  103.8 0.7 fusion.10
  104.4 9.2 %all-to-all-done = bf16[32,8,1024]{2,1,0:T(8,128)(2,1)S(1)} async-done(((bf16[32,8,1024]{2,1,0:T(8,128)(2,1)}), bf16[32,8,1024]{2,1,0:T(8,128)(2,1)S(1)}, u32[]{:S(2)}, u32[]{:S(2)}) %all-to-all-start) | async-done | bytes 524320 | tf_op jit(solution)/shard_map/all_to_all | solution.py:194
  113.6 0.8 copy.17
  (22 shorter events, 0.4 us)
Async XLA Ops:
  0.6 0.9 copy-start.1
  0.6 6.9 %copy-start = (bf16[4,64,1024]{2,1,0:T(8,128)(2,1)S(1)}, bf16[4,64,1024]{2,1,0:T(8,128)(2,1)}, u32[]{:S(2)}) copy-start(bf16[4,64,1024]{2,1,0:T(8,128)(2,1)} %param.9) | copy-start | bytes 1572868
  2.4 11.5 %collective-permute-start.2 = (bf16[80,256]{1,0:T(8,128)(2,1)S(1)}, bf16[80,256]{1,0:T(8,128)(2,1)S(1)}, u32[]{:S(2)}, u32[]{:S(2)}) collective-permute-start(bf16[80,256]{1,0:T(8,128)(2,1)S(1)} %get-tuple-element.24), channel_id=1, source_target_pairs={{0,144},{16,128},{128,16},{144,0},{1,145},{17,129},{129,17},{145,1... | collective-permute-start | bytes 122888 | tf_op jit(solution)/shard_map/ppermute | solution.py:141
  6.9 7.1 %collective-permute-start.1 = (bf16[80,256]{1,0:T(8,128)(2,1)S(1)}, bf16[80,256]{1,0:T(8,128)(2,1)S(1)}, u32[]{:S(2)}, u32[]{:S(2)}) collective-permute-start(bf16[80,256]{1,0:T(8,128)(2,1)S(1)} %get-tuple-element.25), channel_id=1, source_target_pairs={{0,128},{16,144},{128,0},{144,16},{1,129},{17,145},{129,1},{145,17... | collective-permute-start | bytes 122888 | tf_op jit(solution)/shard_map/ppermute | solution.py:141
  7.4 6.6 %collective-permute-start = (bf16[80,256]{1,0:T(8,128)(2,1)S(1)}, bf16[80,256]{1,0:T(8,128)(2,1)S(1)}, u32[]{:S(2)}, u32[]{:S(2)}) collective-permute-start(bf16[80,256]{1,0:T(8,128)(2,1)S(1)} %get-tuple-element.26), channel_id=1, source_target_pairs={{0,16},{16,0},{128,144},{144,128},{1,17},{17,1},{129,145},{145,129... | collective-permute-start | bytes 122888 | tf_op jit(solution)/shard_map/ppermute | solution.py:141
  8.8 26.8 %collective-permute-start.4 = (bf16[2,64,1024]{2,1,0:T(8,128)(2,1)S(1)}, bf16[2,64,1024]{2,1,0:T(8,128)(2,1)S(1)}, u32[]{:S(2)}, u32[]{:S(2)}) collective-permute-start(bf16[2,64,1024]{2,1,0:T(8,128)(2,1)S(1)} %pad_maximum_fusion.2), channel_id=1, source_target_pairs={{0,128},{16,144},{128,0},{144,16},{1,129},{17,145},{129,1},{145,17... | collective-permute-start | bytes 786440 | tf_op jit(solution)/shard_map/ppermute | solution.py:141
  11.9 23.8 %collective-permute-start.3 = (bf16[2,64,1024]{2,1,0:T(8,128)(2,1)S(1)}, bf16[2,64,1024]{2,1,0:T(8,128)(2,1)S(1)}, u32[]{:S(2)}, u32[]{:S(2)}) collective-permute-start(bf16[2,64,1024]{2,1,0:T(8,128)(2,1)S(1)} %pad_maximum_fusion.1), channel_id=1, source_target_pairs={{0,16},{16,0},{128,144},{144,128},{1,17},{17,1},{129,145},{145,129... | collective-permute-start | bytes 786440 | tf_op jit(solution)/shard_map/ppermute | solution.py:141
  14.0 18.0 %collective-permute-start.10 = (bf16[4,80,256]{2,1,0:T(8,128)(2,1)S(1)}, bf16[4,80,256]{2,1,0:T(8,128)(2,1)S(1)}, u32[]{:S(2)}, u32[]{:S(2)}) collective-permute-start(bf16[4,80,256]{2,1,0:T(8,128)(2,1)S(1)} %pad_maximum_fusion.5.refs_4_), channel_id=1, source_target_pairs={{0,8},{8,0},{1,9},{9,1},{2,10},{10,2},{3,11},{11,3},{4,12},{12,4},... | collective-permute-start | bytes 491528 | tf_op jit(solution)/shard_map/ppermute | solution.py:141
  14.1 17.1 %collective-permute-start.7 = (bf16[4,80,256]{2,1,0:T(8,128)(2,1)S(1)}, bf16[4,80,256]{2,1,0:T(8,128)(2,1)S(1)}, u32[]{:S(2)}, u32[]{:S(2)}) collective-permute-start(bf16[4,80,256]{2,1,0:T(8,128)(2,1)S(1)} %pad_maximum_fusion.5.refs_4_), channel_id=1, source_target_pairs={{0,32},{32,64},{64,96},{96,0},{1,33},{33,65},{65,97},{97,1},{2,34}... | collective-permute-start | bytes 491528 | tf_op jit(solution)/shard_map/ppermute | solution.py:145
  17.4 13.8 %collective-permute-start.6 = (bf16[4,80,256]{2,1,0:T(8,128)(2,1)S(1)}, bf16[4,80,256]{2,1,0:T(8,128)(2,1)S(1)}, u32[]{:S(2)}, u32[]{:S(2)}) collective-permute-start(bf16[4,80,256]{2,1,0:T(8,128)(2,1)S(1)} %pad_maximum_fusion.5.refs_4_), channel_id=1, source_target_pairs={{0,96},{32,0},{64,32},{96,64},{1,97},{33,1},{65,33},{97,65},{2,98}... | collective-permute-start | bytes 491528 | tf_op jit(solution)/shard_map/ppermute | solution.py:145
  31.2 10.7 %collective-permute-start.5 = (bf16[2,64,1024]{2,1,0:T(8,128)(2,1)S(1)}, bf16[2,64,1024]{2,1,0:T(8,128)(2,1)S(1)}, u32[]{:S(2)}, u32[]{:S(2)}) collective-permute-start(bf16[2,64,1024]{2,1,0:T(8,128)(2,1)S(1)} %pad_maximum_fusion.3), channel_id=1, source_target_pairs={{0,144},{16,128},{128,16},{144,0},{1,145},{17,129},{129,17},{145,1... | collective-permute-start | bytes 786440 | tf_op jit(solution)/shard_map/ppermute | solution.py:141
  31.2 9.4 %collective-permute-start.8 = (bf16[2,80,256]{2,1,0:T(8,128)(2,1)S(1)}, bf16[2,80,256]{2,1,0:T(8,128)(2,1)S(1)}, u32[]{:S(2)}, u32[]{:S(2)}) collective-permute-start(bf16[2,80,256]{2,1,0:T(8,128)(2,1)S(1)} %slice.59), channel_id=1, source_target_pairs={{0,32},{32,64},{64,96},{96,0},{1,33},{33,65},{65,97},{97,1},{2,34}... | collective-permute-start | bytes 245768 | tf_op jit(solution)/shard_map/ppermute | solution.py:145
  32.0 8.7 %collective-permute-start.9 = (bf16[2,80,256]{2,1,0:T(8,128)(2,1)S(1)}, bf16[2,80,256]{2,1,0:T(8,128)(2,1)S(1)}, u32[]{:S(2)}, u32[]{:S(2)}) collective-permute-start(bf16[2,80,256]{2,1,0:T(8,128)(2,1)S(1)} %slice.60), channel_id=1, source_target_pairs={{0,96},{32,0},{64,32},{96,64},{1,97},{33,1},{65,33},{97,65},{2,98}... | collective-permute-start | bytes 245768 | tf_op jit(solution)/shard_map/ppermute | solution.py:145
  35.6 6.5 %collective-permute-start.14 = (bf16[4,80,256]{2,1,0:T(8,128)(2,1)S(1)}, bf16[4,80,256]{2,1,0:T(8,128)(2,1)S(1)}, u32[]{:S(2)}, u32[]{:S(2)}) collective-permute-start(bf16[4,80,256]{2,1,0:T(8,128)(2,1)S(1)} %collective-permute-done.7.refs_8_), channel_id=1, source_target_pairs={{0,8},{8,0},{1,9},{9,1},{2,10},{10,2},{3,11},{11,3},{4,12},{12,4},... | collective-permute-start | bytes 491528 | tf_op jit(solution)/shard_map/ppermute | solution.py:141
  35.6 6.4 %collective-permute-start.11 = (bf16[4,80,256]{2,1,0:T(8,128)(2,1)S(1)}, bf16[4,80,256]{2,1,0:T(8,128)(2,1)S(1)}, u32[]{:S(2)}, u32[]{:S(2)}) collective-permute-start(bf16[4,80,256]{2,1,0:T(8,128)(2,1)S(1)} %collective-permute-done.6.refs_5_), channel_id=1, source_target_pairs={{0,8},{8,0},{1,9},{9,1},{2,10},{10,2},{3,11},{11,3},{4,12},{12,4},... | collective-permute-start | bytes 491528 | tf_op jit(solution)/shard_map/ppermute | solution.py:141
  40.6 1.3 %collective-permute-start.12 = (bf16[2,80,256]{2,1,0:T(8,128)(2,1)S(1)}, bf16[2,80,256]{2,1,0:T(8,128)(2,1)S(1)}, u32[]{:S(2)}, u32[]{:S(2)}) collective-permute-start(bf16[2,80,256]{2,1,0:T(8,128)(2,1)S(1)} %collective-permute-done.8.refs_6_), channel_id=1, source_target_pairs={{0,8},{8,0},{1,9},{9,1},{2,10},{10,2},{3,11},{11,3},{4,12},{12,4},... | collective-permute-start | bytes 245768 | tf_op jit(solution)/shard_map/ppermute | solution.py:141
  40.7 1.4 %collective-permute-start.13 = (bf16[2,80,256]{2,1,0:T(8,128)(2,1)S(1)}, bf16[2,80,256]{2,1,0:T(8,128)(2,1)S(1)}, u32[]{:S(2)}, u32[]{:S(2)}) collective-permute-start(bf16[2,80,256]{2,1,0:T(8,128)(2,1)S(1)} %collective-permute-done.9.refs_7_), channel_id=1, source_target_pairs={{0,8},{8,0},{1,9},{9,1},{2,10},{10,2},{3,11},{11,3},{4,12},{12,4},... | collective-permute-start | bytes 245768 | tf_op jit(solution)/shard_map/ppermute | solution.py:141
  62.8 1.9 %collective-permute-start.15 = (bf16[4,4,64,256]{3,2,1,0:T(8,128)(2,1)S(1)}, bf16[4,4,64,256]{3,2,1,0:T(8,128)(2,1)S(1)}, u32[]{:S(2)}, u32[]{:S(2)}) collective-permute-start(bf16[4,4,64,256]{3,2,1,0:T(8,128)(2,1)S(1)} %get-tuple-element.8), channel_id=1, source_target_pairs={{0,8},{8,0},{1,9},{9,1},{2,10},{10,2},{3,11},{11,3},{4,12},{12,4},... | collective-permute-start | bytes 1572872 | tf_op jit(solution)/shard_map/ppermute | solution.py:141
  64.9 8.0 %collective-permute-start.16 = (bf16[2,64,256]{2,1,0:T(8,128)(2,1)S(1)}, bf16[2,64,256]{2,1,0:T(8,128)(2,1)S(1)}, u32[]{:S(2)}, u32[]{:S(2)}) collective-permute-start(bf16[2,64,256]{2,1,0:T(8,128)(2,1)S(1)} %get-tuple-element.11), channel_id=1, source_target_pairs={{0,32},{32,64},{64,96},{96,0},{1,33},{33,65},{65,97},{97,1},{2,34}... | collective-permute-start | bytes 196616 | tf_op jit(solution)/shard_map/ppermute | solution.py:145
  65.9 6.9 %collective-permute-start.18 = (bf16[2,64,256]{2,1,0:T(8,128)(2,1)S(1)}, bf16[2,64,256]{2,1,0:T(8,128)(2,1)S(1)}, u32[]{:S(2)}, u32[]{:S(2)}) collective-permute-start(bf16[2,64,256]{2,1,0:T(8,128)(2,1)S(1)} %get-tuple-element.12), channel_id=1, source_target_pairs={{0,96},{32,0},{64,32},{96,64},{1,97},{33,1},{65,33},{97,65},{2,98}... | collective-permute-start | bytes 196616 | tf_op jit(solution)/shard_map/ppermute | solution.py:145
  72.9 8.1 %collective-permute-start.19 = (bf16[4,64,256]{2,1,0:T(8,128)(2,1)S(1)}, bf16[4,64,256]{2,1,0:T(8,128)(2,1)S(1)}, u32[]{:S(2)}, u32[]{:S(2)}) collective-permute-start(bf16[4,64,256]{2,1,0:T(8,128)(2,1)S(1)} %pad_maximum_fusion.7), channel_id=1, source_target_pairs={{0,96},{32,0},{64,32},{96,64},{1,97},{33,1},{65,33},{97,65},{2,98}... | collective-permute-start | bytes 393224 | tf_op jit(solution)/shard_map/ppermute | solution.py:145
  76.7 8.8 %collective-permute-start.17 = (bf16[4,64,256]{2,1,0:T(8,128)(2,1)S(1)}, bf16[4,64,256]{2,1,0:T(8,128)(2,1)S(1)}, u32[]{:S(2)}, u32[]{:S(2)}) collective-permute-start(bf16[4,64,256]{2,1,0:T(8,128)(2,1)S(1)} %pad_maximum_fusion.6), channel_id=1, source_target_pairs={{0,32},{32,64},{64,96},{96,0},{1,33},{33,65},{65,97},{97,1},{2,34}... | collective-permute-start | bytes 393224 | tf_op jit(solution)/shard_map/ppermute | solution.py:145
  98.8 14.8 %all-to-all-start = ((bf16[32,8,1024]{2,1,0:T(8,128)(2,1)}), bf16[32,8,1024]{2,1,0:T(8,128)(2,1)S(1)}, u32[]{:S(2)}, u32[]{:S(2)}) async-start(bf16[32,8,1024]{2,1,0:T(8,128)(2,1)} %bitcast.9), calls=%async_computation | async-start | bytes 1048576 | tf_op jit(solution)/shard_map/all_to_all | solution.py:194

commit v3 on v2

v3 whole, which is shorter than its diff:
```python
import functools
import math

import jax
import jax.numpy as jnp
from jax import lax
from jax.experimental import pallas as pl
from jax.experimental.pallas import tpu as pltpu
from jax.sharding import Mesh, PartitionSpec as P

QUERY_HEADS = 64
KEY_VALUE_HEADS = 8
HEAD_SIZE = 128
GROUP = QUERY_HEADS // KEY_VALUE_HEADS
NEG_BIG = -1e30
CODE_SPAN = 2048
META_ROWS = 16
HEADS_PER_STEP = 2
SCALE = 1.0 / math.sqrt(HEAD_SIZE)
EXP2_SCALE = SCALE * math.log2(math.e)

NT = (((1,), (1,)), ((), ()))
NN = (((1,), (0,)), ((), ()))


def dot(a, b, dims):
    return lax.dot_general(a, b, dims, preferred_element_type=jnp.float32)


def key_spans(piece_refs, row_count):
    spans, start = [], 0
    for ref in piece_refs:
        size = ref.shape[0] * row_count
        spans.append((ref, slice(start, start + size), size))
        start += size
    return spans, start


def keys_of(ref, size, row_count):
    return ref[:, 0:row_count, 0:HEAD_SIZE].reshape(size, HEAD_SIZE)


def values_of(ref, size, row_count):
    return ref[:, 0:row_count, HEAD_SIZE:2 * HEAD_SIZE].reshape(size, HEAD_SIZE)


def fill_bias(bias_ref, spans, low_ref, high_ref, row_count):
    rows = low_ref.shape[1]
    for ref, part, size in spans:
        for b in range(ref.shape[0]):
            digits = ref[b, row_count:row_count + META_ROWS, :].astype(jnp.float32)[0:1, :]
            code = digits[:, 0:128] * 128.0 + digits[:, 128:256]
            column = jnp.broadcast_to(code, (128, 128)).T[0:row_count, :]
            begin = part.start + b * row_count
            for r in range(rows // 128):
                low = low_ref[:, r * 128:(r + 1) * 128]
                high = high_ref[:, r * 128:(r + 1) * 128]
                allowed = (column >= low) & (column <= high)
                bias_ref[begin:begin + row_count, r * 128:(r + 1) * 128] = jnp.where(allowed, 0.0, NEG_BIG)


def rows_of(row_refs, lanes, row_count):
    q = jnp.concatenate([ref[0:row_count, lanes] for ref in row_refs], axis=0)
    do = jnp.concatenate([ref[row_count:2 * row_count, lanes] for ref in row_refs], axis=0)
    return q, do


def stats_kernel(first, count, low_ref, high_ref, *refs):
    row_refs, piece_refs, rest = refs[0:4], refs[4:4 + count], refs[4 + count:]
    if first:
        state_ref, bias_ref = rest
    else:
        before_ref, state_ref, bias_ref = rest
    rows = low_ref.shape[1]
    row_count = rows // 4
    spans, _ = key_spans(piece_refs, row_count)
    fill_bias(bias_ref, spans, low_ref, high_ref, row_count)

    def head(h, carry):
        lanes = pl.ds(pl.multiple_of(h * HEAD_SIZE, HEAD_SIZE), HEAD_SIZE)
        q, do = rows_of(row_refs, lanes, row_count)
        if first:
            top = jnp.full((1, rows), NEG_BIG, jnp.float32)
            total = jnp.zeros((1, rows), jnp.float32)
            cross = jnp.zeros((1, rows), jnp.float32)
        else:
            top, total, cross = before_ref[h, 0:1, :], before_ref[h, 1:2, :], before_ref[h, 2:3, :]
        for ref, part, size in spans:
            s = dot(keys_of(ref, size, row_count), q, NT) * EXP2_SCALE + bias_ref[part, :]
            dp = dot(values_of(ref, size, row_count), do, NT)
            peak = jnp.max(s.reshape(size // 8, 8, rows), axis=0)
            new = jnp.maximum(top, jnp.max(peak, axis=0, keepdims=True))
            p = jnp.exp2(s - new)
            factor = jnp.exp2(top - new)
            part_sum = jnp.sum(p.reshape(size // 8, 8, rows), axis=0)
            part_dot = jnp.sum((p * dp).reshape(size // 8, 8, rows), axis=0)
            total = total * factor + jnp.sum(part_sum, axis=0, keepdims=True)
            cross = cross * factor + jnp.sum(part_dot, axis=0, keepdims=True)
            top = new
        state_ref[h, 0:1, :] = top
        state_ref[h, 1:2, :] = total
        state_ref[h, 2:3, :] = cross
        return carry

    lax.fori_loop(0, GROUP, head, 0)


def grads_kernel(first, last, count, place_ref, low_ref, high_ref, state_ref, *refs):
    row_refs, piece_refs, rest = refs[0:4], refs[4:4 + count], refs[4 + count:]
    if not first:
        before_ref, rest = rest[0], rest[1:]
    dq_ref, near_ref, far_ref, bias_ref, kt_ref, ds_ref, acc_ref = rest
    rows = low_ref.shape[1]
    row_count = rows // 4
    heads = HEADS_PER_STEP
    spans, keys = key_spans(piece_refs, row_count)
    fill_bias(bias_ref, spans, low_ref, high_ref, row_count)
    for ref, part, size in spans:
        kt_ref[:, part] = keys_of(ref, size, row_count).T
    acc_ref[...] = jnp.zeros_like(acc_ref)
    place = place_ref[0]

    def step(g, carry):
        q, do, offsets, deltas, lanes = [], [], [], [], []
        for j in range(heads):
            h = g * heads + j
            lanes.append(pl.ds(pl.multiple_of(h * HEAD_SIZE, HEAD_SIZE), HEAD_SIZE))
            one_q, one_do = rows_of(row_refs, lanes[j], row_count)
            q.append(one_q)
            do.append(one_do)
            total = state_ref[h, 1:2, :]
            offsets.append(state_ref[h, 0:1, :] + jnp.log2(total))
            deltas.append(state_ref[h, 2:3, :] / total)
        q_all, do_all = jnp.concatenate(q, axis=0), jnp.concatenate(do, axis=0)
        for ref, part, size in spans:
            p_low, ds_low = [], []
            for j in range(heads):
                s = dot(keys_of(ref, size, row_count), q[j], NT) * EXP2_SCALE + bias_ref[part, :]
                dp = dot(values_of(ref, size, row_count), do[j], NT)
                p = jnp.exp2(s - offsets[j])
                p_low.append(p.astype(jnp.bfloat16))
                ds_low.append((p * (dp - deltas[j])).astype(jnp.bfloat16))
            p_all, ds_all = jnp.concatenate(p_low, axis=1), jnp.concatenate(ds_low, axis=1)
            ds_ref[part, :] = ds_all
            acc_ref[part, HEAD_SIZE:2 * HEAD_SIZE] += dot(p_all, do_all, NN)
            acc_ref[part, 0:HEAD_SIZE] += dot(ds_all, q_all, NN)
        dqt = dot(kt_ref[...], ds_ref[...], NN)
        for j in range(heads):
            part = dqt[:, j * rows:(j + 1) * rows]
            if not first:
                part = part + before_ref[g * heads + j]
            if last:
                dq = (part * SCALE).T.astype(jnp.bfloat16)
                for r in range(4):
                    dq_ref[place ^ r, :, lanes[j]] = dq[r * row_count:(r + 1) * row_count, :]
            else:
                dq_ref[g * heads + j] = part
        return carry

    lax.fori_loop(0, GROUP // heads, step, 0)
    sources = near_ref.shape[0]
    for i, out_ref in enumerate((near_ref, far_ref)):
        part = slice(i * sources * row_count, (i + 1) * sources * row_count)
        shape = (sources, row_count, HEAD_SIZE)
        out_ref[:, :, 0:HEAD_SIZE] = (acc_ref[part, 0:HEAD_SIZE] * SCALE).astype(jnp.bfloat16).reshape(shape)
        out_ref[:, :, HEAD_SIZE:2 * HEAD_SIZE] = acc_ref[part, HEAD_SIZE:2 * HEAD_SIZE].astype(jnp.bfloat16).reshape(shape)


VMEM = pl.BlockSpec(memory_space=pltpu.VMEM)
SMEM = pl.BlockSpec(memory_space=pltpu.SMEM)


def stats(low, high, row_arrays, pieces, state):
    rows = low.shape[1]
    keys = sum(piece.shape[0] for piece in pieces) * rows // 4
    first = state is None
    inputs = (low, high, *row_arrays, *pieces) + (() if first else (state,))
    return pl.pallas_call(
        functools.partial(stats_kernel, first, len(pieces)),
        out_shape=jax.ShapeDtypeStruct((GROUP, 8, rows), jnp.float32),
        in_specs=[VMEM] * len(inputs),
        out_specs=VMEM,
        scratch_shapes=[pltpu.VMEM((keys, rows), jnp.float32)],
        compiler_params=pltpu.CompilerParams(vmem_limit_bytes=24 * 1024 * 1024),
        cost_estimate=pl.CostEstimate(
            flops=8 * keys * rows * HEAD_SIZE * GROUP, bytes_accessed=1024 * 1024,
            transcendentals=keys * rows * GROUP),
    )(*inputs)


def grads(place, low, high, state, row_arrays, pieces, before, last):
    rows = low.shape[1]
    row_count = rows // 4
    sources = sum(piece.shape[0] for piece in pieces)
    keys = sources * row_count
    width = 2 * HEAD_SIZE
    first = before is None
    inputs = (low, high, state, *row_arrays, *pieces) + (() if first else (before,))
    part = jax.ShapeDtypeStruct((sources // 2, row_count, width), jnp.bfloat16)
    if last:
        dq = jax.ShapeDtypeStruct((4, row_count, GROUP * HEAD_SIZE + width), jnp.bfloat16)
    else:
        dq = jax.ShapeDtypeStruct((GROUP, HEAD_SIZE, rows), jnp.float32)
    return pl.pallas_call(
        functools.partial(grads_kernel, first, last, len(pieces)),
        out_shape=(dq, part, part),
        in_specs=[SMEM] + [VMEM] * len(inputs),
        out_specs=(VMEM, VMEM, VMEM),
        scratch_shapes=[
            pltpu.VMEM((keys, rows), jnp.float32),
            pltpu.VMEM((HEAD_SIZE, keys), jnp.bfloat16),
            pltpu.VMEM((keys, HEADS_PER_STEP * rows), jnp.bfloat16),
            pltpu.VMEM((keys, width), jnp.float32),
        ],
        compiler_params=pltpu.CompilerParams(vmem_limit_bytes=24 * 1024 * 1024),
        cost_estimate=pl.CostEstimate(
            flops=16 * keys * rows * HEAD_SIZE * GROUP, bytes_accessed=2 * 1024 * 1024,
            transcendentals=keys * rows * GROUP),
    )(place, *inputs)


def pack_kernel(place_ref, code_ref, q_ref, do_ref, k_ref, v_ref, *out_refs):
    row_count = q_ref.shape[1]
    wide = q_ref.shape[2]
    fold = wide // (2 * HEAD_SIZE)
    lines = row_count // fold
    half = fold * HEAD_SIZE
    place = place_ref[0]
    for r, out_ref in enumerate(out_refs):
        w = place ^ r
        out_ref[0:row_count, :] = q_ref[w]
        out_ref[row_count:2 * row_count, :] = do_ref[w]
        begin = 2 * row_count
        for g in range(fold):
            from_rows = slice(g * lines, (g + 1) * lines)
            out_ref[begin:begin + lines, g * HEAD_SIZE:(g + 1) * HEAD_SIZE] = k_ref[w, from_rows, :]
            out_ref[begin:begin + lines, half + g * HEAD_SIZE:half + (g + 1) * HEAD_SIZE] = v_ref[w, from_rows, :]
        code = code_ref[pl.ds(w, 1), :]
        begin += lines
        for i, digit in enumerate((code >> 7, code & 127)):
            spread = jnp.broadcast_to(digit.astype(jnp.float32), (META_ROWS, 128)).astype(jnp.bfloat16)
            out_ref[begin:begin + META_ROWS, i * 128:(i + 1) * 128] = spread
        out_ref[begin:begin + META_ROWS, 256:] = jnp.zeros((META_ROWS, wide - 256), jnp.bfloat16)


def unpack_kernel(*refs):
    load_refs, (own_ref, low_ref, high_ref) = refs[0:4], refs[4:]
    row_count = own_ref.shape[1] - META_ROWS
    wide = load_refs[0].shape[1]
    fold = wide // (2 * HEAD_SIZE)
    lines = row_count // fold
    half = fold * HEAD_SIZE
    codes = []
    for r, ref in enumerate(load_refs):
        begin = 2 * row_count
        for g in range(fold):
            to_rows = slice(g * lines, (g + 1) * lines)
            own_ref[r, to_rows, 0:HEAD_SIZE] = ref[begin:begin + lines, g * HEAD_SIZE:(g + 1) * HEAD_SIZE]
            own_ref[r, to_rows, HEAD_SIZE:] = ref[begin:begin + lines, half + g * HEAD_SIZE:half + (g + 1) * HEAD_SIZE]
        meta = ref[begin + lines:begin + lines + META_ROWS, 0:256]
        own_ref[r, row_count:, :] = meta
        digits = meta.astype(jnp.float32)[0:8, :]
        codes.append(digits[:, 0:128] * 128.0 + digits[:, 128:256])
    lane = lax.broadcasted_iota(jnp.int32, (8, 128), 1)
    for i in range(2):
        code = jnp.where(lane < row_count, codes[2 * i], pltpu.roll(codes[2 * i + 1], row_count, 1))[0:1, :]
        high_ref[:, i * 128:(i + 1) * 128] = code
        low_ref[:, i * 128:(i + 1) * 128] = jnp.floor(code * (1.0 / CODE_SPAN)) * CODE_SPAN


def pack(place, code, queries, output_gradient, key_vectors, value_vectors):
    row_count, wide = queries.shape[1:]
    load = jax.ShapeDtypeStruct((2 * row_count + row_count * 2 * HEAD_SIZE // wide + META_ROWS, wide), jnp.bfloat16)
    return pl.pallas_call(
        pack_kernel,
        out_shape=(load,) * 4,
        in_specs=[SMEM] + [VMEM] * 5,
        out_specs=(VMEM,) * 4,
        compiler_params=pltpu.CompilerParams(vmem_limit_bytes=24 * 1024 * 1024),
    )(place, code, queries, output_gradient, key_vectors, value_vectors)


def unpack(loads, row_count):
    row = jax.ShapeDtypeStruct((1, 4 * row_count), jnp.float32)
    own = jax.ShapeDtypeStruct((4, row_count + META_ROWS, 2 * HEAD_SIZE), jnp.bfloat16)
    return pl.pallas_call(
        unpack_kernel,
        out_shape=(own, row, row),
        in_specs=[VMEM] * 4,
        out_specs=(VMEM,) * 3,
        compiler_params=pltpu.CompilerParams(vmem_limit_bytes=24 * 1024 * 1024),
    )(*loads)


PLANE = ("xh", "zp")
FINAL = ("xh", "zp", "y", "xl")
RING = 4


def swapped(array, axes, by, count):
    return lax.ppermute(array, axes, [(i, i ^ by) for i in range(count)])


def other_core(array):
    return swapped(array, "core", 1, 2)


def turned(array, by):
    return lax.ppermute(array, "zq", [(i, (i + by) % RING) for i in range(RING)])


def plus(*arrays):
    return sum(a.astype(jnp.float32) for a in arrays).astype(jnp.bfloat16)


def on_device(queries, key_vectors, value_vectors, output_gradient, positions, segments):
    window_count, row_count, _ = queries.shape
    across, pair = lax.axis_index("xh"), lax.axis_index("zp")
    place = across * 2 + pair

    spot = place.reshape(1).astype(jnp.int32)
    code = jnp.pad(segments * CODE_SPAN + positions, ((0, 0), (0, 128 - row_count)))
    loads = pack(spot, code, queries, output_gradient, key_vectors, value_vectors)
    row_arrays = [loads[0]] + [swapped(loads[r], PLANE, r, 4) for r in (1, 2, 3)]
    own, low, high = unpack(row_arrays, row_count)

    tied = lax.optimization_barrier
    before = turned(own, 1)
    after = turned(own, -1)
    far_own = other_core(own)
    state = stats(low, high, row_arrays, [own], None)
    state, before, after = tied((state, before, after))
    opposite = (turned(before[0:2], 1), turned(after[2:4], -1))
    far_after, far_before = other_core(after), other_core(before)
    state = stats(low, high, row_arrays, [after, before, far_own, far_after, far_before], state)
    state, opposite = tied((state, opposite))
    far_opposite = tuple(other_core(piece) for piece in opposite)
    state = stats(low, high, row_arrays, [*opposite, *far_opposite], state)

    dq, near_2, far_2 = grads(spot, low, high, state, row_arrays, [*opposite, *far_opposite], None, False)
    sum_2 = plus(near_2, other_core(far_2))
    spot, dq, first_up, first_down = tied((spot, dq, sum_2[0:2], sum_2[2:4]))
    up, down = turned(first_up, 1), turned(first_down, -1)
    dq, near_1, far_1 = grads(spot, low, high, state, row_arrays, [after, before, far_after, far_before], dq, False)
    dq, near_1, far_1, up, down = tied((dq, near_1, far_1, up, down))
    sum_1 = plus(near_1, other_core(far_1))
    next_up = jnp.concatenate([plus(sum_1[0:2], up), sum_1[2:4]])
    next_down = jnp.concatenate([sum_1[4:6], plus(sum_1[6:8], down)])
    spot, dq, next_up, next_down = tied((spot, dq, next_up, next_down))
    to_up, to_down = turned(next_up, 1), turned(next_down, -1)
    dq, near_0, far_0 = grads(spot, low, high, state, row_arrays, [own, far_own], dq, True)
    dq, near_0, far_0, to_up, to_down = tied((dq, near_0, far_0, to_up, to_down))
    dkv_own = plus(near_0, other_core(far_0), to_up, to_down)

    flip = dkv_own.reshape((2, 2) + dkv_own.shape[1:])
    flip = jnp.where(across == 1, flip[::-1], flip)
    flip = jnp.where(pair == 1, flip[:, ::-1], flip)

    heads = KEY_VALUE_HEADS
    out_rows = row_count // heads
    split = GROUP * HEAD_SIZE
    leaving = dq.at[:, :, split:].set(flip.reshape(dkv_own.shape)).reshape(window_count * heads, out_rows, split + 2 * HEAD_SIZE)
    final = lax.all_to_all(leaving, FINAL, 0, 0, tiled=True)

    def merged(array):
        width = array.shape[-1]
        return array.reshape(window_count, heads, out_rows, width).transpose(0, 2, 1, 3).reshape(window_count, out_rows, heads * width)

    return (
        merged(final[..., 0:split]),
        merged(final[..., split:split + HEAD_SIZE]),
        merged(final[..., split + HEAD_SIZE:]),
    )


def solution(mesh):
    fine = Mesh(mesh.devices.reshape(2, RING, 2, 2, 4, 2), ("xh", "zq", "zp", "core", "y", "xl"))
    ctx, head = ("xh", "zq", "zp", "core"), ("y", "xl")
    vectors = P(None, ctx, head)
    out = P(None, ctx + head, None)
    return jax.shard_map(
        on_device,
        mesh=fine,
        in_specs=(vectors, vectors, vectors, vectors, P(None, ctx), P(None, ctx)),
        out_specs=(out, out, out),
        check_vma=False,
    )
```

time: 115 us -> 109 us (0.948)
  the two profiles are of different devices: /device:TPU:8 before, /device:TPU:1 now
where the time goes in v3:
time: 109 us
  starting transfers between devices  32.8 us (30%)
  Pallas kernels  26.8 us (25%)
  waiting for transfers between devices  21.8 us (20%)
  blocking collectives  20.6 us (19%)
  local copies, waits for them, and re-layouts  6.01 us (6%)
    all_to_all x1, blocking collectives, on_device(): final = lax.all_to_all(leaving, FINAL, 0, 0, tiled=True)  20.6 us
    ppermute x11, waiting for transfers between devices, swapped(): return lax.ppermute(array, axes, [(i, i ^ by) for i in range(count)])  18.6 us
    ppermute x8, starting transfers between devices, turned(): lax.ppermute(array, 'zq', [(i, (i + by) % RING) for i in range(RING)])  16.6 us
    ppermute x11, starting transfers between devices, swapped(): return lax.ppermute(array, axes, [(i, i ^ by) for i in range(count)])  16.2 us
    pallas_call x3, Pallas kernels, grads(): pl.pallas_call(functools.partial(grads_kernel, first, last, len(pieces)),...  15.2 us
    pallas_call x3, Pallas kernels, stats(): pl.pallas_call(functools.partial(stats_kernel, first, len(pieces)), out_s...  11.5 us
    unnamed x12, local copies, waits for them, and re-layouts  4.44 us
    ppermute x8, waiting for transfers between devices, turned(): lax.ppermute(array, 'zq', [(i, (i + by) % RING) for i in range(RING)])  3.19 us
  transfers between devices with their start and end apart: 19, of which 10 were waited for; matrix products, arithmetic and copies ran while one was open for 0% of the time, Pallas kernels for 17%

profile of v3, /device:TPU:1, one launch (start us, length us, event | category | flops | bytes accessed | tf_op | source)
XLA Modules:
  0.0 109.1 jit_solution(17748259073317385714)
XLA Ops:
  0.6 0.0 copy-start.5
  0.6 0.0 copy-start.4
  0.7 0.7 copy-done.5
  1.3 0.0 copy-done.4
  1.3 0.0 copy-start
  1.4 1.0 copy-done
  2.4 0.0 copy-start.1
  2.4 1.0 copy-done.1
  3.4 0.0 copy-start.2
  3.4 0.8 copy-done.2
  4.3 0.0 copy-start.3
  4.3 0.8 copy-done.3
  5.1 0.1 shard_map.85
  5.2 2.6 %collective-permute-start = (bf16[160,1024]{1,0:T(8,128)(2,1)S(1)}, bf16[160,1024]{1,0:T(8,128)(2,1)S(1)}, u32[]{:S(2)}, u32[]{:S(2)}) collective-permute-start(bf16[160,1024]{1,0:T(8,128)(2,1)S(1)} %get-tuple-element.56), channel_id=1, source_target_pairs={{0,16},{16,0},{128,144},{144,128},{1,17},{17,1},{129,145},{145,129... | collective-permute-start | bytes 983048 | tf_op jit(solution)/shard_map/ppermute | solution.py:301
  7.8 2.7 %collective-permute-start.1 = (bf16[160,1024]{1,0:T(8,128)(2,1)S(1)}, bf16[160,1024]{1,0:T(8,128)(2,1)S(1)}, u32[]{:S(2)}, u32[]{:S(2)}) collective-permute-start(bf16[160,1024]{1,0:T(8,128)(2,1)S(1)} %get-tuple-element.57), channel_id=1, source_target_pairs={{0,128},{16,144},{128,0},{144,16},{1,129},{17,145},{129,1},{145,17... | collective-permute-start | bytes 983048 | tf_op jit(solution)/shard_map/ppermute | solution.py:301
  10.5 0.0 collective-permute-start.2
  10.6 3.6 %collective-permute-done.refs_1_ = bf16[160,1024]{1,0:T(8,128)(2,1)S(1)} collective-permute-done((bf16[160,1024]{1,0:T(8,128)(2,1)S(1)}, bf16[160,1024]{1,0:T(8,128)(2,1)S(1)}, u32[]{:S(2)}, u32[]{:S(2)}) %collective-permute-start) | collective-permute-done | bytes 327712 | tf_op jit(solution)/shard_map/ppermute | solution.py:301
  14.1 9.5 %collective-permute-done.1.refs_2_ = bf16[160,1024]{1,0:T(8,128)(2,1)S(1)} collective-permute-done((bf16[160,1024]{1,0:T(8,128)(2,1)S(1)}, bf16[160,1024]{1,0:T(8,128)(2,1)S(1)}, u32[]{:S(2)}, u32[]{:S(2)}) %collective-permute-start.1) | collective-permute-done | bytes 327712 | tf_op jit(solution)/shard_map/ppermute | solution.py:301
  23.7 0.9 collective-permute-done.2.refs_3_
  24.6 0.1 shard_map.86
  24.7 5.6 %collective-permute-start.4 = (bf16[4,80,256]{2,1,0:T(8,128)(2,1)S(1)}, bf16[4,80,256]{2,1,0:T(8,128)(2,1)S(1)}, u32[]{:S(2)}, u32[]{:S(2)}) collective-permute-start(bf16[4,80,256]{2,1,0:T(8,128)(2,1)S(1)} %get-tuple-element.61.refs_4_), channel_id=1, source_target_pairs={{0,96},{32,0},{64,32},{96,64},{1,97},{33,1},{65,33},{97,65},{2,98}... | collective-permute-start | bytes 491528 | tf_op jit(solution)/shard_map/ppermute | solution.py:309
  30.3 0.0 collective-permute-start.3
  30.3 1.8 %collective-permute-start.5 = (bf16[4,80,256]{2,1,0:T(8,128)(2,1)S(1)}, bf16[4,80,256]{2,1,0:T(8,128)(2,1)S(1)}, u32[]{:S(2)}, u32[]{:S(2)}) collective-permute-start(bf16[4,80,256]{2,1,0:T(8,128)(2,1)S(1)} %get-tuple-element.61.refs_4_), channel_id=1, source_target_pairs={{0,8},{8,0},{1,9},{9,1},{2,10},{10,2},{3,11},{11,3},{4,12},{12,4},... | collective-permute-start | bytes 491528 | tf_op jit(solution)/shard_map/ppermute | solution.py:301
  32.2 2.6 %shard_map.87.refs_9_ = f32[8,8,256]{2,1,0:T(8,128)S(1)} custom-call(f32[1,256]{1,0:T(1,128)S(1)} %get-tuple-element.59.low_ref, f32[1,256]{1,0:T(1,128)S(1)} %get-tuple-element.60.high_ref, bf16[160,1024]{1,0:T(8,128)(2,1)S(1)} %get-tuple-element.55.refs_0_, bf16[160,1024]{1,0:T(8,128)(2,1)S(1)} %collective-permute-done.refs_1_, ...), custom_call_target="tpu_custom_call" | custom-call | flops 536870912 | bytes 1048576 | tf_op jit(solution)/shard_map/pallas_call | solution.py:178
  34.8 0.1 collective-permute-done.4.refs_4_
  34.9 3.1 %collective-permute-done.3.refs_5_ = bf16[4,80,256]{2,1,0:T(8,128)(2,1)S(1)} collective-permute-done((bf16[4,80,256]{2,1,0:T(8,128)(2,1)S(1)}, bf16[4,80,256]{2,1,0:T(8,128)(2,1)S(1)}, u32[]{:S(2)}, u32[]{:S(2)}) %collective-permute-start.3) | collective-permute-done | bytes 163872 | tf_op jit(solution)/shard_map/ppermute | solution.py:309
  37.9 4.2 %collective-permute-start.6 = (bf16[4,80,256]{2,1,0:T(8,128)(2,1)S(1)}, bf16[4,80,256]{2,1,0:T(8,128)(2,1)S(1)}, u32[]{:S(2)}, u32[]{:S(2)}) collective-permute-start(bf16[4,80,256]{2,1,0:T(8,128)(2,1)S(1)} %collective-permute-done.4.refs_4_), channel_id=1, source_target_pairs={{0,8},{8,0},{1,9},{9,1},{2,10},{10,2},{3,11},{11,3},{4,12},{12,4},... | collective-permute-start | bytes 491528 | tf_op jit(solution)/shard_map/ppermute | solution.py:301
  42.1 0.0 collective-permute-start.7
  42.1 0.1 collective-permute-start.8
  42.2 3.6 %collective-permute-start.9 = (bf16[2,80,256]{2,1,0:T(8,128)(2,1)S(1)}, bf16[2,80,256]{2,1,0:T(8,128)(2,1)S(1)}, u32[]{:S(2)}, u32[]{:S(2)}) collective-permute-start(bf16[2,80,256]{2,1,0:T(8,128)(2,1)S(1)} %slice.56), channel_id=1, source_target_pairs={{0,96},{32,0},{64,32},{96,64},{1,97},{33,1},{65,33},{97,65},{2,98}... | collective-permute-start | bytes 245768 | tf_op jit(solution)/shard_map/ppermute | solution.py:309
  45.8 0.0 collective-permute-done.5.refs_6_.refs_5_
  45.8 0.0 collective-permute-done.6.refs_7_.refs_6_
  45.8 0.0 collective-permute-done.7.refs_8_.refs_7_
  45.8 5.6 %shard_map.88.refs_8_ = f32[8,8,256]{2,1,0:T(8,128)S(1)} custom-call(f32[1,256]{1,0:T(1,128)S(1)} %get-tuple-element.59.low_ref, f32[1,256]{1,0:T(1,128)S(1)} %get-tuple-element.60.high_ref, bf16[160,1024]{1,0:T(8,128)(2,1)S(1)} %get-tuple-element.55.refs_0_, bf16[160,1024]{1,0:T(8,128)(2,1)S(1)} %collective-permute-done.refs_1_, ...), custom_call_target="tpu_custom_call" | custom-call | flops 2684354560 | bytes 1048576 | tf_op jit(solution)/shard_map/pallas_call | solution.py:178
  51.5 0.0 collective-permute-done.8.refs_4_
  51.5 0.0 collective-permute-done.9.refs_5_
  51.5 1.1 %collective-permute-start.10 = (bf16[2,80,256]{2,1,0:T(8,128)(2,1)S(1)}, bf16[2,80,256]{2,1,0:T(8,128)(2,1)S(1)}, u32[]{:S(2)}, u32[]{:S(2)}) collective-permute-start(bf16[2,80,256]{2,1,0:T(8,128)(2,1)S(1)} %collective-permute-done.8.refs_4_), channel_id=1, source_target_pairs={{0,8},{8,0},{1,9},{9,1},{2,10},{10,2},{3,11},{11,3},{4,12},{12,4},... | collective-permute-start | bytes 245768 | tf_op jit(solution)/shard_map/ppermute | solution.py:301
  52.6 0.1 collective-permute-start.11
  52.7 0.8 collective-permute-done.10.refs_6_
  53.5 0.4 collective-permute-done.11.refs_7_
  53.9 3.3 %shard_map.89.state_ref = f32[8,8,256]{2,1,0:T(8,128)S(1)} custom-call(f32[1,256]{1,0:T(1,128)S(1)} %get-tuple-element.59.low_ref, f32[1,256]{1,0:T(1,128)S(1)} %get-tuple-element.60.high_ref, bf16[160,1024]{1,0:T(8,128)(2,1)S(1)} %get-tuple-element.55.refs_0_, bf16[160,1024]{1,0:T(8,128)(2,1)S(1)} %collective-permute-done.refs_1_, ...), custom_call_target="tpu_custom_call" | custom-call | flops 1073741824 | bytes 1048576 | tf_op jit(solution)/shard_map/pallas_call | solution.py:178
  57.2 4.8 %shard_map.90 = (f32[8,128,256]{2,1,0:T(8,128)S(1)}, bf16[4,64,256]{2,1,0:T(8,128)(2,1)S(1)}, bf16[4,64,256]{2,1,0:T(8,128)(2,1)S(1)}) custom-call(s32[1]{0:T(128)} %bitcast.place_ref, f32[1,256]{1,0:T(1,128)S(1)} %get-tuple-element.59.low_ref, f32[1,256]{1,0:T(1,128)S(1)} %get-tuple-element.60.high_ref, f32[8,8,256]{2,1,0:T(8,128)S(1)} %shard_map.89.state_ref, ...), custom_call_target="tpu_custom_call" | custom-call | flops 2147483648 | bytes 2097152 | tf_op jit(solution)/shard_map/pallas_call | solution.py:204
  62.0 0.3 collective-permute-start.12
  62.2 1.2 %collective-permute-done.12 = bf16[4,64,256]{2,1,0:T(8,128)(2,1)S(1)} collective-permute-done((bf16[4,64,256]{2,1,0:T(8,128)(2,1)S(1)}, bf16[4,64,256]{2,1,0:T(8,128)(2,1)S(1)}, u32[]{:S(2)}, u32[]{:S(2)}) %collective-permute-start.12) | collective-permute-done | bytes 131104 | tf_op jit(solution)/shard_map/ppermute | solution.py:301
  63.5 0.1 collective-permute-start.13
  63.5 3.6 %collective-permute-start.14 = (bf16[2,64,256]{2,1,0:T(8,128)(2,1)S(1)}, bf16[2,64,256]{2,1,0:T(8,128)(2,1)S(1)}, u32[]{:S(2)}, u32[]{:S(2)}) collective-permute-start(bf16[2,64,256]{2,1,0:T(8,128)(2,1)S(1)} %get-tuple-element.77), channel_id=1, source_target_pairs={{0,96},{32,0},{64,32},{96,64},{1,97},{33,1},{65,33},{97,65},{2,98}... | collective-permute-start | bytes 196616 | tf_op jit(solution)/shard_map/ppermute | solution.py:309
  67.1 6.4 %shard_map.91 = (f32[8,128,256]{2,1,0:T(8,128)S(1)}, bf16[8,64,256]{2,1,0:T(8,128)(2,1)S(1)}, bf16[8,64,256]{2,1,0:T(8,128)(2,1)S(1)}) custom-call(s32[1]{0:T(128)} %bitcast.place_ref, f32[1,256]{1,0:T(1,128)S(1)} %get-tuple-element.59.low_ref, f32[1,256]{1,0:T(1,128)S(1)} %get-tuple-element.60.high_ref, f32[8,8,256]{2,1,0:T(8,128)S(1)} %shard_map.89.state_ref, ...), custom_call_target="tpu_custom_call" | custom-call | flops 4294967296 | bytes 2097152 | tf_op jit(solution)/shard_map/pallas_call | solution.py:204
  73.5 0.0 collective-permute-done.13
  73.5 0.0 collective-permute-done.14
  73.5 0.8 collective-permute-start.15
  74.4 1.2 %collective-permute-done.15 = bf16[8,64,256]{2,1,0:T(8,128)(2,1)S(1)} collective-permute-done((bf16[8,64,256]{2,1,0:T(8,128)(2,1)S(1)}, bf16[8,64,256]{2,1,0:T(8,128)(2,1)S(1)}, u32[]{:S(2)}, u32[]{:S(2)}) %collective-permute-start.15) | collective-permute-done | bytes 262176 | tf_op jit(solution)/shard_map/ppermute | solution.py:301
  75.5 0.1 add_convert_fusion
  75.7 0.1 collective-permute-start.16
  75.8 3.6 %collective-permute-start.17 = (bf16[4,64,256]{2,1,0:T(8,128)(2,1)S(1)}, bf16[4,64,256]{2,1,0:T(8,128)(2,1)S(1)}, u32[]{:S(2)}, u32[]{:S(2)}) collective-permute-start(bf16[4,64,256]{2,1,0:T(8,128)(2,1)S(1)} %get-tuple-element.89), channel_id=1, source_target_pairs={{0,96},{32,0},{64,32},{96,64},{1,97},{33,1},{65,33},{97,65},{2,98}... | collective-permute-start | bytes 393224 | tf_op jit(solution)/shard_map/ppermute | solution.py:309
  79.3 4.0 %shard_map.92 = (bf16[4,64,1280]{2,1,0:T(8,128)(2,1)S(1)}, bf16[4,64,256]{2,1,0:T(8,128)(2,1)S(1)}, bf16[4,64,256]{2,1,0:T(8,128)(2,1)S(1)}) custom-call(s32[1]{0:T(128)} %bitcast.place_ref, f32[1,256]{1,0:T(1,128)S(1)} %get-tuple-element.59.low_ref, f32[1,256]{1,0:T(1,128)S(1)} %get-tuple-element.60.high_ref, f32[8,8,256]{2,1,0:T(8,128)S(1)} %shard_map.89.state_ref, ...), custom_call_target="tpu_custom_call" | custom-call | flops 2147483648 | bytes 2097152 | tf_op jit(solution)/shard_map/pallas_call | solution.py:204
  83.3 0.0 collective-permute-done.16
  83.3 0.0 collective-permute-done.17
  83.3 2.5 %collective-permute-start.18 = (bf16[4,64,256]{2,1,0:T(8,128)(2,1)S(1)}, bf16[4,64,256]{2,1,0:T(8,128)(2,1)S(1)}, u32[]{:S(2)}, u32[]{:S(2)}) collective-permute-start(bf16[4,64,256]{2,1,0:T(8,128)(2,1)S(1)} %get-tuple-element.92), channel_id=1, source_target_pairs={{0,8},{8,0},{1,9},{9,1},{2,10},{10,2},{3,11},{11,3},{4,12},{12,4},... | collective-permute-start | bytes 393224 | tf_op jit(solution)/shard_map/ppermute | solution.py:301
  85.9 1.0 collective-permute-done.18
  86.9 0.1 add_convert_fusion.1
  87.0 20.6 %all_to_all.5 = bf16[32,8,1280]{2,1,0:T(8,128)(2,1)S(1)} all-to-all(bf16[32,8,1280]{2,1,0:T(8,128)(2,1)S(1)} %bitcast.19), channel_id=1, replica_groups=mesh['xh'=2,'zq'=4,'zp'=2,'core'=2,'y'=4,'xl'=2] {'xh','zp','y','xl'}, dimensions={0} | all-to-all | bytes 1310720 | tf_op jit(solution)/shard_map/all_to_all | solution.py:363
  107.6 0.7 fusion
  108.3 0.9 slice.72
  (12 shorter events, 0.2 us)
Async XLA Ops:
  0.6 0.7 copy-start.5
  0.6 0.7 copy-start.4
  1.3 1.0 copy-start
  2.4 1.0 copy-start.1
  3.4 0.8 copy-start.2
  4.3 0.8 copy-start.3
  5.2 8.9 %collective-permute-start = (bf16[160,1024]{1,0:T(8,128)(2,1)S(1)}, bf16[160,1024]{1,0:T(8,128)(2,1)S(1)}, u32[]{:S(2)}, u32[]{:S(2)}) collective-permute-start(bf16[160,1024]{1,0:T(8,128)(2,1)S(1)} %get-tuple-element.56), channel_id=1, source_target_pairs={{0,16},{16,0},{128,144},{144,128},{1,17},{17,1},{129,145},{145,129... | collective-permute-start | bytes 983048 | tf_op jit(solution)/shard_map/ppermute | solution.py:301
  7.8 15.9 %collective-permute-start.1 = (bf16[160,1024]{1,0:T(8,128)(2,1)S(1)}, bf16[160,1024]{1,0:T(8,128)(2,1)S(1)}, u32[]{:S(2)}, u32[]{:S(2)}) collective-permute-start(bf16[160,1024]{1,0:T(8,128)(2,1)S(1)} %get-tuple-element.57), channel_id=1, source_target_pairs={{0,128},{16,144},{128,0},{144,16},{1,129},{17,145},{129,1},{145,17... | collective-permute-start | bytes 983048 | tf_op jit(solution)/shard_map/ppermute | solution.py:301
  10.5 14.1 %collective-permute-start.2 = (bf16[160,1024]{1,0:T(8,128)(2,1)S(1)}, bf16[160,1024]{1,0:T(8,128)(2,1)S(1)}, u32[]{:S(2)}, u32[]{:S(2)}) collective-permute-start(bf16[160,1024]{1,0:T(8,128)(2,1)S(1)} %get-tuple-element.58), channel_id=1, source_target_pairs={{0,144},{16,128},{128,16},{144,0},{1,145},{17,129},{129,17},{145,1... | collective-permute-start | bytes 983048 | tf_op jit(solution)/shard_map/ppermute | solution.py:301
  24.7 10.2 %collective-permute-start.4 = (bf16[4,80,256]{2,1,0:T(8,128)(2,1)S(1)}, bf16[4,80,256]{2,1,0:T(8,128)(2,1)S(1)}, u32[]{:S(2)}, u32[]{:S(2)}) collective-permute-start(bf16[4,80,256]{2,1,0:T(8,128)(2,1)S(1)} %get-tuple-element.61.refs_4_), channel_id=1, source_target_pairs={{0,96},{32,0},{64,32},{96,64},{1,97},{33,1},{65,33},{97,65},{2,98}... | collective-permute-start | bytes 491528 | tf_op jit(solution)/shard_map/ppermute | solution.py:309
  30.3 7.6 %collective-permute-start.3 = (bf16[4,80,256]{2,1,0:T(8,128)(2,1)S(1)}, bf16[4,80,256]{2,1,0:T(8,128)(2,1)S(1)}, u32[]{:S(2)}, u32[]{:S(2)}) collective-permute-start(bf16[4,80,256]{2,1,0:T(8,128)(2,1)S(1)} %get-tuple-element.61.refs_4_), channel_id=1, source_target_pairs={{0,32},{32,64},{64,96},{96,0},{1,33},{33,65},{65,97},{97,1},{2,34}... | collective-permute-start | bytes 491528 | tf_op jit(solution)/shard_map/ppermute | solution.py:309
  30.3 15.5 %collective-permute-start.5 = (bf16[4,80,256]{2,1,0:T(8,128)(2,1)S(1)}, bf16[4,80,256]{2,1,0:T(8,128)(2,1)S(1)}, u32[]{:S(2)}, u32[]{:S(2)}) collective-permute-start(bf16[4,80,256]{2,1,0:T(8,128)(2,1)S(1)} %get-tuple-element.61.refs_4_), channel_id=1, source_target_pairs={{0,8},{8,0},{1,9},{9,1},{2,10},{10,2},{3,11},{11,3},{4,12},{12,4},... | collective-permute-start | bytes 491528 | tf_op jit(solution)/shard_map/ppermute | solution.py:301
  37.9 7.9 %collective-permute-start.6 = (bf16[4,80,256]{2,1,0:T(8,128)(2,1)S(1)}, bf16[4,80,256]{2,1,0:T(8,128)(2,1)S(1)}, u32[]{:S(2)}, u32[]{:S(2)}) collective-permute-start(bf16[4,80,256]{2,1,0:T(8,128)(2,1)S(1)} %collective-permute-done.4.refs_4_), channel_id=1, source_target_pairs={{0,8},{8,0},{1,9},{9,1},{2,10},{10,2},{3,11},{11,3},{4,12},{12,4},... | collective-permute-start | bytes 491528 | tf_op jit(solution)/shard_map/ppermute | solution.py:301
  42.1 3.7 %collective-permute-start.7 = (bf16[4,80,256]{2,1,0:T(8,128)(2,1)S(1)}, bf16[4,80,256]{2,1,0:T(8,128)(2,1)S(1)}, u32[]{:S(2)}, u32[]{:S(2)}) collective-permute-start(bf16[4,80,256]{2,1,0:T(8,128)(2,1)S(1)} %collective-permute-done.3.refs_5_), channel_id=1, source_target_pairs={{0,8},{8,0},{1,9},{9,1},{2,10},{10,2},{3,11},{11,3},{4,12},{12,4},... | collective-permute-start | bytes 491528 | tf_op jit(solution)/shard_map/ppermute | solution.py:301
  42.1 9.3 %collective-permute-start.8 = (bf16[2,80,256]{2,1,0:T(8,128)(2,1)S(1)}, bf16[2,80,256]{2,1,0:T(8,128)(2,1)S(1)}, u32[]{:S(2)}, u32[]{:S(2)}) collective-permute-start(bf16[2,80,256]{2,1,0:T(8,128)(2,1)S(1)} %slice.55), channel_id=1, source_target_pairs={{0,32},{32,64},{64,96},{96,0},{1,33},{33,65},{65,97},{97,1},{2,34}... | collective-permute-start | bytes 245768 | tf_op jit(solution)/shard_map/ppermute | solution.py:309
  42.2 9.2 %collective-permute-start.9 = (bf16[2,80,256]{2,1,0:T(8,128)(2,1)S(1)}, bf16[2,80,256]{2,1,0:T(8,128)(2,1)S(1)}, u32[]{:S(2)}, u32[]{:S(2)}) collective-permute-start(bf16[2,80,256]{2,1,0:T(8,128)(2,1)S(1)} %slice.56), channel_id=1, source_target_pairs={{0,96},{32,0},{64,32},{96,64},{1,97},{33,1},{65,33},{97,65},{2,98}... | collective-permute-start | bytes 245768 | tf_op jit(solution)/shard_map/ppermute | solution.py:309
  51.5 2.1 %collective-permute-start.10 = (bf16[2,80,256]{2,1,0:T(8,128)(2,1)S(1)}, bf16[2,80,256]{2,1,0:T(8,128)(2,1)S(1)}, u32[]{:S(2)}, u32[]{:S(2)}) collective-permute-start(bf16[2,80,256]{2,1,0:T(8,128)(2,1)S(1)} %collective-permute-done.8.refs_4_), channel_id=1, source_target_pairs={{0,8},{8,0},{1,9},{9,1},{2,10},{10,2},{3,11},{11,3},{4,12},{12,4},... | collective-permute-start | bytes 245768 | tf_op jit(solution)/shard_map/ppermute | solution.py:301
  52.6 1.3 %collective-permute-start.11 = (bf16[2,80,256]{2,1,0:T(8,128)(2,1)S(1)}, bf16[2,80,256]{2,1,0:T(8,128)(2,1)S(1)}, u32[]{:S(2)}, u32[]{:S(2)}) collective-permute-start(bf16[2,80,256]{2,1,0:T(8,128)(2,1)S(1)} %collective-permute-done.9.refs_5_), channel_id=1, source_target_pairs={{0,8},{8,0},{1,9},{9,1},{2,10},{10,2},{3,11},{11,3},{4,12},{12,4},... | collective-permute-start | bytes 245768 | tf_op jit(solution)/shard_map/ppermute | solution.py:301
  62.0 1.4 %collective-permute-start.12 = (bf16[4,64,256]{2,1,0:T(8,128)(2,1)S(1)}, bf16[4,64,256]{2,1,0:T(8,128)(2,1)S(1)}, u32[]{:S(2)}, u32[]{:S(2)}) collective-permute-start(bf16[4,64,256]{2,1,0:T(8,128)(2,1)S(1)} %get-tuple-element.70), channel_id=1, source_target_pairs={{0,8},{8,0},{1,9},{9,1},{2,10},{10,2},{3,11},{11,3},{4,12},{12,4},... | collective-permute-start | bytes 393224 | tf_op jit(solution)/shard_map/ppermute | solution.py:301
  63.5 10.1 %collective-permute-start.13 = (bf16[2,64,256]{2,1,0:T(8,128)(2,1)S(1)}, bf16[2,64,256]{2,1,0:T(8,128)(2,1)S(1)}, u32[]{:S(2)}, u32[]{:S(2)}) collective-permute-start(bf16[2,64,256]{2,1,0:T(8,128)(2,1)S(1)} %get-tuple-element.76), channel_id=1, source_target_pairs={{0,32},{32,64},{64,96},{96,0},{1,33},{33,65},{65,97},{97,1},{2,34}... | collective-permute-start | bytes 196616 | tf_op jit(solution)/shard_map/ppermute | solution.py:309
  63.5 10.0 %collective-permute-start.14 = (bf16[2,64,256]{2,1,0:T(8,128)(2,1)S(1)}, bf16[2,64,256]{2,1,0:T(8,128)(2,1)S(1)}, u32[]{:S(2)}, u32[]{:S(2)}) collective-permute-start(bf16[2,64,256]{2,1,0:T(8,128)(2,1)S(1)} %get-tuple-element.77), channel_id=1, source_target_pairs={{0,96},{32,0},{64,32},{96,64},{1,97},{33,1},{65,33},{97,65},{2,98}... | collective-permute-start | bytes 196616 | tf_op jit(solution)/shard_map/ppermute | solution.py:309
  73.5 2.0 %collective-permute-start.15 = (bf16[8,64,256]{2,1,0:T(8,128)(2,1)S(1)}, bf16[8,64,256]{2,1,0:T(8,128)(2,1)S(1)}, u32[]{:S(2)}, u32[]{:S(2)}) collective-permute-start(bf16[8,64,256]{2,1,0:T(8,128)(2,1)S(1)} %get-tuple-element.80), channel_id=1, source_target_pairs={{0,8},{8,0},{1,9},{9,1},{2,10},{10,2},{3,11},{11,3},{4,12},{12,4},... | collective-permute-start | bytes 786440 | tf_op jit(solution)/shard_map/ppermute | solution.py:301
  75.7 7.6 %collective-permute-start.16 = (bf16[4,64,256]{2,1,0:T(8,128)(2,1)S(1)}, bf16[4,64,256]{2,1,0:T(8,128)(2,1)S(1)}, u32[]{:S(2)}, u32[]{:S(2)}) collective-permute-start(bf16[4,64,256]{2,1,0:T(8,128)(2,1)S(1)} %get-tuple-element.88), channel_id=1, source_target_pairs={{0,32},{32,64},{64,96},{96,0},{1,33},{33,65},{65,97},{97,1},{2,34}... | collective-permute-start | bytes 393224 | tf_op jit(solution)/shard_map/ppermute | solution.py:309
  75.8 7.6 %collective-permute-start.17 = (bf16[4,64,256]{2,1,0:T(8,128)(2,1)S(1)}, bf16[4,64,256]{2,1,0:T(8,128)(2,1)S(1)}, u32[]{:S(2)}, u32[]{:S(2)}) collective-permute-start(bf16[4,64,256]{2,1,0:T(8,128)(2,1)S(1)} %get-tuple-element.89), channel_id=1, source_target_pairs={{0,96},{32,0},{64,32},{96,64},{1,97},{33,1},{65,33},{97,65},{2,98}... | collective-permute-start | bytes 393224 | tf_op jit(solution)/shard_map/ppermute | solution.py:309
  83.3 3.5 %collective-permute-start.18 = (bf16[4,64,256]{2,1,0:T(8,128)(2,1)S(1)}, bf16[4,64,256]{2,1,0:T(8,128)(2,1)S(1)}, u32[]{:S(2)}, u32[]{:S(2)}) collective-permute-start(bf16[4,64,256]{2,1,0:T(8,128)(2,1)S(1)} %get-tuple-element.92), channel_id=1, source_target_pairs={{0,8},{8,0},{1,9},{9,1},{2,10},{10,2},{3,11},{11,3},{4,12},{12,4},... | collective-permute-start | bytes 393224 | tf_op jit(solution)/shard_map/ppermute | solution.py:301

commit v4 on v3

v4 whole, which is shorter than its diff:
```python
import functools
import math

import jax
import jax.numpy as jnp
from jax import lax
from jax.experimental import pallas as pl
from jax.experimental.pallas import tpu as pltpu
from jax.sharding import Mesh, PartitionSpec as P

QUERY_HEADS = 64
KEY_VALUE_HEADS = 8
HEAD_SIZE = 128
GROUP = QUERY_HEADS // KEY_VALUE_HEADS
NEG_BIG = -1e30
CODE_SPAN = 2048
META_ROWS = 16
HEADS_PER_STEP = 4
SCALE = 1.0 / math.sqrt(HEAD_SIZE)
EXP2_SCALE = SCALE * math.log2(math.e)

NT = (((1,), (1,)), ((), ()))
NN = (((1,), (0,)), ((), ()))


def dot(a, b, dims):
    return lax.dot_general(a, b, dims, preferred_element_type=jnp.float32)


def key_spans(piece_refs, row_count):
    spans, start = [], 0
    for ref in piece_refs:
        size = ref.shape[0] * row_count
        spans.append((ref, slice(start, start + size), size))
        start += size
    return spans, start


def keys_of(ref, size, row_count):
    return ref[:, 0:row_count, 0:HEAD_SIZE].reshape(size, HEAD_SIZE)


def values_of(ref, size, row_count):
    return ref[:, 0:row_count, HEAD_SIZE:2 * HEAD_SIZE].reshape(size, HEAD_SIZE)


def fill_bias(bias_ref, spans, low_ref, high_ref, row_count):
    rows = low_ref.shape[1]
    for ref, part, size in spans:
        for b in range(ref.shape[0]):
            digits = ref[b, row_count:row_count + META_ROWS, :].astype(jnp.float32)[0:1, :]
            code = digits[:, 0:128] * 128.0 + digits[:, 128:256]
            column = jnp.broadcast_to(code, (128, 128)).T[0:row_count, :]
            begin = part.start + b * row_count
            for r in range(rows // 128):
                low = low_ref[:, r * 128:(r + 1) * 128]
                high = high_ref[:, r * 128:(r + 1) * 128]
                allowed = (column >= low) & (column <= high)
                bias_ref[begin:begin + row_count, r * 128:(r + 1) * 128] = jnp.where(allowed, 0.0, NEG_BIG)


def rows_of(row_refs, lanes, row_count):
    q = jnp.concatenate([ref[0:row_count, lanes] for ref in row_refs], axis=0)
    do = jnp.concatenate([ref[row_count:2 * row_count, lanes] for ref in row_refs], axis=0)
    return q, do


def absorbed(top, total, cross, scores, softmax_grads):
    rows = top.shape[1]
    new = top
    for s in scores:
        peak = jnp.max(s.reshape(s.shape[0] // 8, 8, rows), axis=0)
        new = jnp.maximum(new, jnp.max(peak, axis=0, keepdims=True))
    factor = jnp.exp2(top - new)
    total, cross = total * factor, cross * factor
    weights = [jnp.exp2(s - new) for s in scores]
    for p, dp in zip(weights, softmax_grads):
        part_sum = jnp.sum(p.reshape(p.shape[0] // 8, 8, rows), axis=0)
        part_dot = jnp.sum((p * dp).reshape(p.shape[0] // 8, 8, rows), axis=0)
        total = total + jnp.sum(part_sum, axis=0, keepdims=True)
        cross = cross + jnp.sum(part_dot, axis=0, keepdims=True)
    return new, total, cross, weights


def stats_kernel(count, low_ref, high_ref, *refs):
    row_refs, piece_refs, (state_ref, bias_ref) = refs[0:4], refs[4:4 + count], refs[4 + count:]
    rows = low_ref.shape[1]
    row_count = rows // 4
    spans, _ = key_spans(piece_refs, row_count)
    fill_bias(bias_ref, spans, low_ref, high_ref, row_count)

    def step(g, carry):
        for j in range(HEADS_PER_STEP):
            h = g * HEADS_PER_STEP + j
            lanes = pl.ds(pl.multiple_of(h * HEAD_SIZE, HEAD_SIZE), HEAD_SIZE)
            q, do = rows_of(row_refs, lanes, row_count)
            top = jnp.full((1, rows), NEG_BIG, jnp.float32)
            total = jnp.zeros((1, rows), jnp.float32)
            cross = jnp.zeros((1, rows), jnp.float32)
            for ref, part, size in spans:
                s = dot(keys_of(ref, size, row_count), q, NT) * EXP2_SCALE + bias_ref[part, :]
                dp = dot(values_of(ref, size, row_count), do, NT)
                top, total, cross = absorbed(top, total, cross, [s], [dp])[0:3]
            state_ref[h, 0:1, :] = top
            state_ref[h, 1:2, :] = total
            state_ref[h, 2:3, :] = cross
        return carry

    lax.fori_loop(0, GROUP // HEADS_PER_STEP, step, 0)


def grads_kernel(first, last, count, place_ref, low_ref, high_ref, state_ref, *refs):
    row_refs, piece_refs, rest = refs[0:4], refs[4:4 + count], refs[4 + count:]
    if first:
        dq_ref, near_ref, far_ref, final_ref, bias_ref, kt_ref, ds_ref, acc_ref = rest
    else:
        before_ref, dq_ref, near_ref, far_ref, bias_ref, kt_ref, ds_ref, acc_ref = rest
    rows = low_ref.shape[1]
    row_count = rows // 4
    heads = HEADS_PER_STEP
    spans, keys = key_spans(piece_refs, row_count)
    fill_bias(bias_ref, spans, low_ref, high_ref, row_count)
    for ref, part, size in spans:
        kt_ref[:, part] = keys_of(ref, size, row_count).T
    acc_ref[...] = jnp.zeros_like(acc_ref)
    place = place_ref[0]

    def step(g, carry):
        q, do, lanes, p_low, ds_low = [], [], [], [], []
        for j in range(heads):
            h = g * heads + j
            lanes.append(pl.ds(pl.multiple_of(h * HEAD_SIZE, HEAD_SIZE), HEAD_SIZE))
            one_q, one_do = rows_of(row_refs, lanes[j], row_count)
            q.append(one_q)
            do.append(one_do)

            def products(ref, part, size):
                s = dot(keys_of(ref, size, row_count), one_q, NT) * EXP2_SCALE + bias_ref[part, :]
                return s, dot(values_of(ref, size, row_count), one_do, NT)

            if first:
                pairs = [products(*span) for span in spans]
                top, total, cross, weights = absorbed(
                    state_ref[h, 0:1, :], state_ref[h, 1:2, :], state_ref[h, 2:3, :],
                    [s for s, _ in pairs], [dp for _, dp in pairs])
                inverse = 1.0 / total
                delta = cross * inverse
                final_ref[h, 0:1, :] = top + jnp.log2(total)
                final_ref[h, 1:2, :] = delta
                softmax = [p * inverse for p in weights]
                softmax_grads = [dp for _, dp in pairs]
            else:
                offset, delta = state_ref[h, 0:1, :], state_ref[h, 1:2, :]
                softmax, softmax_grads = [], []
                for span in spans:
                    s, dp = products(*span)
                    softmax.append(jnp.exp2(s - offset))
                    softmax_grads.append(dp)
            p_low.append([p.astype(jnp.bfloat16) for p in softmax])
            ds_low.append([(p * (dp - delta)).astype(jnp.bfloat16) for p, dp in zip(softmax, softmax_grads)])
        q_all, do_all = jnp.concatenate(q, axis=0), jnp.concatenate(do, axis=0)
        for i, (ref, part, size) in enumerate(spans):
            p_all = jnp.concatenate([p_low[j][i] for j in range(heads)], axis=1)
            ds_all = jnp.concatenate([ds_low[j][i] for j in range(heads)], axis=1)
            ds_ref[part, :] = ds_all
            acc_ref[part, HEAD_SIZE:2 * HEAD_SIZE] += dot(p_all, do_all, NN)
            acc_ref[part, 0:HEAD_SIZE] += dot(ds_all, q_all, NN)
        dqt = dot(kt_ref[...], ds_ref[...], NN)
        for j in range(heads):
            part = dqt[:, j * rows:(j + 1) * rows]
            if not first:
                part = part + before_ref[g * heads + j]
            if last:
                dq = (part * SCALE).T.astype(jnp.bfloat16)
                for r in range(4):
                    dq_ref[place ^ r, :, lanes[j]] = dq[r * row_count:(r + 1) * row_count, :]
            else:
                dq_ref[g * heads + j] = part
        return carry

    lax.fori_loop(0, GROUP // heads, step, 0)
    sources = near_ref.shape[0]
    for i, out_ref in enumerate((near_ref, far_ref)):
        part = slice(i * sources * row_count, (i + 1) * sources * row_count)
        shape = (sources, row_count, HEAD_SIZE)
        out_ref[:, :, 0:HEAD_SIZE] = (acc_ref[part, 0:HEAD_SIZE] * SCALE).astype(jnp.bfloat16).reshape(shape)
        out_ref[:, :, HEAD_SIZE:2 * HEAD_SIZE] = acc_ref[part, HEAD_SIZE:2 * HEAD_SIZE].astype(jnp.bfloat16).reshape(shape)


VMEM = pl.BlockSpec(memory_space=pltpu.VMEM)
SMEM = pl.BlockSpec(memory_space=pltpu.SMEM)
ANY = pl.BlockSpec(memory_space=pltpu.HBM)


def stats(low, high, row_arrays, pieces):
    rows = low.shape[1]
    keys = sum(piece.shape[0] for piece in pieces) * rows // 4
    inputs = (low, high, *row_arrays, *pieces)
    return pl.pallas_call(
        functools.partial(stats_kernel, len(pieces)),
        out_shape=jax.ShapeDtypeStruct((GROUP, 8, rows), jnp.float32),
        in_specs=[VMEM] * len(inputs),
        out_specs=VMEM,
        scratch_shapes=[pltpu.VMEM((keys, rows), jnp.float32)],
        compiler_params=pltpu.CompilerParams(vmem_limit_bytes=32 * 1024 * 1024),
        cost_estimate=pl.CostEstimate(
            flops=8 * keys * rows * HEAD_SIZE * GROUP, bytes_accessed=1024 * 1024,
            transcendentals=keys * rows * GROUP),
    )(*inputs)


def grads(place, low, high, state, row_arrays, pieces, before, last):
    rows = low.shape[1]
    row_count = rows // 4
    sources = sum(piece.shape[0] for piece in pieces)
    keys = sources * row_count
    width = 2 * HEAD_SIZE
    first = before is None
    inputs = (low, high, state, *row_arrays, *pieces) + (() if first else (before,))
    part = jax.ShapeDtypeStruct((sources // 2, row_count, width), jnp.bfloat16)
    extra = (jax.ShapeDtypeStruct((GROUP, 8, rows), jnp.float32),) if first else ()
    if last:
        dq = jax.ShapeDtypeStruct((4, row_count, GROUP * HEAD_SIZE + width), jnp.bfloat16)
    else:
        dq = jax.ShapeDtypeStruct((GROUP, HEAD_SIZE, rows), jnp.float32)
    return pl.pallas_call(
        functools.partial(grads_kernel, first, last, len(pieces)),
        out_shape=(dq, part, part) + extra,
        in_specs=[SMEM] + [VMEM] * len(inputs),
        out_specs=(VMEM,) * (3 + len(extra)),
        scratch_shapes=[
            pltpu.VMEM((keys, rows), jnp.float32),
            pltpu.VMEM((HEAD_SIZE, keys), jnp.bfloat16),
            pltpu.VMEM((keys, HEADS_PER_STEP * rows), jnp.bfloat16),
            pltpu.VMEM((keys, width), jnp.float32),
        ],
        compiler_params=pltpu.CompilerParams(vmem_limit_bytes=32 * 1024 * 1024),
        cost_estimate=pl.CostEstimate(
            flops=16 * keys * rows * HEAD_SIZE * GROUP, bytes_accessed=2 * 1024 * 1024,
            transcendentals=keys * rows * GROUP),
    )(place, *inputs)


def copies(pairs, sems):
    started = [pltpu.make_async_copy(source, target, sems.at[i]) for i, (source, target) in enumerate(pairs)]
    for copy in started:
        copy.start()
    for copy in started:
        copy.wait()


def pack_keys_kernel(place_ref, code_ref, k_ref, v_ref, self_ref, pair_ref, across_ref, sems):
    row_count = k_ref.shape[1]
    place = place_ref[0]
    targets = ((0, self_ref), (1, pair_ref.at[0]), (3, pair_ref.at[1]), (2, across_ref))
    pairs = []
    for r, target in targets:
        pairs.append((k_ref.at[place ^ r], target.at[0:row_count, 0:HEAD_SIZE]))
        pairs.append((v_ref.at[place ^ r], target.at[0:row_count, HEAD_SIZE:2 * HEAD_SIZE]))
    for r, target in targets:
        code = code_ref[pl.ds(place ^ r, 1), :]
        for i, digit in enumerate((code >> 7, code & 127)):
            spread = jnp.broadcast_to(digit.astype(jnp.float32), (META_ROWS, 128)).astype(jnp.bfloat16)
            target[row_count:row_count + META_ROWS, i * 128:(i + 1) * 128] = spread
    copies(pairs, sems)


def pack_rows_kernel(place_ref, q_ref, do_ref, *refs):
    out_refs, sems = refs[0:4], refs[4]
    row_count = q_ref.shape[1]
    place = place_ref[0]
    pairs = []
    for r, target in enumerate(out_refs):
        pairs.append((q_ref.at[place ^ r], target.at[0:row_count]))
        pairs.append((do_ref.at[place ^ r], target.at[row_count:2 * row_count]))
    copies(pairs, sems)


def own_kernel(self_ref, pair_ref, across_ref, own_ref, low_ref, high_ref):
    row_count = self_ref.shape[0] - META_ROWS
    codes = []
    for r, value in enumerate((self_ref[...], pair_ref[0], across_ref[0], across_ref[1])):
        own_ref[r] = value
        digits = value[row_count:, :].astype(jnp.float32)[0:8, :]
        codes.append(digits[:, 0:128] * 128.0 + digits[:, 128:256])
    lane = lax.broadcasted_iota(jnp.int32, (8, 128), 1)
    for i in range(2):
        code = jnp.where(lane < row_count, codes[2 * i], pltpu.roll(codes[2 * i + 1], row_count, 1))[0:1, :]
        high_ref[:, i * 128:(i + 1) * 128] = code
        low_ref[:, i * 128:(i + 1) * 128] = jnp.floor(code * (1.0 / CODE_SPAN)) * CODE_SPAN


def pack_keys(place, code, key_vectors, value_vectors):
    lines = key_vectors.shape[1] + META_ROWS
    one = jax.ShapeDtypeStruct((lines, 2 * HEAD_SIZE), jnp.bfloat16)
    two = jax.ShapeDtypeStruct((2, lines, 2 * HEAD_SIZE), jnp.bfloat16)
    return pl.pallas_call(
        pack_keys_kernel,
        out_shape=(one, two, one),
        in_specs=[SMEM, VMEM, ANY, ANY],
        out_specs=(VMEM,) * 3,
        scratch_shapes=[pltpu.SemaphoreType.DMA((8,))],
        compiler_params=pltpu.CompilerParams(vmem_limit_bytes=32 * 1024 * 1024),
    )(place, code, key_vectors, value_vectors)


def pack_rows(place, queries, output_gradient):
    row_count, wide = queries.shape[1:]
    return pl.pallas_call(
        pack_rows_kernel,
        out_shape=(jax.ShapeDtypeStruct((2 * row_count, wide), jnp.bfloat16),) * 4,
        in_specs=[SMEM, ANY, ANY],
        out_specs=(VMEM,) * 4,
        scratch_shapes=[pltpu.SemaphoreType.DMA((8,))],
        compiler_params=pltpu.CompilerParams(vmem_limit_bytes=32 * 1024 * 1024),
    )(place, queries, output_gradient)


def own_keys(mine, paired, crossed):
    rows = 4 * (mine.shape[0] - META_ROWS)
    row = jax.ShapeDtypeStruct((1, rows), jnp.float32)
    own = jax.ShapeDtypeStruct((4,) + mine.shape, jnp.bfloat16)
    return pl.pallas_call(
        own_kernel,
        out_shape=(own, row, row),
        in_specs=[VMEM] * 3,
        out_specs=(VMEM,) * 3,
        compiler_params=pltpu.CompilerParams(vmem_limit_bytes=32 * 1024 * 1024),
    )(mine, paired, crossed)


PLANE = ("xh", "zp")
FINAL = ("xh", "zp", "y", "xl")
RING = 4


def swapped(array, axes, by, count):
    return lax.ppermute(array, axes, [(i, i ^ by) for i in range(count)])


def other_core(array):
    return swapped(array, "core", 1, 2)


def turned(array, by):
    return lax.ppermute(array, "zq", [(i, (i + by) % RING) for i in range(RING)])


def plus(*arrays):
    return sum(a.astype(jnp.float32) for a in arrays).astype(jnp.bfloat16)


def on_device(queries, key_vectors, value_vectors, output_gradient, positions, segments):
    window_count, row_count, _ = queries.shape
    across, pair = lax.axis_index("xh"), lax.axis_index("zp")
    place = across * 2 + pair

    spot = place.reshape(1).astype(jnp.int32)
    code = jnp.pad(segments * CODE_SPAN + positions, ((0, 0), (0, 128 - row_count)))
    tied = lax.optimization_barrier
    mine, to_pair, across_part = pack_keys(spot, code, key_vectors, value_vectors)
    paired = swapped(to_pair, PLANE, 1, 4)
    spot, to_pair = tied((spot, to_pair))
    loads = pack_rows(spot, queries, output_gradient)
    row_arrays = [loads[0]] + [swapped(loads[r], PLANE, r, 4) for r in (1, 2, 3)]
    crossed = swapped(jnp.stack([across_part, paired[1]]), PLANE, 2, 4)
    own, low, high = own_keys(mine, paired, crossed)

    before = turned(own, 1)
    after = turned(own, -1)
    far_own = other_core(own)
    opposite = turned(before, 1)
    far_after, far_before = other_core(after), other_core(before)
    state = stats(low, high, row_arrays, [own, far_own, after, far_after, before, far_before])
    state, opposite = tied((state, opposite))
    far_opposite = other_core(opposite)

    dq, near_2, far_2, state = grads(spot, low, high, state, row_arrays, [opposite, far_opposite], None, False)
    sum_2 = plus(near_2, other_core(far_2))
    spot, dq, sum_2 = tied((spot, dq, sum_2))
    passed = turned(sum_2, 1)
    dq, near_1, far_1 = grads(spot, low, high, state, row_arrays, [after, before, far_after, far_before], dq, False)
    dq, near_1, far_1, passed = tied((dq, near_1, far_1, passed))
    beside = other_core(far_1)
    next_up = plus(near_1[0:4], beside[0:4], passed)
    next_down = plus(near_1[4:8], beside[4:8])
    spot, dq, next_up, next_down = tied((spot, dq, next_up, next_down))
    to_up, to_down = turned(next_up, 1), turned(next_down, -1)
    dq, near_0, far_0 = grads(spot, low, high, state, row_arrays, [own, far_own], dq, True)
    dq, near_0, far_0, to_up, to_down = tied((dq, near_0, far_0, to_up, to_down))
    dkv_own = plus(near_0, other_core(far_0), to_up, to_down)

    flip = dkv_own.reshape((2, 2) + dkv_own.shape[1:])
    flip = jnp.where(across == 1, flip[::-1], flip)
    flip = jnp.where(pair == 1, flip[:, ::-1], flip)

    heads = KEY_VALUE_HEADS
    out_rows = row_count // heads
    split = GROUP * HEAD_SIZE
    leaving = dq.at[:, :, split:].set(flip.reshape(dkv_own.shape)).reshape(window_count * heads, out_rows, split + 2 * HEAD_SIZE)
    final = lax.all_to_all(leaving, FINAL, 0, 0, tiled=True)

    def merged(array):
        width = array.shape[-1]
        return array.reshape(window_count, heads, out_rows, width).transpose(0, 2, 1, 3).reshape(window_count, out_rows, heads * width)

    return (
        merged(final[..., 0:split]),
        merged(final[..., split:split + HEAD_SIZE]),
        merged(final[..., split + HEAD_SIZE:]),
    )


def solution(mesh):
    fine = Mesh(mesh.devices.reshape(2, RING, 2, 2, 4, 2), ("xh", "zq", "zp", "core", "y", "xl"))
    ctx, head = ("xh", "zq", "zp", "core"), ("y", "xl")
    vectors = P(None, ctx, head)
    out = P(None, ctx + head, None)
    return jax.shard_map(
        on_device,
        mesh=fine,
        in_specs=(vectors, vectors, vectors, vectors, P(None, ctx), P(None, ctx)),
        out_specs=(out, out, out),
        check_vma=False,
    )
```

time: 109 us -> 98.9 us (0.907)
  Pallas kernels: 26.8 us -> 20.7 us
  waiting for transfers between devices: 21.8 us -> 15.9 us
  starting transfers between devices: 32.8 us -> 33.9 us
    ppermute x11 -> x12, waiting for transfers between devices: 18.6 us -> 10.4 us  [swapped(): return lax.ppermute(array, axes, [(i, i ^ by) for i in range(count)])]
    pallas_call x5 -> x4, Pallas kernels: 11.7 us -> 6.97 us  [the longest x1 5.37 us: stats(): pl.pallas_call(functools.partial(stats_kernel, len(pieces)), out_shape=ja...]
    ppermute x11 -> x12, starting transfers between devices: 16.2 us -> 19.1 us  [swapped(): return lax.ppermute(array, axes, [(i, i ^ by) for i in range(count)])]
    ppermute x8 -> x6, waiting for transfers between devices: 3.19 us -> 5.56 us  [turned(): lax.ppermute(array, 'zq', [(i, (i + by) % RING) for i in range(RING)])]
    ppermute x8 -> x6, starting transfers between devices: 16.6 us -> 14.7 us  [turned(): lax.ppermute(array, 'zq', [(i, (i + by) % RING) for i in range(RING)])]
    pallas_call x3, Pallas kernels: 15.2 us -> 13.7 us  [grads(): pl.pallas_call(functools.partial(grads_kernel, first, last, len(pieces)),...]
  transfers between devices with their start and end apart: 19 -> 18, of which waited for: 10 -> 7; matrix products, arithmetic and copies ran while one was open for 0% -> 0% of each run, Pallas kernels for 17% -> 16%
where the time goes in v4:
time: 98.9 us; the launch traced here: 98 us
  starting transfers between devices  33.9 us (34%)
  Pallas kernels  20.7 us (21%)
  blocking collectives  20.5 us (21%)
  waiting for transfers between devices  15.9 us (16%)
  local copies, waits for them, and re-layouts  5.98 us (6%)
    all_to_all x1, blocking collectives, on_device(): final = lax.all_to_all(leaving, FINAL, 0, 0, tiled=True)  20.5 us
    ppermute x12, starting transfers between devices, swapped(): return lax.ppermute(array, axes, [(i, i ^ by) for i in range(count)])  19.1 us
    ppermute x6, starting transfers between devices, turned(): lax.ppermute(array, 'zq', [(i, (i + by) % RING) for i in range(RING)])  14.7 us
    pallas_call x3, Pallas kernels, grads(): pl.pallas_call(functools.partial(grads_kernel, first, last, len(pieces)),...  13.7 us
    ppermute x12, waiting for transfers between devices, swapped(): return lax.ppermute(array, axes, [(i, i ^ by) for i in range(count)])  10.4 us
    ppermute x6, waiting for transfers between devices, turned(): lax.ppermute(array, 'zq', [(i, (i + by) % RING) for i in range(RING)])  5.56 us
    pallas_call x1, Pallas kernels, stats(): pl.pallas_call(functools.partial(stats_kernel, len(pieces)), out_shape=ja...  5.37 us
    unnamed x12, local copies, waits for them, and re-layouts  4.44 us
  transfers between devices with their start and end apart: 18, of which 7 were waited for; matrix products, arithmetic and copies ran while one was open for 0% of the time, Pallas kernels for 16%

profile of v4, /device:TPU:1, one launch (start us, length us, event | category | flops | bytes accessed | tf_op | source)
XLA Modules:
  0.0 98.0 jit_solution(3117833601911929839)
XLA Ops:
  0.6 0.0 copy-start.5
  0.6 0.0 copy-start.4
  0.7 0.7 copy-done.5
  1.3 0.0 copy-done.4
  1.3 0.0 copy-start.2
  1.4 0.8 copy-done.2
  2.2 0.0 copy-start.3
  2.2 0.8 copy-done.3
  3.0 0.1 shard_map.85
  3.2 2.6 %collective-permute-start = (bf16[2,80,256]{2,1,0:T(8,128)(2,1)S(1)}, bf16[2,80,256]{2,1,0:T(8,128)(2,1)S(1)}, u32[]{:S(2)}, u32[]{:S(2)}) collective-permute-start(bf16[2,80,256]{2,1,0:T(8,128)(2,1)S(1)} %get-tuple-element.54), channel_id=1, source_target_pairs={{0,16},{16,0},{128,144},{144,128},{1,17},{17,1},{129,145},{145,129... | collective-permute-start | bytes 245768 | tf_op jit(solution)/shard_map/ppermute | solution.py:338
  5.7 0.0 copy-start
  5.7 1.0 %copy-done = bf16[4,64,1024]{2,1,0:T(8,128)(2,1)S(1)} copy-done((bf16[4,64,1024]{2,1,0:T(8,128)(2,1)S(1)}, bf16[4,64,1024]{2,1,0:T(8,128)(2,1)}, u32[]{:S(2)}) %copy-start) | copy-done | bytes 524312
  6.8 0.0 copy-start.1
  6.8 1.0 %copy-done.1 = bf16[4,64,1024]{2,1,0:T(8,128)(2,1)S(1)} copy-done((bf16[4,64,1024]{2,1,0:T(8,128)(2,1)S(1)}, bf16[4,64,1024]{2,1,0:T(8,128)(2,1)}, u32[]{:S(2)}) %copy-start.1) | copy-done | bytes 524312
  7.8 1.4 %shard_map.87 = (bf16[128,1024]{1,0:T(8,128)(2,1)S(1)}, bf16[128,1024]{1,0:T(8,128)(2,1)S(1)}, bf16[128,1024]{1,0:T(8,128)(2,1)S(1)}, bf16[128,1024]{1,0:T(8,128)(2,1)S(1)}) custom-call(s32[1]{0:T(128)} %bitcast.place_ref, bf16[4,64,1024]{2,1,0:T(8,128)(2,1)S(1)} %copy-done, bf16[4,64,1024]{2,1,0:T(8,128)(2,1)S(1)} %copy-done.1), custom_call_target="tpu_custom_call" | custom-call | tf_op jit(solution)/shard_map/pallas_call | solution.py:309
  9.2 0.1 collective-permute-start.2
  9.3 0.0 collective-permute-done.pair_ref
  9.3 2.8 %collective-permute-start.1 = (bf16[2,80,256]{2,1,0:T(8,128)(2,1)S(1)}, bf16[2,80,256]{2,1,0:T(8,128)(2,1)S(1)}, u32[]{:S(2)}, u32[]{:S(2)}) collective-permute-start(bf16[2,80,256]{2,1,0:T(8,128)(2,1)S(1)} %pad_maximum_fusion), channel_id=1, source_target_pairs={{0,128},{16,144},{128,0},{144,16},{1,129},{17,145},{129,1},{145,17... | collective-permute-start | bytes 245768 | tf_op jit(solution)/shard_map/ppermute | solution.py:338
  12.2 2.1 %collective-permute-done.1.across_ref = bf16[2,80,256]{2,1,0:T(8,128)(2,1)S(1)} collective-permute-done((bf16[2,80,256]{2,1,0:T(8,128)(2,1)S(1)}, bf16[2,80,256]{2,1,0:T(8,128)(2,1)S(1)}, u32[]{:S(2)}, u32[]{:S(2)}) %collective-permute-start.1) | collective-permute-done | bytes 81952 | tf_op jit(solution)/shard_map/ppermute | solution.py:338
  14.2 0.1 shard_map.86
  14.3 3.0 %collective-permute-start.8 = (bf16[4,80,256]{2,1,0:T(8,128)(2,1)S(1)}, bf16[4,80,256]{2,1,0:T(8,128)(2,1)S(1)}, u32[]{:S(2)}, u32[]{:S(2)}) collective-permute-start(bf16[4,80,256]{2,1,0:T(8,128)(2,1)S(1)} %get-tuple-element.64.refs_4_), channel_id=1, source_target_pairs={{0,32},{32,64},{64,96},{96,0},{1,33},{33,65},{65,97},{97,1},{2,34}... | collective-permute-start | bytes 491528 | tf_op jit(solution)/shard_map/ppermute | solution.py:346
  17.3 2.9 %collective-permute-start.6 = (bf16[4,80,256]{2,1,0:T(8,128)(2,1)S(1)}, bf16[4,80,256]{2,1,0:T(8,128)(2,1)S(1)}, u32[]{:S(2)}, u32[]{:S(2)}) collective-permute-start(bf16[4,80,256]{2,1,0:T(8,128)(2,1)S(1)} %get-tuple-element.64.refs_4_), channel_id=1, source_target_pairs={{0,96},{32,0},{64,32},{96,64},{1,97},{33,1},{65,33},{97,65},{2,98}... | collective-permute-start | bytes 491528 | tf_op jit(solution)/shard_map/ppermute | solution.py:346
  20.2 2.7 %collective-permute-start.3 = (bf16[128,1024]{1,0:T(8,128)(2,1)S(1)}, bf16[128,1024]{1,0:T(8,128)(2,1)S(1)}, u32[]{:S(2)}, u32[]{:S(2)}) collective-permute-start(bf16[128,1024]{1,0:T(8,128)(2,1)S(1)} %get-tuple-element.62), channel_id=1, source_target_pairs={{0,128},{16,144},{128,0},{144,16},{1,129},{17,145},{129,1},{145,17... | collective-permute-start | bytes 786440 | tf_op jit(solution)/shard_map/ppermute | solution.py:338
  23.0 0.7 collective-permute-start.4
  23.7 0.0 collective-permute-done.2.refs_1_
  23.7 3.2 %collective-permute-start.5 = (bf16[4,80,256]{2,1,0:T(8,128)(2,1)S(1)}, bf16[4,80,256]{2,1,0:T(8,128)(2,1)S(1)}, u32[]{:S(2)}, u32[]{:S(2)}) collective-permute-start(bf16[4,80,256]{2,1,0:T(8,128)(2,1)S(1)} %get-tuple-element.64.refs_4_), channel_id=1, source_target_pairs={{0,8},{8,0},{1,9},{9,1},{2,10},{10,2},{3,11},{11,3},{4,12},{12,4},... | collective-permute-start | bytes 491528 | tf_op jit(solution)/shard_map/ppermute | solution.py:338
  26.9 0.0 collective-permute-done.8.refs_8_.refs_5_
  26.9 1.6 %collective-permute-start.9 = (bf16[4,80,256]{2,1,0:T(8,128)(2,1)S(1)}, bf16[4,80,256]{2,1,0:T(8,128)(2,1)S(1)}, u32[]{:S(2)}, u32[]{:S(2)}) collective-permute-start(bf16[4,80,256]{2,1,0:T(8,128)(2,1)S(1)} %collective-permute-done.8.refs_8_.refs_5_), channel_id=1, source_target_pairs={{0,8},{8,0},{1,9},{9,1},{2,10},{10,2},{3,11},{11,3},{4,12},{12,4},... | collective-permute-start | bytes 491528 | tf_op jit(solution)/shard_map/ppermute | solution.py:338
  28.5 0.0 collective-permute-done.6.refs_6_.refs_4_
  28.5 0.4 collective-permute-start.7
  28.9 0.0 collective-permute-done.3.refs_2_
  28.9 2.9 %collective-permute-start.10 = (bf16[4,80,256]{2,1,0:T(8,128)(2,1)S(1)}, bf16[4,80,256]{2,1,0:T(8,128)(2,1)S(1)}, u32[]{:S(2)}, u32[]{:S(2)}) collective-permute-start(bf16[4,80,256]{2,1,0:T(8,128)(2,1)S(1)} %collective-permute-done.8.refs_8_.refs_5_), channel_id=1, source_target_pairs={{0,32},{32,64},{64,96},{96,0},{1,33},{33,65},{65,97},{97,1},{2,34}... | collective-permute-start | bytes 491528 | tf_op jit(solution)/shard_map/ppermute | solution.py:346
  31.8 4.1 %collective-permute-done.4.refs_3_ = bf16[128,1024]{1,0:T(8,128)(2,1)S(1)} collective-permute-done((bf16[128,1024]{1,0:T(8,128)(2,1)S(1)}, bf16[128,1024]{1,0:T(8,128)(2,1)S(1)}, u32[]{:S(2)}, u32[]{:S(2)}) %collective-permute-start.4) | collective-permute-done | bytes 262176 | tf_op jit(solution)/shard_map/ppermute | solution.py:338
  36.0 0.0 collective-permute-done.5.refs_5_
  36.0 0.0 collective-permute-done.9.refs_9_.refs_7_
  36.0 0.0 collective-permute-done.7.refs_7_.refs_6_
  36.0 5.4 %shard_map.88.state_ref = f32[8,8,256]{2,1,0:T(8,128)S(1)} custom-call(f32[1,256]{1,0:T(1,128)S(1)} %get-tuple-element.58.low_ref, f32[1,256]{1,0:T(1,128)S(1)} %get-tuple-element.59.high_ref, bf16[128,1024]{1,0:T(8,128)(2,1)S(1)} %get-tuple-element.60.refs_0_, bf16[128,1024]{1,0:T(8,128)(2,1)S(1)} %collective-permute-done.2.refs_1_, ...), custom_call_target="tpu_custom_call" | custom-call | flops 3221225472 | bytes 1048576 | tf_op jit(solution)/shard_map/pallas_call | solution.py:199
  41.3 0.0 collective-permute-done.10.refs_4_
  41.4 2.4 %collective-permute-start.11 = (bf16[4,80,256]{2,1,0:T(8,128)(2,1)S(1)}, bf16[4,80,256]{2,1,0:T(8,128)(2,1)S(1)}, u32[]{:S(2)}, u32[]{:S(2)}) collective-permute-start(bf16[4,80,256]{2,1,0:T(8,128)(2,1)S(1)} %collective-permute-done.10.refs_4_), channel_id=1, source_target_pairs={{0,8},{8,0},{1,9},{9,1},{2,10},{10,2},{3,11},{11,3},{4,12},{12,4},... | collective-permute-start | bytes 491528 | tf_op jit(solution)/shard_map/ppermute | solution.py:338
  43.7 1.0 %collective-permute-done.11.refs_5_ = bf16[4,80,256]{2,1,0:T(8,128)(2,1)S(1)} collective-permute-done((bf16[4,80,256]{2,1,0:T(8,128)(2,1)S(1)}, bf16[4,80,256]{2,1,0:T(8,128)(2,1)S(1)}, u32[]{:S(2)}, u32[]{:S(2)}) %collective-permute-start.11) | collective-permute-done | bytes 163872 | tf_op jit(solution)/shard_map/ppermute | solution.py:338
  44.8 4.6 %shard_map.89 = (f32[8,128,256]{2,1,0:T(8,128)S(1)}, bf16[4,64,256]{2,1,0:T(8,128)(2,1)S(1)}, bf16[4,64,256]{2,1,0:T(8,128)(2,1)S(1)}, f32[8,8,256]{2,1,0:T(8,128)S(1)}) custom-call(s32[1]{0:T(128)} %bitcast.place_ref, f32[1,256]{1,0:T(1,128)S(1)} %get-tuple-element.58.low_ref, f32[1,256]{1,0:T(1,128)S(1)} %get-tuple-element.59.high_ref, ...), custom_call_target="tpu_custom_call" | custom-call | flops 2147483648 | bytes 2097152 | tf_op jit(solution)/shard_map/pallas_call | solution.py:226
  49.4 0.4 collective-permute-start.12
  49.8 1.0 %collective-permute-done.12 = bf16[4,64,256]{2,1,0:T(8,128)(2,1)S(1)} collective-permute-done((bf16[4,64,256]{2,1,0:T(8,128)(2,1)S(1)}, bf16[4,64,256]{2,1,0:T(8,128)(2,1)S(1)}, u32[]{:S(2)}, u32[]{:S(2)}) %collective-permute-start.12) | collective-permute-done | bytes 131104 | tf_op jit(solution)/shard_map/ppermute | solution.py:338
  50.8 2.2 %collective-permute-start.13 = (bf16[4,64,256]{2,1,0:T(8,128)(2,1)S(1)}, bf16[4,64,256]{2,1,0:T(8,128)(2,1)S(1)}, u32[]{:S(2)}, u32[]{:S(2)}) collective-permute-start(bf16[4,64,256]{2,1,0:T(8,128)(2,1)S(1)} %add_convert_fusion.3), channel_id=1, source_target_pairs={{0,32},{32,64},{64,96},{96,0},{1,33},{33,65},{65,97},{97,1},{2,34}... | collective-permute-start | bytes 393224 | tf_op jit(solution)/shard_map/ppermute | solution.py:346
  53.1 5.8 %shard_map.90 = (f32[8,128,256]{2,1,0:T(8,128)S(1)}, bf16[8,64,256]{2,1,0:T(8,128)(2,1)S(1)}, bf16[8,64,256]{2,1,0:T(8,128)(2,1)S(1)}) custom-call(s32[1]{0:T(128)} %bitcast.place_ref, f32[1,256]{1,0:T(1,128)S(1)} %get-tuple-element.58.low_ref, f32[1,256]{1,0:T(1,128)S(1)} %get-tuple-element.59.high_ref, f32[8,8,256]{2,1,0:T(8,128)S(1)} %get-tuple-element.71.state_ref, ...), custom_call_target="tpu_custom_call" | custom-call | flops 4294967296 | bytes 2097152 | tf_op jit(solution)/shard_map/pallas_call | solution.py:226
  58.9 0.0 collective-permute-done.13
  58.9 0.7 collective-permute-start.14
  59.7 1.2 %collective-permute-done.14 = bf16[8,64,256]{2,1,0:T(8,128)(2,1)S(1)} collective-permute-done((bf16[8,64,256]{2,1,0:T(8,128)(2,1)S(1)}, bf16[8,64,256]{2,1,0:T(8,128)(2,1)S(1)}, u32[]{:S(2)}, u32[]{:S(2)}) %collective-permute-start.14) | collective-permute-done | bytes 262176 | tf_op jit(solution)/shard_map/ppermute | solution.py:338
  60.8 0.1 add_convert_fusion.1
  60.9 2.4 %collective-permute-start.15 = (bf16[4,64,256]{2,1,0:T(8,128)(2,1)S(1)}, bf16[4,64,256]{2,1,0:T(8,128)(2,1)S(1)}, u32[]{:S(2)}, u32[]{:S(2)}) collective-permute-start(bf16[4,64,256]{2,1,0:T(8,128)(2,1)S(1)} %get-tuple-element.86), channel_id=1, source_target_pairs={{0,32},{32,64},{64,96},{96,0},{1,33},{33,65},{65,97},{97,1},{2,34}... | collective-permute-start | bytes 393224 | tf_op jit(solution)/shard_map/ppermute | solution.py:346
  63.3 1.3 %collective-permute-start.16 = (bf16[4,64,256]{2,1,0:T(8,128)(2,1)S(1)}, bf16[4,64,256]{2,1,0:T(8,128)(2,1)S(1)}, u32[]{:S(2)}, u32[]{:S(2)}) collective-permute-start(bf16[4,64,256]{2,1,0:T(8,128)(2,1)S(1)} %get-tuple-element.87), channel_id=1, source_target_pairs={{0,96},{32,0},{64,32},{96,64},{1,97},{33,1},{65,33},{97,65},{2,98}... | collective-permute-start | bytes 393224 | tf_op jit(solution)/shard_map/ppermute | solution.py:346
  64.6 3.3 %shard_map.91 = (bf16[4,64,1280]{2,1,0:T(8,128)(2,1)S(1)}, bf16[4,64,256]{2,1,0:T(8,128)(2,1)S(1)}, bf16[4,64,256]{2,1,0:T(8,128)(2,1)S(1)}) custom-call(s32[1]{0:T(128)} %bitcast.place_ref, f32[1,256]{1,0:T(1,128)S(1)} %get-tuple-element.58.low_ref, f32[1,256]{1,0:T(1,128)S(1)} %get-tuple-element.59.high_ref, f32[8,8,256]{2,1,0:T(8,128)S(1)} %get-tuple-element.71.state_ref, ...), custom_call_target="tpu_custom_call" | custom-call | flops 2147483648 | bytes 2097152 | tf_op jit(solution)/shard_map/pallas_call | solution.py:226
  67.9 0.0 collective-permute-done.15
  67.9 5.5 %collective-permute-done.16 = bf16[4,64,256]{2,1,0:T(8,128)(2,1)S(1)} collective-permute-done((bf16[4,64,256]{2,1,0:T(8,128)(2,1)S(1)}, bf16[4,64,256]{2,1,0:T(8,128)(2,1)S(1)}, u32[]{:S(2)}, u32[]{:S(2)}) %collective-permute-start.16) | collective-permute-done | bytes 131104 | tf_op jit(solution)/shard_map/ppermute | solution.py:346
  73.4 1.4 %collective-permute-start.17 = (bf16[4,64,256]{2,1,0:T(8,128)(2,1)S(1)}, bf16[4,64,256]{2,1,0:T(8,128)(2,1)S(1)}, u32[]{:S(2)}, u32[]{:S(2)}) collective-permute-start(bf16[4,64,256]{2,1,0:T(8,128)(2,1)S(1)} %get-tuple-element.90), channel_id=1, source_target_pairs={{0,8},{8,0},{1,9},{9,1},{2,10},{10,2},{3,11},{11,3},{4,12},{12,4},... | collective-permute-start | bytes 393224 | tf_op jit(solution)/shard_map/ppermute | solution.py:338
  74.9 1.0 %collective-permute-done.17 = bf16[4,64,256]{2,1,0:T(8,128)(2,1)S(1)} collective-permute-done((bf16[4,64,256]{2,1,0:T(8,128)(2,1)S(1)}, bf16[4,64,256]{2,1,0:T(8,128)(2,1)S(1)}, u32[]{:S(2)}, u32[]{:S(2)}) %collective-permute-start.17) | collective-permute-done | bytes 131104 | tf_op jit(solution)/shard_map/ppermute | solution.py:338
  75.9 0.1 add_convert_fusion
  76.0 20.5 %all_to_all.5 = bf16[32,8,1280]{2,1,0:T(8,128)(2,1)S(1)} all-to-all(bf16[32,8,1280]{2,1,0:T(8,128)(2,1)S(1)} %bitcast.20), channel_id=1, replica_groups=mesh['xh'=2,'zq'=4,'zp'=2,'core'=2,'y'=4,'xl'=2] {'xh','zp','y','xl'}, dimensions={0} | all-to-all | bytes 1310720 | tf_op jit(solution)/shard_map/all_to_all | solution.py:401
  96.5 0.7 fusion
  97.2 0.9 slice.57
  (8 shorter events, 0.1 us)
Async XLA Ops:
  0.6 0.7 copy-start.5
  0.6 0.7 copy-start.4
  1.3 0.8 copy-start.2
  2.2 0.8 copy-start.3
  3.2 6.2 %collective-permute-start = (bf16[2,80,256]{2,1,0:T(8,128)(2,1)S(1)}, bf16[2,80,256]{2,1,0:T(8,128)(2,1)S(1)}, u32[]{:S(2)}, u32[]{:S(2)}) collective-permute-start(bf16[2,80,256]{2,1,0:T(8,128)(2,1)S(1)} %get-tuple-element.54), channel_id=1, source_target_pairs={{0,16},{16,0},{128,144},{144,128},{1,17},{17,1},{129,145},{145,129... | collective-permute-start | bytes 245768 | tf_op jit(solution)/shard_map/ppermute | solution.py:338
  5.7 1.0 %copy-start = (bf16[4,64,1024]{2,1,0:T(8,128)(2,1)S(1)}, bf16[4,64,1024]{2,1,0:T(8,128)(2,1)}, u32[]{:S(2)}) copy-start(bf16[4,64,1024]{2,1,0:T(8,128)(2,1)} %q_ref.1) | copy-start | bytes 1572868
  6.8 1.0 %copy-start.1 = (bf16[4,64,1024]{2,1,0:T(8,128)(2,1)S(1)}, bf16[4,64,1024]{2,1,0:T(8,128)(2,1)}, u32[]{:S(2)}) copy-start(bf16[4,64,1024]{2,1,0:T(8,128)(2,1)} %do_ref.1) | copy-start | bytes 1572868
  9.2 14.5 %collective-permute-start.2 = (bf16[128,1024]{1,0:T(8,128)(2,1)S(1)}, bf16[128,1024]{1,0:T(8,128)(2,1)S(1)}, u32[]{:S(2)}, u32[]{:S(2)}) collective-permute-start(bf16[128,1024]{1,0:T(8,128)(2,1)S(1)} %get-tuple-element.61), channel_id=1, source_target_pairs={{0,16},{16,0},{128,144},{144,128},{1,17},{17,1},{129,145},{145,129... | collective-permute-start | bytes 786440 | tf_op jit(solution)/shard_map/ppermute | solution.py:338
  9.3 4.9 %collective-permute-start.1 = (bf16[2,80,256]{2,1,0:T(8,128)(2,1)S(1)}, bf16[2,80,256]{2,1,0:T(8,128)(2,1)S(1)}, u32[]{:S(2)}, u32[]{:S(2)}) collective-permute-start(bf16[2,80,256]{2,1,0:T(8,128)(2,1)S(1)} %pad_maximum_fusion), channel_id=1, source_target_pairs={{0,128},{16,144},{128,0},{144,16},{1,129},{17,145},{129,1},{145,17... | collective-permute-start | bytes 245768 | tf_op jit(solution)/shard_map/ppermute | solution.py:338
  14.3 12.6 %collective-permute-start.8 = (bf16[4,80,256]{2,1,0:T(8,128)(2,1)S(1)}, bf16[4,80,256]{2,1,0:T(8,128)(2,1)S(1)}, u32[]{:S(2)}, u32[]{:S(2)}) collective-permute-start(bf16[4,80,256]{2,1,0:T(8,128)(2,1)S(1)} %get-tuple-element.64.refs_4_), channel_id=1, source_target_pairs={{0,32},{32,64},{64,96},{96,0},{1,33},{33,65},{65,97},{97,1},{2,34}... | collective-permute-start | bytes 491528 | tf_op jit(solution)/shard_map/ppermute | solution.py:346
  17.3 11.2 %collective-permute-start.6 = (bf16[4,80,256]{2,1,0:T(8,128)(2,1)S(1)}, bf16[4,80,256]{2,1,0:T(8,128)(2,1)S(1)}, u32[]{:S(2)}, u32[]{:S(2)}) collective-permute-start(bf16[4,80,256]{2,1,0:T(8,128)(2,1)S(1)} %get-tuple-element.64.refs_4_), channel_id=1, source_target_pairs={{0,96},{32,0},{64,32},{96,64},{1,97},{33,1},{65,33},{97,65},{2,98}... | collective-permute-start | bytes 491528 | tf_op jit(solution)/shard_map/ppermute | solution.py:346
  20.2 8.7 %collective-permute-start.3 = (bf16[128,1024]{1,0:T(8,128)(2,1)S(1)}, bf16[128,1024]{1,0:T(8,128)(2,1)S(1)}, u32[]{:S(2)}, u32[]{:S(2)}) collective-permute-start(bf16[128,1024]{1,0:T(8,128)(2,1)S(1)} %get-tuple-element.62), channel_id=1, source_target_pairs={{0,128},{16,144},{128,0},{144,16},{1,129},{17,145},{129,1},{145,17... | collective-permute-start | bytes 786440 | tf_op jit(solution)/shard_map/ppermute | solution.py:338
  23.0 13.0 %collective-permute-start.4 = (bf16[128,1024]{1,0:T(8,128)(2,1)S(1)}, bf16[128,1024]{1,0:T(8,128)(2,1)S(1)}, u32[]{:S(2)}, u32[]{:S(2)}) collective-permute-start(bf16[128,1024]{1,0:T(8,128)(2,1)S(1)} %get-tuple-element.63), channel_id=1, source_target_pairs={{0,144},{16,128},{128,16},{144,0},{1,145},{17,129},{129,17},{145,1... | collective-permute-start | bytes 786440 | tf_op jit(solution)/shard_map/ppermute | solution.py:338
  23.7 12.3 %collective-permute-start.5 = (bf16[4,80,256]{2,1,0:T(8,128)(2,1)S(1)}, bf16[4,80,256]{2,1,0:T(8,128)(2,1)S(1)}, u32[]{:S(2)}, u32[]{:S(2)}) collective-permute-start(bf16[4,80,256]{2,1,0:T(8,128)(2,1)S(1)} %get-tuple-element.64.refs_4_), channel_id=1, source_target_pairs={{0,8},{8,0},{1,9},{9,1},{2,10},{10,2},{3,11},{11,3},{4,12},{12,4},... | collective-permute-start | bytes 491528 | tf_op jit(solution)/shard_map/ppermute | solution.py:338
  26.9 9.1 %collective-permute-start.9 = (bf16[4,80,256]{2,1,0:T(8,128)(2,1)S(1)}, bf16[4,80,256]{2,1,0:T(8,128)(2,1)S(1)}, u32[]{:S(2)}, u32[]{:S(2)}) collective-permute-start(bf16[4,80,256]{2,1,0:T(8,128)(2,1)S(1)} %collective-permute-done.8.refs_8_.refs_5_), channel_id=1, source_target_pairs={{0,8},{8,0},{1,9},{9,1},{2,10},{10,2},{3,11},{11,3},{4,12},{12,4},... | collective-permute-start | bytes 491528 | tf_op jit(solution)/shard_map/ppermute | solution.py:338
  28.5 7.5 %collective-permute-start.7 = (bf16[4,80,256]{2,1,0:T(8,128)(2,1)S(1)}, bf16[4,80,256]{2,1,0:T(8,128)(2,1)S(1)}, u32[]{:S(2)}, u32[]{:S(2)}) collective-permute-start(bf16[4,80,256]{2,1,0:T(8,128)(2,1)S(1)} %collective-permute-done.6.refs_6_.refs_4_), channel_id=1, source_target_pairs={{0,8},{8,0},{1,9},{9,1},{2,10},{10,2},{3,11},{11,3},{4,12},{12,4},... | collective-permute-start | bytes 491528 | tf_op jit(solution)/shard_map/ppermute | solution.py:338
  28.9 12.5 %collective-permute-start.10 = (bf16[4,80,256]{2,1,0:T(8,128)(2,1)S(1)}, bf16[4,80,256]{2,1,0:T(8,128)(2,1)S(1)}, u32[]{:S(2)}, u32[]{:S(2)}) collective-permute-start(bf16[4,80,256]{2,1,0:T(8,128)(2,1)S(1)} %collective-permute-done.8.refs_8_.refs_5_), channel_id=1, source_target_pairs={{0,32},{32,64},{64,96},{96,0},{1,33},{33,65},{65,97},{97,1},{2,34}... | collective-permute-start | bytes 491528 | tf_op jit(solution)/shard_map/ppermute | solution.py:346
  41.4 3.4 %collective-permute-start.11 = (bf16[4,80,256]{2,1,0:T(8,128)(2,1)S(1)}, bf16[4,80,256]{2,1,0:T(8,128)(2,1)S(1)}, u32[]{:S(2)}, u32[]{:S(2)}) collective-permute-start(bf16[4,80,256]{2,1,0:T(8,128)(2,1)S(1)} %collective-permute-done.10.refs_4_), channel_id=1, source_target_pairs={{0,8},{8,0},{1,9},{9,1},{2,10},{10,2},{3,11},{11,3},{4,12},{12,4},... | collective-permute-start | bytes 491528 | tf_op jit(solution)/shard_map/ppermute | solution.py:338
  49.4 1.4 %collective-permute-start.12 = (bf16[4,64,256]{2,1,0:T(8,128)(2,1)S(1)}, bf16[4,64,256]{2,1,0:T(8,128)(2,1)S(1)}, u32[]{:S(2)}, u32[]{:S(2)}) collective-permute-start(bf16[4,64,256]{2,1,0:T(8,128)(2,1)S(1)} %get-tuple-element.69), channel_id=1, source_target_pairs={{0,8},{8,0},{1,9},{9,1},{2,10},{10,2},{3,11},{11,3},{4,12},{12,4},... | collective-permute-start | bytes 393224 | tf_op jit(solution)/shard_map/ppermute | solution.py:338
  50.8 8.1 %collective-permute-start.13 = (bf16[4,64,256]{2,1,0:T(8,128)(2,1)S(1)}, bf16[4,64,256]{2,1,0:T(8,128)(2,1)S(1)}, u32[]{:S(2)}, u32[]{:S(2)}) collective-permute-start(bf16[4,64,256]{2,1,0:T(8,128)(2,1)S(1)} %add_convert_fusion.3), channel_id=1, source_target_pairs={{0,32},{32,64},{64,96},{96,0},{1,33},{33,65},{65,97},{97,1},{2,34}... | collective-permute-start | bytes 393224 | tf_op jit(solution)/shard_map/ppermute | solution.py:346
  58.9 1.9 %collective-permute-start.14 = (bf16[8,64,256]{2,1,0:T(8,128)(2,1)S(1)}, bf16[8,64,256]{2,1,0:T(8,128)(2,1)S(1)}, u32[]{:S(2)}, u32[]{:S(2)}) collective-permute-start(bf16[8,64,256]{2,1,0:T(8,128)(2,1)S(1)} %get-tuple-element.79), channel_id=1, source_target_pairs={{0,8},{8,0},{1,9},{9,1},{2,10},{10,2},{3,11},{11,3},{4,12},{12,4},... | collective-permute-start | bytes 786440 | tf_op jit(solution)/shard_map/ppermute | solution.py:338
  60.9 6.9 %collective-permute-start.15 = (bf16[4,64,256]{2,1,0:T(8,128)(2,1)S(1)}, bf16[4,64,256]{2,1,0:T(8,128)(2,1)S(1)}, u32[]{:S(2)}, u32[]{:S(2)}) collective-permute-start(bf16[4,64,256]{2,1,0:T(8,128)(2,1)S(1)} %get-tuple-element.86), channel_id=1, source_target_pairs={{0,32},{32,64},{64,96},{96,0},{1,33},{33,65},{65,97},{97,1},{2,34}... | collective-permute-start | bytes 393224 | tf_op jit(solution)/shard_map/ppermute | solution.py:346
  63.3 10.1 %collective-permute-start.16 = (bf16[4,64,256]{2,1,0:T(8,128)(2,1)S(1)}, bf16[4,64,256]{2,1,0:T(8,128)(2,1)S(1)}, u32[]{:S(2)}, u32[]{:S(2)}) collective-permute-start(bf16[4,64,256]{2,1,0:T(8,128)(2,1)S(1)} %get-tuple-element.87), channel_id=1, source_target_pairs={{0,96},{32,0},{64,32},{96,64},{1,97},{33,1},{65,33},{97,65},{2,98}... | collective-permute-start | bytes 393224 | tf_op jit(solution)/shard_map/ppermute | solution.py:346
  73.4 2.4 %collective-permute-start.17 = (bf16[4,64,256]{2,1,0:T(8,128)(2,1)S(1)}, bf16[4,64,256]{2,1,0:T(8,128)(2,1)S(1)}, u32[]{:S(2)}, u32[]{:S(2)}) collective-permute-start(bf16[4,64,256]{2,1,0:T(8,128)(2,1)S(1)} %get-tuple-element.90), channel_id=1, source_target_pairs={{0,8},{8,0},{1,9},{9,1},{2,10},{10,2},{3,11},{11,3},{4,12},{12,4},... | collective-permute-start | bytes 393224 | tf_op jit(solution)/shard_map/ppermute | solution.py:338

commit v5 on v4

--- a/solution.py
+++ b/solution.py
@@ -220,7 +220,7 @@
     part = jax.ShapeDtypeStruct((sources // 2, row_count, width), jnp.bfloat16)
     extra = (jax.ShapeDtypeStruct((GROUP, 8, rows), jnp.float32),) if first else ()
     if last:
-        dq = jax.ShapeDtypeStruct((4, row_count, GROUP * HEAD_SIZE + width), jnp.bfloat16)
+        dq = jax.ShapeDtypeStruct((4, row_count, GROUP * HEAD_SIZE), jnp.bfloat16)
     else:
         dq = jax.ShapeDtypeStruct((GROUP, HEAD_SIZE, rows), jnp.float32)
     return pl.pallas_call(
@@ -369,6 +369,7 @@
     before = turned(own, 1)
     after = turned(own, -1)
     far_own = other_core(own)
+    before, row_arrays = tied((before, row_arrays))
     opposite = turned(before, 1)
     far_after, far_before = other_core(after), other_core(before)
     state = stats(low, high, row_arrays, [own, far_own, after, far_after, before, far_before])
@@ -382,32 +383,34 @@
     dq, near_1, far_1 = grads(spot, low, high, state, row_arrays, [after, before, far_after, far_before], dq, False)
     dq, near_1, far_1, passed = tied((dq, near_1, far_1, passed))
     beside = other_core(far_1)
+    dq, near_0, far_0 = grads(spot, low, high, state, row_arrays, [own, far_own], dq, True)
+    dq, near_0, far_0, beside = tied((dq, near_0, far_0, beside))
+
+    heads = KEY_VALUE_HEADS
+    out_rows = row_count // heads
+
+    def delivered(array):
+        return lax.all_to_all(array.reshape(window_count * heads, out_rows, array.shape[-1]), FINAL, 0, 0, tiled=True)
+
+    dq_final = delivered(dq)
     next_up = plus(near_1[0:4], beside[0:4], passed)
     next_down = plus(near_1[4:8], beside[4:8])
-    spot, dq, next_up, next_down = tied((spot, dq, next_up, next_down))
     to_up, to_down = turned(next_up, 1), turned(next_down, -1)
-    dq, near_0, far_0 = grads(spot, low, high, state, row_arrays, [own, far_own], dq, True)
-    dq, near_0, far_0, to_up, to_down = tied((dq, near_0, far_0, to_up, to_down))
     dkv_own = plus(near_0, other_core(far_0), to_up, to_down)
-
     flip = dkv_own.reshape((2, 2) + dkv_own.shape[1:])
     flip = jnp.where(across == 1, flip[::-1], flip)
     flip = jnp.where(pair == 1, flip[:, ::-1], flip)
-
-    heads = KEY_VALUE_HEADS
-    out_rows = row_count // heads
-    split = GROUP * HEAD_SIZE
-    leaving = dq.at[:, :, split:].set(flip.reshape(dkv_own.shape)).reshape(window_count * heads, out_rows, split + 2 * HEAD_SIZE)
-    final = lax.all_to_all(leaving, FINAL, 0, 0, tiled=True)
+    flip, dq_final = tied((flip, dq_final))
+    dkv_final = delivered(flip.reshape(dkv_own.shape))
 
     def merged(array):
         width = array.shape[-1]
         return array.reshape(window_count, heads, out_rows, width).transpose(0, 2, 1, 3).reshape(window_count, out_rows, heads * width)
 
     return (
-        merged(final[..., 0:split]),
-        merged(final[..., split:split + HEAD_SIZE]),
-        merged(final[..., split + HEAD_SIZE:]),
+        merged(dq_final),
+        merged(dkv_final[..., 0:HEAD_SIZE]),
+        merged(dkv_final[..., HEAD_SIZE:]),
     )
 
 

time: 98.9 us -> 113 us (1.14)
  blocking collectives: 20.5 us -> 0 us
  starting transfers between devices: 33.9 us -> 50.6 us
  waiting for transfers between devices: 15.9 us -> 32.3 us
    all_to_all x1 -> x0, blocking collectives: 20.5 us -> none  [on_device(): final = lax.all_to_all(leaving, FINAL, 0, 0, tiled=True)]
    all_to_all x0 -> x2, starting transfers between devices: none -> 13.9 us  [delivered(): lax.all_to_all(array.reshape(window_count * heads, out_rows, array.shape[...]
    all_to_all x0 -> x2, waiting for transfers between devices: none -> 9.38 us  [delivered(): lax.all_to_all(array.reshape(window_count * heads, out_rows, array.shape[...]
    ppermute x6, waiting for transfers between devices: 5.56 us -> 13 us  [turned(): lax.ppermute(array, 'zq', [(i, (i + by) % RING) for i in range(RING)])]
    ppermute x12, starting transfers between devices: 19.1 us -> 22 us  [swapped(): return lax.ppermute(array, axes, [(i, i ^ by) for i in range(count)])]
    unnamed x12 -> x13, local copies, waits for them, and re-layouts: 4.44 us -> 5.23 us
  transfers between devices with their start and end apart: 18 -> 20, of which waited for: 7 -> 8; matrix products, arithmetic and copies ran while one was open for 0% -> 1% of each run, Pallas kernels for 16% -> 15%
where the time goes in v5:
time: 113 us; the launch traced here: 112 us
  starting transfers between devices  50.6 us (45%)
  waiting for transfers between devices  32.3 us (29%)
  Pallas kernels  21.4 us (19%)
  local copies, waits for them, and re-layouts  5.9 us (5%)
    ppermute x12, starting transfers between devices, swapped(): return lax.ppermute(array, axes, [(i, i ^ by) for i in range(count)])  22 us
    ppermute x6, starting transfers between devices, turned(): lax.ppermute(array, 'zq', [(i, (i + by) % RING) for i in range(RING)])  14.7 us
    pallas_call x3, Pallas kernels, grads(): pl.pallas_call(functools.partial(grads_kernel, first, last, len(pieces)),...  14.5 us
    all_to_all x2, starting transfers between devices, delivered(): lax.all_to_all(array.reshape(window_count * heads, out_rows, array.shape[...  13.9 us
    ppermute x6, waiting for transfers between devices, turned(): lax.ppermute(array, 'zq', [(i, (i + by) % RING) for i in range(RING)])  13 us
    ppermute x12, waiting for transfers between devices, swapped(): return lax.ppermute(array, axes, [(i, i ^ by) for i in range(count)])  9.9 us
    all_to_all x2, waiting for transfers between devices, delivered(): lax.all_to_all(array.reshape(window_count * heads, out_rows, array.shape[...  9.38 us
    pallas_call x1, Pallas kernels, stats(): pl.pallas_call(functools.partial(stats_kernel, len(pieces)), out_shape=ja...  5.29 us
  transfers between devices with their start and end apart: 20, of which 8 were waited for; matrix products, arithmetic and copies ran while one was open for 1% of the time, Pallas kernels for 15%

profile of v5, /device:TPU:1, one launch (start us, length us, event | category | flops | bytes accessed | tf_op | source)
XLA Modules:
  0.0 111.8 jit_solution(13526289919711051572)
XLA Ops:
  0.6 0.0 copy-start.5
  0.6 0.0 copy-start.4
  0.7 0.7 copy-done.5
  1.3 0.0 copy-done.4
  1.3 0.0 copy-start.2
  1.4 0.8 copy-done.2
  2.2 0.0 copy-start.3
  2.2 0.8 copy-done.3
  3.0 0.1 shard_map.85
  3.2 2.6 %collective-permute-start = (bf16[2,80,256]{2,1,0:T(8,128)(2,1)S(1)}, bf16[2,80,256]{2,1,0:T(8,128)(2,1)S(1)}, u32[]{:S(2)}, u32[]{:S(2)}) collective-permute-start(bf16[2,80,256]{2,1,0:T(8,128)(2,1)S(1)} %get-tuple-element.44), channel_id=1, source_target_pairs={{0,16},{16,0},{128,144},{144,128},{1,17},{17,1},{129,145},{145,129... | collective-permute-start | bytes 245768 | tf_op jit(solution)/shard_map/ppermute | solution.py:338
  5.7 0.0 copy-start
  5.7 1.0 copy-done
  6.8 0.0 copy-start.1
  6.8 1.0 copy-done.1
  7.8 1.4 %shard_map.87 = (bf16[128,1024]{1,0:T(8,128)(2,1)S(1)}, bf16[128,1024]{1,0:T(8,128)(2,1)S(1)}, bf16[128,1024]{1,0:T(8,128)(2,1)S(1)}, bf16[128,1024]{1,0:T(8,128)(2,1)S(1)}) custom-call(s32[1]{0:T(128)} %bitcast.place_ref, bf16[4,64,1024]{2,1,0:T(8,128)(2,1)S(1)} %copy-done, bf16[4,64,1024]{2,1,0:T(8,128)(2,1)S(1)} %copy-done.1), custom_call_target="tpu_custom_call" | custom-call | tf_op jit(solution)/shard_map/pallas_call | solution.py:309
  9.2 0.1 collective-permute-start.3
  9.3 2.8 %collective-permute-start.4 = (bf16[128,1024]{1,0:T(8,128)(2,1)S(1)}, bf16[128,1024]{1,0:T(8,128)(2,1)S(1)}, u32[]{:S(2)}, u32[]{:S(2)}) collective-permute-start(bf16[128,1024]{1,0:T(8,128)(2,1)S(1)} %get-tuple-element.53), channel_id=1, source_target_pairs={{0,128},{16,144},{128,0},{144,16},{1,129},{17,145},{129,1},{145,17... | collective-permute-start | bytes 786440 | tf_op jit(solution)/shard_map/ppermute | solution.py:338
  12.1 1.3 %collective-permute-start.5 = (bf16[128,1024]{1,0:T(8,128)(2,1)S(1)}, bf16[128,1024]{1,0:T(8,128)(2,1)S(1)}, u32[]{:S(2)}, u32[]{:S(2)}) collective-permute-start(bf16[128,1024]{1,0:T(8,128)(2,1)S(1)} %get-tuple-element.54), channel_id=1, source_target_pairs={{0,144},{16,128},{128,16},{144,0},{1,145},{17,129},{129,17},{145,1... | collective-permute-start | bytes 786440 | tf_op jit(solution)/shard_map/ppermute | solution.py:338
  13.4 0.0 collective-permute-done.pair_ref
  13.5 2.8 %collective-permute-start.1 = (bf16[2,80,256]{2,1,0:T(8,128)(2,1)S(1)}, bf16[2,80,256]{2,1,0:T(8,128)(2,1)S(1)}, u32[]{:S(2)}, u32[]{:S(2)}) collective-permute-start(bf16[2,80,256]{2,1,0:T(8,128)(2,1)S(1)} %pad_maximum_fusion), channel_id=1, source_target_pairs={{0,128},{16,144},{128,0},{144,16},{1,129},{17,145},{129,1},{145,17... | collective-permute-start | bytes 245768 | tf_op jit(solution)/shard_map/ppermute | solution.py:338
  16.3 7.9 %collective-permute-done.1.across_ref = bf16[2,80,256]{2,1,0:T(8,128)(2,1)S(1)} collective-permute-done((bf16[2,80,256]{2,1,0:T(8,128)(2,1)S(1)}, bf16[2,80,256]{2,1,0:T(8,128)(2,1)S(1)}, u32[]{:S(2)}, u32[]{:S(2)}) %collective-permute-start.1) | collective-permute-done | bytes 81952 | tf_op jit(solution)/shard_map/ppermute | solution.py:338
  24.2 0.1 shard_map.86
  24.2 3.0 %collective-permute-start.2 = (bf16[4,80,256]{2,1,0:T(8,128)(2,1)S(1)}, bf16[4,80,256]{2,1,0:T(8,128)(2,1)S(1)}, u32[]{:S(2)}, u32[]{:S(2)}) collective-permute-start(bf16[4,80,256]{2,1,0:T(8,128)(2,1)S(1)} %get-tuple-element.50.refs_4_), channel_id=1, source_target_pairs={{0,32},{32,64},{64,96},{96,0},{1,33},{33,65},{65,97},{97,1},{2,34}... | collective-permute-start | bytes 491528 | tf_op jit(solution)/shard_map/ppermute | solution.py:346
  27.2 2.6 %collective-permute-start.7 = (bf16[4,80,256]{2,1,0:T(8,128)(2,1)S(1)}, bf16[4,80,256]{2,1,0:T(8,128)(2,1)S(1)}, u32[]{:S(2)}, u32[]{:S(2)}) collective-permute-start(bf16[4,80,256]{2,1,0:T(8,128)(2,1)S(1)} %get-tuple-element.50.refs_4_), channel_id=1, source_target_pairs={{0,96},{32,0},{64,32},{96,64},{1,97},{33,1},{65,33},{97,65},{2,98}... | collective-permute-start | bytes 491528 | tf_op jit(solution)/shard_map/ppermute | solution.py:346
  29.8 0.0 collective-permute-done.3.refs_1_
  29.8 3.4 %collective-permute-start.6 = (bf16[4,80,256]{2,1,0:T(8,128)(2,1)S(1)}, bf16[4,80,256]{2,1,0:T(8,128)(2,1)S(1)}, u32[]{:S(2)}, u32[]{:S(2)}) collective-permute-start(bf16[4,80,256]{2,1,0:T(8,128)(2,1)S(1)} %get-tuple-element.50.refs_4_), channel_id=1, source_target_pairs={{0,8},{8,0},{1,9},{9,1},{2,10},{10,2},{3,11},{11,3},{4,12},{12,4},... | collective-permute-start | bytes 491528 | tf_op jit(solution)/shard_map/ppermute | solution.py:338
  33.2 0.0 collective-permute-done.4.refs_2_
  33.2 0.0 collective-permute-done.5.refs_3_
  33.2 0.0 collective-permute-done.2.refs_8_.refs_5_
  33.2 2.4 %collective-permute-done.7.refs_6_.refs_4_ = bf16[4,80,256]{2,1,0:T(8,128)(2,1)S(1)} collective-permute-done((bf16[4,80,256]{2,1,0:T(8,128)(2,1)S(1)}, bf16[4,80,256]{2,1,0:T(8,128)(2,1)S(1)}, u32[]{:S(2)}, u32[]{:S(2)}) %collective-permute-start.7) | collective-permute-done | bytes 163872 | tf_op jit(solution)/shard_map/ppermute | solution.py:346
  35.6 4.0 %collective-permute-start.8 = (bf16[4,80,256]{2,1,0:T(8,128)(2,1)S(1)}, bf16[4,80,256]{2,1,0:T(8,128)(2,1)S(1)}, u32[]{:S(2)}, u32[]{:S(2)}) collective-permute-start(bf16[4,80,256]{2,1,0:T(8,128)(2,1)S(1)} %collective-permute-done.7.refs_6_.refs_4_), channel_id=1, source_target_pairs={{0,8},{8,0},{1,9},{9,1},{2,10},{10,2},{3,11},{11,3},{4,12},{12,4},... | collective-permute-start | bytes 491528 | tf_op jit(solution)/shard_map/ppermute | solution.py:338
  39.6 0.0 collective-permute-start.9
  39.6 3.9 %collective-permute-start.10 = (bf16[4,80,256]{2,1,0:T(8,128)(2,1)S(1)}, bf16[4,80,256]{2,1,0:T(8,128)(2,1)S(1)}, u32[]{:S(2)}, u32[]{:S(2)}) collective-permute-start(bf16[4,80,256]{2,1,0:T(8,128)(2,1)S(1)} %collective-permute-done.2.refs_8_.refs_5_), channel_id=1, source_target_pairs={{0,32},{32,64},{64,96},{96,0},{1,33},{33,65},{65,97},{97,1},{2,34}... | collective-permute-start | bytes 491528 | tf_op jit(solution)/shard_map/ppermute | solution.py:346
  43.5 0.0 collective-permute-done.6.refs_5_
  43.5 0.0 collective-permute-done.8.refs_7_.refs_6_
  43.5 0.0 collective-permute-done.9.refs_9_.refs_7_
  43.5 5.3 %shard_map.88.state_ref = f32[8,8,256]{2,1,0:T(8,128)S(1)} custom-call(f32[1,256]{1,0:T(1,128)S(1)} %get-tuple-element.48.low_ref, f32[1,256]{1,0:T(1,128)S(1)} %get-tuple-element.49.high_ref, bf16[128,1024]{1,0:T(8,128)(2,1)S(1)} %get-tuple-element.55.refs_0_, bf16[128,1024]{1,0:T(8,128)(2,1)S(1)} %collective-permute-done.3.refs_1_, ...), custom_call_target="tpu_custom_call" | custom-call | flops 3221225472 | bytes 1048576 | tf_op jit(solution)/shard_map/pallas_call | solution.py:199
  48.8 0.0 collective-permute-done.10.refs_4_
  48.8 3.1 %collective-permute-start.11 = (bf16[4,80,256]{2,1,0:T(8,128)(2,1)S(1)}, bf16[4,80,256]{2,1,0:T(8,128)(2,1)S(1)}, u32[]{:S(2)}, u32[]{:S(2)}) collective-permute-start(bf16[4,80,256]{2,1,0:T(8,128)(2,1)S(1)} %collective-permute-done.10.refs_4_), channel_id=1, source_target_pairs={{0,8},{8,0},{1,9},{9,1},{2,10},{10,2},{3,11},{11,3},{4,12},{12,4},... | collective-permute-start | bytes 491528 | tf_op jit(solution)/shard_map/ppermute | solution.py:338
  51.9 1.0 collective-permute-done.11.refs_5_
  52.9 4.6 %shard_map.89 = (f32[8,128,256]{2,1,0:T(8,128)S(1)}, bf16[4,64,256]{2,1,0:T(8,128)(2,1)S(1)}, bf16[4,64,256]{2,1,0:T(8,128)(2,1)S(1)}, f32[8,8,256]{2,1,0:T(8,128)S(1)}) custom-call(s32[1]{0:T(128)} %bitcast.place_ref, f32[1,256]{1,0:T(1,128)S(1)} %get-tuple-element.48.low_ref, f32[1,256]{1,0:T(1,128)S(1)} %get-tuple-element.49.high_ref, ...), custom_call_target="tpu_custom_call" | custom-call | flops 2147483648 | bytes 2097152 | tf_op jit(solution)/shard_map/pallas_call | solution.py:226
  57.5 0.5 collective-permute-start.12
  58.0 1.0 collective-permute-done.12
  59.0 1.6 %collective-permute-start.13 = (bf16[4,64,256]{2,1,0:T(8,128)(2,1)S(1)}, bf16[4,64,256]{2,1,0:T(8,128)(2,1)S(1)}, u32[]{:S(2)}, u32[]{:S(2)}) collective-permute-start(bf16[4,64,256]{2,1,0:T(8,128)(2,1)S(1)} %add_convert_fusion.3), channel_id=1, source_target_pairs={{0,32},{32,64},{64,96},{96,0},{1,33},{33,65},{65,97},{97,1},{2,34}... | collective-permute-start | bytes 393224 | tf_op jit(solution)/shard_map/ppermute | solution.py:346
  60.7 5.8 %shard_map.90 = (f32[8,128,256]{2,1,0:T(8,128)S(1)}, bf16[8,64,256]{2,1,0:T(8,128)(2,1)S(1)}, bf16[8,64,256]{2,1,0:T(8,128)(2,1)S(1)}) custom-call(s32[1]{0:T(128)} %bitcast.place_ref, f32[1,256]{1,0:T(1,128)S(1)} %get-tuple-element.48.low_ref, f32[1,256]{1,0:T(1,128)S(1)} %get-tuple-element.49.high_ref, f32[8,8,256]{2,1,0:T(8,128)S(1)} %get-tuple-element.66.state_ref, ...), custom_call_target="tpu_custom_call" | custom-call | flops 4294967296 | bytes 2097152 | tf_op jit(solution)/shard_map/pallas_call | solution.py:226
  66.5 2.3 %collective-permute-done.13 = bf16[4,64,256]{2,1,0:T(8,128)(2,1)S(1)} collective-permute-done((bf16[4,64,256]{2,1,0:T(8,128)(2,1)S(1)}, bf16[4,64,256]{2,1,0:T(8,128)(2,1)S(1)}, u32[]{:S(2)}, u32[]{:S(2)}) %collective-permute-start.13) | collective-permute-done | bytes 131104 | tf_op jit(solution)/shard_map/ppermute | solution.py:346
  68.8 1.1 collective-permute-start.14
  69.9 4.0 %shard_map.91 = (bf16[4,64,1024]{2,1,0:T(8,128)(2,1)}, bf16[4,64,256]{2,1,0:T(8,128)(2,1)S(1)}, bf16[4,64,256]{2,1,0:T(8,128)(2,1)S(1)}) custom-call(s32[1]{0:T(128)} %bitcast.place_ref, f32[1,256]{1,0:T(1,128)S(1)} %get-tuple-element.48.low_ref, f32[1,256]{1,0:T(1,128)S(1)} %get-tuple-element.49.high_ref, f32[8,8,256]{2,1,0:T(8,128)S(1)} %get-tuple-element.66.state_ref, ...), custom_call_target="tpu_custom_call" | custom-call | flops 2147483648 | bytes 2097152 | tf_op jit(solution)/shard_map/pallas_call | solution.py:226
  74.0 0.0 collective-permute-done.14
  74.0 7.8 %all-to-all-start = ((bf16[32,8,1024]{2,1,0:T(8,128)(2,1)}), bf16[32,8,1024]{2,1,0:T(8,128)(2,1)S(1)}, u32[]{:S(2)}, u32[]{:S(2)}) async-start(bf16[32,8,1024]{2,1,0:T(8,128)(2,1)} %bitcast.3), calls=%async_computation | async-start | bytes 1048576 | tf_op jit(solution)/shard_map/all_to_all | solution.py:393
  81.8 0.4 collective-permute-start.15
  82.1 0.1 add_convert_fusion.2
  82.2 0.6 collective-permute-start.16
  82.8 3.1 %collective-permute-start.17 = (bf16[4,64,256]{2,1,0:T(8,128)(2,1)S(1)}, bf16[4,64,256]{2,1,0:T(8,128)(2,1)S(1)}, u32[]{:S(2)}, u32[]{:S(2)}) collective-permute-start(bf16[4,64,256]{2,1,0:T(8,128)(2,1)S(1)} %get-tuple-element.86), channel_id=1, source_target_pairs={{0,96},{32,0},{64,32},{96,64},{1,97},{33,1},{65,33},{97,65},{2,98}... | collective-permute-start | bytes 393224 | tf_op jit(solution)/shard_map/ppermute | solution.py:346
  85.9 0.0 collective-permute-done.15
  85.9 8.2 %collective-permute-done.16 = bf16[4,64,256]{2,1,0:T(8,128)(2,1)S(1)} collective-permute-done((bf16[4,64,256]{2,1,0:T(8,128)(2,1)S(1)}, bf16[4,64,256]{2,1,0:T(8,128)(2,1)S(1)}, u32[]{:S(2)}, u32[]{:S(2)}) %collective-permute-start.16) | collective-permute-done | bytes 131104 | tf_op jit(solution)/shard_map/ppermute | solution.py:346
  94.1 0.0 collective-permute-done.17
  94.1 0.1 add_convert_fusion
  94.2 0.7 reverse_select_fusion
  94.9 1.7 %all-to-all-done = bf16[32,8,1024]{2,1,0:T(8,128)(2,1)S(1)} async-done(((bf16[32,8,1024]{2,1,0:T(8,128)(2,1)}), bf16[32,8,1024]{2,1,0:T(8,128)(2,1)S(1)}, u32[]{:S(2)}, u32[]{:S(2)}) %all-to-all-start) | async-done | bytes 524320 | tf_op jit(solution)/shard_map/all_to_all | solution.py:393
  96.6 6.1 %all-to-all-start.1 = ((bf16[32,8,256]{2,1,0:T(8,128)(2,1)}), bf16[32,8,256]{2,1,0:T(8,128)(2,1)S(1)}, u32[]{:S(2)}, u32[]{:S(2)}) async-start(bf16[32,8,256]{2,1,0:T(8,128)(2,1)} %bitcast.7), calls=%async_computation.1 | async-start | bytes 262144 | tf_op jit(solution)/shard_map/all_to_all | solution.py:393
  102.7 7.7 %all-to-all-done.1 = bf16[32,8,256]{2,1,0:T(8,128)(2,1)S(1)} async-done(((bf16[32,8,256]{2,1,0:T(8,128)(2,1)}), bf16[32,8,256]{2,1,0:T(8,128)(2,1)S(1)}, u32[]{:S(2)}, u32[]{:S(2)}) %all-to-all-start.1) | async-done | bytes 131104 | tf_op jit(solution)/shard_map/all_to_all | solution.py:393
  110.4 0.7 fusion
  111.0 0.8 copy.10
  (6 shorter events, 0.1 us)
Async XLA Ops:
  0.6 0.7 copy-start.5
  0.6 0.7 copy-start.4
  1.3 0.8 copy-start.2
  2.2 0.8 copy-start.3
  3.2 10.3 %collective-permute-start = (bf16[2,80,256]{2,1,0:T(8,128)(2,1)S(1)}, bf16[2,80,256]{2,1,0:T(8,128)(2,1)S(1)}, u32[]{:S(2)}, u32[]{:S(2)}) collective-permute-start(bf16[2,80,256]{2,1,0:T(8,128)(2,1)S(1)} %get-tuple-element.44), channel_id=1, source_target_pairs={{0,16},{16,0},{128,144},{144,128},{1,17},{17,1},{129,145},{145,129... | collective-permute-start | bytes 245768 | tf_op jit(solution)/shard_map/ppermute | solution.py:338
  5.7 1.0 copy-start
  6.8 1.0 copy-start.1
  9.2 20.6 %collective-permute-start.3 = (bf16[128,1024]{1,0:T(8,128)(2,1)S(1)}, bf16[128,1024]{1,0:T(8,128)(2,1)S(1)}, u32[]{:S(2)}, u32[]{:S(2)}) collective-permute-start(bf16[128,1024]{1,0:T(8,128)(2,1)S(1)} %get-tuple-element.52), channel_id=1, source_target_pairs={{0,16},{16,0},{128,144},{144,128},{1,17},{17,1},{129,145},{145,129... | collective-permute-start | bytes 786440 | tf_op jit(solution)/shard_map/ppermute | solution.py:338
  9.3 23.9 %collective-permute-start.4 = (bf16[128,1024]{1,0:T(8,128)(2,1)S(1)}, bf16[128,1024]{1,0:T(8,128)(2,1)S(1)}, u32[]{:S(2)}, u32[]{:S(2)}) collective-permute-start(bf16[128,1024]{1,0:T(8,128)(2,1)S(1)} %get-tuple-element.53), channel_id=1, source_target_pairs={{0,128},{16,144},{128,0},{144,16},{1,129},{17,145},{129,1},{145,17... | collective-permute-start | bytes 786440 | tf_op jit(solution)/shard_map/ppermute | solution.py:338
  12.1 21.1 %collective-permute-start.5 = (bf16[128,1024]{1,0:T(8,128)(2,1)S(1)}, bf16[128,1024]{1,0:T(8,128)(2,1)S(1)}, u32[]{:S(2)}, u32[]{:S(2)}) collective-permute-start(bf16[128,1024]{1,0:T(8,128)(2,1)S(1)} %get-tuple-element.54), channel_id=1, source_target_pairs={{0,144},{16,128},{128,16},{144,0},{1,145},{17,129},{129,17},{145,1... | collective-permute-start | bytes 786440 | tf_op jit(solution)/shard_map/ppermute | solution.py:338
  13.5 10.7 %collective-permute-start.1 = (bf16[2,80,256]{2,1,0:T(8,128)(2,1)S(1)}, bf16[2,80,256]{2,1,0:T(8,128)(2,1)S(1)}, u32[]{:S(2)}, u32[]{:S(2)}) collective-permute-start(bf16[2,80,256]{2,1,0:T(8,128)(2,1)S(1)} %pad_maximum_fusion), channel_id=1, source_target_pairs={{0,128},{16,144},{128,0},{144,16},{1,129},{17,145},{129,1},{145,17... | collective-permute-start | bytes 245768 | tf_op jit(solution)/shard_map/ppermute | solution.py:338
  24.2 9.0 %collective-permute-start.2 = (bf16[4,80,256]{2,1,0:T(8,128)(2,1)S(1)}, bf16[4,80,256]{2,1,0:T(8,128)(2,1)S(1)}, u32[]{:S(2)}, u32[]{:S(2)}) collective-permute-start(bf16[4,80,256]{2,1,0:T(8,128)(2,1)S(1)} %get-tuple-element.50.refs_4_), channel_id=1, source_target_pairs={{0,32},{32,64},{64,96},{96,0},{1,33},{33,65},{65,97},{97,1},{2,34}... | collective-permute-start | bytes 491528 | tf_op jit(solution)/shard_map/ppermute | solution.py:346
  27.2 8.4 %collective-permute-start.7 = (bf16[4,80,256]{2,1,0:T(8,128)(2,1)S(1)}, bf16[4,80,256]{2,1,0:T(8,128)(2,1)S(1)}, u32[]{:S(2)}, u32[]{:S(2)}) collective-permute-start(bf16[4,80,256]{2,1,0:T(8,128)(2,1)S(1)} %get-tuple-element.50.refs_4_), channel_id=1, source_target_pairs={{0,96},{32,0},{64,32},{96,64},{1,97},{33,1},{65,33},{97,65},{2,98}... | collective-permute-start | bytes 491528 | tf_op jit(solution)/shard_map/ppermute | solution.py:346
  29.8 13.7 %collective-permute-start.6 = (bf16[4,80,256]{2,1,0:T(8,128)(2,1)S(1)}, bf16[4,80,256]{2,1,0:T(8,128)(2,1)S(1)}, u32[]{:S(2)}, u32[]{:S(2)}) collective-permute-start(bf16[4,80,256]{2,1,0:T(8,128)(2,1)S(1)} %get-tuple-element.50.refs_4_), channel_id=1, source_target_pairs={{0,8},{8,0},{1,9},{9,1},{2,10},{10,2},{3,11},{11,3},{4,12},{12,4},... | collective-permute-start | bytes 491528 | tf_op jit(solution)/shard_map/ppermute | solution.py:338
  35.6 7.8 %collective-permute-start.8 = (bf16[4,80,256]{2,1,0:T(8,128)(2,1)S(1)}, bf16[4,80,256]{2,1,0:T(8,128)(2,1)S(1)}, u32[]{:S(2)}, u32[]{:S(2)}) collective-permute-start(bf16[4,80,256]{2,1,0:T(8,128)(2,1)S(1)} %collective-permute-done.7.refs_6_.refs_4_), channel_id=1, source_target_pairs={{0,8},{8,0},{1,9},{9,1},{2,10},{10,2},{3,11},{11,3},{4,12},{12,4},... | collective-permute-start | bytes 491528 | tf_op jit(solution)/shard_map/ppermute | solution.py:338
  39.6 3.9 %collective-permute-start.9 = (bf16[4,80,256]{2,1,0:T(8,128)(2,1)S(1)}, bf16[4,80,256]{2,1,0:T(8,128)(2,1)S(1)}, u32[]{:S(2)}, u32[]{:S(2)}) collective-permute-start(bf16[4,80,256]{2,1,0:T(8,128)(2,1)S(1)} %collective-permute-done.2.refs_8_.refs_5_), channel_id=1, source_target_pairs={{0,8},{8,0},{1,9},{9,1},{2,10},{10,2},{3,11},{11,3},{4,12},{12,4},... | collective-permute-start | bytes 491528 | tf_op jit(solution)/shard_map/ppermute | solution.py:338
  39.6 9.2 %collective-permute-start.10 = (bf16[4,80,256]{2,1,0:T(8,128)(2,1)S(1)}, bf16[4,80,256]{2,1,0:T(8,128)(2,1)S(1)}, u32[]{:S(2)}, u32[]{:S(2)}) collective-permute-start(bf16[4,80,256]{2,1,0:T(8,128)(2,1)S(1)} %collective-permute-done.2.refs_8_.refs_5_), channel_id=1, source_target_pairs={{0,32},{32,64},{64,96},{96,0},{1,33},{33,65},{65,97},{97,1},{2,34}... | collective-permute-start | bytes 491528 | tf_op jit(solution)/shard_map/ppermute | solution.py:346
  48.8 4.1 %collective-permute-start.11 = (bf16[4,80,256]{2,1,0:T(8,128)(2,1)S(1)}, bf16[4,80,256]{2,1,0:T(8,128)(2,1)S(1)}, u32[]{:S(2)}, u32[]{:S(2)}) collective-permute-start(bf16[4,80,256]{2,1,0:T(8,128)(2,1)S(1)} %collective-permute-done.10.refs_4_), channel_id=1, source_target_pairs={{0,8},{8,0},{1,9},{9,1},{2,10},{10,2},{3,11},{11,3},{4,12},{12,4},... | collective-permute-start | bytes 491528 | tf_op jit(solution)/shard_map/ppermute | solution.py:338
  57.5 1.4 %collective-permute-start.12 = (bf16[4,64,256]{2,1,0:T(8,128)(2,1)S(1)}, bf16[4,64,256]{2,1,0:T(8,128)(2,1)S(1)}, u32[]{:S(2)}, u32[]{:S(2)}) collective-permute-start(bf16[4,64,256]{2,1,0:T(8,128)(2,1)S(1)} %get-tuple-element.64), channel_id=1, source_target_pairs={{0,8},{8,0},{1,9},{9,1},{2,10},{10,2},{3,11},{11,3},{4,12},{12,4},... | collective-permute-start | bytes 393224 | tf_op jit(solution)/shard_map/ppermute | solution.py:338
  59.0 9.8 %collective-permute-start.13 = (bf16[4,64,256]{2,1,0:T(8,128)(2,1)S(1)}, bf16[4,64,256]{2,1,0:T(8,128)(2,1)S(1)}, u32[]{:S(2)}, u32[]{:S(2)}) collective-permute-start(bf16[4,64,256]{2,1,0:T(8,128)(2,1)S(1)} %add_convert_fusion.3), channel_id=1, source_target_pairs={{0,32},{32,64},{64,96},{96,0},{1,33},{33,65},{65,97},{97,1},{2,34}... | collective-permute-start | bytes 393224 | tf_op jit(solution)/shard_map/ppermute | solution.py:346
  68.8 5.1 %collective-permute-start.14 = (bf16[8,64,256]{2,1,0:T(8,128)(2,1)S(1)}, bf16[8,64,256]{2,1,0:T(8,128)(2,1)S(1)}, u32[]{:S(2)}, u32[]{:S(2)}) collective-permute-start(bf16[8,64,256]{2,1,0:T(8,128)(2,1)S(1)} %get-tuple-element.76), channel_id=1, source_target_pairs={{0,8},{8,0},{1,9},{9,1},{2,10},{10,2},{3,11},{11,3},{4,12},{12,4},... | collective-permute-start | bytes 786440 | tf_op jit(solution)/shard_map/ppermute | solution.py:338
  74.0 22.7 %all-to-all-start = ((bf16[32,8,1024]{2,1,0:T(8,128)(2,1)}), bf16[32,8,1024]{2,1,0:T(8,128)(2,1)S(1)}, u32[]{:S(2)}, u32[]{:S(2)}) async-start(bf16[32,8,1024]{2,1,0:T(8,128)(2,1)} %bitcast.3), calls=%async_computation | async-start | bytes 1048576 | tf_op jit(solution)/shard_map/all_to_all | solution.py:393
  81.8 4.1 %collective-permute-start.15 = (bf16[4,64,256]{2,1,0:T(8,128)(2,1)S(1)}, bf16[4,64,256]{2,1,0:T(8,128)(2,1)S(1)}, u32[]{:S(2)}, u32[]{:S(2)}) collective-permute-start(bf16[4,64,256]{2,1,0:T(8,128)(2,1)S(1)} %get-tuple-element.78), channel_id=1, source_target_pairs={{0,8},{8,0},{1,9},{9,1},{2,10},{10,2},{3,11},{11,3},{4,12},{12,4},... | collective-permute-start | bytes 393224 | tf_op jit(solution)/shard_map/ppermute | solution.py:338
  82.2 11.9 %collective-permute-start.16 = (bf16[4,64,256]{2,1,0:T(8,128)(2,1)S(1)}, bf16[4,64,256]{2,1,0:T(8,128)(2,1)S(1)}, u32[]{:S(2)}, u32[]{:S(2)}) collective-permute-start(bf16[4,64,256]{2,1,0:T(8,128)(2,1)S(1)} %get-tuple-element.85), channel_id=1, source_target_pairs={{0,32},{32,64},{64,96},{96,0},{1,33},{33,65},{65,97},{97,1},{2,34}... | collective-permute-start | bytes 393224 | tf_op jit(solution)/shard_map/ppermute | solution.py:346
  82.8 11.3 %collective-permute-start.17 = (bf16[4,64,256]{2,1,0:T(8,128)(2,1)S(1)}, bf16[4,64,256]{2,1,0:T(8,128)(2,1)S(1)}, u32[]{:S(2)}, u32[]{:S(2)}) collective-permute-start(bf16[4,64,256]{2,1,0:T(8,128)(2,1)S(1)} %get-tuple-element.86), channel_id=1, source_target_pairs={{0,96},{32,0},{64,32},{96,64},{1,97},{33,1},{65,33},{97,65},{2,98}... | collective-permute-start | bytes 393224 | tf_op jit(solution)/shard_map/ppermute | solution.py:346
  96.6 13.7 %all-to-all-start.1 = ((bf16[32,8,256]{2,1,0:T(8,128)(2,1)}), bf16[32,8,256]{2,1,0:T(8,128)(2,1)S(1)}, u32[]{:S(2)}, u32[]{:S(2)}) async-start(bf16[32,8,256]{2,1,0:T(8,128)(2,1)} %bitcast.7), calls=%async_computation.1 | async-start | bytes 262144 | tf_op jit(solution)/shard_map/all_to_all | solution.py:393

commit v6 on v4

--- a/solution.py
+++ b/solution.py
@@ -362,13 +362,15 @@
     paired = swapped(to_pair, PLANE, 1, 4)
     spot, to_pair = tied((spot, to_pair))
     loads = pack_rows(spot, queries, output_gradient)
-    row_arrays = [loads[0]] + [swapped(loads[r], PLANE, r, 4) for r in (1, 2, 3)]
     crossed = swapped(jnp.stack([across_part, paired[1]]), PLANE, 2, 4)
+    crossed, far_rows = tied((crossed, loads[2:4]))
+    row_arrays = [loads[0], swapped(loads[1], PLANE, 1, 4)] + [swapped(far_rows[r - 2], PLANE, r, 4) for r in (2, 3)]
     own, low, high = own_keys(mine, paired, crossed)
 
     before = turned(own, 1)
     after = turned(own, -1)
     far_own = other_core(own)
+    before, row_arrays = tied((before, row_arrays))
     opposite = turned(before, 1)
     far_after, far_before = other_core(after), other_core(before)
     state = stats(low, high, row_arrays, [own, far_own, after, far_after, before, far_before])
@@ -387,7 +389,7 @@
     spot, dq, next_up, next_down = tied((spot, dq, next_up, next_down))
     to_up, to_down = turned(next_up, 1), turned(next_down, -1)
     dq, near_0, far_0 = grads(spot, low, high, state, row_arrays, [own, far_own], dq, True)
-    dq, near_0, far_0, to_up, to_down = tied((dq, near_0, far_0, to_up, to_down))
+    dq, to_up, to_down = tied((dq, to_up, to_down))
     dkv_own = plus(near_0, other_core(far_0), to_up, to_down)
 
     flip = dkv_own.reshape((2, 2) + dkv_own.shape[1:])

time: 98.9 us -> 100 us (1.011)
  blocking collectives: 20.5 us -> 17.5 us
  waiting for transfers between devices: 15.9 us -> 18.8 us
  starting transfers between devices: 33.9 us -> 35.3 us
    ppermute x6, waiting for transfers between devices: 5.56 us -> 12.7 us  [turned(): lax.ppermute(array, 'zq', [(i, (i + by) % RING) for i in range(RING)])]
    ppermute x12, starting transfers between devices: 19.1 us -> 25.5 us  [swapped(): return lax.ppermute(array, axes, [(i, i ^ by) for i in range(count)])]
    ppermute x6, starting transfers between devices: 14.7 us -> 9.82 us  [turned(): lax.ppermute(array, 'zq', [(i, (i + by) % RING) for i in range(RING)])]
    ppermute x12, waiting for transfers between devices: 10.4 us -> 6.04 us  [swapped(): return lax.ppermute(array, axes, [(i, i ^ by) for i in range(count)])]
    all_to_all x1, blocking collectives: 20.5 us -> 17.5 us  [on_device(): final = lax.all_to_all(leaving, FINAL, 0, 0, tiled=True)]
  transfers between devices with their start and end apart: 18 -> 18, of which waited for: 7 -> 9; matrix products, arithmetic and copies ran while one was open for 0% -> 0% of each run, Pallas kernels for 16% -> 16%
where the time goes in v6:
time: 100 us; the launch traced here: 99.2 us
  starting transfers between devices  35.3 us (35%)
  Pallas kernels  20.6 us (21%)
  waiting for transfers between devices  18.8 us (19%)
  blocking collectives  17.5 us (18%)
  local copies, waits for them, and re-layouts  5.98 us (6%)
    ppermute x12, starting transfers between devices, swapped(): return lax.ppermute(array, axes, [(i, i ^ by) for i in range(count)])  25.5 us
    all_to_all x1, blocking collectives, on_device(): final = lax.all_to_all(leaving, FINAL, 0, 0, tiled=True)  17.5 us
    pallas_call x3, Pallas kernels, grads(): pl.pallas_call(functools.partial(grads_kernel, first, last, len(pieces)),...  13.7 us
    ppermute x6, waiting for transfers between devices, turned(): lax.ppermute(array, 'zq', [(i, (i + by) % RING) for i in range(RING)])  12.7 us
    ppermute x6, starting transfers between devices, turned(): lax.ppermute(array, 'zq', [(i, (i + by) % RING) for i in range(RING)])  9.82 us
    ppermute x12, waiting for transfers between devices, swapped(): return lax.ppermute(array, axes, [(i, i ^ by) for i in range(count)])  6.04 us
    pallas_call x1, Pallas kernels, stats(): pl.pallas_call(functools.partial(stats_kernel, len(pieces)), out_shape=ja...  5.3 us
    unnamed x12, local copies, waits for them, and re-layouts  4.44 us
  transfers between devices with their start and end apart: 18, of which 9 were waited for; matrix products, arithmetic and copies ran while one was open for 0% of the time, Pallas kernels for 16%

profile of v6, /device:TPU:1, one launch (start us, length us, event | category | flops | bytes accessed | tf_op | source)
XLA Modules:
  0.0 99.2 jit_solution(8090900101537620272)
XLA Ops:
  0.6 0.0 copy-start.5
  0.6 0.0 copy-start.4
  0.7 0.7 copy-done.5
  1.3 0.0 copy-done.4
  1.3 0.0 copy-start.2
  1.4 0.8 copy-done.2
  2.2 0.0 copy-start.3
  2.2 0.8 copy-done.3
  3.0 0.1 shard_map.85
  3.2 2.6 %collective-permute-start = (bf16[2,80,256]{2,1,0:T(8,128)(2,1)S(1)}, bf16[2,80,256]{2,1,0:T(8,128)(2,1)S(1)}, u32[]{:S(2)}, u32[]{:S(2)}) collective-permute-start(bf16[2,80,256]{2,1,0:T(8,128)(2,1)S(1)} %get-tuple-element.60), channel_id=1, source_target_pairs={{0,16},{16,0},{128,144},{144,128},{1,17},{17,1},{129,145},{145,129... | collective-permute-start | bytes 245768 | tf_op jit(solution)/shard_map/ppermute | solution.py:338
  5.7 1.8 %collective-permute-done.pair_ref = bf16[2,80,256]{2,1,0:T(8,128)(2,1)S(1)} collective-permute-done((bf16[2,80,256]{2,1,0:T(8,128)(2,1)S(1)}, bf16[2,80,256]{2,1,0:T(8,128)(2,1)S(1)}, u32[]{:S(2)}, u32[]{:S(2)}) %collective-permute-start) | collective-permute-done | bytes 81952 | tf_op jit(solution)/shard_map/ppermute | solution.py:338
  7.6 2.8 %collective-permute-start.1 = (bf16[2,80,256]{2,1,0:T(8,128)(2,1)S(1)}, bf16[2,80,256]{2,1,0:T(8,128)(2,1)S(1)}, u32[]{:S(2)}, u32[]{:S(2)}) collective-permute-start(bf16[2,80,256]{2,1,0:T(8,128)(2,1)S(1)} %pad_maximum_fusion), channel_id=1, source_target_pairs={{0,128},{16,144},{128,0},{144,16},{1,129},{17,145},{129,1},{145,17... | collective-permute-start | bytes 245768 | tf_op jit(solution)/shard_map/ppermute | solution.py:338
  10.4 0.0 copy-start
  10.4 1.0 %copy-done = bf16[4,64,1024]{2,1,0:T(8,128)(2,1)S(1)} copy-done((bf16[4,64,1024]{2,1,0:T(8,128)(2,1)S(1)}, bf16[4,64,1024]{2,1,0:T(8,128)(2,1)}, u32[]{:S(2)}) %copy-start) | copy-done | bytes 524312
  11.4 0.0 copy-start.1
  11.4 1.0 %copy-done.1 = bf16[4,64,1024]{2,1,0:T(8,128)(2,1)S(1)} copy-done((bf16[4,64,1024]{2,1,0:T(8,128)(2,1)S(1)}, bf16[4,64,1024]{2,1,0:T(8,128)(2,1)}, u32[]{:S(2)}) %copy-start.1) | copy-done | bytes 524312
  12.5 1.4 %shard_map.86 = (bf16[128,1024]{1,0:T(8,128)(2,1)S(1)}, bf16[128,1024]{1,0:T(8,128)(2,1)S(1)}, bf16[128,1024]{1,0:T(8,128)(2,1)S(1)}, bf16[128,1024]{1,0:T(8,128)(2,1)S(1)}) custom-call(s32[1]{0:T(128)} %bitcast.place_ref, bf16[4,64,1024]{2,1,0:T(8,128)(2,1)S(1)} %copy-done, bf16[4,64,1024]{2,1,0:T(8,128)(2,1)S(1)} %copy-done.1), custom_call_target="tpu_custom_call" | custom-call | tf_op jit(solution)/shard_map/pallas_call | solution.py:309
  13.9 1.5 %collective-permute-start.3 = (bf16[128,1024]{1,0:T(8,128)(2,1)S(1)}, bf16[128,1024]{1,0:T(8,128)(2,1)S(1)}, u32[]{:S(2)}, u32[]{:S(2)}) collective-permute-start(bf16[128,1024]{1,0:T(8,128)(2,1)S(1)} %get-tuple-element.71), channel_id=1, source_target_pairs={{0,16},{16,0},{128,144},{144,128},{1,17},{17,1},{129,145},{145,129... | collective-permute-start | bytes 786440 | tf_op jit(solution)/shard_map/ppermute | solution.py:338
  15.4 0.0 collective-permute-done.1.across_ref
  15.4 0.2 collective-permute-start.4
  15.7 2.6 %collective-permute-start.5 = (bf16[128,1024]{1,0:T(8,128)(2,1)S(1)}, bf16[128,1024]{1,0:T(8,128)(2,1)S(1)}, u32[]{:S(2)}, u32[]{:S(2)}) collective-permute-start(bf16[128,1024]{1,0:T(8,128)(2,1)S(1)} %get-tuple-element.73), channel_id=1, source_target_pairs={{0,144},{16,128},{128,16},{144,0},{1,145},{17,129},{129,17},{145,1... | collective-permute-start | bytes 786440 | tf_op jit(solution)/shard_map/ppermute | solution.py:338
  18.2 0.1 shard_map.87
  18.3 5.8 %collective-permute-start.7 = (bf16[4,80,256]{2,1,0:T(8,128)(2,1)S(1)}, bf16[4,80,256]{2,1,0:T(8,128)(2,1)S(1)}, u32[]{:S(2)}, u32[]{:S(2)}) collective-permute-start(bf16[4,80,256]{2,1,0:T(8,128)(2,1)S(1)} %get-tuple-element.69.refs_4_), channel_id=1, source_target_pairs={{0,96},{32,0},{64,32},{96,64},{1,97},{33,1},{65,33},{97,65},{2,98}... | collective-permute-start | bytes 491528 | tf_op jit(solution)/shard_map/ppermute | solution.py:346
  24.1 0.0 collective-permute-start.2
  24.1 0.0 collective-permute-done.3.refs_1_
  24.1 3.2 %collective-permute-start.6 = (bf16[4,80,256]{2,1,0:T(8,128)(2,1)S(1)}, bf16[4,80,256]{2,1,0:T(8,128)(2,1)S(1)}, u32[]{:S(2)}, u32[]{:S(2)}) collective-permute-start(bf16[4,80,256]{2,1,0:T(8,128)(2,1)S(1)} %get-tuple-element.69.refs_4_), channel_id=1, source_target_pairs={{0,8},{8,0},{1,9},{9,1},{2,10},{10,2},{3,11},{11,3},{4,12},{12,4},... | collective-permute-start | bytes 491528 | tf_op jit(solution)/shard_map/ppermute | solution.py:338
  27.3 0.0 collective-permute-done.7.refs_6_.refs_4_
  27.3 3.4 %collective-permute-start.8 = (bf16[4,80,256]{2,1,0:T(8,128)(2,1)S(1)}, bf16[4,80,256]{2,1,0:T(8,128)(2,1)S(1)}, u32[]{:S(2)}, u32[]{:S(2)}) collective-permute-start(bf16[4,80,256]{2,1,0:T(8,128)(2,1)S(1)} %collective-permute-done.7.refs_6_.refs_4_), channel_id=1, source_target_pairs={{0,8},{8,0},{1,9},{9,1},{2,10},{10,2},{3,11},{11,3},{4,12},{12,4},... | collective-permute-start | bytes 491528 | tf_op jit(solution)/shard_map/ppermute | solution.py:338
  30.7 6.8 %collective-permute-done.2.refs_8_.refs_5_ = bf16[4,80,256]{2,1,0:T(8,128)(2,1)S(1)} collective-permute-done((bf16[4,80,256]{2,1,0:T(8,128)(2,1)S(1)}, bf16[4,80,256]{2,1,0:T(8,128)(2,1)S(1)}, u32[]{:S(2)}, u32[]{:S(2)}) %collective-permute-start.2) | collective-permute-done | bytes 163872 | tf_op jit(solution)/shard_map/ppermute | solution.py:346
  37.5 0.0 collective-permute-done.4.refs_2_
  37.5 0.0 collective-permute-done.5.refs_3_
  37.5 2.9 %collective-permute-start.9 = (bf16[4,80,256]{2,1,0:T(8,128)(2,1)S(1)}, bf16[4,80,256]{2,1,0:T(8,128)(2,1)S(1)}, u32[]{:S(2)}, u32[]{:S(2)}) collective-permute-start(bf16[4,80,256]{2,1,0:T(8,128)(2,1)S(1)} %collective-permute-done.2.refs_8_.refs_5_), channel_id=1, source_target_pairs={{0,8},{8,0},{1,9},{9,1},{2,10},{10,2},{3,11},{11,3},{4,12},{12,4},... | collective-permute-start | bytes 491528 | tf_op jit(solution)/shard_map/ppermute | solution.py:338
  40.5 0.0 collective-permute-start.10
  40.5 0.0 collective-permute-done.6.refs_5_
  40.5 0.0 collective-permute-done.8.refs_7_.refs_6_
  40.5 1.0 %collective-permute-done.9.refs_9_.refs_7_ = bf16[4,80,256]{2,1,0:T(8,128)(2,1)S(1)} collective-permute-done((bf16[4,80,256]{2,1,0:T(8,128)(2,1)S(1)}, bf16[4,80,256]{2,1,0:T(8,128)(2,1)S(1)}, u32[]{:S(2)}, u32[]{:S(2)}) %collective-permute-start.9) | collective-permute-done | bytes 163872 | tf_op jit(solution)/shard_map/ppermute | solution.py:338
  41.5 5.3 %shard_map.88.state_ref = f32[8,8,256]{2,1,0:T(8,128)S(1)} custom-call(f32[1,256]{1,0:T(1,128)S(1)} %get-tuple-element.67.low_ref, f32[1,256]{1,0:T(1,128)S(1)} %get-tuple-element.68.high_ref, bf16[128,1024]{1,0:T(8,128)(2,1)S(1)} %get-tuple-element.74.refs_0_, bf16[128,1024]{1,0:T(8,128)(2,1)S(1)} %collective-permute-done.3.refs_1_, ...), custom_call_target="tpu_custom_call" | custom-call | flops 3221225472 | bytes 1048576 | tf_op jit(solution)/shard_map/pallas_call | solution.py:199
  46.8 3.5 %collective-permute-done.10.refs_4_ = bf16[4,80,256]{2,1,0:T(8,128)(2,1)S(1)} collective-permute-done((bf16[4,80,256]{2,1,0:T(8,128)(2,1)S(1)}, bf16[4,80,256]{2,1,0:T(8,128)(2,1)S(1)}, u32[]{:S(2)}, u32[]{:S(2)}) %collective-permute-start.10) | collective-permute-done | bytes 163872 | tf_op jit(solution)/shard_map/ppermute | solution.py:346
  50.3 0.9 collective-permute-start.11
  51.2 1.0 %collective-permute-done.11.refs_5_ = bf16[4,80,256]{2,1,0:T(8,128)(2,1)S(1)} collective-permute-done((bf16[4,80,256]{2,1,0:T(8,128)(2,1)S(1)}, bf16[4,80,256]{2,1,0:T(8,128)(2,1)S(1)}, u32[]{:S(2)}, u32[]{:S(2)}) %collective-permute-start.11) | collective-permute-done | bytes 163872 | tf_op jit(solution)/shard_map/ppermute | solution.py:338
  52.2 4.6 %shard_map.89 = (f32[8,128,256]{2,1,0:T(8,128)S(1)}, bf16[4,64,256]{2,1,0:T(8,128)(2,1)S(1)}, bf16[4,64,256]{2,1,0:T(8,128)(2,1)S(1)}, f32[8,8,256]{2,1,0:T(8,128)S(1)}) custom-call(s32[1]{0:T(128)} %bitcast.place_ref, f32[1,256]{1,0:T(1,128)S(1)} %get-tuple-element.67.low_ref, f32[1,256]{1,0:T(1,128)S(1)} %get-tuple-element.68.high_ref, ...), custom_call_target="tpu_custom_call" | custom-call | flops 2147483648 | bytes 2097152 | tf_op jit(solution)/shard_map/pallas_call | solution.py:226
  56.9 0.5 collective-permute-start.12
  57.3 1.0 collective-permute-done.12
  58.3 0.4 collective-permute-start.13
  58.7 5.8 %shard_map.90 = (f32[8,128,256]{2,1,0:T(8,128)S(1)}, bf16[8,64,256]{2,1,0:T(8,128)(2,1)S(1)}, bf16[8,64,256]{2,1,0:T(8,128)(2,1)S(1)}) custom-call(s32[1]{0:T(128)} %bitcast.place_ref, f32[1,256]{1,0:T(1,128)S(1)} %get-tuple-element.67.low_ref, f32[1,256]{1,0:T(1,128)S(1)} %get-tuple-element.68.high_ref, f32[8,8,256]{2,1,0:T(8,128)S(1)} %get-tuple-element.85.state_ref, ...), custom_call_target="tpu_custom_call" | custom-call | flops 4294967296 | bytes 2097152 | tf_op jit(solution)/shard_map/pallas_call | solution.py:226
  64.6 0.7 collective-permute-done.13
  65.3 3.9 %collective-permute-start.14 = (bf16[8,64,256]{2,1,0:T(8,128)(2,1)S(1)}, bf16[8,64,256]{2,1,0:T(8,128)(2,1)S(1)}, u32[]{:S(2)}, u32[]{:S(2)}) collective-permute-start(bf16[8,64,256]{2,1,0:T(8,128)(2,1)S(1)} %get-tuple-element.93), channel_id=1, source_target_pairs={{0,8},{8,0},{1,9},{9,1},{2,10},{10,2},{3,11},{11,3},{4,12},{12,4},... | collective-permute-start | bytes 786440 | tf_op jit(solution)/shard_map/ppermute | solution.py:338
  69.1 1.2 %collective-permute-done.14 = bf16[8,64,256]{2,1,0:T(8,128)(2,1)S(1)} collective-permute-done((bf16[8,64,256]{2,1,0:T(8,128)(2,1)S(1)}, bf16[8,64,256]{2,1,0:T(8,128)(2,1)S(1)}, u32[]{:S(2)}, u32[]{:S(2)}) %collective-permute-start.14) | collective-permute-done | bytes 262176 | tf_op jit(solution)/shard_map/ppermute | solution.py:338
  70.3 0.1 add_convert_fusion.1
  70.4 0.1 collective-permute-start.15
  70.5 3.6 %collective-permute-start.16 = (bf16[4,64,256]{2,1,0:T(8,128)(2,1)S(1)}, bf16[4,64,256]{2,1,0:T(8,128)(2,1)S(1)}, u32[]{:S(2)}, u32[]{:S(2)}) collective-permute-start(bf16[4,64,256]{2,1,0:T(8,128)(2,1)S(1)} %get-tuple-element.99), channel_id=1, source_target_pairs={{0,96},{32,0},{64,32},{96,64},{1,97},{33,1},{65,33},{97,65},{2,98}... | collective-permute-start | bytes 393224 | tf_op jit(solution)/shard_map/ppermute | solution.py:346
  74.0 3.3 %shard_map.91 = (bf16[4,64,1280]{2,1,0:T(8,128)(2,1)S(1)}, bf16[4,64,256]{2,1,0:T(8,128)(2,1)S(1)}, bf16[4,64,256]{2,1,0:T(8,128)(2,1)S(1)}) custom-call(s32[1]{0:T(128)} %bitcast.place_ref, f32[1,256]{1,0:T(1,128)S(1)} %get-tuple-element.67.low_ref, f32[1,256]{1,0:T(1,128)S(1)} %get-tuple-element.68.high_ref, f32[8,8,256]{2,1,0:T(8,128)S(1)} %get-tuple-element.85.state_ref, ...), custom_call_target="tpu_custom_call" | custom-call | flops 2147483648 | bytes 2097152 | tf_op jit(solution)/shard_map/pallas_call | solution.py:226
  77.3 1.0 %collective-permute-start.17 = (bf16[4,64,256]{2,1,0:T(8,128)(2,1)S(1)}, bf16[4,64,256]{2,1,0:T(8,128)(2,1)S(1)}, u32[]{:S(2)}, u32[]{:S(2)}) collective-permute-start(bf16[4,64,256]{2,1,0:T(8,128)(2,1)S(1)} %get-tuple-element.102), channel_id=1, source_target_pairs={{0,8},{8,0},{1,9},{9,1},{2,10},{10,2},{3,11},{11,3},{4,12},{12,4},... | collective-permute-start | bytes 393224 | tf_op jit(solution)/shard_map/ppermute | solution.py:338
  78.4 1.6 %collective-permute-done.15 = bf16[4,64,256]{2,1,0:T(8,128)(2,1)S(1)} collective-permute-done((bf16[4,64,256]{2,1,0:T(8,128)(2,1)S(1)}, bf16[4,64,256]{2,1,0:T(8,128)(2,1)S(1)}, u32[]{:S(2)}, u32[]{:S(2)}) %collective-permute-start.15) | collective-permute-done | bytes 131104 | tf_op jit(solution)/shard_map/ppermute | solution.py:346
  80.0 0.0 collective-permute-done.16
  80.0 0.0 collective-permute-done.17
  80.0 0.1 add_convert_fusion
  80.2 17.5 %all_to_all.5 = bf16[32,8,1280]{2,1,0:T(8,128)(2,1)S(1)} all-to-all(bf16[32,8,1280]{2,1,0:T(8,128)(2,1)S(1)} %bitcast.20), channel_id=1, replica_groups=mesh['xh'=2,'zq'=4,'zp'=2,'core'=2,'y'=4,'xl'=2] {'xh','zp','y','xl'}, dimensions={0} | all-to-all | bytes 1310720 | tf_op jit(solution)/shard_map/all_to_all | solution.py:403
  97.7 0.7 fusion
  98.4 0.9 slice.57
  (8 shorter events, 0.1 us)
Async XLA Ops:
  0.6 0.7 copy-start.5
  0.6 0.7 copy-start.4
  1.3 0.8 copy-start.2
  2.2 0.8 copy-start.3
  3.2 4.4 %collective-permute-start = (bf16[2,80,256]{2,1,0:T(8,128)(2,1)S(1)}, bf16[2,80,256]{2,1,0:T(8,128)(2,1)S(1)}, u32[]{:S(2)}, u32[]{:S(2)}) collective-permute-start(bf16[2,80,256]{2,1,0:T(8,128)(2,1)S(1)} %get-tuple-element.60), channel_id=1, source_target_pairs={{0,16},{16,0},{128,144},{144,128},{1,17},{17,1},{129,145},{145,129... | collective-permute-start | bytes 245768 | tf_op jit(solution)/shard_map/ppermute | solution.py:338
  7.6 7.9 %collective-permute-start.1 = (bf16[2,80,256]{2,1,0:T(8,128)(2,1)S(1)}, bf16[2,80,256]{2,1,0:T(8,128)(2,1)S(1)}, u32[]{:S(2)}, u32[]{:S(2)}) collective-permute-start(bf16[2,80,256]{2,1,0:T(8,128)(2,1)S(1)} %pad_maximum_fusion), channel_id=1, source_target_pairs={{0,128},{16,144},{128,0},{144,16},{1,129},{17,145},{129,1},{145,17... | collective-permute-start | bytes 245768 | tf_op jit(solution)/shard_map/ppermute | solution.py:338
  10.4 1.0 %copy-start = (bf16[4,64,1024]{2,1,0:T(8,128)(2,1)S(1)}, bf16[4,64,1024]{2,1,0:T(8,128)(2,1)}, u32[]{:S(2)}) copy-start(bf16[4,64,1024]{2,1,0:T(8,128)(2,1)} %q_ref.1) | copy-start | bytes 1572868
  11.4 1.0 %copy-start.1 = (bf16[4,64,1024]{2,1,0:T(8,128)(2,1)S(1)}, bf16[4,64,1024]{2,1,0:T(8,128)(2,1)}, u32[]{:S(2)}) copy-start(bf16[4,64,1024]{2,1,0:T(8,128)(2,1)} %do_ref.1) | copy-start | bytes 1572868
  13.9 10.2 %collective-permute-start.3 = (bf16[128,1024]{1,0:T(8,128)(2,1)S(1)}, bf16[128,1024]{1,0:T(8,128)(2,1)S(1)}, u32[]{:S(2)}, u32[]{:S(2)}) collective-permute-start(bf16[128,1024]{1,0:T(8,128)(2,1)S(1)} %get-tuple-element.71), channel_id=1, source_target_pairs={{0,16},{16,0},{128,144},{144,128},{1,17},{17,1},{129,145},{145,129... | collective-permute-start | bytes 786440 | tf_op jit(solution)/shard_map/ppermute | solution.py:338
  15.4 22.1 %collective-permute-start.4 = (bf16[128,1024]{1,0:T(8,128)(2,1)S(1)}, bf16[128,1024]{1,0:T(8,128)(2,1)S(1)}, u32[]{:S(2)}, u32[]{:S(2)}) collective-permute-start(bf16[128,1024]{1,0:T(8,128)(2,1)S(1)} %get-tuple-element.72), channel_id=1, source_target_pairs={{0,128},{16,144},{128,0},{144,16},{1,129},{17,145},{129,1},{145,17... | collective-permute-start | bytes 786440 | tf_op jit(solution)/shard_map/ppermute | solution.py:338
  15.7 21.9 %collective-permute-start.5 = (bf16[128,1024]{1,0:T(8,128)(2,1)S(1)}, bf16[128,1024]{1,0:T(8,128)(2,1)S(1)}, u32[]{:S(2)}, u32[]{:S(2)}) collective-permute-start(bf16[128,1024]{1,0:T(8,128)(2,1)S(1)} %get-tuple-element.73), channel_id=1, source_target_pairs={{0,144},{16,128},{128,16},{144,0},{1,145},{17,129},{129,17},{145,1... | collective-permute-start | bytes 786440 | tf_op jit(solution)/shard_map/ppermute | solution.py:338
  18.3 9.0 %collective-permute-start.7 = (bf16[4,80,256]{2,1,0:T(8,128)(2,1)S(1)}, bf16[4,80,256]{2,1,0:T(8,128)(2,1)S(1)}, u32[]{:S(2)}, u32[]{:S(2)}) collective-permute-start(bf16[4,80,256]{2,1,0:T(8,128)(2,1)S(1)} %get-tuple-element.69.refs_4_), channel_id=1, source_target_pairs={{0,96},{32,0},{64,32},{96,64},{1,97},{33,1},{65,33},{97,65},{2,98}... | collective-permute-start | bytes 491528 | tf_op jit(solution)/shard_map/ppermute | solution.py:346
  24.1 13.5 %collective-permute-start.2 = (bf16[4,80,256]{2,1,0:T(8,128)(2,1)S(1)}, bf16[4,80,256]{2,1,0:T(8,128)(2,1)S(1)}, u32[]{:S(2)}, u32[]{:S(2)}) collective-permute-start(bf16[4,80,256]{2,1,0:T(8,128)(2,1)S(1)} %get-tuple-element.69.refs_4_), channel_id=1, source_target_pairs={{0,32},{32,64},{64,96},{96,0},{1,33},{33,65},{65,97},{97,1},{2,34}... | collective-permute-start | bytes 491528 | tf_op jit(solution)/shard_map/ppermute | solution.py:346
  24.1 16.4 %collective-permute-start.6 = (bf16[4,80,256]{2,1,0:T(8,128)(2,1)S(1)}, bf16[4,80,256]{2,1,0:T(8,128)(2,1)S(1)}, u32[]{:S(2)}, u32[]{:S(2)}) collective-permute-start(bf16[4,80,256]{2,1,0:T(8,128)(2,1)S(1)} %get-tuple-element.69.refs_4_), channel_id=1, source_target_pairs={{0,8},{8,0},{1,9},{9,1},{2,10},{10,2},{3,11},{11,3},{4,12},{12,4},... | collective-permute-start | bytes 491528 | tf_op jit(solution)/shard_map/ppermute | solution.py:338
  27.3 13.2 %collective-permute-start.8 = (bf16[4,80,256]{2,1,0:T(8,128)(2,1)S(1)}, bf16[4,80,256]{2,1,0:T(8,128)(2,1)S(1)}, u32[]{:S(2)}, u32[]{:S(2)}) collective-permute-start(bf16[4,80,256]{2,1,0:T(8,128)(2,1)S(1)} %collective-permute-done.7.refs_6_.refs_4_), channel_id=1, source_target_pairs={{0,8},{8,0},{1,9},{9,1},{2,10},{10,2},{3,11},{11,3},{4,12},{12,4},... | collective-permute-start | bytes 491528 | tf_op jit(solution)/shard_map/ppermute | solution.py:338
  37.5 3.9 %collective-permute-start.9 = (bf16[4,80,256]{2,1,0:T(8,128)(2,1)S(1)}, bf16[4,80,256]{2,1,0:T(8,128)(2,1)S(1)}, u32[]{:S(2)}, u32[]{:S(2)}) collective-permute-start(bf16[4,80,256]{2,1,0:T(8,128)(2,1)S(1)} %collective-permute-done.2.refs_8_.refs_5_), channel_id=1, source_target_pairs={{0,8},{8,0},{1,9},{9,1},{2,10},{10,2},{3,11},{11,3},{4,12},{12,4},... | collective-permute-start | bytes 491528 | tf_op jit(solution)/shard_map/ppermute | solution.py:338
  40.5 9.9 %collective-permute-start.10 = (bf16[4,80,256]{2,1,0:T(8,128)(2,1)S(1)}, bf16[4,80,256]{2,1,0:T(8,128)(2,1)S(1)}, u32[]{:S(2)}, u32[]{:S(2)}) collective-permute-start(bf16[4,80,256]{2,1,0:T(8,128)(2,1)S(1)} %collective-permute-done.2.refs_8_.refs_5_), channel_id=1, source_target_pairs={{0,32},{32,64},{64,96},{96,0},{1,33},{33,65},{65,97},{97,1},{2,34}... | collective-permute-start | bytes 491528 | tf_op jit(solution)/shard_map/ppermute | solution.py:346
  50.3 1.9 %collective-permute-start.11 = (bf16[4,80,256]{2,1,0:T(8,128)(2,1)S(1)}, bf16[4,80,256]{2,1,0:T(8,128)(2,1)S(1)}, u32[]{:S(2)}, u32[]{:S(2)}) collective-permute-start(bf16[4,80,256]{2,1,0:T(8,128)(2,1)S(1)} %collective-permute-done.10.refs_4_), channel_id=1, source_target_pairs={{0,8},{8,0},{1,9},{9,1},{2,10},{10,2},{3,11},{11,3},{4,12},{12,4},... | collective-permute-start | bytes 491528 | tf_op jit(solution)/shard_map/ppermute | solution.py:338
  56.9 1.4 %collective-permute-start.12 = (bf16[4,64,256]{2,1,0:T(8,128)(2,1)S(1)}, bf16[4,64,256]{2,1,0:T(8,128)(2,1)S(1)}, u32[]{:S(2)}, u32[]{:S(2)}) collective-permute-start(bf16[4,64,256]{2,1,0:T(8,128)(2,1)S(1)} %get-tuple-element.83), channel_id=1, source_target_pairs={{0,8},{8,0},{1,9},{9,1},{2,10},{10,2},{3,11},{11,3},{4,12},{12,4},... | collective-permute-start | bytes 393224 | tf_op jit(solution)/shard_map/ppermute | solution.py:338
  58.3 7.0 %collective-permute-start.13 = (bf16[4,64,256]{2,1,0:T(8,128)(2,1)S(1)}, bf16[4,64,256]{2,1,0:T(8,128)(2,1)S(1)}, u32[]{:S(2)}, u32[]{:S(2)}) collective-permute-start(bf16[4,64,256]{2,1,0:T(8,128)(2,1)S(1)} %add_convert_fusion.3), channel_id=1, source_target_pairs={{0,32},{32,64},{64,96},{96,0},{1,33},{33,65},{65,97},{97,1},{2,34}... | collective-permute-start | bytes 393224 | tf_op jit(solution)/shard_map/ppermute | solution.py:346
  65.3 5.0 %collective-permute-start.14 = (bf16[8,64,256]{2,1,0:T(8,128)(2,1)S(1)}, bf16[8,64,256]{2,1,0:T(8,128)(2,1)S(1)}, u32[]{:S(2)}, u32[]{:S(2)}) collective-permute-start(bf16[8,64,256]{2,1,0:T(8,128)(2,1)S(1)} %get-tuple-element.93), channel_id=1, source_target_pairs={{0,8},{8,0},{1,9},{9,1},{2,10},{10,2},{3,11},{11,3},{4,12},{12,4},... | collective-permute-start | bytes 786440 | tf_op jit(solution)/shard_map/ppermute | solution.py:338
  70.4 9.6 %collective-permute-start.15 = (bf16[4,64,256]{2,1,0:T(8,128)(2,1)S(1)}, bf16[4,64,256]{2,1,0:T(8,128)(2,1)S(1)}, u32[]{:S(2)}, u32[]{:S(2)}) collective-permute-start(bf16[4,64,256]{2,1,0:T(8,128)(2,1)S(1)} %get-tuple-element.98), channel_id=1, source_target_pairs={{0,32},{32,64},{64,96},{96,0},{1,33},{33,65},{65,97},{97,1},{2,34}... | collective-permute-start | bytes 393224 | tf_op jit(solution)/shard_map/ppermute | solution.py:346
  70.5 9.5 %collective-permute-start.16 = (bf16[4,64,256]{2,1,0:T(8,128)(2,1)S(1)}, bf16[4,64,256]{2,1,0:T(8,128)(2,1)S(1)}, u32[]{:S(2)}, u32[]{:S(2)}) collective-permute-start(bf16[4,64,256]{2,1,0:T(8,128)(2,1)S(1)} %get-tuple-element.99), channel_id=1, source_target_pairs={{0,96},{32,0},{64,32},{96,64},{1,97},{33,1},{65,33},{97,65},{2,98}... | collective-permute-start | bytes 393224 | tf_op jit(solution)/shard_map/ppermute | solution.py:346
  77.3 2.7 %collective-permute-start.17 = (bf16[4,64,256]{2,1,0:T(8,128)(2,1)S(1)}, bf16[4,64,256]{2,1,0:T(8,128)(2,1)S(1)}, u32[]{:S(2)}, u32[]{:S(2)}) collective-permute-start(bf16[4,64,256]{2,1,0:T(8,128)(2,1)S(1)} %get-tuple-element.102), channel_id=1, source_target_pairs={{0,8},{8,0},{1,9},{9,1},{2,10},{10,2},{3,11},{11,3},{4,12},{12,4},... | collective-permute-start | bytes 393224 | tf_op jit(solution)/shard_map/ppermute | solution.py:338

commit v7 on v6

--- a/solution.py
+++ b/solution.py
@@ -82,8 +82,9 @@
     return new, total, cross, weights
 
 
-def stats_kernel(count, low_ref, high_ref, *refs):
-    row_refs, piece_refs, (state_ref, bias_ref) = refs[0:4], refs[4:4 + count], refs[4 + count:]
+def stats_kernel(first, count, low_ref, high_ref, *refs):
+    row_refs, piece_refs, rest = refs[0:4], refs[4:4 + count], refs[4 + count:]
+    state_ref, bias_ref = rest[-2:]
     rows = low_ref.shape[1]
     row_count = rows // 4
     spans, _ = key_spans(piece_refs, row_count)
@@ -94,9 +95,12 @@
             h = g * HEADS_PER_STEP + j
             lanes = pl.ds(pl.multiple_of(h * HEAD_SIZE, HEAD_SIZE), HEAD_SIZE)
             q, do = rows_of(row_refs, lanes, row_count)
-            top = jnp.full((1, rows), NEG_BIG, jnp.float32)
-            total = jnp.zeros((1, rows), jnp.float32)
-            cross = jnp.zeros((1, rows), jnp.float32)
+            if first:
+                top = jnp.full((1, rows), NEG_BIG, jnp.float32)
+                total = jnp.zeros((1, rows), jnp.float32)
+                cross = jnp.zeros((1, rows), jnp.float32)
+            else:
+                top, total, cross = rest[0][h, 0:1, :], rest[0][h, 1:2, :], rest[0][h, 2:3, :]
             for ref, part, size in spans:
                 s = dot(keys_of(ref, size, row_count), q, NT) * EXP2_SCALE + bias_ref[part, :]
                 dp = dot(values_of(ref, size, row_count), do, NT)
@@ -111,10 +115,12 @@
 
 def grads_kernel(first, last, count, place_ref, low_ref, high_ref, state_ref, *refs):
     row_refs, piece_refs, rest = refs[0:4], refs[4:4 + count], refs[4 + count:]
+    if not first:
+        before_ref, rest = rest[0], rest[1:]
+    dq_ref, out_refs, rest = rest[0], rest[1:1 + count], rest[1 + count:]
     if first:
-        dq_ref, near_ref, far_ref, final_ref, bias_ref, kt_ref, ds_ref, acc_ref = rest
-    else:
-        before_ref, dq_ref, near_ref, far_ref, bias_ref, kt_ref, ds_ref, acc_ref = rest
+        final_ref, rest = rest[0], rest[1:]
+    bias_ref, kt_ref, ds_ref, acc_ref = rest
     rows = low_ref.shape[1]
     row_count = rows // 4
     heads = HEADS_PER_STEP
@@ -179,10 +185,8 @@
         return carry
 
     lax.fori_loop(0, GROUP // heads, step, 0)
-    sources = near_ref.shape[0]
-    for i, out_ref in enumerate((near_ref, far_ref)):
-        part = slice(i * sources * row_count, (i + 1) * sources * row_count)
-        shape = (sources, row_count, HEAD_SIZE)
+    for out_ref, (_, part, size) in zip(out_refs, spans):
+        shape = (size // row_count, row_count, HEAD_SIZE)
         out_ref[:, :, 0:HEAD_SIZE] = (acc_ref[part, 0:HEAD_SIZE] * SCALE).astype(jnp.bfloat16).reshape(shape)
         out_ref[:, :, HEAD_SIZE:2 * HEAD_SIZE] = acc_ref[part, HEAD_SIZE:2 * HEAD_SIZE].astype(jnp.bfloat16).reshape(shape)
 
@@ -192,12 +196,13 @@
 ANY = pl.BlockSpec(memory_space=pltpu.HBM)
 
 
-def stats(low, high, row_arrays, pieces):
+def stats(low, high, row_arrays, pieces, state):
     rows = low.shape[1]
     keys = sum(piece.shape[0] for piece in pieces) * rows // 4
-    inputs = (low, high, *row_arrays, *pieces)
+    first = state is None
+    inputs = (low, high, *row_arrays, *pieces) + (() if first else (state,))
     return pl.pallas_call(
-        functools.partial(stats_kernel, len(pieces)),
+        functools.partial(stats_kernel, first, len(pieces)),
         out_shape=jax.ShapeDtypeStruct((GROUP, 8, rows), jnp.float32),
         in_specs=[VMEM] * len(inputs),
         out_specs=VMEM,
@@ -217,7 +222,7 @@
     width = 2 * HEAD_SIZE
     first = before is None
     inputs = (low, high, state, *row_arrays, *pieces) + (() if first else (before,))
-    part = jax.ShapeDtypeStruct((sources // 2, row_count, width), jnp.bfloat16)
+    parts = tuple(jax.ShapeDtypeStruct((piece.shape[0], row_count, width), jnp.bfloat16) for piece in pieces)
     extra = (jax.ShapeDtypeStruct((GROUP, 8, rows), jnp.float32),) if first else ()
     if last:
         dq = jax.ShapeDtypeStruct((4, row_count, GROUP * HEAD_SIZE + width), jnp.bfloat16)
@@ -225,9 +230,9 @@
         dq = jax.ShapeDtypeStruct((GROUP, HEAD_SIZE, rows), jnp.float32)
     return pl.pallas_call(
         functools.partial(grads_kernel, first, last, len(pieces)),
-        out_shape=(dq, part, part) + extra,
+        out_shape=(dq,) + parts + extra,
         in_specs=[SMEM] + [VMEM] * len(inputs),
-        out_specs=(VMEM,) * (3 + len(extra)),
+        out_specs=(VMEM,) * (1 + len(parts) + len(extra)),
         scratch_shapes=[
             pltpu.VMEM((keys, rows), jnp.float32),
             pltpu.VMEM((HEAD_SIZE, keys), jnp.bfloat16),
@@ -329,21 +334,17 @@
     )(mine, paired, crossed)
 
 
-PLANE = ("xh", "zp")
-FINAL = ("xh", "zp", "y", "xl")
-RING = 4
+PLANE = ("xh", "core")
+FINAL = ("xh", "core", "y", "xl")
+RING = 8
 
 
 def swapped(array, axes, by, count):
     return lax.ppermute(array, axes, [(i, i ^ by) for i in range(count)])
 
 
-def other_core(array):
-    return swapped(array, "core", 1, 2)
-
-
 def turned(array, by):
-    return lax.ppermute(array, "zq", [(i, (i + by) % RING) for i in range(RING)])
+    return lax.ppermute(array, "z", [(i, (i + by) % RING) for i in range(RING)])
 
 
 def plus(*arrays):
@@ -352,7 +353,7 @@
 
 def on_device(queries, key_vectors, value_vectors, output_gradient, positions, segments):
     window_count, row_count, _ = queries.shape
-    across, pair = lax.axis_index("xh"), lax.axis_index("zp")
+    across, pair = lax.axis_index("xh"), lax.axis_index("core")
     place = across * 2 + pair
 
     spot = place.reshape(1).astype(jnp.int32)
@@ -367,30 +368,37 @@
     row_arrays = [loads[0], swapped(loads[1], PLANE, 1, 4)] + [swapped(far_rows[r - 2], PLANE, r, 4) for r in (2, 3)]
     own, low, high = own_keys(mine, paired, crossed)
 
-    before = turned(own, 1)
-    after = turned(own, -1)
-    far_own = other_core(own)
-    before, row_arrays = tied((before, row_arrays))
-    opposite = turned(before, 1)
-    far_after, far_before = other_core(after), other_core(before)
-    state = stats(low, high, row_arrays, [own, far_own, after, far_after, before, far_before])
+    below, above = [own], [own]
+    for _ in range(2):
+        below.append(turned(below[-1], 1))
+        above.append(turned(above[-1], -1))
+    below.append(turned(below[2], 1))
+    above.append(turned(above[2], -1))
+    state = stats(low, high, row_arrays, [own, below[1], above[1]], None)
+    state, below[3], above[3] = tied((state, below[3], above[3]))
+    opposite = turned(below[3], 1)
+    state = stats(low, high, row_arrays, [below[2], above[2], below[3], above[3]], state)
     state, opposite = tied((state, opposite))
-    far_opposite = other_core(opposite)
-
-    dq, near_2, far_2, state = grads(spot, low, high, state, row_arrays, [opposite, far_opposite], None, False)
-    sum_2 = plus(near_2, other_core(far_2))
-    spot, dq, sum_2 = tied((spot, dq, sum_2))
-    passed = turned(sum_2, 1)
-    dq, near_1, far_1 = grads(spot, low, high, state, row_arrays, [after, before, far_after, far_before], dq, False)
-    dq, near_1, far_1, passed = tied((dq, near_1, far_1, passed))
-    beside = other_core(far_1)
-    next_up = plus(near_1[0:4], beside[0:4], passed)
-    next_down = plus(near_1[4:8], beside[4:8])
-    spot, dq, next_up, next_down = tied((spot, dq, next_up, next_down))
-    to_up, to_down = turned(next_up, 1), turned(next_down, -1)
-    dq, near_0, far_0 = grads(spot, low, high, state, row_arrays, [own, far_own], dq, True)
-    dq, to_up, to_down = tied((dq, to_up, to_down))
-    dkv_own = plus(near_0, other_core(far_0), to_up, to_down)
+
+    def gradients(pieces, before, last=False):
+        return grads(spot, low, high, state, row_arrays, pieces, before, last)
+
+    dq, to_up, state = gradients([opposite], None)
+    spot, dq, to_up = tied((spot, dq, to_up))
+    up = turned(to_up, 1)
+    dq, up_grad, down_grad = gradients([above[3], below[3]], dq)
+    dq, up_grad, down_grad, up = tied((dq, up_grad, down_grad, up))
+    to_up, to_down = plus(up_grad, up), down_grad
+    for k in (2, 1, 0):
+        spot, dq, to_up, to_down = tied((spot, dq, to_up, to_down))
+        up, down = turned(to_up, 1), turned(to_down, -1)
+        if k:
+            dq, up_grad, down_grad = gradients([above[k], below[k]], dq)
+            dq, up_grad, down_grad, up, down = tied((dq, up_grad, down_grad, up, down))
+            to_up, to_down = plus(up_grad, up), plus(down_grad, down)
+    dq, own_grad = gradients([own], dq, True)
+    dq, own_grad, up, down = tied((dq, own_grad, up, down))
+    dkv_own = plus(own_grad, up, down)
 
     flip = dkv_own.reshape((2, 2) + dkv_own.shape[1:])
     flip = jnp.where(across == 1, flip[::-1], flip)
@@ -414,8 +422,8 @@
 
 
 def solution(mesh):
-    fine = Mesh(mesh.devices.reshape(2, RING, 2, 2, 4, 2), ("xh", "zq", "zp", "core", "y", "xl"))
-    ctx, head = ("xh", "zq", "zp", "core"), ("y", "xl")
+    fine = Mesh(mesh.devices.reshape(2, RING, 2, 4, 2), ("xh", "z", "core", "y", "xl"))
+    ctx, head = ("xh", "z", "core"), ("y", "xl")
     vectors = P(None, ctx, head)
     out = P(None, ctx + head, None)
     return jax.shard_map(

time: 100 us -> 95.7 us (0.957)
  blocking collectives: 17.5 us -> 25.3 us
  starting transfers between devices: 35.3 us -> 28.4 us
  waiting for transfers between devices: 18.8 us -> 12.3 us
  Pallas kernels: 20.6 us -> 22.3 us
    ppermute x12 -> x5, starting transfers between devices: 25.5 us -> 8.48 us  [swapped(): return lax.ppermute(array, axes, [(i, i ^ by) for i in range(count)])]
    ppermute x6 -> x14, starting transfers between devices: 9.82 us -> 19.9 us  [turned(): return lax.ppermute(array, 'z', [(i, (i + by) % RING) for i in range(RING)])]
    all_to_all x1, blocking collectives: 17.5 us -> 25.3 us  [on_device(): final = lax.all_to_all(leaving, FINAL, 0, 0, tiled=True)]
    ppermute x6 -> x14, waiting for transfers between devices: 12.7 us -> 7.78 us  [turned(): return lax.ppermute(array, 'z', [(i, (i + by) % RING) for i in range(RING)])]
    ppermute x12 -> x5, waiting for transfers between devices: 6.04 us -> 4.52 us  [swapped(): return lax.ppermute(array, axes, [(i, i ^ by) for i in range(count)])]
    pallas_call x1 -> x2, Pallas kernels: 5.3 us -> 6.8 us  [stats(): pl.pallas_call(functools.partial(stats_kernel, first, len(pieces)), out_s...]
    pallas_call x3 -> x5, Pallas kernels: 13.7 us -> 13.9 us  [grads(): pl.pallas_call(functools.partial(grads_kernel, first, last, len(pieces)),...]
  transfers between devices with their start and end apart: 18 -> 19, of which waited for: 9 -> 7; matrix products, arithmetic and copies ran while one was open for 0% -> 0% of each run, Pallas kernels for 16% -> 20%
where the time goes in v7:
time: 95.7 us; the launch traced here: 95.4 us
  starting transfers between devices  28.4 us (30%)
  blocking collectives  25.3 us (26%)
  Pallas kernels  22.3 us (23%)
  waiting for transfers between devices  12.3 us (13%)
  local copies, waits for them, and re-layouts  5.98 us (6%)
    all_to_all x1, blocking collectives, on_device(): final = lax.all_to_all(leaving, FINAL, 0, 0, tiled=True)  25.3 us
    ppermute x14, starting transfers between devices, turned(): return lax.ppermute(array, 'z', [(i, (i + by) % RING) for i in range(RING)])  19.9 us
    pallas_call x5, Pallas kernels, grads(): pl.pallas_call(functools.partial(grads_kernel, first, last, len(pieces)),...  13.9 us
    ppermute x5, starting transfers between devices, swapped(): return lax.ppermute(array, axes, [(i, i ^ by) for i in range(count)])  8.48 us
    ppermute x14, waiting for transfers between devices, turned(): return lax.ppermute(array, 'z', [(i, (i + by) % RING) for i in range(RING)])  7.78 us
    pallas_call x2, Pallas kernels, stats(): pl.pallas_call(functools.partial(stats_kernel, first, len(pieces)), out_s...  6.8 us
    ppermute x5, waiting for transfers between devices, swapped(): return lax.ppermute(array, axes, [(i, i ^ by) for i in range(count)])  4.52 us
    unnamed x12, local copies, waits for them, and re-layouts  4.44 us
  transfers between devices with their start and end apart: 19, of which 7 were waited for; matrix products, arithmetic and copies ran while one was open for 0% of the time, Pallas kernels for 20%

profile of v7, /device:TPU:1, one launch (start us, length us, event | category | flops | bytes accessed | tf_op | source)
XLA Modules:
  0.0 95.4 jit_solution(9777048005592700698)
XLA Ops:
  0.6 0.0 copy-start.5
  0.6 0.0 copy-start.4
  0.7 0.7 copy-done.5
  1.3 0.0 copy-done.4
  1.3 0.0 copy-start.2
  1.4 0.8 copy-done.2
  2.2 0.0 copy-start.3
  2.2 0.8 copy-done.3
  3.0 0.1 shard_map.85
  3.2 3.3 %collective-permute-start = (bf16[2,80,256]{2,1,0:T(8,128)(2,1)S(1)}, bf16[2,80,256]{2,1,0:T(8,128)(2,1)S(1)}, u32[]{:S(2)}, u32[]{:S(2)}) collective-permute-start(bf16[2,80,256]{2,1,0:T(8,128)(2,1)S(1)} %get-tuple-element.81), channel_id=1, source_target_pairs={{0,8},{8,0},{128,136},{136,128},{1,9},{9,1},{129,137},{137,129},{2... | collective-permute-start | bytes 245768 | tf_op jit(solution)/shard_map/ppermute | solution.py:343
  6.5 0.9 collective-permute-done.pair_ref
  7.4 1.1 %collective-permute-start.1 = (bf16[2,80,256]{2,1,0:T(8,128)(2,1)S(1)}, bf16[2,80,256]{2,1,0:T(8,128)(2,1)S(1)}, u32[]{:S(2)}, u32[]{:S(2)}) collective-permute-start(bf16[2,80,256]{2,1,0:T(8,128)(2,1)S(1)} %pad_maximum_fusion), channel_id=1, source_target_pairs={{0,128},{8,136},{128,0},{136,8},{1,129},{9,137},{129,1},{137,9},{2... | collective-permute-start | bytes 245768 | tf_op jit(solution)/shard_map/ppermute | solution.py:343
  8.5 0.0 copy-start
  8.5 1.0 %copy-done = bf16[4,64,1024]{2,1,0:T(8,128)(2,1)S(1)} copy-done((bf16[4,64,1024]{2,1,0:T(8,128)(2,1)S(1)}, bf16[4,64,1024]{2,1,0:T(8,128)(2,1)}, u32[]{:S(2)}) %copy-start) | copy-done | bytes 524312
  9.6 1.0 %copy-done.1 = bf16[4,64,1024]{2,1,0:T(8,128)(2,1)S(1)} copy-done((bf16[4,64,1024]{2,1,0:T(8,128)(2,1)S(1)}, bf16[4,64,1024]{2,1,0:T(8,128)(2,1)}, u32[]{:S(2)}) %copy-start.1) | copy-done | bytes 524312
  10.6 1.4 %shard_map.86 = (bf16[128,1024]{1,0:T(8,128)(2,1)S(1)}, bf16[128,1024]{1,0:T(8,128)(2,1)S(1)}, bf16[128,1024]{1,0:T(8,128)(2,1)S(1)}, bf16[128,1024]{1,0:T(8,128)(2,1)S(1)}) custom-call(s32[1]{0:T(128)} %bitcast.place_ref, bf16[4,64,1024]{2,1,0:T(8,128)(2,1)S(1)} %copy-done, bf16[4,64,1024]{2,1,0:T(8,128)(2,1)S(1)} %copy-done.1), custom_call_target="tpu_custom_call" | custom-call | tf_op jit(solution)/shard_map/pallas_call | solution.py:314
  12.0 0.7 collective-permute-done.1.across_ref
  12.7 0.1 shard_map.87
  12.8 4.9 %collective-permute-start.7 = (bf16[4,80,256]{2,1,0:T(8,128)(2,1)S(1)}, bf16[4,80,256]{2,1,0:T(8,128)(2,1)S(1)}, u32[]{:S(2)}, u32[]{:S(2)}) collective-permute-start(bf16[4,80,256]{2,1,0:T(8,128)(2,1)S(1)} %get-tuple-element.94.refs_4_), channel_id=1, source_target_pairs={{0,112},{16,0},{32,16},{48,32},{64,48},{80,64},{96,80},{112,96},{1... | collective-permute-start | bytes 491528 | tf_op jit(solution)/shard_map/ppermute | solution.py:347
  17.7 0.0 collective-permute-start.5
  17.7 0.9 collective-permute-start.2
  18.6 2.2 %collective-permute-start.3 = (bf16[128,1024]{1,0:T(8,128)(2,1)S(1)}, bf16[128,1024]{1,0:T(8,128)(2,1)S(1)}, u32[]{:S(2)}, u32[]{:S(2)}) collective-permute-start(bf16[128,1024]{1,0:T(8,128)(2,1)S(1)} %get-tuple-element.92), channel_id=1, source_target_pairs={{0,128},{8,136},{128,0},{136,8},{1,129},{9,137},{129,1},{137,9},{2... | collective-permute-start | bytes 786440 | tf_op jit(solution)/shard_map/ppermute | solution.py:343
  20.8 0.9 collective-permute-start.4
  21.8 0.0 collective-permute-done.7.refs_6_.refs_4_
  21.8 3.0 %collective-permute-start.8 = (bf16[4,80,256]{2,1,0:T(8,128)(2,1)S(1)}, bf16[4,80,256]{2,1,0:T(8,128)(2,1)S(1)}, u32[]{:S(2)}, u32[]{:S(2)}) collective-permute-start(bf16[4,80,256]{2,1,0:T(8,128)(2,1)S(1)} %collective-permute-done.7.refs_6_.refs_4_), channel_id=1, source_target_pairs={{0,112},{16,0},{32,16},{48,32},{64,48},{80,64},{96,80},{112,96},{1... | collective-permute-start | bytes 491528 | tf_op jit(solution)/shard_map/ppermute | solution.py:347
  24.7 0.0 collective-permute-done.5.refs_5_
  24.7 0.0 collective-permute-start.6
  24.7 2.7 %collective-permute-done.8.refs_5_.refs_4_ = bf16[4,80,256]{2,1,0:T(8,128)(2,1)S(1)} collective-permute-done((bf16[4,80,256]{2,1,0:T(8,128)(2,1)S(1)}, bf16[4,80,256]{2,1,0:T(8,128)(2,1)S(1)}, u32[]{:S(2)}, u32[]{:S(2)}) %collective-permute-start.8) | collective-permute-done | bytes 163872 | tf_op jit(solution)/shard_map/ppermute | solution.py:347
  27.4 3.4 %collective-permute-start.10 = (bf16[4,80,256]{2,1,0:T(8,128)(2,1)S(1)}, bf16[4,80,256]{2,1,0:T(8,128)(2,1)S(1)}, u32[]{:S(2)}, u32[]{:S(2)}) collective-permute-start(bf16[4,80,256]{2,1,0:T(8,128)(2,1)S(1)} %collective-permute-done.8.refs_5_.refs_4_), channel_id=1, source_target_pairs={{0,112},{16,0},{32,16},{48,32},{64,48},{80,64},{96,80},{112,96},{1... | collective-permute-start | bytes 491528 | tf_op jit(solution)/shard_map/ppermute | solution.py:347
  30.8 0.0 collective-permute-done.6.refs_4_.refs_5_
  30.8 0.0 collective-permute-start.9
  30.9 0.0 collective-permute-done.2.refs_1_
  30.9 0.0 collective-permute-done.3.refs_2_
  30.9 2.9 %collective-permute-done.4.refs_3_ = bf16[128,1024]{1,0:T(8,128)(2,1)S(1)} collective-permute-done((bf16[128,1024]{1,0:T(8,128)(2,1)S(1)}, bf16[128,1024]{1,0:T(8,128)(2,1)S(1)}, u32[]{:S(2)}, u32[]{:S(2)}) %collective-permute-start.4) | collective-permute-done | bytes 262176 | tf_op jit(solution)/shard_map/ppermute | solution.py:343
  33.8 3.0 %shard_map.88.refs_8_ = f32[8,8,256]{2,1,0:T(8,128)S(1)} custom-call(f32[1,256]{1,0:T(1,128)S(1)} %get-tuple-element.88.low_ref, f32[1,256]{1,0:T(1,128)S(1)} %get-tuple-element.89.high_ref, bf16[128,1024]{1,0:T(8,128)(2,1)S(1)} %get-tuple-element.90.refs_0_, bf16[128,1024]{1,0:T(8,128)(2,1)S(1)} %collective-permute-done.2.refs_1_, ...), custom_call_target="tpu_custom_call" | custom-call | flops 1610612736 | bytes 1048576 | tf_op jit(solution)/shard_map/pallas_call | solution.py:204
  36.7 0.0 collective-permute-done.10.refs_7_.refs_4_
  36.8 0.0 collective-permute-done.9.refs_6_.refs_5_
  36.8 0.3 collective-permute-start.11
  37.0 3.8 %shard_map.89.state_ref = f32[8,8,256]{2,1,0:T(8,128)S(1)} custom-call(f32[1,256]{1,0:T(1,128)S(1)} %get-tuple-element.88.low_ref, f32[1,256]{1,0:T(1,128)S(1)} %get-tuple-element.89.high_ref, bf16[128,1024]{1,0:T(8,128)(2,1)S(1)} %get-tuple-element.90.refs_0_, bf16[128,1024]{1,0:T(8,128)(2,1)S(1)} %collective-permute-done.2.refs_1_, ...), custom_call_target="tpu_custom_call" | custom-call | flops 2147483648 | bytes 1048576 | tf_op jit(solution)/shard_map/pallas_call | solution.py:204
  40.9 1.8 %collective-permute-done.11.refs_4_ = bf16[4,80,256]{2,1,0:T(8,128)(2,1)S(1)} collective-permute-done((bf16[4,80,256]{2,1,0:T(8,128)(2,1)S(1)}, bf16[4,80,256]{2,1,0:T(8,128)(2,1)S(1)}, u32[]{:S(2)}, u32[]{:S(2)}) %collective-permute-start.11) | collective-permute-done | bytes 163872 | tf_op jit(solution)/shard_map/ppermute | solution.py:347
  42.7 2.5 %shard_map.90 = (f32[8,128,256]{2,1,0:T(8,128)S(1)}, bf16[4,64,256]{2,1,0:T(8,128)(2,1)S(1)}, f32[8,8,256]{2,1,0:T(8,128)S(1)}) custom-call(s32[1]{0:T(128)} %bitcast.place_ref, f32[1,256]{1,0:T(1,128)S(1)} %get-tuple-element.88.low_ref, f32[1,256]{1,0:T(1,128)S(1)} %get-tuple-element.89.high_ref, f32[8,8,256]{2,1,0:T(8,128)S(1)} %shard_map.89.state_ref, ...), custom_call_target="tpu_custom_call" | custom-call | flops 1073741824 | bytes 2097152 | tf_op jit(solution)/shard_map/pallas_call | solution.py:231
  45.2 0.1 collective-permute-start.12
  45.3 3.1 %shard_map.91 = (f32[8,128,256]{2,1,0:T(8,128)S(1)}, bf16[4,64,256]{2,1,0:T(8,128)(2,1)S(1)}, bf16[4,64,256]{2,1,0:T(8,128)(2,1)S(1)}) custom-call(s32[1]{0:T(128)} %bitcast.place_ref, f32[1,256]{1,0:T(1,128)S(1)} %get-tuple-element.88.low_ref, f32[1,256]{1,0:T(1,128)S(1)} %get-tuple-element.89.high_ref, f32[8,8,256]{2,1,0:T(8,128)S(1)} %get-tuple-element.103.state_ref, ...), custom_call_target="tpu_custom_call" | custom-call | flops 2147483648 | bytes 2097152 | tf_op jit(solution)/shard_map/pallas_call | solution.py:231
  48.5 2.0 %collective-permute-done.12 = bf16[4,64,256]{2,1,0:T(8,128)(2,1)S(1)} collective-permute-done((bf16[4,64,256]{2,1,0:T(8,128)(2,1)S(1)}, bf16[4,64,256]{2,1,0:T(8,128)(2,1)S(1)}, u32[]{:S(2)}, u32[]{:S(2)}) %collective-permute-start.12) | collective-permute-done | bytes 131104 | tf_op jit(solution)/shard_map/ppermute | solution.py:347
  50.5 0.1 collective-permute-start.13
  50.6 2.7 %collective-permute-start.14 = (bf16[4,64,256]{2,1,0:T(8,128)(2,1)S(1)}, bf16[4,64,256]{2,1,0:T(8,128)(2,1)S(1)}, u32[]{:S(2)}, u32[]{:S(2)}) collective-permute-start(bf16[4,64,256]{2,1,0:T(8,128)(2,1)S(1)} %get-tuple-element.119), channel_id=1, source_target_pairs={{0,112},{16,0},{32,16},{48,32},{64,48},{80,64},{96,80},{112,96},{1... | collective-permute-start | bytes 393224 | tf_op jit(solution)/shard_map/ppermute | solution.py:347
  53.2 3.1 %shard_map.92 = (f32[8,128,256]{2,1,0:T(8,128)S(1)}, bf16[4,64,256]{2,1,0:T(8,128)(2,1)S(1)}, bf16[4,64,256]{2,1,0:T(8,128)(2,1)S(1)}) custom-call(s32[1]{0:T(128)} %bitcast.place_ref, f32[1,256]{1,0:T(1,128)S(1)} %get-tuple-element.88.low_ref, f32[1,256]{1,0:T(1,128)S(1)} %get-tuple-element.89.high_ref, f32[8,8,256]{2,1,0:T(8,128)S(1)} %get-tuple-element.103.state_ref, ...), custom_call_target="tpu_custom_call" | custom-call | flops 2147483648 | bytes 2097152 | tf_op jit(solution)/shard_map/pallas_call | solution.py:231
  56.4 0.0 collective-permute-done.13
  56.4 0.0 collective-permute-done.14
  56.4 0.1 add_convert_fusion.3
  56.5 0.1 collective-permute-start.15
  56.5 2.7 %collective-permute-start.16 = (bf16[4,64,256]{2,1,0:T(8,128)(2,1)S(1)}, bf16[4,64,256]{2,1,0:T(8,128)(2,1)S(1)}, u32[]{:S(2)}, u32[]{:S(2)}) collective-permute-start(bf16[4,64,256]{2,1,0:T(8,128)(2,1)S(1)} %get-tuple-element.131), channel_id=1, source_target_pairs={{0,112},{16,0},{32,16},{48,32},{64,48},{80,64},{96,80},{112,96},{1... | collective-permute-start | bytes 393224 | tf_op jit(solution)/shard_map/ppermute | solution.py:347
  59.2 3.1 %shard_map.93 = (f32[8,128,256]{2,1,0:T(8,128)S(1)}, bf16[4,64,256]{2,1,0:T(8,128)(2,1)S(1)}, bf16[4,64,256]{2,1,0:T(8,128)(2,1)S(1)}) custom-call(s32[1]{0:T(128)} %bitcast.place_ref, f32[1,256]{1,0:T(1,128)S(1)} %get-tuple-element.88.low_ref, f32[1,256]{1,0:T(1,128)S(1)} %get-tuple-element.89.high_ref, f32[8,8,256]{2,1,0:T(8,128)S(1)} %get-tuple-element.103.state_ref, ...), custom_call_target="tpu_custom_call" | custom-call | flops 2147483648 | bytes 2097152 | tf_op jit(solution)/shard_map/pallas_call | solution.py:231
  62.3 0.0 collective-permute-done.15
  62.4 0.0 collective-permute-done.16
  62.5 0.5 collective-permute-start.17
  63.0 2.2 %collective-permute-start.18 = (bf16[4,64,256]{2,1,0:T(8,128)(2,1)S(1)}, bf16[4,64,256]{2,1,0:T(8,128)(2,1)S(1)}, u32[]{:S(2)}, u32[]{:S(2)}) collective-permute-start(bf16[4,64,256]{2,1,0:T(8,128)(2,1)S(1)} %add_convert_fusion.1), channel_id=1, source_target_pairs={{0,112},{16,0},{32,16},{48,32},{64,48},{80,64},{96,80},{112,96},{1... | collective-permute-start | bytes 393224 | tf_op jit(solution)/shard_map/ppermute | solution.py:347
  65.2 2.0 %shard_map.94 = (bf16[4,64,1280]{2,1,0:T(8,128)(2,1)S(1)}, bf16[4,64,256]{2,1,0:T(8,128)(2,1)S(1)}) custom-call(s32[1]{0:T(128)} %bitcast.place_ref, f32[1,256]{1,0:T(1,128)S(1)} %get-tuple-element.88.low_ref, f32[1,256]{1,0:T(1,128)S(1)} %get-tuple-element.89.high_ref, f32[8,8,256]{2,1,0:T(8,128)S(1)} %get-tuple-element.103.state_ref, ...), custom_call_target="tpu_custom_call" | custom-call | flops 1073741824 | bytes 2097152 | tf_op jit(solution)/shard_map/pallas_call | solution.py:231
  67.2 1.3 %collective-permute-done.17 = bf16[4,64,256]{2,1,0:T(8,128)(2,1)S(1)} collective-permute-done((bf16[4,64,256]{2,1,0:T(8,128)(2,1)S(1)}, bf16[4,64,256]{2,1,0:T(8,128)(2,1)S(1)}, u32[]{:S(2)}, u32[]{:S(2)}) %collective-permute-start.17) | collective-permute-done | bytes 131104 | tf_op jit(solution)/shard_map/ppermute | solution.py:347
  68.4 0.0 collective-permute-done.18
  68.4 0.1 add_convert_fusion
  68.6 25.3 %all_to_all.5 = bf16[32,8,1280]{2,1,0:T(8,128)(2,1)S(1)} all-to-all(bf16[32,8,1280]{2,1,0:T(8,128)(2,1)S(1)} %bitcast.20), channel_id=1, replica_groups=mesh['xh'=2,'z'=8,'core'=2,'y'=4,'xl'=2] {'xh','core','y','xl'}, dimensions={0} | all-to-all | bytes 1310720 | tf_op jit(solution)/shard_map/all_to_all | solution.py:411
  93.9 0.7 fusion
  94.5 0.9 slice.39
  (11 shorter events, 0.2 us)
Async XLA Ops:
  0.6 0.7 copy-start.5
  0.6 0.7 copy-start.4
  1.3 0.8 copy-start.2
  2.2 0.8 copy-start.3
  3.2 4.3 %collective-permute-start = (bf16[2,80,256]{2,1,0:T(8,128)(2,1)S(1)}, bf16[2,80,256]{2,1,0:T(8,128)(2,1)S(1)}, u32[]{:S(2)}, u32[]{:S(2)}) collective-permute-start(bf16[2,80,256]{2,1,0:T(8,128)(2,1)S(1)} %get-tuple-element.81), channel_id=1, source_target_pairs={{0,8},{8,0},{128,136},{136,128},{1,9},{9,1},{129,137},{137,129},{2... | collective-permute-start | bytes 245768 | tf_op jit(solution)/shard_map/ppermute | solution.py:343
  7.4 5.3 %collective-permute-start.1 = (bf16[2,80,256]{2,1,0:T(8,128)(2,1)S(1)}, bf16[2,80,256]{2,1,0:T(8,128)(2,1)S(1)}, u32[]{:S(2)}, u32[]{:S(2)}) collective-permute-start(bf16[2,80,256]{2,1,0:T(8,128)(2,1)S(1)} %pad_maximum_fusion), channel_id=1, source_target_pairs={{0,128},{8,136},{128,0},{136,8},{1,129},{9,137},{129,1},{137,9},{2... | collective-permute-start | bytes 245768 | tf_op jit(solution)/shard_map/ppermute | solution.py:343
  8.5 1.0 %copy-start = (bf16[4,64,1024]{2,1,0:T(8,128)(2,1)S(1)}, bf16[4,64,1024]{2,1,0:T(8,128)(2,1)}, u32[]{:S(2)}) copy-start(bf16[4,64,1024]{2,1,0:T(8,128)(2,1)} %q_ref.1) | copy-start | bytes 1572868
  9.6 1.0 %copy-start.1 = (bf16[4,64,1024]{2,1,0:T(8,128)(2,1)S(1)}, bf16[4,64,1024]{2,1,0:T(8,128)(2,1)}, u32[]{:S(2)}) copy-start(bf16[4,64,1024]{2,1,0:T(8,128)(2,1)} %do_ref.1) | copy-start | bytes 1572868
  12.8 9.0 %collective-permute-start.7 = (bf16[4,80,256]{2,1,0:T(8,128)(2,1)S(1)}, bf16[4,80,256]{2,1,0:T(8,128)(2,1)S(1)}, u32[]{:S(2)}, u32[]{:S(2)}) collective-permute-start(bf16[4,80,256]{2,1,0:T(8,128)(2,1)S(1)} %get-tuple-element.94.refs_4_), channel_id=1, source_target_pairs={{0,112},{16,0},{32,16},{48,32},{64,48},{80,64},{96,80},{112,96},{1... | collective-permute-start | bytes 491528 | tf_op jit(solution)/shard_map/ppermute | solution.py:347
  17.7 7.0 %collective-permute-start.5 = (bf16[4,80,256]{2,1,0:T(8,128)(2,1)S(1)}, bf16[4,80,256]{2,1,0:T(8,128)(2,1)S(1)}, u32[]{:S(2)}, u32[]{:S(2)}) collective-permute-start(bf16[4,80,256]{2,1,0:T(8,128)(2,1)S(1)} %get-tuple-element.94.refs_4_), channel_id=1, source_target_pairs={{0,16},{16,32},{32,48},{48,64},{64,80},{80,96},{96,112},{112,0},{1... | collective-permute-start | bytes 491528 | tf_op jit(solution)/shard_map/ppermute | solution.py:347
  17.7 13.1 %collective-permute-start.2 = (bf16[128,1024]{1,0:T(8,128)(2,1)S(1)}, bf16[128,1024]{1,0:T(8,128)(2,1)S(1)}, u32[]{:S(2)}, u32[]{:S(2)}) collective-permute-start(bf16[128,1024]{1,0:T(8,128)(2,1)S(1)} %get-tuple-element.91), channel_id=1, source_target_pairs={{0,8},{8,0},{128,136},{136,128},{1,9},{9,1},{129,137},{137,129},{2... | collective-permute-start | bytes 786440 | tf_op jit(solution)/shard_map/ppermute | solution.py:343
  18.6 12.2 %collective-permute-start.3 = (bf16[128,1024]{1,0:T(8,128)(2,1)S(1)}, bf16[128,1024]{1,0:T(8,128)(2,1)S(1)}, u32[]{:S(2)}, u32[]{:S(2)}) collective-permute-start(bf16[128,1024]{1,0:T(8,128)(2,1)S(1)} %get-tuple-element.92), channel_id=1, source_target_pairs={{0,128},{8,136},{128,0},{136,8},{1,129},{9,137},{129,1},{137,9},{2... | collective-permute-start | bytes 786440 | tf_op jit(solution)/shard_map/ppermute | solution.py:343
  20.8 12.9 %collective-permute-start.4 = (bf16[128,1024]{1,0:T(8,128)(2,1)S(1)}, bf16[128,1024]{1,0:T(8,128)(2,1)S(1)}, u32[]{:S(2)}, u32[]{:S(2)}) collective-permute-start(bf16[128,1024]{1,0:T(8,128)(2,1)S(1)} %get-tuple-element.93), channel_id=1, source_target_pairs={{0,136},{8,128},{128,8},{136,0},{1,137},{9,129},{129,9},{137,1},{2... | collective-permute-start | bytes 786440 | tf_op jit(solution)/shard_map/ppermute | solution.py:343
  21.8 5.7 %collective-permute-start.8 = (bf16[4,80,256]{2,1,0:T(8,128)(2,1)S(1)}, bf16[4,80,256]{2,1,0:T(8,128)(2,1)S(1)}, u32[]{:S(2)}, u32[]{:S(2)}) collective-permute-start(bf16[4,80,256]{2,1,0:T(8,128)(2,1)S(1)} %collective-permute-done.7.refs_6_.refs_4_), channel_id=1, source_target_pairs={{0,112},{16,0},{32,16},{48,32},{64,48},{80,64},{96,80},{112,96},{1... | collective-permute-start | bytes 491528 | tf_op jit(solution)/shard_map/ppermute | solution.py:347
  24.7 6.1 %collective-permute-start.6 = (bf16[4,80,256]{2,1,0:T(8,128)(2,1)S(1)}, bf16[4,80,256]{2,1,0:T(8,128)(2,1)S(1)}, u32[]{:S(2)}, u32[]{:S(2)}) collective-permute-start(bf16[4,80,256]{2,1,0:T(8,128)(2,1)S(1)} %collective-permute-done.5.refs_5_), channel_id=1, source_target_pairs={{0,16},{16,32},{32,48},{48,64},{64,80},{80,96},{96,112},{112,0},{1... | collective-permute-start | bytes 491528 | tf_op jit(solution)/shard_map/ppermute | solution.py:347
  27.4 9.3 %collective-permute-start.10 = (bf16[4,80,256]{2,1,0:T(8,128)(2,1)S(1)}, bf16[4,80,256]{2,1,0:T(8,128)(2,1)S(1)}, u32[]{:S(2)}, u32[]{:S(2)}) collective-permute-start(bf16[4,80,256]{2,1,0:T(8,128)(2,1)S(1)} %collective-permute-done.8.refs_5_.refs_4_), channel_id=1, source_target_pairs={{0,112},{16,0},{32,16},{48,32},{64,48},{80,64},{96,80},{112,96},{1... | collective-permute-start | bytes 491528 | tf_op jit(solution)/shard_map/ppermute | solution.py:347
  30.8 5.9 %collective-permute-start.9 = (bf16[4,80,256]{2,1,0:T(8,128)(2,1)S(1)}, bf16[4,80,256]{2,1,0:T(8,128)(2,1)S(1)}, u32[]{:S(2)}, u32[]{:S(2)}) collective-permute-start(bf16[4,80,256]{2,1,0:T(8,128)(2,1)S(1)} %collective-permute-done.6.refs_4_.refs_5_), channel_id=1, source_target_pairs={{0,16},{16,32},{32,48},{48,64},{64,80},{80,96},{96,112},{112,0},{1... | collective-permute-start | bytes 491528 | tf_op jit(solution)/shard_map/ppermute | solution.py:347
  36.8 5.9 %collective-permute-start.11 = (bf16[4,80,256]{2,1,0:T(8,128)(2,1)S(1)}, bf16[4,80,256]{2,1,0:T(8,128)(2,1)S(1)}, u32[]{:S(2)}, u32[]{:S(2)}) collective-permute-start(bf16[4,80,256]{2,1,0:T(8,128)(2,1)S(1)} %collective-permute-done.9.refs_6_.refs_5_), channel_id=1, source_target_pairs={{0,16},{16,32},{32,48},{48,64},{64,80},{80,96},{96,112},{112,0},{1... | collective-permute-start | bytes 491528 | tf_op jit(solution)/shard_map/ppermute | solution.py:347
  45.2 5.2 %collective-permute-start.12 = (bf16[4,64,256]{2,1,0:T(8,128)(2,1)S(1)}, bf16[4,64,256]{2,1,0:T(8,128)(2,1)S(1)}, u32[]{:S(2)}, u32[]{:S(2)}) collective-permute-start(bf16[4,64,256]{2,1,0:T(8,128)(2,1)S(1)} %get-tuple-element.108), channel_id=1, source_target_pairs={{0,16},{16,32},{32,48},{48,64},{64,80},{80,96},{96,112},{112,0},{1... | collective-permute-start | bytes 393224 | tf_op jit(solution)/shard_map/ppermute | solution.py:347
  50.5 5.9 %collective-permute-start.13 = (bf16[4,64,256]{2,1,0:T(8,128)(2,1)S(1)}, bf16[4,64,256]{2,1,0:T(8,128)(2,1)S(1)}, u32[]{:S(2)}, u32[]{:S(2)}) collective-permute-start(bf16[4,64,256]{2,1,0:T(8,128)(2,1)S(1)} %add_convert_fusion.5), channel_id=1, source_target_pairs={{0,16},{16,32},{32,48},{48,64},{64,80},{80,96},{96,112},{112,0},{1... | collective-permute-start | bytes 393224 | tf_op jit(solution)/shard_map/ppermute | solution.py:347
  50.6 5.8 %collective-permute-start.14 = (bf16[4,64,256]{2,1,0:T(8,128)(2,1)S(1)}, bf16[4,64,256]{2,1,0:T(8,128)(2,1)S(1)}, u32[]{:S(2)}, u32[]{:S(2)}) collective-permute-start(bf16[4,64,256]{2,1,0:T(8,128)(2,1)S(1)} %get-tuple-element.119), channel_id=1, source_target_pairs={{0,112},{16,0},{32,16},{48,32},{64,48},{80,64},{96,80},{112,96},{1... | collective-permute-start | bytes 393224 | tf_op jit(solution)/shard_map/ppermute | solution.py:347
  56.5 5.9 %collective-permute-start.15 = (bf16[4,64,256]{2,1,0:T(8,128)(2,1)S(1)}, bf16[4,64,256]{2,1,0:T(8,128)(2,1)S(1)}, u32[]{:S(2)}, u32[]{:S(2)}) collective-permute-start(bf16[4,64,256]{2,1,0:T(8,128)(2,1)S(1)} %get-tuple-element.130), channel_id=1, source_target_pairs={{0,16},{16,32},{32,48},{48,64},{64,80},{80,96},{96,112},{112,0},{1... | collective-permute-start | bytes 393224 | tf_op jit(solution)/shard_map/ppermute | solution.py:347
  56.5 5.8 %collective-permute-start.16 = (bf16[4,64,256]{2,1,0:T(8,128)(2,1)S(1)}, bf16[4,64,256]{2,1,0:T(8,128)(2,1)S(1)}, u32[]{:S(2)}, u32[]{:S(2)}) collective-permute-start(bf16[4,64,256]{2,1,0:T(8,128)(2,1)S(1)} %get-tuple-element.131), channel_id=1, source_target_pairs={{0,112},{16,0},{32,16},{48,32},{64,48},{80,64},{96,80},{112,96},{1... | collective-permute-start | bytes 393224 | tf_op jit(solution)/shard_map/ppermute | solution.py:347
  62.5 6.0 %collective-permute-start.17 = (bf16[4,64,256]{2,1,0:T(8,128)(2,1)S(1)}, bf16[4,64,256]{2,1,0:T(8,128)(2,1)S(1)}, u32[]{:S(2)}, u32[]{:S(2)}) collective-permute-start(bf16[4,64,256]{2,1,0:T(8,128)(2,1)S(1)} %add_convert_fusion.2), channel_id=1, source_target_pairs={{0,16},{16,32},{32,48},{48,64},{64,80},{80,96},{96,112},{112,0},{1... | collective-permute-start | bytes 393224 | tf_op jit(solution)/shard_map/ppermute | solution.py:347
  63.0 5.5 %collective-permute-start.18 = (bf16[4,64,256]{2,1,0:T(8,128)(2,1)S(1)}, bf16[4,64,256]{2,1,0:T(8,128)(2,1)S(1)}, u32[]{:S(2)}, u32[]{:S(2)}) collective-permute-start(bf16[4,64,256]{2,1,0:T(8,128)(2,1)S(1)} %add_convert_fusion.1), channel_id=1, source_target_pairs={{0,112},{16,0},{32,16},{48,32},{64,48},{80,64},{96,80},{112,96},{1... | collective-permute-start | bytes 393224 | tf_op jit(solution)/shard_map/ppermute | solution.py:347

commit v8 on v7

--- a/solution.py
+++ b/solution.py
@@ -27,30 +27,30 @@
     return lax.dot_general(a, b, dims, preferred_element_type=jnp.float32)
 
 
-def key_spans(piece_refs, row_count):
+def key_spans(piece_refs):
     spans, start = [], 0
     for ref in piece_refs:
-        size = ref.shape[0] * row_count
+        size = ref.shape[0] - META_ROWS
         spans.append((ref, slice(start, start + size), size))
         start += size
     return spans, start
 
 
-def keys_of(ref, size, row_count):
-    return ref[:, 0:row_count, 0:HEAD_SIZE].reshape(size, HEAD_SIZE)
-
-
-def values_of(ref, size, row_count):
-    return ref[:, 0:row_count, HEAD_SIZE:2 * HEAD_SIZE].reshape(size, HEAD_SIZE)
+def keys_of(ref, size):
+    return ref[0:size, 0:HEAD_SIZE]
+
+
+def values_of(ref, size):
+    return ref[0:size, HEAD_SIZE:2 * HEAD_SIZE]
 
 
 def fill_bias(bias_ref, spans, low_ref, high_ref, row_count):
     rows = low_ref.shape[1]
     for ref, part, size in spans:
-        for b in range(ref.shape[0]):
-            digits = ref[b, row_count:row_count + META_ROWS, :].astype(jnp.float32)[0:1, :]
-            code = digits[:, 0:128] * 128.0 + digits[:, 128:256]
-            column = jnp.broadcast_to(code, (128, 128)).T[0:row_count, :]
+        digits = ref[size:size + META_ROWS, :].astype(jnp.float32)
+        codes = digits[:, 0:128] * 128.0 + digits[:, 128:256]
+        for b in range(size // row_count):
+            column = jnp.broadcast_to(codes[b:b + 1, :], (128, 128)).T[0:row_count, :]
             begin = part.start + b * row_count
             for r in range(rows // 128):
                 low = low_ref[:, r * 128:(r + 1) * 128]
@@ -87,7 +87,7 @@
     state_ref, bias_ref = rest[-2:]
     rows = low_ref.shape[1]
     row_count = rows // 4
-    spans, _ = key_spans(piece_refs, row_count)
+    spans, _ = key_spans(piece_refs)
     fill_bias(bias_ref, spans, low_ref, high_ref, row_count)
 
     def step(g, carry):
@@ -102,8 +102,8 @@
             else:
                 top, total, cross = rest[0][h, 0:1, :], rest[0][h, 1:2, :], rest[0][h, 2:3, :]
             for ref, part, size in spans:
-                s = dot(keys_of(ref, size, row_count), q, NT) * EXP2_SCALE + bias_ref[part, :]
-                dp = dot(values_of(ref, size, row_count), do, NT)
+                s = dot(keys_of(ref, size), q, NT) * EXP2_SCALE + bias_ref[part, :]
+                dp = dot(values_of(ref, size), do, NT)
                 top, total, cross = absorbed(top, total, cross, [s], [dp])[0:3]
             state_ref[h, 0:1, :] = top
             state_ref[h, 1:2, :] = total
@@ -124,10 +124,10 @@
     rows = low_ref.shape[1]
     row_count = rows // 4
     heads = HEADS_PER_STEP
-    spans, keys = key_spans(piece_refs, row_count)
+    spans, keys = key_spans(piece_refs)
     fill_bias(bias_ref, spans, low_ref, high_ref, row_count)
     for ref, part, size in spans:
-        kt_ref[:, part] = keys_of(ref, size, row_count).T
+        kt_ref[:, part] = keys_of(ref, size).T
     acc_ref[...] = jnp.zeros_like(acc_ref)
     place = place_ref[0]
 
@@ -141,8 +141,8 @@
             do.append(one_do)
 
             def products(ref, part, size):
-                s = dot(keys_of(ref, size, row_count), one_q, NT) * EXP2_SCALE + bias_ref[part, :]
-                return s, dot(values_of(ref, size, row_count), one_do, NT)
+                s = dot(keys_of(ref, size), one_q, NT) * EXP2_SCALE + bias_ref[part, :]
+                return s, dot(values_of(ref, size), one_do, NT)
 
             if first:
                 pairs = [products(*span) for span in spans]
@@ -198,7 +198,7 @@
 
 def stats(low, high, row_arrays, pieces, state):
     rows = low.shape[1]
-    keys = sum(piece.shape[0] for piece in pieces) * rows // 4
+    keys = sum(piece.shape[0] - META_ROWS for piece in pieces)
     first = state is None
     inputs = (low, high, *row_arrays, *pieces) + (() if first else (state,))
     return pl.pallas_call(
@@ -217,12 +217,11 @@
 def grads(place, low, high, state, row_arrays, pieces, before, last):
     rows = low.shape[1]
     row_count = rows // 4
-    sources = sum(piece.shape[0] for piece in pieces)
-    keys = sources * row_count
+    keys = sum(piece.shape[0] - META_ROWS for piece in pieces)
     width = 2 * HEAD_SIZE
     first = before is None
     inputs = (low, high, state, *row_arrays, *pieces) + (() if first else (before,))
-    parts = tuple(jax.ShapeDtypeStruct((piece.shape[0], row_count, width), jnp.bfloat16) for piece in pieces)
+    parts = tuple(jax.ShapeDtypeStruct((4, row_count, width), jnp.bfloat16) for piece in pieces)
     extra = (jax.ShapeDtypeStruct((GROUP, 8, rows), jnp.float32),) if first else ()
     if last:
         dq = jax.ShapeDtypeStruct((4, row_count, GROUP * HEAD_SIZE + width), jnp.bfloat16)
@@ -283,11 +282,15 @@
 
 def own_kernel(self_ref, pair_ref, across_ref, own_ref, low_ref, high_ref):
     row_count = self_ref.shape[0] - META_ROWS
+    line = lax.broadcasted_iota(jnp.int32, (META_ROWS, 2 * HEAD_SIZE), 0)
+    meta = jnp.zeros((META_ROWS, 2 * HEAD_SIZE), jnp.float32)
     codes = []
     for r, value in enumerate((self_ref[...], pair_ref[0], across_ref[0], across_ref[1])):
-        own_ref[r] = value
-        digits = value[row_count:, :].astype(jnp.float32)[0:8, :]
-        codes.append(digits[:, 0:128] * 128.0 + digits[:, 128:256])
+        own_ref[r * row_count:(r + 1) * row_count, :] = value[0:row_count, :]
+        digits = value[row_count:, :].astype(jnp.float32)
+        meta = jnp.where(line == r, digits, meta)
+        codes.append(digits[0:8, 0:128] * 128.0 + digits[0:8, 128:256])
+    own_ref[4 * row_count:, :] = meta.astype(jnp.bfloat16)
     lane = lax.broadcasted_iota(jnp.int32, (8, 128), 1)
     for i in range(2):
         code = jnp.where(lane < row_count, codes[2 * i], pltpu.roll(codes[2 * i + 1], row_count, 1))[0:1, :]
@@ -324,7 +327,7 @@
 def own_keys(mine, paired, crossed):
     rows = 4 * (mine.shape[0] - META_ROWS)
     row = jax.ShapeDtypeStruct((1, rows), jnp.float32)
-    own = jax.ShapeDtypeStruct((4,) + mine.shape, jnp.bfloat16)
+    own = jax.ShapeDtypeStruct((rows + META_ROWS, mine.shape[1]), jnp.bfloat16)
     return pl.pallas_call(
         own_kernel,
         out_shape=(own, row, row),
@@ -374,10 +377,10 @@
         above.append(turned(above[-1], -1))
     below.append(turned(below[2], 1))
     above.append(turned(above[2], -1))
-    state = stats(low, high, row_arrays, [own, below[1], above[1]], None)
+    state = stats(low, high, row_arrays, [own, below[1], above[1], below[2], above[2]], None)
     state, below[3], above[3] = tied((state, below[3], above[3]))
     opposite = turned(below[3], 1)
-    state = stats(low, high, row_arrays, [below[2], above[2], below[3], above[3]], state)
+    state = stats(low, high, row_arrays, [below[3], above[3]], state)
     state, opposite = tied((state, opposite))
 
     def gradients(pieces, before, last=False):

time: 95.7 us -> 95.6 us (level)
  waiting for transfers between devices: 12.3 us -> 14.6 us
  blocking collectives: 25.3 us -> 23.1 us
    ppermute x14, waiting for transfers between devices: 7.78 us -> 10.1 us  [turned(): return lax.ppermute(array, 'z', [(i, (i + by) % RING) for i in range(RING)])]
    all_to_all x1, blocking collectives: 25.3 us -> 23.1 us  [on_device(): final = lax.all_to_all(leaving, FINAL, 0, 0, tiled=True)]
where the time goes in v8:
time: 95.6 us; the launch traced here: 95.3 us
  starting transfers between devices  28.4 us (30%)
  blocking collectives  23.1 us (24%)
  Pallas kernels  22.1 us (23%)
  waiting for transfers between devices  14.6 us (15%)
  local copies, waits for them, and re-layouts  5.98 us (6%)
    all_to_all x1, blocking collectives, on_device(): final = lax.all_to_all(leaving, FINAL, 0, 0, tiled=True)  23.1 us
    ppermute x14, starting transfers between devices, turned(): return lax.ppermute(array, 'z', [(i, (i + by) % RING) for i in range(RING)])  19.9 us
    pallas_call x5, Pallas kernels, grads(): pl.pallas_call(functools.partial(grads_kernel, first, last, len(pieces)),...  13.8 us
    ppermute x14, waiting for transfers between devices, turned(): return lax.ppermute(array, 'z', [(i, (i + by) % RING) for i in range(RING)])  10.1 us
    ppermute x5, starting transfers between devices, swapped(): return lax.ppermute(array, axes, [(i, i ^ by) for i in range(count)])  8.48 us
    pallas_call x2, Pallas kernels, stats(): pl.pallas_call(functools.partial(stats_kernel, first, len(pieces)), out_s...  6.62 us
    ppermute x5, waiting for transfers between devices, swapped(): return lax.ppermute(array, axes, [(i, i ^ by) for i in range(count)])  4.45 us
    unnamed x12, local copies, waits for them, and re-layouts  4.44 us
  transfers between devices with their start and end apart: 19, of which 7 were waited for; matrix products, arithmetic and copies ran while one was open for 0% of the time, Pallas kernels for 20%

profile of v8, /device:TPU:1, one launch (start us, length us, event | category | flops | bytes accessed | tf_op | source)
XLA Modules:
  0.0 95.3 jit_solution(3704003172683849201)
XLA Ops:
  0.6 0.0 copy-start.5
  0.6 0.0 copy-start.4
  0.7 0.7 copy-done.5
  1.3 0.0 copy-done.4
  1.3 0.0 copy-start.2
  1.4 0.8 copy-done.2
  2.2 0.0 copy-start.3
  2.2 0.8 copy-done.3
  3.0 0.1 shard_map.85
  3.2 3.3 %collective-permute-start = (bf16[2,80,256]{2,1,0:T(8,128)(2,1)S(1)}, bf16[2,80,256]{2,1,0:T(8,128)(2,1)S(1)}, u32[]{:S(2)}, u32[]{:S(2)}) collective-permute-start(bf16[2,80,256]{2,1,0:T(8,128)(2,1)S(1)} %get-tuple-element.81), channel_id=1, source_target_pairs={{0,8},{8,0},{128,136},{136,128},{1,9},{9,1},{129,137},{137,129},{2... | collective-permute-start | bytes 245768 | tf_op jit(solution)/shard_map/ppermute | solution.py:346
  6.5 0.9 collective-permute-done.pair_ref
  7.4 1.1 %collective-permute-start.1 = (bf16[2,80,256]{2,1,0:T(8,128)(2,1)S(1)}, bf16[2,80,256]{2,1,0:T(8,128)(2,1)S(1)}, u32[]{:S(2)}, u32[]{:S(2)}) collective-permute-start(bf16[2,80,256]{2,1,0:T(8,128)(2,1)S(1)} %pad_maximum_fusion), channel_id=1, source_target_pairs={{0,128},{8,136},{128,0},{136,8},{1,129},{9,137},{129,1},{137,9},{2... | collective-permute-start | bytes 245768 | tf_op jit(solution)/shard_map/ppermute | solution.py:346
  8.5 0.0 copy-start
  8.5 1.0 %copy-done = bf16[4,64,1024]{2,1,0:T(8,128)(2,1)S(1)} copy-done((bf16[4,64,1024]{2,1,0:T(8,128)(2,1)S(1)}, bf16[4,64,1024]{2,1,0:T(8,128)(2,1)}, u32[]{:S(2)}) %copy-start) | copy-done | bytes 524312
  9.6 1.0 %copy-done.1 = bf16[4,64,1024]{2,1,0:T(8,128)(2,1)S(1)} copy-done((bf16[4,64,1024]{2,1,0:T(8,128)(2,1)S(1)}, bf16[4,64,1024]{2,1,0:T(8,128)(2,1)}, u32[]{:S(2)}) %copy-start.1) | copy-done | bytes 524312
  10.6 1.4 %shard_map.86 = (bf16[128,1024]{1,0:T(8,128)(2,1)S(1)}, bf16[128,1024]{1,0:T(8,128)(2,1)S(1)}, bf16[128,1024]{1,0:T(8,128)(2,1)S(1)}, bf16[128,1024]{1,0:T(8,128)(2,1)S(1)}) custom-call(s32[1]{0:T(128)} %bitcast.place_ref, bf16[4,64,1024]{2,1,0:T(8,128)(2,1)S(1)} %copy-done, bf16[4,64,1024]{2,1,0:T(8,128)(2,1)S(1)} %copy-done.1), custom_call_target="tpu_custom_call" | custom-call | tf_op jit(solution)/shard_map/pallas_call | solution.py:317
  12.0 0.7 collective-permute-done.1.across_ref
  12.7 0.1 shard_map.87
  12.8 4.9 %collective-permute-start.6 = (bf16[272,256]{1,0:T(8,128)(2,1)S(1)}, bf16[272,256]{1,0:T(8,128)(2,1)S(1)}, u32[]{:S(2)}, u32[]{:S(2)}) collective-permute-start(bf16[272,256]{1,0:T(8,128)(2,1)S(1)} %get-tuple-element.94.refs_4_), channel_id=1, source_target_pairs={{0,112},{16,0},{32,16},{48,32},{64,48},{80,64},{96,80},{112,96},{1... | collective-permute-start | bytes 417800 | tf_op jit(solution)/shard_map/ppermute | solution.py:350
  17.7 0.0 collective-permute-start.5
  17.7 0.9 collective-permute-start.2
  18.6 2.2 %collective-permute-start.3 = (bf16[128,1024]{1,0:T(8,128)(2,1)S(1)}, bf16[128,1024]{1,0:T(8,128)(2,1)S(1)}, u32[]{:S(2)}, u32[]{:S(2)}) collective-permute-start(bf16[128,1024]{1,0:T(8,128)(2,1)S(1)} %get-tuple-element.92), channel_id=1, source_target_pairs={{0,128},{8,136},{128,0},{136,8},{1,129},{9,137},{129,1},{137,9},{2... | collective-permute-start | bytes 786440 | tf_op jit(solution)/shard_map/ppermute | solution.py:346
  20.8 0.9 collective-permute-start.4
  21.8 0.0 collective-permute-done.6.refs_6_.refs_4_
  21.8 3.0 %collective-permute-start.8 = (bf16[272,256]{1,0:T(8,128)(2,1)S(1)}, bf16[272,256]{1,0:T(8,128)(2,1)S(1)}, u32[]{:S(2)}, u32[]{:S(2)}) collective-permute-start(bf16[272,256]{1,0:T(8,128)(2,1)S(1)} %collective-permute-done.6.refs_6_.refs_4_), channel_id=1, source_target_pairs={{0,112},{16,0},{32,16},{48,32},{64,48},{80,64},{96,80},{112,96},{1... | collective-permute-start | bytes 417800 | tf_op jit(solution)/shard_map/ppermute | solution.py:350
  24.7 0.0 collective-permute-done.5.refs_5_
  24.7 0.0 collective-permute-start.7
  24.7 2.8 %collective-permute-done.8.refs_8_.refs_4_ = bf16[272,256]{1,0:T(8,128)(2,1)S(1)} collective-permute-done((bf16[272,256]{1,0:T(8,128)(2,1)S(1)}, bf16[272,256]{1,0:T(8,128)(2,1)S(1)}, u32[]{:S(2)}, u32[]{:S(2)}) %collective-permute-start.8) | collective-permute-done | bytes 139296 | tf_op jit(solution)/shard_map/ppermute | solution.py:350
  27.5 3.4 %collective-permute-start.10 = (bf16[272,256]{1,0:T(8,128)(2,1)S(1)}, bf16[272,256]{1,0:T(8,128)(2,1)S(1)}, u32[]{:S(2)}, u32[]{:S(2)}) collective-permute-start(bf16[272,256]{1,0:T(8,128)(2,1)S(1)} %collective-permute-done.8.refs_8_.refs_4_), channel_id=1, source_target_pairs={{0,112},{16,0},{32,16},{48,32},{64,48},{80,64},{96,80},{112,96},{1... | collective-permute-start | bytes 417800 | tf_op jit(solution)/shard_map/ppermute | solution.py:350
  30.9 0.0 collective-permute-done.7.refs_7_.refs_5_
  30.9 0.0 collective-permute-start.9
  30.9 0.0 collective-permute-done.2.refs_1_
  30.9 0.0 collective-permute-done.3.refs_2_
  30.9 2.8 %collective-permute-done.4.refs_3_ = bf16[128,1024]{1,0:T(8,128)(2,1)S(1)} collective-permute-done((bf16[128,1024]{1,0:T(8,128)(2,1)S(1)}, bf16[128,1024]{1,0:T(8,128)(2,1)S(1)}, u32[]{:S(2)}, u32[]{:S(2)}) %collective-permute-start.4) | collective-permute-done | bytes 262176 | tf_op jit(solution)/shard_map/ppermute | solution.py:346
  33.8 4.5 %shard_map.88.refs_6_ = f32[8,8,256]{2,1,0:T(8,128)S(1)} custom-call(f32[1,256]{1,0:T(1,128)S(1)} %get-tuple-element.88.low_ref, f32[1,256]{1,0:T(1,128)S(1)} %get-tuple-element.89.high_ref, bf16[128,1024]{1,0:T(8,128)(2,1)S(1)} %get-tuple-element.90.refs_0_, bf16[128,1024]{1,0:T(8,128)(2,1)S(1)} %collective-permute-done.2.refs_1_, ...), custom_call_target="tpu_custom_call" | custom-call | flops 2684354560 | bytes 1048576 | tf_op jit(solution)/shard_map/pallas_call | solution.py:204
  38.3 0.0 collective-permute-done.10.refs_5_.refs_4_
  38.3 0.0 collective-permute-done.9.refs_4_.refs_5_
  38.3 0.3 collective-permute-start.11
  38.6 2.1 %shard_map.89.state_ref = f32[8,8,256]{2,1,0:T(8,128)S(1)} custom-call(f32[1,256]{1,0:T(1,128)S(1)} %get-tuple-element.88.low_ref, f32[1,256]{1,0:T(1,128)S(1)} %get-tuple-element.89.high_ref, bf16[128,1024]{1,0:T(8,128)(2,1)S(1)} %get-tuple-element.90.refs_0_, bf16[128,1024]{1,0:T(8,128)(2,1)S(1)} %collective-permute-done.2.refs_1_, ...), custom_call_target="tpu_custom_call" | custom-call | flops 1073741824 | bytes 1048576 | tf_op jit(solution)/shard_map/pallas_call | solution.py:204
  40.7 4.6 %collective-permute-done.11.refs_4_ = bf16[272,256]{1,0:T(8,128)(2,1)S(1)} collective-permute-done((bf16[272,256]{1,0:T(8,128)(2,1)S(1)}, bf16[272,256]{1,0:T(8,128)(2,1)S(1)}, u32[]{:S(2)}, u32[]{:S(2)}) %collective-permute-start.11) | collective-permute-done | bytes 139296 | tf_op jit(solution)/shard_map/ppermute | solution.py:350
  45.4 2.5 %shard_map.90 = (f32[8,128,256]{2,1,0:T(8,128)S(1)}, bf16[4,64,256]{2,1,0:T(8,128)(2,1)S(1)}, f32[8,8,256]{2,1,0:T(8,128)S(1)}) custom-call(s32[1]{0:T(128)} %bitcast.place_ref, f32[1,256]{1,0:T(1,128)S(1)} %get-tuple-element.88.low_ref, f32[1,256]{1,0:T(1,128)S(1)} %get-tuple-element.89.high_ref, f32[8,8,256]{2,1,0:T(8,128)S(1)} %shard_map.89.state_ref, ...), custom_call_target="tpu_custom_call" | custom-call | flops 1073741824 | bytes 2097152 | tf_op jit(solution)/shard_map/pallas_call | solution.py:230
  47.9 0.1 collective-permute-start.12
  48.0 3.1 %shard_map.91 = (f32[8,128,256]{2,1,0:T(8,128)S(1)}, bf16[4,64,256]{2,1,0:T(8,128)(2,1)S(1)}, bf16[4,64,256]{2,1,0:T(8,128)(2,1)S(1)}) custom-call(s32[1]{0:T(128)} %bitcast.place_ref, f32[1,256]{1,0:T(1,128)S(1)} %get-tuple-element.88.low_ref, f32[1,256]{1,0:T(1,128)S(1)} %get-tuple-element.89.high_ref, f32[8,8,256]{2,1,0:T(8,128)S(1)} %get-tuple-element.103.state_ref, ...), custom_call_target="tpu_custom_call" | custom-call | flops 2147483648 | bytes 2097152 | tf_op jit(solution)/shard_map/pallas_call | solution.py:230
  51.1 2.3 %collective-permute-done.12 = bf16[4,64,256]{2,1,0:T(8,128)(2,1)S(1)} collective-permute-done((bf16[4,64,256]{2,1,0:T(8,128)(2,1)S(1)}, bf16[4,64,256]{2,1,0:T(8,128)(2,1)S(1)}, u32[]{:S(2)}, u32[]{:S(2)}) %collective-permute-start.12) | collective-permute-done | bytes 131104 | tf_op jit(solution)/shard_map/ppermute | solution.py:350
  53.4 0.1 collective-permute-start.13
  53.5 2.7 %collective-permute-start.14 = (bf16[4,64,256]{2,1,0:T(8,128)(2,1)S(1)}, bf16[4,64,256]{2,1,0:T(8,128)(2,1)S(1)}, u32[]{:S(2)}, u32[]{:S(2)}) collective-permute-start(bf16[4,64,256]{2,1,0:T(8,128)(2,1)S(1)} %get-tuple-element.119), channel_id=1, source_target_pairs={{0,112},{16,0},{32,16},{48,32},{64,48},{80,64},{96,80},{112,96},{1... | collective-permute-start | bytes 393224 | tf_op jit(solution)/shard_map/ppermute | solution.py:350
  56.2 3.1 %shard_map.92 = (f32[8,128,256]{2,1,0:T(8,128)S(1)}, bf16[4,64,256]{2,1,0:T(8,128)(2,1)S(1)}, bf16[4,64,256]{2,1,0:T(8,128)(2,1)S(1)}) custom-call(s32[1]{0:T(128)} %bitcast.place_ref, f32[1,256]{1,0:T(1,128)S(1)} %get-tuple-element.88.low_ref, f32[1,256]{1,0:T(1,128)S(1)} %get-tuple-element.89.high_ref, f32[8,8,256]{2,1,0:T(8,128)S(1)} %get-tuple-element.103.state_ref, ...), custom_call_target="tpu_custom_call" | custom-call | flops 2147483648 | bytes 2097152 | tf_op jit(solution)/shard_map/pallas_call | solution.py:230
  59.3 0.0 collective-permute-done.13
  59.3 0.0 collective-permute-done.14
  59.3 0.1 add_convert_fusion.3
  59.4 0.1 collective-permute-start.15
  59.5 2.7 %collective-permute-start.16 = (bf16[4,64,256]{2,1,0:T(8,128)(2,1)S(1)}, bf16[4,64,256]{2,1,0:T(8,128)(2,1)S(1)}, u32[]{:S(2)}, u32[]{:S(2)}) collective-permute-start(bf16[4,64,256]{2,1,0:T(8,128)(2,1)S(1)} %get-tuple-element.131), channel_id=1, source_target_pairs={{0,112},{16,0},{32,16},{48,32},{64,48},{80,64},{96,80},{112,96},{1... | collective-permute-start | bytes 393224 | tf_op jit(solution)/shard_map/ppermute | solution.py:350
  62.2 3.1 %shard_map.93 = (f32[8,128,256]{2,1,0:T(8,128)S(1)}, bf16[4,64,256]{2,1,0:T(8,128)(2,1)S(1)}, bf16[4,64,256]{2,1,0:T(8,128)(2,1)S(1)}) custom-call(s32[1]{0:T(128)} %bitcast.place_ref, f32[1,256]{1,0:T(1,128)S(1)} %get-tuple-element.88.low_ref, f32[1,256]{1,0:T(1,128)S(1)} %get-tuple-element.89.high_ref, f32[8,8,256]{2,1,0:T(8,128)S(1)} %get-tuple-element.103.state_ref, ...), custom_call_target="tpu_custom_call" | custom-call | flops 2147483648 | bytes 2097152 | tf_op jit(solution)/shard_map/pallas_call | solution.py:230
  65.3 0.0 collective-permute-done.15
  65.3 0.0 collective-permute-done.16
  65.4 0.1 collective-permute-start.17
  65.5 2.7 %collective-permute-start.18 = (bf16[4,64,256]{2,1,0:T(8,128)(2,1)S(1)}, bf16[4,64,256]{2,1,0:T(8,128)(2,1)S(1)}, u32[]{:S(2)}, u32[]{:S(2)}) collective-permute-start(bf16[4,64,256]{2,1,0:T(8,128)(2,1)S(1)} %add_convert_fusion.1), channel_id=1, source_target_pairs={{0,112},{16,0},{32,16},{48,32},{64,48},{80,64},{96,80},{112,96},{1... | collective-permute-start | bytes 393224 | tf_op jit(solution)/shard_map/ppermute | solution.py:350
  68.1 2.0 %shard_map.94 = (bf16[4,64,1280]{2,1,0:T(8,128)(2,1)S(1)}, bf16[4,64,256]{2,1,0:T(8,128)(2,1)S(1)}) custom-call(s32[1]{0:T(128)} %bitcast.place_ref, f32[1,256]{1,0:T(1,128)S(1)} %get-tuple-element.88.low_ref, f32[1,256]{1,0:T(1,128)S(1)} %get-tuple-element.89.high_ref, f32[8,8,256]{2,1,0:T(8,128)S(1)} %get-tuple-element.103.state_ref, ...), custom_call_target="tpu_custom_call" | custom-call | flops 1073741824 | bytes 2097152 | tf_op jit(solution)/shard_map/pallas_call | solution.py:230
  70.1 0.4 collective-permute-done.17
  70.5 0.0 collective-permute-done.18
  70.5 0.1 add_convert_fusion
  70.6 23.1 %all_to_all.5 = bf16[32,8,1280]{2,1,0:T(8,128)(2,1)S(1)} all-to-all(bf16[32,8,1280]{2,1,0:T(8,128)(2,1)S(1)} %bitcast.20), channel_id=1, replica_groups=mesh['xh'=2,'z'=8,'core'=2,'y'=4,'xl'=2] {'xh','core','y','xl'}, dimensions={0} | all-to-all | bytes 1310720 | tf_op jit(solution)/shard_map/all_to_all | solution.py:414
  93.7 0.7 fusion
  94.4 0.9 slice.39
  (11 shorter events, 0.2 us)
Async XLA Ops:
  0.6 0.7 copy-start.5
  0.6 0.7 copy-start.4
  1.3 0.8 copy-start.2
  2.2 0.8 copy-start.3
  3.2 4.3 %collective-permute-start = (bf16[2,80,256]{2,1,0:T(8,128)(2,1)S(1)}, bf16[2,80,256]{2,1,0:T(8,128)(2,1)S(1)}, u32[]{:S(2)}, u32[]{:S(2)}) collective-permute-start(bf16[2,80,256]{2,1,0:T(8,128)(2,1)S(1)} %get-tuple-element.81), channel_id=1, source_target_pairs={{0,8},{8,0},{128,136},{136,128},{1,9},{9,1},{129,137},{137,129},{2... | collective-permute-start | bytes 245768 | tf_op jit(solution)/shard_map/ppermute | solution.py:346
  7.4 5.3 %collective-permute-start.1 = (bf16[2,80,256]{2,1,0:T(8,128)(2,1)S(1)}, bf16[2,80,256]{2,1,0:T(8,128)(2,1)S(1)}, u32[]{:S(2)}, u32[]{:S(2)}) collective-permute-start(bf16[2,80,256]{2,1,0:T(8,128)(2,1)S(1)} %pad_maximum_fusion), channel_id=1, source_target_pairs={{0,128},{8,136},{128,0},{136,8},{1,129},{9,137},{129,1},{137,9},{2... | collective-permute-start | bytes 245768 | tf_op jit(solution)/shard_map/ppermute | solution.py:346
  8.5 1.0 %copy-start = (bf16[4,64,1024]{2,1,0:T(8,128)(2,1)S(1)}, bf16[4,64,1024]{2,1,0:T(8,128)(2,1)}, u32[]{:S(2)}) copy-start(bf16[4,64,1024]{2,1,0:T(8,128)(2,1)} %q_ref.1) | copy-start | bytes 1572868
  9.6 1.0 %copy-start.1 = (bf16[4,64,1024]{2,1,0:T(8,128)(2,1)S(1)}, bf16[4,64,1024]{2,1,0:T(8,128)(2,1)}, u32[]{:S(2)}) copy-start(bf16[4,64,1024]{2,1,0:T(8,128)(2,1)} %do_ref.1) | copy-start | bytes 1572868
  12.8 9.0 %collective-permute-start.6 = (bf16[272,256]{1,0:T(8,128)(2,1)S(1)}, bf16[272,256]{1,0:T(8,128)(2,1)S(1)}, u32[]{:S(2)}, u32[]{:S(2)}) collective-permute-start(bf16[272,256]{1,0:T(8,128)(2,1)S(1)} %get-tuple-element.94.refs_4_), channel_id=1, source_target_pairs={{0,112},{16,0},{32,16},{48,32},{64,48},{80,64},{96,80},{112,96},{1... | collective-permute-start | bytes 417800 | tf_op jit(solution)/shard_map/ppermute | solution.py:350
  17.7 7.0 %collective-permute-start.5 = (bf16[272,256]{1,0:T(8,128)(2,1)S(1)}, bf16[272,256]{1,0:T(8,128)(2,1)S(1)}, u32[]{:S(2)}, u32[]{:S(2)}) collective-permute-start(bf16[272,256]{1,0:T(8,128)(2,1)S(1)} %get-tuple-element.94.refs_4_), channel_id=1, source_target_pairs={{0,16},{16,32},{32,48},{48,64},{64,80},{80,96},{96,112},{112,0},{1... | collective-permute-start | bytes 417800 | tf_op jit(solution)/shard_map/ppermute | solution.py:350
  17.7 13.2 %collective-permute-start.2 = (bf16[128,1024]{1,0:T(8,128)(2,1)S(1)}, bf16[128,1024]{1,0:T(8,128)(2,1)S(1)}, u32[]{:S(2)}, u32[]{:S(2)}) collective-permute-start(bf16[128,1024]{1,0:T(8,128)(2,1)S(1)} %get-tuple-element.91), channel_id=1, source_target_pairs={{0,8},{8,0},{128,136},{136,128},{1,9},{9,1},{129,137},{137,129},{2... | collective-permute-start | bytes 786440 | tf_op jit(solution)/shard_map/ppermute | solution.py:346
  18.6 12.3 %collective-permute-start.3 = (bf16[128,1024]{1,0:T(8,128)(2,1)S(1)}, bf16[128,1024]{1,0:T(8,128)(2,1)S(1)}, u32[]{:S(2)}, u32[]{:S(2)}) collective-permute-start(bf16[128,1024]{1,0:T(8,128)(2,1)S(1)} %get-tuple-element.92), channel_id=1, source_target_pairs={{0,128},{8,136},{128,0},{136,8},{1,129},{9,137},{129,1},{137,9},{2... | collective-permute-start | bytes 786440 | tf_op jit(solution)/shard_map/ppermute | solution.py:346
  20.8 12.9 %collective-permute-start.4 = (bf16[128,1024]{1,0:T(8,128)(2,1)S(1)}, bf16[128,1024]{1,0:T(8,128)(2,1)S(1)}, u32[]{:S(2)}, u32[]{:S(2)}) collective-permute-start(bf16[128,1024]{1,0:T(8,128)(2,1)S(1)} %get-tuple-element.93), channel_id=1, source_target_pairs={{0,136},{8,128},{128,8},{136,0},{1,137},{9,129},{129,9},{137,1},{2... | collective-permute-start | bytes 786440 | tf_op jit(solution)/shard_map/ppermute | solution.py:346
  21.8 5.7 %collective-permute-start.8 = (bf16[272,256]{1,0:T(8,128)(2,1)S(1)}, bf16[272,256]{1,0:T(8,128)(2,1)S(1)}, u32[]{:S(2)}, u32[]{:S(2)}) collective-permute-start(bf16[272,256]{1,0:T(8,128)(2,1)S(1)} %collective-permute-done.6.refs_6_.refs_4_), channel_id=1, source_target_pairs={{0,112},{16,0},{32,16},{48,32},{64,48},{80,64},{96,80},{112,96},{1... | collective-permute-start | bytes 417800 | tf_op jit(solution)/shard_map/ppermute | solution.py:350
  24.7 6.2 %collective-permute-start.7 = (bf16[272,256]{1,0:T(8,128)(2,1)S(1)}, bf16[272,256]{1,0:T(8,128)(2,1)S(1)}, u32[]{:S(2)}, u32[]{:S(2)}) collective-permute-start(bf16[272,256]{1,0:T(8,128)(2,1)S(1)} %collective-permute-done.5.refs_5_), channel_id=1, source_target_pairs={{0,16},{16,32},{32,48},{48,64},{64,80},{80,96},{96,112},{112,0},{1... | collective-permute-start | bytes 417800 | tf_op jit(solution)/shard_map/ppermute | solution.py:350
  27.5 10.8 %collective-permute-start.10 = (bf16[272,256]{1,0:T(8,128)(2,1)S(1)}, bf16[272,256]{1,0:T(8,128)(2,1)S(1)}, u32[]{:S(2)}, u32[]{:S(2)}) collective-permute-start(bf16[272,256]{1,0:T(8,128)(2,1)S(1)} %collective-permute-done.8.refs_8_.refs_4_), channel_id=1, source_target_pairs={{0,112},{16,0},{32,16},{48,32},{64,48},{80,64},{96,80},{112,96},{1... | collective-permute-start | bytes 417800 | tf_op jit(solution)/shard_map/ppermute | solution.py:350
  30.9 7.4 %collective-permute-start.9 = (bf16[272,256]{1,0:T(8,128)(2,1)S(1)}, bf16[272,256]{1,0:T(8,128)(2,1)S(1)}, u32[]{:S(2)}, u32[]{:S(2)}) collective-permute-start(bf16[272,256]{1,0:T(8,128)(2,1)S(1)} %collective-permute-done.7.refs_7_.refs_5_), channel_id=1, source_target_pairs={{0,16},{16,32},{32,48},{48,64},{64,80},{80,96},{96,112},{112,0},{1... | collective-permute-start | bytes 417800 | tf_op jit(solution)/shard_map/ppermute | solution.py:350
  38.3 7.0 %collective-permute-start.11 = (bf16[272,256]{1,0:T(8,128)(2,1)S(1)}, bf16[272,256]{1,0:T(8,128)(2,1)S(1)}, u32[]{:S(2)}, u32[]{:S(2)}) collective-permute-start(bf16[272,256]{1,0:T(8,128)(2,1)S(1)} %collective-permute-done.9.refs_4_.refs_5_), channel_id=1, source_target_pairs={{0,16},{16,32},{32,48},{48,64},{64,80},{80,96},{96,112},{112,0},{1... | collective-permute-start | bytes 417800 | tf_op jit(solution)/shard_map/ppermute | solution.py:350
  47.9 5.5 %collective-permute-start.12 = (bf16[4,64,256]{2,1,0:T(8,128)(2,1)S(1)}, bf16[4,64,256]{2,1,0:T(8,128)(2,1)S(1)}, u32[]{:S(2)}, u32[]{:S(2)}) collective-permute-start(bf16[4,64,256]{2,1,0:T(8,128)(2,1)S(1)} %get-tuple-element.108), channel_id=1, source_target_pairs={{0,16},{16,32},{32,48},{48,64},{64,80},{80,96},{96,112},{112,0},{1... | collective-permute-start | bytes 393224 | tf_op jit(solution)/shard_map/ppermute | solution.py:350
  53.4 5.9 %collective-permute-start.13 = (bf16[4,64,256]{2,1,0:T(8,128)(2,1)S(1)}, bf16[4,64,256]{2,1,0:T(8,128)(2,1)S(1)}, u32[]{:S(2)}, u32[]{:S(2)}) collective-permute-start(bf16[4,64,256]{2,1,0:T(8,128)(2,1)S(1)} %add_convert_fusion.5), channel_id=1, source_target_pairs={{0,16},{16,32},{32,48},{48,64},{64,80},{80,96},{96,112},{112,0},{1... | collective-permute-start | bytes 393224 | tf_op jit(solution)/shard_map/ppermute | solution.py:350
  53.5 5.8 %collective-permute-start.14 = (bf16[4,64,256]{2,1,0:T(8,128)(2,1)S(1)}, bf16[4,64,256]{2,1,0:T(8,128)(2,1)S(1)}, u32[]{:S(2)}, u32[]{:S(2)}) collective-permute-start(bf16[4,64,256]{2,1,0:T(8,128)(2,1)S(1)} %get-tuple-element.119), channel_id=1, source_target_pairs={{0,112},{16,0},{32,16},{48,32},{64,48},{80,64},{96,80},{112,96},{1... | collective-permute-start | bytes 393224 | tf_op jit(solution)/shard_map/ppermute | solution.py:350
  59.4 5.9 %collective-permute-start.15 = (bf16[4,64,256]{2,1,0:T(8,128)(2,1)S(1)}, bf16[4,64,256]{2,1,0:T(8,128)(2,1)S(1)}, u32[]{:S(2)}, u32[]{:S(2)}) collective-permute-start(bf16[4,64,256]{2,1,0:T(8,128)(2,1)S(1)} %get-tuple-element.130), channel_id=1, source_target_pairs={{0,16},{16,32},{32,48},{48,64},{64,80},{80,96},{96,112},{112,0},{1... | collective-permute-start | bytes 393224 | tf_op jit(solution)/shard_map/ppermute | solution.py:350
  59.5 5.8 %collective-permute-start.16 = (bf16[4,64,256]{2,1,0:T(8,128)(2,1)S(1)}, bf16[4,64,256]{2,1,0:T(8,128)(2,1)S(1)}, u32[]{:S(2)}, u32[]{:S(2)}) collective-permute-start(bf16[4,64,256]{2,1,0:T(8,128)(2,1)S(1)} %get-tuple-element.131), channel_id=1, source_target_pairs={{0,112},{16,0},{32,16},{48,32},{64,48},{80,64},{96,80},{112,96},{1... | collective-permute-start | bytes 393224 | tf_op jit(solution)/shard_map/ppermute | solution.py:350
  65.4 5.1 %collective-permute-start.17 = (bf16[4,64,256]{2,1,0:T(8,128)(2,1)S(1)}, bf16[4,64,256]{2,1,0:T(8,128)(2,1)S(1)}, u32[]{:S(2)}, u32[]{:S(2)}) collective-permute-start(bf16[4,64,256]{2,1,0:T(8,128)(2,1)S(1)} %add_convert_fusion.2), channel_id=1, source_target_pairs={{0,16},{16,32},{32,48},{48,64},{64,80},{80,96},{96,112},{112,0},{1... | collective-permute-start | bytes 393224 | tf_op jit(solution)/shard_map/ppermute | solution.py:350
  65.5 5.0 %collective-permute-start.18 = (bf16[4,64,256]{2,1,0:T(8,128)(2,1)S(1)}, bf16[4,64,256]{2,1,0:T(8,128)(2,1)S(1)}, u32[]{:S(2)}, u32[]{:S(2)}) collective-permute-start(bf16[4,64,256]{2,1,0:T(8,128)(2,1)S(1)} %add_convert_fusion.1), channel_id=1, source_target_pairs={{0,112},{16,0},{32,16},{48,32},{64,48},{80,64},{96,80},{112,96},{1... | collective-permute-start | bytes 393224 | tf_op jit(solution)/shard_map/ppermute | solution.py:350

commit v9 on v8

--- a/solution.py
+++ b/solution.py
@@ -389,12 +389,19 @@
     dq, to_up, state = gradients([opposite], None)
     spot, dq, to_up = tied((spot, dq, to_up))
     up = turned(to_up, 1)
-    dq, up_grad, down_grad = gradients([above[3], below[3]], dq)
-    dq, up_grad, down_grad, up = tied((dq, up_grad, down_grad, up))
-    to_up, to_down = plus(up_grad, up), down_grad
+    dq, to_down = gradients([below[3]], dq)
+    spot, dq, to_down = tied((spot, dq, to_down))
+    down = turned(to_down, -1)
+    dq, up_grad = gradients([above[3]], dq)
+    dq, up_grad, up = tied((dq, up_grad, up))
+    to_up = plus(up_grad, up)
     for k in (2, 1, 0):
-        spot, dq, to_up, to_down = tied((spot, dq, to_up, to_down))
-        up, down = turned(to_up, 1), turned(to_down, -1)
+        if k == 2:
+            spot, dq, to_up = tied((spot, dq, to_up))
+        else:
+            spot, dq, to_up, to_down = tied((spot, dq, to_up, to_down))
+            down = turned(to_down, -1)
+        up = turned(to_up, 1)
         if k:
             dq, up_grad, down_grad = gradients([above[k], below[k]], dq)
             dq, up_grad, down_grad, up, down = tied((dq, up_grad, down_grad, up, down))

time: 95.6 us -> 95.8 us (level)
    pallas_call x5 -> x6, Pallas kernels: 13.8 us -> 14.3 us  [grads(): pl.pallas_call(functools.partial(grads_kernel, first, last, len(pieces)),...]
  transfers between devices with their start and end apart: 19 -> 19, of which waited for: 7 -> 7; matrix products, arithmetic and copies ran while one was open for 0% -> 0% of each run, Pallas kernels for 20% -> 21%
where the time goes in v9:
time: 95.8 us; the launch traced here: 95.4 us
  starting transfers between devices  28.4 us (30%)
  blocking collectives  23.1 us (24%)
  Pallas kernels  22.5 us (23%)
  waiting for transfers between devices  14.2 us (15%)
  local copies, waits for them, and re-layouts  5.98 us (6%)
    all_to_all x1, blocking collectives, on_device(): final = lax.all_to_all(leaving, FINAL, 0, 0, tiled=True)  23.1 us
    ppermute x14, starting transfers between devices, turned(): return lax.ppermute(array, 'z', [(i, (i + by) % RING) for i in range(RING)])  20 us
    pallas_call x6, Pallas kernels, grads(): pl.pallas_call(functools.partial(grads_kernel, first, last, len(pieces)),...  14.3 us
    ppermute x14, waiting for transfers between devices, turned(): return lax.ppermute(array, 'z', [(i, (i + by) % RING) for i in range(RING)])  9.72 us
    ppermute x5, starting transfers between devices, swapped(): return lax.ppermute(array, axes, [(i, i ^ by) for i in range(count)])  8.48 us
    pallas_call x2, Pallas kernels, stats(): pl.pallas_call(functools.partial(stats_kernel, first, len(pieces)), out_s...  6.62 us
    ppermute x5, waiting for transfers between devices, swapped(): return lax.ppermute(array, axes, [(i, i ^ by) for i in range(count)])  4.45 us
    unnamed x12, local copies, waits for them, and re-layouts  4.44 us
  transfers between devices with their start and end apart: 19, of which 7 were waited for; matrix products, arithmetic and copies ran while one was open for 0% of the time, Pallas kernels for 21%

profile of v9, /device:TPU:1, one launch (start us, length us, event | category | flops | bytes accessed | tf_op | source)
XLA Modules:
  0.0 95.4 jit_solution(1273537687862874006)
XLA Ops:
  0.6 0.0 copy-start.5
  0.6 0.0 copy-start.4
  0.7 0.7 copy-done.5
  1.3 0.0 copy-done.4
  1.3 0.0 copy-start.2
  1.4 0.8 copy-done.2
  2.2 0.0 copy-start.3
  2.2 0.8 copy-done.3
  3.0 0.1 shard_map.85
  3.2 3.3 %collective-permute-start = (bf16[2,80,256]{2,1,0:T(8,128)(2,1)S(1)}, bf16[2,80,256]{2,1,0:T(8,128)(2,1)S(1)}, u32[]{:S(2)}, u32[]{:S(2)}) collective-permute-start(bf16[2,80,256]{2,1,0:T(8,128)(2,1)S(1)} %get-tuple-element.83), channel_id=1, source_target_pairs={{0,8},{8,0},{128,136},{136,128},{1,9},{9,1},{129,137},{137,129},{2... | collective-permute-start | bytes 245768 | tf_op jit(solution)/shard_map/ppermute | solution.py:346
  6.5 0.9 collective-permute-done.pair_ref
  7.4 1.1 %collective-permute-start.1 = (bf16[2,80,256]{2,1,0:T(8,128)(2,1)S(1)}, bf16[2,80,256]{2,1,0:T(8,128)(2,1)S(1)}, u32[]{:S(2)}, u32[]{:S(2)}) collective-permute-start(bf16[2,80,256]{2,1,0:T(8,128)(2,1)S(1)} %pad_maximum_fusion), channel_id=1, source_target_pairs={{0,128},{8,136},{128,0},{136,8},{1,129},{9,137},{129,1},{137,9},{2... | collective-permute-start | bytes 245768 | tf_op jit(solution)/shard_map/ppermute | solution.py:346
  8.5 1.0 %copy-done = bf16[4,64,1024]{2,1,0:T(8,128)(2,1)S(1)} copy-done((bf16[4,64,1024]{2,1,0:T(8,128)(2,1)S(1)}, bf16[4,64,1024]{2,1,0:T(8,128)(2,1)}, u32[]{:S(2)}) %copy-start) | copy-done | bytes 524312
  9.6 1.0 %copy-done.1 = bf16[4,64,1024]{2,1,0:T(8,128)(2,1)S(1)} copy-done((bf16[4,64,1024]{2,1,0:T(8,128)(2,1)S(1)}, bf16[4,64,1024]{2,1,0:T(8,128)(2,1)}, u32[]{:S(2)}) %copy-start.1) | copy-done | bytes 524312
  10.6 1.4 %shard_map.86 = (bf16[128,1024]{1,0:T(8,128)(2,1)S(1)}, bf16[128,1024]{1,0:T(8,128)(2,1)S(1)}, bf16[128,1024]{1,0:T(8,128)(2,1)S(1)}, bf16[128,1024]{1,0:T(8,128)(2,1)S(1)}) custom-call(s32[1]{0:T(128)} %bitcast.place_ref, bf16[4,64,1024]{2,1,0:T(8,128)(2,1)S(1)} %copy-done, bf16[4,64,1024]{2,1,0:T(8,128)(2,1)S(1)} %copy-done.1), custom_call_target="tpu_custom_call" | custom-call | tf_op jit(solution)/shard_map/pallas_call | solution.py:317
  12.0 0.7 collective-permute-done.1.across_ref
  12.7 0.1 shard_map.87
  12.8 4.9 %collective-permute-start.6 = (bf16[272,256]{1,0:T(8,128)(2,1)S(1)}, bf16[272,256]{1,0:T(8,128)(2,1)S(1)}, u32[]{:S(2)}, u32[]{:S(2)}) collective-permute-start(bf16[272,256]{1,0:T(8,128)(2,1)S(1)} %get-tuple-element.96.refs_4_), channel_id=1, source_target_pairs={{0,112},{16,0},{32,16},{48,32},{64,48},{80,64},{96,80},{112,96},{1... | collective-permute-start | bytes 417800 | tf_op jit(solution)/shard_map/ppermute | solution.py:350
  17.7 0.0 collective-permute-start.5
  17.7 0.9 collective-permute-start.2
  18.6 2.2 %collective-permute-start.3 = (bf16[128,1024]{1,0:T(8,128)(2,1)S(1)}, bf16[128,1024]{1,0:T(8,128)(2,1)S(1)}, u32[]{:S(2)}, u32[]{:S(2)}) collective-permute-start(bf16[128,1024]{1,0:T(8,128)(2,1)S(1)} %get-tuple-element.94), channel_id=1, source_target_pairs={{0,128},{8,136},{128,0},{136,8},{1,129},{9,137},{129,1},{137,9},{2... | collective-permute-start | bytes 786440 | tf_op jit(solution)/shard_map/ppermute | solution.py:346
  20.8 0.9 collective-permute-start.4
  21.8 0.0 collective-permute-done.6.refs_6_.refs_4_
  21.8 3.0 %collective-permute-start.8 = (bf16[272,256]{1,0:T(8,128)(2,1)S(1)}, bf16[272,256]{1,0:T(8,128)(2,1)S(1)}, u32[]{:S(2)}, u32[]{:S(2)}) collective-permute-start(bf16[272,256]{1,0:T(8,128)(2,1)S(1)} %collective-permute-done.6.refs_6_.refs_4_), channel_id=1, source_target_pairs={{0,112},{16,0},{32,16},{48,32},{64,48},{80,64},{96,80},{112,96},{1... | collective-permute-start | bytes 417800 | tf_op jit(solution)/shard_map/ppermute | solution.py:350
  24.7 0.0 collective-permute-done.5.refs_5_
  24.7 0.0 collective-permute-start.7
  24.7 2.8 %collective-permute-done.8.refs_8_.refs_4_ = bf16[272,256]{1,0:T(8,128)(2,1)S(1)} collective-permute-done((bf16[272,256]{1,0:T(8,128)(2,1)S(1)}, bf16[272,256]{1,0:T(8,128)(2,1)S(1)}, u32[]{:S(2)}, u32[]{:S(2)}) %collective-permute-start.8) | collective-permute-done | bytes 139296 | tf_op jit(solution)/shard_map/ppermute | solution.py:350
  27.5 3.4 %collective-permute-start.10 = (bf16[272,256]{1,0:T(8,128)(2,1)S(1)}, bf16[272,256]{1,0:T(8,128)(2,1)S(1)}, u32[]{:S(2)}, u32[]{:S(2)}) collective-permute-start(bf16[272,256]{1,0:T(8,128)(2,1)S(1)} %collective-permute-done.8.refs_8_.refs_4_), channel_id=1, source_target_pairs={{0,112},{16,0},{32,16},{48,32},{64,48},{80,64},{96,80},{112,96},{1... | collective-permute-start | bytes 417800 | tf_op jit(solution)/shard_map/ppermute | solution.py:350
  30.9 0.0 collective-permute-done.7.refs_7_.refs_5_
  30.9 0.0 collective-permute-start.9
  30.9 0.0 collective-permute-done.2.refs_1_
  30.9 0.0 collective-permute-done.3.refs_2_
  30.9 2.8 %collective-permute-done.4.refs_3_ = bf16[128,1024]{1,0:T(8,128)(2,1)S(1)} collective-permute-done((bf16[128,1024]{1,0:T(8,128)(2,1)S(1)}, bf16[128,1024]{1,0:T(8,128)(2,1)S(1)}, u32[]{:S(2)}, u32[]{:S(2)}) %collective-permute-start.4) | collective-permute-done | bytes 262176 | tf_op jit(solution)/shard_map/ppermute | solution.py:346
  33.8 4.5 %shard_map.88.refs_6_ = f32[8,8,256]{2,1,0:T(8,128)S(1)} custom-call(f32[1,256]{1,0:T(1,128)S(1)} %get-tuple-element.90.low_ref, f32[1,256]{1,0:T(1,128)S(1)} %get-tuple-element.91.high_ref, bf16[128,1024]{1,0:T(8,128)(2,1)S(1)} %get-tuple-element.92.refs_0_, bf16[128,1024]{1,0:T(8,128)(2,1)S(1)} %collective-permute-done.2.refs_1_, ...), custom_call_target="tpu_custom_call" | custom-call | flops 2684354560 | bytes 1048576 | tf_op jit(solution)/shard_map/pallas_call | solution.py:204
  38.3 0.0 collective-permute-done.10.refs_5_.refs_4_
  38.3 0.0 collective-permute-done.9.refs_4_
  38.3 0.3 collective-permute-start.11
  38.6 2.1 %shard_map.89.state_ref = f32[8,8,256]{2,1,0:T(8,128)S(1)} custom-call(f32[1,256]{1,0:T(1,128)S(1)} %get-tuple-element.90.low_ref, f32[1,256]{1,0:T(1,128)S(1)} %get-tuple-element.91.high_ref, bf16[128,1024]{1,0:T(8,128)(2,1)S(1)} %get-tuple-element.92.refs_0_, bf16[128,1024]{1,0:T(8,128)(2,1)S(1)} %collective-permute-done.2.refs_1_, ...), custom_call_target="tpu_custom_call" | custom-call | flops 1073741824 | bytes 1048576 | tf_op jit(solution)/shard_map/pallas_call | solution.py:204
  40.7 4.6 %collective-permute-done.11.refs_4_ = bf16[272,256]{1,0:T(8,128)(2,1)S(1)} collective-permute-done((bf16[272,256]{1,0:T(8,128)(2,1)S(1)}, bf16[272,256]{1,0:T(8,128)(2,1)S(1)}, u32[]{:S(2)}, u32[]{:S(2)}) %collective-permute-start.11) | collective-permute-done | bytes 139296 | tf_op jit(solution)/shard_map/ppermute | solution.py:350
  45.4 2.5 %shard_map.90 = (f32[8,128,256]{2,1,0:T(8,128)S(1)}, bf16[4,64,256]{2,1,0:T(8,128)(2,1)S(1)}, f32[8,8,256]{2,1,0:T(8,128)S(1)}) custom-call(s32[1]{0:T(128)} %bitcast.place_ref, f32[1,256]{1,0:T(1,128)S(1)} %get-tuple-element.90.low_ref, f32[1,256]{1,0:T(1,128)S(1)} %get-tuple-element.91.high_ref, f32[8,8,256]{2,1,0:T(8,128)S(1)} %shard_map.89.state_ref, ...), custom_call_target="tpu_custom_call" | custom-call | flops 1073741824 | bytes 2097152 | tf_op jit(solution)/shard_map/pallas_call | solution.py:230
  47.9 0.1 collective-permute-start.12
  48.0 1.8 %shard_map.91 = (f32[8,128,256]{2,1,0:T(8,128)S(1)}, bf16[4,64,256]{2,1,0:T(8,128)(2,1)S(1)}) custom-call(s32[1]{0:T(128)} %bitcast.place_ref, f32[1,256]{1,0:T(1,128)S(1)} %get-tuple-element.90.low_ref, f32[1,256]{1,0:T(1,128)S(1)} %get-tuple-element.91.high_ref, f32[8,8,256]{2,1,0:T(8,128)S(1)} %get-tuple-element.105.state_ref, ...), custom_call_target="tpu_custom_call" | custom-call | flops 1073741824 | bytes 2097152 | tf_op jit(solution)/shard_map/pallas_call | solution.py:230
  49.8 2.7 %collective-permute-start.14 = (bf16[4,64,256]{2,1,0:T(8,128)(2,1)S(1)}, bf16[4,64,256]{2,1,0:T(8,128)(2,1)S(1)}, u32[]{:S(2)}, u32[]{:S(2)}) collective-permute-start(bf16[4,64,256]{2,1,0:T(8,128)(2,1)S(1)} %get-tuple-element.123), channel_id=1, source_target_pairs={{0,112},{16,0},{32,16},{48,32},{64,48},{80,64},{96,80},{112,96},{1... | collective-permute-start | bytes 393224 | tf_op jit(solution)/shard_map/ppermute | solution.py:350
  52.5 1.8 %shard_map.92 = (f32[8,128,256]{2,1,0:T(8,128)S(1)}, bf16[4,64,256]{2,1,0:T(8,128)(2,1)S(1)}) custom-call(s32[1]{0:T(128)} %bitcast.place_ref, f32[1,256]{1,0:T(1,128)S(1)} %get-tuple-element.90.low_ref, f32[1,256]{1,0:T(1,128)S(1)} %get-tuple-element.91.high_ref, f32[8,8,256]{2,1,0:T(8,128)S(1)} %get-tuple-element.105.state_ref, ...), custom_call_target="tpu_custom_call" | custom-call | flops 1073741824 | bytes 2097152 | tf_op jit(solution)/shard_map/pallas_call | solution.py:230
  54.3 0.0 collective-permute-done.12
  54.4 0.1 collective-permute-start.13
  54.5 3.1 %shard_map.93 = (f32[8,128,256]{2,1,0:T(8,128)S(1)}, bf16[4,64,256]{2,1,0:T(8,128)(2,1)S(1)}, bf16[4,64,256]{2,1,0:T(8,128)(2,1)S(1)}) custom-call(s32[1]{0:T(128)} %bitcast.place_ref, f32[1,256]{1,0:T(1,128)S(1)} %get-tuple-element.90.low_ref, f32[1,256]{1,0:T(1,128)S(1)} %get-tuple-element.91.high_ref, f32[8,8,256]{2,1,0:T(8,128)S(1)} %get-tuple-element.105.state_ref, ...), custom_call_target="tpu_custom_call" | custom-call | flops 2147483648 | bytes 2097152 | tf_op jit(solution)/shard_map/pallas_call | solution.py:230
  57.6 0.0 collective-permute-done.14
  57.6 1.9 %collective-permute-done.13 = bf16[4,64,256]{2,1,0:T(8,128)(2,1)S(1)} collective-permute-done((bf16[4,64,256]{2,1,0:T(8,128)(2,1)S(1)}, bf16[4,64,256]{2,1,0:T(8,128)(2,1)S(1)}, u32[]{:S(2)}, u32[]{:S(2)}) %collective-permute-start.13) | collective-permute-done | bytes 131104 | tf_op jit(solution)/shard_map/ppermute | solution.py:350
  59.5 0.1 add_convert_fusion.3
  59.5 0.1 collective-permute-start.15
  59.6 2.7 %collective-permute-start.16 = (bf16[4,64,256]{2,1,0:T(8,128)(2,1)S(1)}, bf16[4,64,256]{2,1,0:T(8,128)(2,1)S(1)}, u32[]{:S(2)}, u32[]{:S(2)}) collective-permute-start(bf16[4,64,256]{2,1,0:T(8,128)(2,1)S(1)} %get-tuple-element.135), channel_id=1, source_target_pairs={{0,112},{16,0},{32,16},{48,32},{64,48},{80,64},{96,80},{112,96},{1... | collective-permute-start | bytes 393224 | tf_op jit(solution)/shard_map/ppermute | solution.py:350
  62.3 3.1 %shard_map.94 = (f32[8,128,256]{2,1,0:T(8,128)S(1)}, bf16[4,64,256]{2,1,0:T(8,128)(2,1)S(1)}, bf16[4,64,256]{2,1,0:T(8,128)(2,1)S(1)}) custom-call(s32[1]{0:T(128)} %bitcast.place_ref, f32[1,256]{1,0:T(1,128)S(1)} %get-tuple-element.90.low_ref, f32[1,256]{1,0:T(1,128)S(1)} %get-tuple-element.91.high_ref, f32[8,8,256]{2,1,0:T(8,128)S(1)} %get-tuple-element.105.state_ref, ...), custom_call_target="tpu_custom_call" | custom-call | flops 2147483648 | bytes 2097152 | tf_op jit(solution)/shard_map/pallas_call | solution.py:230
  65.4 0.0 collective-permute-done.15
  65.4 0.0 collective-permute-done.16
  65.5 0.1 collective-permute-start.17
  65.6 2.7 %collective-permute-start.18 = (bf16[4,64,256]{2,1,0:T(8,128)(2,1)S(1)}, bf16[4,64,256]{2,1,0:T(8,128)(2,1)S(1)}, u32[]{:S(2)}, u32[]{:S(2)}) collective-permute-start(bf16[4,64,256]{2,1,0:T(8,128)(2,1)S(1)} %add_convert_fusion.1), channel_id=1, source_target_pairs={{0,112},{16,0},{32,16},{48,32},{64,48},{80,64},{96,80},{112,96},{1... | collective-permute-start | bytes 393224 | tf_op jit(solution)/shard_map/ppermute | solution.py:350
  68.3 2.0 %shard_map.95 = (bf16[4,64,1280]{2,1,0:T(8,128)(2,1)S(1)}, bf16[4,64,256]{2,1,0:T(8,128)(2,1)S(1)}) custom-call(s32[1]{0:T(128)} %bitcast.place_ref, f32[1,256]{1,0:T(1,128)S(1)} %get-tuple-element.90.low_ref, f32[1,256]{1,0:T(1,128)S(1)} %get-tuple-element.91.high_ref, f32[8,8,256]{2,1,0:T(8,128)S(1)} %get-tuple-element.105.state_ref, ...), custom_call_target="tpu_custom_call" | custom-call | flops 1073741824 | bytes 2097152 | tf_op jit(solution)/shard_map/pallas_call | solution.py:230
  70.3 0.4 collective-permute-done.17
  70.6 0.0 collective-permute-done.18
  70.6 0.1 add_convert_fusion
  70.8 23.1 %all_to_all.5 = bf16[32,8,1280]{2,1,0:T(8,128)(2,1)S(1)} all-to-all(bf16[32,8,1280]{2,1,0:T(8,128)(2,1)S(1)} %bitcast.20), channel_id=1, replica_groups=mesh['xh'=2,'z'=8,'core'=2,'y'=4,'xl'=2] {'xh','core','y','xl'}, dimensions={0} | all-to-all | bytes 1310720 | tf_op jit(solution)/shard_map/all_to_all | solution.py:421
  93.9 0.7 fusion
  94.6 0.9 slice.39
  (12 shorter events, 0.2 us)
Async XLA Ops:
  0.6 0.7 copy-start.5
  0.6 0.7 copy-start.4
  1.3 0.8 copy-start.2
  2.2 0.8 copy-start.3
  3.2 4.3 %collective-permute-start = (bf16[2,80,256]{2,1,0:T(8,128)(2,1)S(1)}, bf16[2,80,256]{2,1,0:T(8,128)(2,1)S(1)}, u32[]{:S(2)}, u32[]{:S(2)}) collective-permute-start(bf16[2,80,256]{2,1,0:T(8,128)(2,1)S(1)} %get-tuple-element.83), channel_id=1, source_target_pairs={{0,8},{8,0},{128,136},{136,128},{1,9},{9,1},{129,137},{137,129},{2... | collective-permute-start | bytes 245768 | tf_op jit(solution)/shard_map/ppermute | solution.py:346
  7.4 5.3 %collective-permute-start.1 = (bf16[2,80,256]{2,1,0:T(8,128)(2,1)S(1)}, bf16[2,80,256]{2,1,0:T(8,128)(2,1)S(1)}, u32[]{:S(2)}, u32[]{:S(2)}) collective-permute-start(bf16[2,80,256]{2,1,0:T(8,128)(2,1)S(1)} %pad_maximum_fusion), channel_id=1, source_target_pairs={{0,128},{8,136},{128,0},{136,8},{1,129},{9,137},{129,1},{137,9},{2... | collective-permute-start | bytes 245768 | tf_op jit(solution)/shard_map/ppermute | solution.py:346
  8.5 1.0 %copy-start = (bf16[4,64,1024]{2,1,0:T(8,128)(2,1)S(1)}, bf16[4,64,1024]{2,1,0:T(8,128)(2,1)}, u32[]{:S(2)}) copy-start(bf16[4,64,1024]{2,1,0:T(8,128)(2,1)} %q_ref.1) | copy-start | bytes 1572868
  9.6 1.0 %copy-start.1 = (bf16[4,64,1024]{2,1,0:T(8,128)(2,1)S(1)}, bf16[4,64,1024]{2,1,0:T(8,128)(2,1)}, u32[]{:S(2)}) copy-start(bf16[4,64,1024]{2,1,0:T(8,128)(2,1)} %do_ref.1) | copy-start | bytes 1572868
  12.8 9.0 %collective-permute-start.6 = (bf16[272,256]{1,0:T(8,128)(2,1)S(1)}, bf16[272,256]{1,0:T(8,128)(2,1)S(1)}, u32[]{:S(2)}, u32[]{:S(2)}) collective-permute-start(bf16[272,256]{1,0:T(8,128)(2,1)S(1)} %get-tuple-element.96.refs_4_), channel_id=1, source_target_pairs={{0,112},{16,0},{32,16},{48,32},{64,48},{80,64},{96,80},{112,96},{1... | collective-permute-start | bytes 417800 | tf_op jit(solution)/shard_map/ppermute | solution.py:350
  17.7 7.0 %collective-permute-start.5 = (bf16[272,256]{1,0:T(8,128)(2,1)S(1)}, bf16[272,256]{1,0:T(8,128)(2,1)S(1)}, u32[]{:S(2)}, u32[]{:S(2)}) collective-permute-start(bf16[272,256]{1,0:T(8,128)(2,1)S(1)} %get-tuple-element.96.refs_4_), channel_id=1, source_target_pairs={{0,16},{16,32},{32,48},{48,64},{64,80},{80,96},{96,112},{112,0},{1... | collective-permute-start | bytes 417800 | tf_op jit(solution)/shard_map/ppermute | solution.py:350
  17.7 13.2 %collective-permute-start.2 = (bf16[128,1024]{1,0:T(8,128)(2,1)S(1)}, bf16[128,1024]{1,0:T(8,128)(2,1)S(1)}, u32[]{:S(2)}, u32[]{:S(2)}) collective-permute-start(bf16[128,1024]{1,0:T(8,128)(2,1)S(1)} %get-tuple-element.93), channel_id=1, source_target_pairs={{0,8},{8,0},{128,136},{136,128},{1,9},{9,1},{129,137},{137,129},{2... | collective-permute-start | bytes 786440 | tf_op jit(solution)/shard_map/ppermute | solution.py:346
  18.6 12.3 %collective-permute-start.3 = (bf16[128,1024]{1,0:T(8,128)(2,1)S(1)}, bf16[128,1024]{1,0:T(8,128)(2,1)S(1)}, u32[]{:S(2)}, u32[]{:S(2)}) collective-permute-start(bf16[128,1024]{1,0:T(8,128)(2,1)S(1)} %get-tuple-element.94), channel_id=1, source_target_pairs={{0,128},{8,136},{128,0},{136,8},{1,129},{9,137},{129,1},{137,9},{2... | collective-permute-start | bytes 786440 | tf_op jit(solution)/shard_map/ppermute | solution.py:346
  20.8 12.9 %collective-permute-start.4 = (bf16[128,1024]{1,0:T(8,128)(2,1)S(1)}, bf16[128,1024]{1,0:T(8,128)(2,1)S(1)}, u32[]{:S(2)}, u32[]{:S(2)}) collective-permute-start(bf16[128,1024]{1,0:T(8,128)(2,1)S(1)} %get-tuple-element.95), channel_id=1, source_target_pairs={{0,136},{8,128},{128,8},{136,0},{1,137},{9,129},{129,9},{137,1},{2... | collective-permute-start | bytes 786440 | tf_op jit(solution)/shard_map/ppermute | solution.py:346
  21.8 5.7 %collective-permute-start.8 = (bf16[272,256]{1,0:T(8,128)(2,1)S(1)}, bf16[272,256]{1,0:T(8,128)(2,1)S(1)}, u32[]{:S(2)}, u32[]{:S(2)}) collective-permute-start(bf16[272,256]{1,0:T(8,128)(2,1)S(1)} %collective-permute-done.6.refs_6_.refs_4_), channel_id=1, source_target_pairs={{0,112},{16,0},{32,16},{48,32},{64,48},{80,64},{96,80},{112,96},{1... | collective-permute-start | bytes 417800 | tf_op jit(solution)/shard_map/ppermute | solution.py:350
  24.7 6.2 %collective-permute-start.7 = (bf16[272,256]{1,0:T(8,128)(2,1)S(1)}, bf16[272,256]{1,0:T(8,128)(2,1)S(1)}, u32[]{:S(2)}, u32[]{:S(2)}) collective-permute-start(bf16[272,256]{1,0:T(8,128)(2,1)S(1)} %collective-permute-done.5.refs_5_), channel_id=1, source_target_pairs={{0,16},{16,32},{32,48},{48,64},{64,80},{80,96},{96,112},{112,0},{1... | collective-permute-start | bytes 417800 | tf_op jit(solution)/shard_map/ppermute | solution.py:350
  27.5 10.8 %collective-permute-start.10 = (bf16[272,256]{1,0:T(8,128)(2,1)S(1)}, bf16[272,256]{1,0:T(8,128)(2,1)S(1)}, u32[]{:S(2)}, u32[]{:S(2)}) collective-permute-start(bf16[272,256]{1,0:T(8,128)(2,1)S(1)} %collective-permute-done.8.refs_8_.refs_4_), channel_id=1, source_target_pairs={{0,112},{16,0},{32,16},{48,32},{64,48},{80,64},{96,80},{112,96},{1... | collective-permute-start | bytes 417800 | tf_op jit(solution)/shard_map/ppermute | solution.py:350
  30.9 7.4 %collective-permute-start.9 = (bf16[272,256]{1,0:T(8,128)(2,1)S(1)}, bf16[272,256]{1,0:T(8,128)(2,1)S(1)}, u32[]{:S(2)}, u32[]{:S(2)}) collective-permute-start(bf16[272,256]{1,0:T(8,128)(2,1)S(1)} %collective-permute-done.7.refs_7_.refs_5_), channel_id=1, source_target_pairs={{0,16},{16,32},{32,48},{48,64},{64,80},{80,96},{96,112},{112,0},{1... | collective-permute-start | bytes 417800 | tf_op jit(solution)/shard_map/ppermute | solution.py:350
  38.3 7.0 %collective-permute-start.11 = (bf16[272,256]{1,0:T(8,128)(2,1)S(1)}, bf16[272,256]{1,0:T(8,128)(2,1)S(1)}, u32[]{:S(2)}, u32[]{:S(2)}) collective-permute-start(bf16[272,256]{1,0:T(8,128)(2,1)S(1)} %collective-permute-done.9.refs_4_), channel_id=1, source_target_pairs={{0,16},{16,32},{32,48},{48,64},{64,80},{80,96},{96,112},{112,0},{1... | collective-permute-start | bytes 417800 | tf_op jit(solution)/shard_map/ppermute | solution.py:350
  47.9 6.4 %collective-permute-start.12 = (bf16[4,64,256]{2,1,0:T(8,128)(2,1)S(1)}, bf16[4,64,256]{2,1,0:T(8,128)(2,1)S(1)}, u32[]{:S(2)}, u32[]{:S(2)}) collective-permute-start(bf16[4,64,256]{2,1,0:T(8,128)(2,1)S(1)} %get-tuple-element.113), channel_id=1, source_target_pairs={{0,16},{16,32},{32,48},{48,64},{64,80},{80,96},{96,112},{112,0},{1... | collective-permute-start | bytes 393224 | tf_op jit(solution)/shard_map/ppermute | solution.py:350
  49.8 7.8 %collective-permute-start.14 = (bf16[4,64,256]{2,1,0:T(8,128)(2,1)S(1)}, bf16[4,64,256]{2,1,0:T(8,128)(2,1)S(1)}, u32[]{:S(2)}, u32[]{:S(2)}) collective-permute-start(bf16[4,64,256]{2,1,0:T(8,128)(2,1)S(1)} %get-tuple-element.123), channel_id=1, source_target_pairs={{0,112},{16,0},{32,16},{48,32},{64,48},{80,64},{96,80},{112,96},{1... | collective-permute-start | bytes 393224 | tf_op jit(solution)/shard_map/ppermute | solution.py:350
  54.4 5.1 %collective-permute-start.13 = (bf16[4,64,256]{2,1,0:T(8,128)(2,1)S(1)}, bf16[4,64,256]{2,1,0:T(8,128)(2,1)S(1)}, u32[]{:S(2)}, u32[]{:S(2)}) collective-permute-start(bf16[4,64,256]{2,1,0:T(8,128)(2,1)S(1)} %add_convert_fusion.5), channel_id=1, source_target_pairs={{0,16},{16,32},{32,48},{48,64},{64,80},{80,96},{96,112},{112,0},{1... | collective-permute-start | bytes 393224 | tf_op jit(solution)/shard_map/ppermute | solution.py:350
  59.5 5.9 %collective-permute-start.15 = (bf16[4,64,256]{2,1,0:T(8,128)(2,1)S(1)}, bf16[4,64,256]{2,1,0:T(8,128)(2,1)S(1)}, u32[]{:S(2)}, u32[]{:S(2)}) collective-permute-start(bf16[4,64,256]{2,1,0:T(8,128)(2,1)S(1)} %get-tuple-element.134), channel_id=1, source_target_pairs={{0,16},{16,32},{32,48},{48,64},{64,80},{80,96},{96,112},{112,0},{1... | collective-permute-start | bytes 393224 | tf_op jit(solution)/shard_map/ppermute | solution.py:350
  59.6 5.8 %collective-permute-start.16 = (bf16[4,64,256]{2,1,0:T(8,128)(2,1)S(1)}, bf16[4,64,256]{2,1,0:T(8,128)(2,1)S(1)}, u32[]{:S(2)}, u32[]{:S(2)}) collective-permute-start(bf16[4,64,256]{2,1,0:T(8,128)(2,1)S(1)} %get-tuple-element.135), channel_id=1, source_target_pairs={{0,112},{16,0},{32,16},{48,32},{64,48},{80,64},{96,80},{112,96},{1... | collective-permute-start | bytes 393224 | tf_op jit(solution)/shard_map/ppermute | solution.py:350
  65.5 5.1 %collective-permute-start.17 = (bf16[4,64,256]{2,1,0:T(8,128)(2,1)S(1)}, bf16[4,64,256]{2,1,0:T(8,128)(2,1)S(1)}, u32[]{:S(2)}, u32[]{:S(2)}) collective-permute-start(bf16[4,64,256]{2,1,0:T(8,128)(2,1)S(1)} %add_convert_fusion.2), channel_id=1, source_target_pairs={{0,16},{16,32},{32,48},{48,64},{64,80},{80,96},{96,112},{112,0},{1... | collective-permute-start | bytes 393224 | tf_op jit(solution)/shard_map/ppermute | solution.py:350
  65.6 5.0 %collective-permute-start.18 = (bf16[4,64,256]{2,1,0:T(8,128)(2,1)S(1)}, bf16[4,64,256]{2,1,0:T(8,128)(2,1)S(1)}, u32[]{:S(2)}, u32[]{:S(2)}) collective-permute-start(bf16[4,64,256]{2,1,0:T(8,128)(2,1)S(1)} %add_convert_fusion.1), channel_id=1, source_target_pairs={{0,112},{16,0},{32,16},{48,32},{64,48},{80,64},{96,80},{112,96},{1... | collective-permute-start | bytes 393224 | tf_op jit(solution)/shard_map/ppermute | solution.py:350

commit v10 on v8

--- a/solution.py
+++ b/solution.py
@@ -377,31 +377,30 @@
         above.append(turned(above[-1], -1))
     below.append(turned(below[2], 1))
     above.append(turned(above[2], -1))
+    opposite = turned(own, RING // 2)
     state = stats(low, high, row_arrays, [own, below[1], above[1], below[2], above[2]], None)
     state, below[3], above[3] = tied((state, below[3], above[3]))
-    opposite = turned(below[3], 1)
     state = stats(low, high, row_arrays, [below[3], above[3]], state)
     state, opposite = tied((state, opposite))
 
     def gradients(pieces, before, last=False):
         return grads(spot, low, high, state, row_arrays, pieces, before, last)
 
-    dq, to_up, state = gradients([opposite], None)
-    spot, dq, to_up = tied((spot, dq, to_up))
-    up = turned(to_up, 1)
-    dq, up_grad, down_grad = gradients([above[3], below[3]], dq)
-    dq, up_grad, down_grad, up = tied((dq, up_grad, down_grad, up))
-    to_up, to_down = plus(up_grad, up), down_grad
+    dq, far_grad, state = gradients([opposite], None)
+    crossing = turned(far_grad, RING // 2)
+    dq, to_up, to_down = gradients([above[3], below[3]], dq)
     for k in (2, 1, 0):
         spot, dq, to_up, to_down = tied((spot, dq, to_up, to_down))
         up, down = turned(to_up, 1), turned(to_down, -1)
         if k:
             dq, up_grad, down_grad = gradients([above[k], below[k]], dq)
+            if k == 1:
+                crossing, dq = tied((crossing, dq))
             dq, up_grad, down_grad, up, down = tied((dq, up_grad, down_grad, up, down))
             to_up, to_down = plus(up_grad, up), plus(down_grad, down)
     dq, own_grad = gradients([own], dq, True)
     dq, own_grad, up, down = tied((dq, own_grad, up, down))
-    dkv_own = plus(own_grad, up, down)
+    dkv_own = plus(own_grad, up, down, crossing)
 
     flip = dkv_own.reshape((2, 2) + dkv_own.shape[1:])
     flip = jnp.where(across == 1, flip[::-1], flip)

time: 95.6 us -> 97.1 us (1.016)
  waiting for transfers between devices: 14.6 us -> 8.65 us
  starting transfers between devices: 28.4 us -> 33.4 us
  blocking collectives: 23.1 us -> 25.6 us
    ppermute x14, starting transfers between devices: 19.9 us -> 24.9 us  [turned(): return lax.ppermute(array, 'z', [(i, (i + by) % RING) for i in range(RING)])]
    ppermute x14, waiting for transfers between devices: 10.1 us -> 7.04 us  [turned(): return lax.ppermute(array, 'z', [(i, (i + by) % RING) for i in range(RING)])]
    ppermute x5, waiting for transfers between devices: 4.45 us -> 1.61 us  [swapped(): return lax.ppermute(array, axes, [(i, i ^ by) for i in range(count)])]
    all_to_all x1, blocking collectives: 23.1 us -> 25.6 us  [on_device(): final = lax.all_to_all(leaving, FINAL, 0, 0, tiled=True)]
  transfers between devices with their start and end apart: 19 -> 19, of which waited for: 7 -> 8; matrix products, arithmetic and copies ran while one was open for 0% -> 0% of each run, Pallas kernels for 20% -> 17%
where the time goes in v10:
time: 97.1 us; the launch traced here: 96.8 us
  starting transfers between devices  33.4 us (34%)
  blocking collectives  25.6 us (26%)
  Pallas kernels  22.1 us (23%)
  waiting for transfers between devices  8.65 us (9%)
  local copies, waits for them, and re-layouts  5.98 us (6%)
    all_to_all x1, blocking collectives, on_device(): final = lax.all_to_all(leaving, FINAL, 0, 0, tiled=True)  25.6 us
    ppermute x14, starting transfers between devices, turned(): return lax.ppermute(array, 'z', [(i, (i + by) % RING) for i in range(RING)])  24.9 us
    pallas_call x5, Pallas kernels, grads(): pl.pallas_call(functools.partial(grads_kernel, first, last, len(pieces)),...  13.8 us
    ppermute x5, starting transfers between devices, swapped(): return lax.ppermute(array, axes, [(i, i ^ by) for i in range(count)])  8.48 us
    ppermute x14, waiting for transfers between devices, turned(): return lax.ppermute(array, 'z', [(i, (i + by) % RING) for i in range(RING)])  7.04 us
    pallas_call x2, Pallas kernels, stats(): pl.pallas_call(functools.partial(stats_kernel, first, len(pieces)), out_s...  6.65 us
    unnamed x12, local copies, waits for them, and re-layouts  4.44 us
  transfers between devices with their start and end apart: 19, of which 8 were waited for; matrix products, arithmetic and copies ran while one was open for 0% of the time, Pallas kernels for 17%

profile of v10, /device:TPU:1, one launch (start us, length us, event | category | flops | bytes accessed | tf_op | source)
XLA Modules:
  0.0 96.8 jit_solution(5456123626183797023)
XLA Ops:
  0.6 0.0 copy-start.5
  0.6 0.0 copy-start.4
  0.7 0.7 copy-done.5
  1.3 0.0 copy-done.4
  1.3 0.0 copy-start.2
  1.4 0.8 copy-done.2
  2.2 0.0 copy-start.3
  2.2 0.8 copy-done.3
  3.0 0.1 shard_map.85
  3.2 3.3 %collective-permute-start = (bf16[2,80,256]{2,1,0:T(8,128)(2,1)S(1)}, bf16[2,80,256]{2,1,0:T(8,128)(2,1)S(1)}, u32[]{:S(2)}, u32[]{:S(2)}) collective-permute-start(bf16[2,80,256]{2,1,0:T(8,128)(2,1)S(1)} %get-tuple-element.76), channel_id=1, source_target_pairs={{0,8},{8,0},{128,136},{136,128},{1,9},{9,1},{129,137},{137,129},{2... | collective-permute-start | bytes 245768 | tf_op jit(solution)/shard_map/ppermute | solution.py:346
  6.5 0.9 collective-permute-done.pair_ref
  7.4 1.1 %collective-permute-start.1 = (bf16[2,80,256]{2,1,0:T(8,128)(2,1)S(1)}, bf16[2,80,256]{2,1,0:T(8,128)(2,1)S(1)}, u32[]{:S(2)}, u32[]{:S(2)}) collective-permute-start(bf16[2,80,256]{2,1,0:T(8,128)(2,1)S(1)} %pad_maximum_fusion), channel_id=1, source_target_pairs={{0,128},{8,136},{128,0},{136,8},{1,129},{9,137},{129,1},{137,9},{2... | collective-permute-start | bytes 245768 | tf_op jit(solution)/shard_map/ppermute | solution.py:346
  8.5 0.0 copy-start
  8.5 1.0 %copy-done = bf16[4,64,1024]{2,1,0:T(8,128)(2,1)S(1)} copy-done((bf16[4,64,1024]{2,1,0:T(8,128)(2,1)S(1)}, bf16[4,64,1024]{2,1,0:T(8,128)(2,1)}, u32[]{:S(2)}) %copy-start) | copy-done | bytes 524312
  9.6 1.0 %copy-done.1 = bf16[4,64,1024]{2,1,0:T(8,128)(2,1)S(1)} copy-done((bf16[4,64,1024]{2,1,0:T(8,128)(2,1)S(1)}, bf16[4,64,1024]{2,1,0:T(8,128)(2,1)}, u32[]{:S(2)}) %copy-start.1) | copy-done | bytes 524312
  10.6 1.4 %shard_map.86 = (bf16[128,1024]{1,0:T(8,128)(2,1)S(1)}, bf16[128,1024]{1,0:T(8,128)(2,1)S(1)}, bf16[128,1024]{1,0:T(8,128)(2,1)S(1)}, bf16[128,1024]{1,0:T(8,128)(2,1)S(1)}) custom-call(s32[1]{0:T(128)} %bitcast.place_ref, bf16[4,64,1024]{2,1,0:T(8,128)(2,1)S(1)} %copy-done, bf16[4,64,1024]{2,1,0:T(8,128)(2,1)S(1)} %copy-done.1), custom_call_target="tpu_custom_call" | custom-call | tf_op jit(solution)/shard_map/pallas_call | solution.py:317
  12.0 0.7 collective-permute-done.1.across_ref
  12.7 0.1 shard_map.87
  12.8 4.9 %collective-permute-start.6 = (bf16[272,256]{1,0:T(8,128)(2,1)S(1)}, bf16[272,256]{1,0:T(8,128)(2,1)S(1)}, u32[]{:S(2)}, u32[]{:S(2)}) collective-permute-start(bf16[272,256]{1,0:T(8,128)(2,1)S(1)} %get-tuple-element.89.refs_4_), channel_id=1, source_target_pairs={{0,112},{16,0},{32,16},{48,32},{64,48},{80,64},{96,80},{112,96},{1... | collective-permute-start | bytes 417800 | tf_op jit(solution)/shard_map/ppermute | solution.py:350
  17.7 0.0 collective-permute-start.5
  17.7 0.9 collective-permute-start.2
  18.6 2.2 %collective-permute-start.3 = (bf16[128,1024]{1,0:T(8,128)(2,1)S(1)}, bf16[128,1024]{1,0:T(8,128)(2,1)S(1)}, u32[]{:S(2)}, u32[]{:S(2)}) collective-permute-start(bf16[128,1024]{1,0:T(8,128)(2,1)S(1)} %get-tuple-element.87), channel_id=1, source_target_pairs={{0,128},{8,136},{128,0},{136,8},{1,129},{9,137},{129,1},{137,9},{2... | collective-permute-start | bytes 786440 | tf_op jit(solution)/shard_map/ppermute | solution.py:346
  20.8 0.9 collective-permute-start.4
  21.8 0.0 collective-permute-done.6.refs_6_.refs_4_
  21.8 3.0 %collective-permute-start.8 = (bf16[272,256]{1,0:T(8,128)(2,1)S(1)}, bf16[272,256]{1,0:T(8,128)(2,1)S(1)}, u32[]{:S(2)}, u32[]{:S(2)}) collective-permute-start(bf16[272,256]{1,0:T(8,128)(2,1)S(1)} %collective-permute-done.6.refs_6_.refs_4_), channel_id=1, source_target_pairs={{0,112},{16,0},{32,16},{48,32},{64,48},{80,64},{96,80},{112,96},{1... | collective-permute-start | bytes 417800 | tf_op jit(solution)/shard_map/ppermute | solution.py:350
  24.7 0.0 collective-permute-done.5.refs_5_
  24.7 0.0 collective-permute-start.7
  24.7 0.0 collective-permute-done.2.refs_1_
  24.7 1.6 %collective-permute-start.11 = (bf16[272,256]{1,0:T(8,128)(2,1)S(1)}, bf16[272,256]{1,0:T(8,128)(2,1)S(1)}, u32[]{:S(2)}, u32[]{:S(2)}) collective-permute-start(bf16[272,256]{1,0:T(8,128)(2,1)S(1)} %get-tuple-element.89.refs_4_), channel_id=1, source_target_pairs={{0,64},{16,80},{32,96},{48,112},{64,0},{80,16},{96,32},{112,48},{1... | collective-permute-start | bytes 417800 | tf_op jit(solution)/shard_map/ppermute | solution.py:350
  26.3 1.2 %collective-permute-done.8.refs_8_.refs_4_ = bf16[272,256]{1,0:T(8,128)(2,1)S(1)} collective-permute-done((bf16[272,256]{1,0:T(8,128)(2,1)S(1)}, bf16[272,256]{1,0:T(8,128)(2,1)S(1)}, u32[]{:S(2)}, u32[]{:S(2)}) %collective-permute-start.8) | collective-permute-done | bytes 139296 | tf_op jit(solution)/shard_map/ppermute | solution.py:350
  27.5 5.4 %collective-permute-start.10 = (bf16[272,256]{1,0:T(8,128)(2,1)S(1)}, bf16[272,256]{1,0:T(8,128)(2,1)S(1)}, u32[]{:S(2)}, u32[]{:S(2)}) collective-permute-start(bf16[272,256]{1,0:T(8,128)(2,1)S(1)} %collective-permute-done.8.refs_8_.refs_4_), channel_id=1, source_target_pairs={{0,112},{16,0},{32,16},{48,32},{64,48},{80,64},{96,80},{112,96},{1... | collective-permute-start | bytes 417800 | tf_op jit(solution)/shard_map/ppermute | solution.py:350
  32.9 2.4 %collective-permute-done.7.refs_7_.refs_5_ = bf16[272,256]{1,0:T(8,128)(2,1)S(1)} collective-permute-done((bf16[272,256]{1,0:T(8,128)(2,1)S(1)}, bf16[272,256]{1,0:T(8,128)(2,1)S(1)}, u32[]{:S(2)}, u32[]{:S(2)}) %collective-permute-start.7) | collective-permute-done | bytes 139296 | tf_op jit(solution)/shard_map/ppermute | solution.py:350
  35.3 0.0 collective-permute-start.9
  35.3 0.0 collective-permute-done.3.refs_2_
  35.3 0.0 collective-permute-done.4.refs_3_
  35.3 4.5 %shard_map.88.refs_6_ = f32[8,8,256]{2,1,0:T(8,128)S(1)} custom-call(f32[1,256]{1,0:T(1,128)S(1)} %get-tuple-element.83.low_ref, f32[1,256]{1,0:T(1,128)S(1)} %get-tuple-element.84.high_ref, bf16[128,1024]{1,0:T(8,128)(2,1)S(1)} %get-tuple-element.85.refs_0_, bf16[128,1024]{1,0:T(8,128)(2,1)S(1)} %collective-permute-done.2.refs_1_, ...), custom_call_target="tpu_custom_call" | custom-call | flops 2684354560 | bytes 1048576 | tf_op jit(solution)/shard_map/pallas_call | solution.py:204
  39.9 0.0 collective-permute-done.10.refs_5_.refs_4_
  39.9 0.6 collective-permute-done.9.refs_4_.refs_5_
  40.4 2.1 %shard_map.89.state_ref = f32[8,8,256]{2,1,0:T(8,128)S(1)} custom-call(f32[1,256]{1,0:T(1,128)S(1)} %get-tuple-element.83.low_ref, f32[1,256]{1,0:T(1,128)S(1)} %get-tuple-element.84.high_ref, bf16[128,1024]{1,0:T(8,128)(2,1)S(1)} %get-tuple-element.85.refs_0_, bf16[128,1024]{1,0:T(8,128)(2,1)S(1)} %collective-permute-done.2.refs_1_, ...), custom_call_target="tpu_custom_call" | custom-call | flops 1073741824 | bytes 1048576 | tf_op jit(solution)/shard_map/pallas_call | solution.py:204
  42.6 0.0 collective-permute-done.11.refs_4_
  42.6 2.5 %shard_map.90 = (f32[8,128,256]{2,1,0:T(8,128)S(1)}, bf16[4,64,256]{2,1,0:T(8,128)(2,1)S(1)}, f32[8,8,256]{2,1,0:T(8,128)S(1)}) custom-call(s32[1]{0:T(128)} %bitcast.place_ref, f32[1,256]{1,0:T(1,128)S(1)} %get-tuple-element.83.low_ref, f32[1,256]{1,0:T(1,128)S(1)} %get-tuple-element.84.high_ref, f32[8,8,256]{2,1,0:T(8,128)S(1)} %shard_map.89.state_ref, ...), custom_call_target="tpu_custom_call" | custom-call | flops 1073741824 | bytes 2097152 | tf_op jit(solution)/shard_map/pallas_call | solution.py:230
  45.1 3.1 %shard_map.91 = (f32[8,128,256]{2,1,0:T(8,128)S(1)}, bf16[4,64,256]{2,1,0:T(8,128)(2,1)S(1)}, bf16[4,64,256]{2,1,0:T(8,128)(2,1)S(1)}) custom-call(s32[1]{0:T(128)} %bitcast.place_ref, f32[1,256]{1,0:T(1,128)S(1)} %get-tuple-element.83.low_ref, f32[1,256]{1,0:T(1,128)S(1)} %get-tuple-element.84.high_ref, f32[8,8,256]{2,1,0:T(8,128)S(1)} %get-tuple-element.95.state_ref, ...), custom_call_target="tpu_custom_call" | custom-call | flops 2147483648 | bytes 2097152 | tf_op jit(solution)/shard_map/pallas_call | solution.py:230
  48.3 0.1 collective-permute-start.12
  48.4 2.7 %collective-permute-start.13 = (bf16[4,64,256]{2,1,0:T(8,128)(2,1)S(1)}, bf16[4,64,256]{2,1,0:T(8,128)(2,1)S(1)}, u32[]{:S(2)}, u32[]{:S(2)}) collective-permute-start(bf16[4,64,256]{2,1,0:T(8,128)(2,1)S(1)} %get-tuple-element.106), channel_id=1, source_target_pairs={{0,112},{16,0},{32,16},{48,32},{64,48},{80,64},{96,80},{112,96},{1... | collective-permute-start | bytes 393224 | tf_op jit(solution)/shard_map/ppermute | solution.py:350
  51.0 1.2 %collective-permute-start.14 = (bf16[4,64,256]{2,1,0:T(8,128)(2,1)S(1)}, bf16[4,64,256]{2,1,0:T(8,128)(2,1)S(1)}, u32[]{:S(2)}, u32[]{:S(2)}) collective-permute-start(bf16[4,64,256]{2,1,0:T(8,128)(2,1)S(1)} %get-tuple-element.113), channel_id=1, source_target_pairs={{0,64},{16,80},{32,96},{48,112},{64,0},{80,16},{96,32},{112,48},{1... | collective-permute-start | bytes 393224 | tf_op jit(solution)/shard_map/ppermute | solution.py:350
  52.3 3.1 %shard_map.92 = (f32[8,128,256]{2,1,0:T(8,128)S(1)}, bf16[4,64,256]{2,1,0:T(8,128)(2,1)S(1)}, bf16[4,64,256]{2,1,0:T(8,128)(2,1)S(1)}) custom-call(s32[1]{0:T(128)} %bitcast.place_ref, f32[1,256]{1,0:T(1,128)S(1)} %get-tuple-element.83.low_ref, f32[1,256]{1,0:T(1,128)S(1)} %get-tuple-element.84.high_ref, f32[8,8,256]{2,1,0:T(8,128)S(1)} %get-tuple-element.95.state_ref, ...), custom_call_target="tpu_custom_call" | custom-call | flops 2147483648 | bytes 2097152 | tf_op jit(solution)/shard_map/pallas_call | solution.py:230
  55.4 0.0 collective-permute-done.12
  55.4 0.0 collective-permute-done.13
  55.4 0.1 add_convert_fusion.3
  55.5 0.1 collective-permute-start.15
  55.6 2.7 %collective-permute-start.16 = (bf16[4,64,256]{2,1,0:T(8,128)(2,1)S(1)}, bf16[4,64,256]{2,1,0:T(8,128)(2,1)S(1)}, u32[]{:S(2)}, u32[]{:S(2)}) collective-permute-start(bf16[4,64,256]{2,1,0:T(8,128)(2,1)S(1)} %get-tuple-element.120), channel_id=1, source_target_pairs={{0,112},{16,0},{32,16},{48,32},{64,48},{80,64},{96,80},{112,96},{1... | collective-permute-start | bytes 393224 | tf_op jit(solution)/shard_map/ppermute | solution.py:350
  58.2 3.1 %shard_map.93 = (f32[8,128,256]{2,1,0:T(8,128)S(1)}, bf16[4,64,256]{2,1,0:T(8,128)(2,1)S(1)}, bf16[4,64,256]{2,1,0:T(8,128)(2,1)S(1)}) custom-call(s32[1]{0:T(128)} %bitcast.place_ref, f32[1,256]{1,0:T(1,128)S(1)} %get-tuple-element.83.low_ref, f32[1,256]{1,0:T(1,128)S(1)} %get-tuple-element.84.high_ref, f32[8,8,256]{2,1,0:T(8,128)S(1)} %get-tuple-element.95.state_ref, ...), custom_call_target="tpu_custom_call" | custom-call | flops 2147483648 | bytes 2097152 | tf_op jit(solution)/shard_map/pallas_call | solution.py:230
  61.3 0.0 collective-permute-done.14
  61.4 0.1 collective-permute-done.15
  61.4 1.0 collective-permute-done.16
  62.5 2.1 %collective-permute-start.17 = (bf16[4,64,256]{2,1,0:T(8,128)(2,1)S(1)}, bf16[4,64,256]{2,1,0:T(8,128)(2,1)S(1)}, u32[]{:S(2)}, u32[]{:S(2)}) collective-permute-start(bf16[4,64,256]{2,1,0:T(8,128)(2,1)S(1)} %add_convert_fusion.2), channel_id=1, source_target_pairs={{0,16},{16,32},{32,48},{48,64},{64,80},{80,96},{96,112},{112,0},{1... | collective-permute-start | bytes 393224 | tf_op jit(solution)/shard_map/ppermute | solution.py:350
  64.6 1.1 %collective-permute-start.18 = (bf16[4,64,256]{2,1,0:T(8,128)(2,1)S(1)}, bf16[4,64,256]{2,1,0:T(8,128)(2,1)S(1)}, u32[]{:S(2)}, u32[]{:S(2)}) collective-permute-start(bf16[4,64,256]{2,1,0:T(8,128)(2,1)S(1)} %add_convert_fusion.1), channel_id=1, source_target_pairs={{0,112},{16,0},{32,16},{48,32},{64,48},{80,64},{96,80},{112,96},{1... | collective-permute-start | bytes 393224 | tf_op jit(solution)/shard_map/ppermute | solution.py:350
  65.7 2.0 %shard_map.94 = (bf16[4,64,1280]{2,1,0:T(8,128)(2,1)S(1)}, bf16[4,64,256]{2,1,0:T(8,128)(2,1)S(1)}) custom-call(s32[1]{0:T(128)} %bitcast.place_ref, f32[1,256]{1,0:T(1,128)S(1)} %get-tuple-element.83.low_ref, f32[1,256]{1,0:T(1,128)S(1)} %get-tuple-element.84.high_ref, f32[8,8,256]{2,1,0:T(8,128)S(1)} %get-tuple-element.95.state_ref, ...), custom_call_target="tpu_custom_call" | custom-call | flops 1073741824 | bytes 2097152 | tf_op jit(solution)/shard_map/pallas_call | solution.py:230
  67.7 1.8 %collective-permute-done.17 = bf16[4,64,256]{2,1,0:T(8,128)(2,1)S(1)} collective-permute-done((bf16[4,64,256]{2,1,0:T(8,128)(2,1)S(1)}, bf16[4,64,256]{2,1,0:T(8,128)(2,1)S(1)}, u32[]{:S(2)}, u32[]{:S(2)}) %collective-permute-start.17) | collective-permute-done | bytes 131104 | tf_op jit(solution)/shard_map/ppermute | solution.py:350
  69.5 0.0 collective-permute-done.18
  69.5 0.1 add_convert_fusion
  69.7 25.6 %all_to_all.5 = bf16[32,8,1280]{2,1,0:T(8,128)(2,1)S(1)} all-to-all(bf16[32,8,1280]{2,1,0:T(8,128)(2,1)S(1)} %bitcast.20), channel_id=1, replica_groups=mesh['xh'=2,'z'=8,'core'=2,'y'=4,'xl'=2] {'xh','core','y','xl'}, dimensions={0} | all-to-all | bytes 1310720 | tf_op jit(solution)/shard_map/all_to_all | solution.py:413
  95.3 0.7 fusion
  95.9 0.9 slice.39
  (10 shorter events, 0.2 us)
Async XLA Ops:
  0.6 0.7 copy-start.5
  0.6 0.7 copy-start.4
  1.3 0.8 copy-start.2
  2.2 0.8 copy-start.3
  3.2 4.3 %collective-permute-start = (bf16[2,80,256]{2,1,0:T(8,128)(2,1)S(1)}, bf16[2,80,256]{2,1,0:T(8,128)(2,1)S(1)}, u32[]{:S(2)}, u32[]{:S(2)}) collective-permute-start(bf16[2,80,256]{2,1,0:T(8,128)(2,1)S(1)} %get-tuple-element.76), channel_id=1, source_target_pairs={{0,8},{8,0},{128,136},{136,128},{1,9},{9,1},{129,137},{137,129},{2... | collective-permute-start | bytes 245768 | tf_op jit(solution)/shard_map/ppermute | solution.py:346
  7.4 5.3 %collective-permute-start.1 = (bf16[2,80,256]{2,1,0:T(8,128)(2,1)S(1)}, bf16[2,80,256]{2,1,0:T(8,128)(2,1)S(1)}, u32[]{:S(2)}, u32[]{:S(2)}) collective-permute-start(bf16[2,80,256]{2,1,0:T(8,128)(2,1)S(1)} %pad_maximum_fusion), channel_id=1, source_target_pairs={{0,128},{8,136},{128,0},{136,8},{1,129},{9,137},{129,1},{137,9},{2... | collective-permute-start | bytes 245768 | tf_op jit(solution)/shard_map/ppermute | solution.py:346
  8.5 1.0 %copy-start = (bf16[4,64,1024]{2,1,0:T(8,128)(2,1)S(1)}, bf16[4,64,1024]{2,1,0:T(8,128)(2,1)}, u32[]{:S(2)}) copy-start(bf16[4,64,1024]{2,1,0:T(8,128)(2,1)} %q_ref.1) | copy-start | bytes 1572868
  9.6 1.0 %copy-start.1 = (bf16[4,64,1024]{2,1,0:T(8,128)(2,1)S(1)}, bf16[4,64,1024]{2,1,0:T(8,128)(2,1)}, u32[]{:S(2)}) copy-start(bf16[4,64,1024]{2,1,0:T(8,128)(2,1)} %do_ref.1) | copy-start | bytes 1572868
  12.8 9.0 %collective-permute-start.6 = (bf16[272,256]{1,0:T(8,128)(2,1)S(1)}, bf16[272,256]{1,0:T(8,128)(2,1)S(1)}, u32[]{:S(2)}, u32[]{:S(2)}) collective-permute-start(bf16[272,256]{1,0:T(8,128)(2,1)S(1)} %get-tuple-element.89.refs_4_), channel_id=1, source_target_pairs={{0,112},{16,0},{32,16},{48,32},{64,48},{80,64},{96,80},{112,96},{1... | collective-permute-start | bytes 417800 | tf_op jit(solution)/shard_map/ppermute | solution.py:350
  17.7 7.0 %collective-permute-start.5 = (bf16[272,256]{1,0:T(8,128)(2,1)S(1)}, bf16[272,256]{1,0:T(8,128)(2,1)S(1)}, u32[]{:S(2)}, u32[]{:S(2)}) collective-permute-start(bf16[272,256]{1,0:T(8,128)(2,1)S(1)} %get-tuple-element.89.refs_4_), channel_id=1, source_target_pairs={{0,16},{16,32},{32,48},{48,64},{64,80},{80,96},{96,112},{112,0},{1... | collective-permute-start | bytes 417800 | tf_op jit(solution)/shard_map/ppermute | solution.py:350
  17.7 7.0 %collective-permute-start.2 = (bf16[128,1024]{1,0:T(8,128)(2,1)S(1)}, bf16[128,1024]{1,0:T(8,128)(2,1)S(1)}, u32[]{:S(2)}, u32[]{:S(2)}) collective-permute-start(bf16[128,1024]{1,0:T(8,128)(2,1)S(1)} %get-tuple-element.86), channel_id=1, source_target_pairs={{0,8},{8,0},{128,136},{136,128},{1,9},{9,1},{129,137},{137,129},{2... | collective-permute-start | bytes 786440 | tf_op jit(solution)/shard_map/ppermute | solution.py:346
  18.6 16.7 %collective-permute-start.3 = (bf16[128,1024]{1,0:T(8,128)(2,1)S(1)}, bf16[128,1024]{1,0:T(8,128)(2,1)S(1)}, u32[]{:S(2)}, u32[]{:S(2)}) collective-permute-start(bf16[128,1024]{1,0:T(8,128)(2,1)S(1)} %get-tuple-element.87), channel_id=1, source_target_pairs={{0,128},{8,136},{128,0},{136,8},{1,129},{9,137},{129,1},{137,9},{2... | collective-permute-start | bytes 786440 | tf_op jit(solution)/shard_map/ppermute | solution.py:346
  20.8 14.5 %collective-permute-start.4 = (bf16[128,1024]{1,0:T(8,128)(2,1)S(1)}, bf16[128,1024]{1,0:T(8,128)(2,1)S(1)}, u32[]{:S(2)}, u32[]{:S(2)}) collective-permute-start(bf16[128,1024]{1,0:T(8,128)(2,1)S(1)} %get-tuple-element.88), channel_id=1, source_target_pairs={{0,136},{8,128},{128,8},{136,0},{1,137},{9,129},{129,9},{137,1},{2... | collective-permute-start | bytes 786440 | tf_op jit(solution)/shard_map/ppermute | solution.py:346
  21.8 5.7 %collective-permute-start.8 = (bf16[272,256]{1,0:T(8,128)(2,1)S(1)}, bf16[272,256]{1,0:T(8,128)(2,1)S(1)}, u32[]{:S(2)}, u32[]{:S(2)}) collective-permute-start(bf16[272,256]{1,0:T(8,128)(2,1)S(1)} %collective-permute-done.6.refs_6_.refs_4_), channel_id=1, source_target_pairs={{0,112},{16,0},{32,16},{48,32},{64,48},{80,64},{96,80},{112,96},{1... | collective-permute-start | bytes 417800 | tf_op jit(solution)/shard_map/ppermute | solution.py:350
  24.7 10.6 %collective-permute-start.7 = (bf16[272,256]{1,0:T(8,128)(2,1)S(1)}, bf16[272,256]{1,0:T(8,128)(2,1)S(1)}, u32[]{:S(2)}, u32[]{:S(2)}) collective-permute-start(bf16[272,256]{1,0:T(8,128)(2,1)S(1)} %collective-permute-done.5.refs_5_), channel_id=1, source_target_pairs={{0,16},{16,32},{32,48},{48,64},{64,80},{80,96},{96,112},{112,0},{1... | collective-permute-start | bytes 417800 | tf_op jit(solution)/shard_map/ppermute | solution.py:350
  24.7 17.9 %collective-permute-start.11 = (bf16[272,256]{1,0:T(8,128)(2,1)S(1)}, bf16[272,256]{1,0:T(8,128)(2,1)S(1)}, u32[]{:S(2)}, u32[]{:S(2)}) collective-permute-start(bf16[272,256]{1,0:T(8,128)(2,1)S(1)} %get-tuple-element.89.refs_4_), channel_id=1, source_target_pairs={{0,64},{16,80},{32,96},{48,112},{64,0},{80,16},{96,32},{112,48},{1... | collective-permute-start | bytes 417800 | tf_op jit(solution)/shard_map/ppermute | solution.py:350
  27.5 12.4 %collective-permute-start.10 = (bf16[272,256]{1,0:T(8,128)(2,1)S(1)}, bf16[272,256]{1,0:T(8,128)(2,1)S(1)}, u32[]{:S(2)}, u32[]{:S(2)}) collective-permute-start(bf16[272,256]{1,0:T(8,128)(2,1)S(1)} %collective-permute-done.8.refs_8_.refs_4_), channel_id=1, source_target_pairs={{0,112},{16,0},{32,16},{48,32},{64,48},{80,64},{96,80},{112,96},{1... | collective-permute-start | bytes 417800 | tf_op jit(solution)/shard_map/ppermute | solution.py:350
  35.3 5.1 %collective-permute-start.9 = (bf16[272,256]{1,0:T(8,128)(2,1)S(1)}, bf16[272,256]{1,0:T(8,128)(2,1)S(1)}, u32[]{:S(2)}, u32[]{:S(2)}) collective-permute-start(bf16[272,256]{1,0:T(8,128)(2,1)S(1)} %collective-permute-done.7.refs_7_.refs_5_), channel_id=1, source_target_pairs={{0,16},{16,32},{32,48},{48,64},{64,80},{80,96},{96,112},{112,0},{1... | collective-permute-start | bytes 417800 | tf_op jit(solution)/shard_map/ppermute | solution.py:350
  48.3 7.1 %collective-permute-start.12 = (bf16[4,64,256]{2,1,0:T(8,128)(2,1)S(1)}, bf16[4,64,256]{2,1,0:T(8,128)(2,1)S(1)}, u32[]{:S(2)}, u32[]{:S(2)}) collective-permute-start(bf16[4,64,256]{2,1,0:T(8,128)(2,1)S(1)} %get-tuple-element.105), channel_id=1, source_target_pairs={{0,16},{16,32},{32,48},{48,64},{64,80},{80,96},{96,112},{112,0},{1... | collective-permute-start | bytes 393224 | tf_op jit(solution)/shard_map/ppermute | solution.py:350
  48.4 7.0 %collective-permute-start.13 = (bf16[4,64,256]{2,1,0:T(8,128)(2,1)S(1)}, bf16[4,64,256]{2,1,0:T(8,128)(2,1)S(1)}, u32[]{:S(2)}, u32[]{:S(2)}) collective-permute-start(bf16[4,64,256]{2,1,0:T(8,128)(2,1)S(1)} %get-tuple-element.106), channel_id=1, source_target_pairs={{0,112},{16,0},{32,16},{48,32},{64,48},{80,64},{96,80},{112,96},{1... | collective-permute-start | bytes 393224 | tf_op jit(solution)/shard_map/ppermute | solution.py:350
  51.0 10.3 %collective-permute-start.14 = (bf16[4,64,256]{2,1,0:T(8,128)(2,1)S(1)}, bf16[4,64,256]{2,1,0:T(8,128)(2,1)S(1)}, u32[]{:S(2)}, u32[]{:S(2)}) collective-permute-start(bf16[4,64,256]{2,1,0:T(8,128)(2,1)S(1)} %get-tuple-element.113), channel_id=1, source_target_pairs={{0,64},{16,80},{32,96},{48,112},{64,0},{80,16},{96,32},{112,48},{1... | collective-permute-start | bytes 393224 | tf_op jit(solution)/shard_map/ppermute | solution.py:350
  55.5 5.9 %collective-permute-start.15 = (bf16[4,64,256]{2,1,0:T(8,128)(2,1)S(1)}, bf16[4,64,256]{2,1,0:T(8,128)(2,1)S(1)}, u32[]{:S(2)}, u32[]{:S(2)}) collective-permute-start(bf16[4,64,256]{2,1,0:T(8,128)(2,1)S(1)} %get-tuple-element.119), channel_id=1, source_target_pairs={{0,16},{16,32},{32,48},{48,64},{64,80},{80,96},{96,112},{112,0},{1... | collective-permute-start | bytes 393224 | tf_op jit(solution)/shard_map/ppermute | solution.py:350
  55.6 6.8 %collective-permute-start.16 = (bf16[4,64,256]{2,1,0:T(8,128)(2,1)S(1)}, bf16[4,64,256]{2,1,0:T(8,128)(2,1)S(1)}, u32[]{:S(2)}, u32[]{:S(2)}) collective-permute-start(bf16[4,64,256]{2,1,0:T(8,128)(2,1)S(1)} %get-tuple-element.120), channel_id=1, source_target_pairs={{0,112},{16,0},{32,16},{48,32},{64,48},{80,64},{96,80},{112,96},{1... | collective-permute-start | bytes 393224 | tf_op jit(solution)/shard_map/ppermute | solution.py:350
  62.5 7.1 %collective-permute-start.17 = (bf16[4,64,256]{2,1,0:T(8,128)(2,1)S(1)}, bf16[4,64,256]{2,1,0:T(8,128)(2,1)S(1)}, u32[]{:S(2)}, u32[]{:S(2)}) collective-permute-start(bf16[4,64,256]{2,1,0:T(8,128)(2,1)S(1)} %add_convert_fusion.2), channel_id=1, source_target_pairs={{0,16},{16,32},{32,48},{48,64},{64,80},{80,96},{96,112},{112,0},{1... | collective-permute-start | bytes 393224 | tf_op jit(solution)/shard_map/ppermute | solution.py:350
  64.6 4.9 %collective-permute-start.18 = (bf16[4,64,256]{2,1,0:T(8,128)(2,1)S(1)}, bf16[4,64,256]{2,1,0:T(8,128)(2,1)S(1)}, u32[]{:S(2)}, u32[]{:S(2)}) collective-permute-start(bf16[4,64,256]{2,1,0:T(8,128)(2,1)S(1)} %add_convert_fusion.1), channel_id=1, source_target_pairs={{0,112},{16,0},{32,16},{48,32},{64,48},{80,64},{96,80},{112,96},{1... | collective-permute-start | bytes 393224 | tf_op jit(solution)/shard_map/ppermute | solution.py:350

commit v11 on v8

--- a/solution.py
+++ b/solution.py
@@ -375,12 +375,12 @@
     for _ in range(2):
         below.append(turned(below[-1], 1))
         above.append(turned(above[-1], -1))
+    below[2], row_arrays[1:3] = tied((below[2], row_arrays[1:3]))
     below.append(turned(below[2], 1))
     above.append(turned(above[2], -1))
-    state = stats(low, high, row_arrays, [own, below[1], above[1], below[2], above[2]], None)
-    state, below[3], above[3] = tied((state, below[3], above[3]))
+    below[3], row_arrays = tied((below[3], row_arrays))
     opposite = turned(below[3], 1)
-    state = stats(low, high, row_arrays, [below[3], above[3]], state)
+    state = stats(low, high, row_arrays, [own, *below[1:], *above[1:]], None)
     state, opposite = tied((state, opposite))
 
     def gradients(pieces, before, last=False):

time: 95.6 us -> 92.4 us (0.967)
  waiting for transfers between devices: 14.6 us -> 8.09 us
  blocking collectives: 23.1 us -> 25.7 us
  starting transfers between devices: 28.4 us -> 29.6 us
    ppermute x14, waiting for transfers between devices: 10.1 us -> 3.02 us  [turned(): return lax.ppermute(array, 'z', [(i, (i + by) % RING) for i in range(RING)])]
    all_to_all x1, blocking collectives: 23.1 us -> 25.7 us  [on_device(): final = lax.all_to_all(leaving, FINAL, 0, 0, tiled=True)]
    ppermute x5, starting transfers between devices: 8.48 us -> 10.9 us  [swapped(): return lax.ppermute(array, axes, [(i, i ^ by) for i in range(count)])]
    ppermute x14, starting transfers between devices: 19.9 us -> 18.7 us  [turned(): return lax.ppermute(array, 'z', [(i, (i + by) % RING) for i in range(RING)])]
    pallas_call x2 -> x1, Pallas kernels: 6.62 us -> 6.11 us  [stats(): pl.pallas_call(functools.partial(stats_kernel, first, len(pieces)), out_s...]
  transfers between devices with their start and end apart: 19 -> 19, of which waited for: 7 -> 8; matrix products, arithmetic and copies ran while one was open for 0% -> 0% of each run, Pallas kernels for 20% -> 20%
where the time goes in v11:
time: 92.4 us; the launch traced here: 92.1 us
  starting transfers between devices  29.6 us (32%)
  blocking collectives  25.7 us (28%)
  Pallas kernels  21.5 us (23%)
  waiting for transfers between devices  8.09 us (9%)
  local copies, waits for them, and re-layouts  5.98 us (6%)
    all_to_all x1, blocking collectives, on_device(): final = lax.all_to_all(leaving, FINAL, 0, 0, tiled=True)  25.7 us
    ppermute x14, starting transfers between devices, turned(): return lax.ppermute(array, 'z', [(i, (i + by) % RING) for i in range(RING)])  18.7 us
    pallas_call x5, Pallas kernels, grads(): pl.pallas_call(functools.partial(grads_kernel, first, last, len(pieces)),...  13.8 us
    ppermute x5, starting transfers between devices, swapped(): return lax.ppermute(array, axes, [(i, i ^ by) for i in range(count)])  10.9 us
    pallas_call x1, Pallas kernels, stats(): pl.pallas_call(functools.partial(stats_kernel, first, len(pieces)), out_s...  6.11 us
    ppermute x5, waiting for transfers between devices, swapped(): return lax.ppermute(array, axes, [(i, i ^ by) for i in range(count)])  5.07 us
    unnamed x12, local copies, waits for them, and re-layouts  4.44 us
    ppermute x14, waiting for transfers between devices, turned(): return lax.ppermute(array, 'z', [(i, (i + by) % RING) for i in range(RING)])  3.02 us
  transfers between devices with their start and end apart: 19, of which 8 were waited for; matrix products, arithmetic and copies ran while one was open for 0% of the time, Pallas kernels for 20%

profile of v11, /device:TPU:1, one launch (start us, length us, event | category | flops | bytes accessed | tf_op | source)
XLA Modules:
  0.0 92.1 jit_solution(12696628791022223361)
XLA Ops:
  0.6 0.0 copy-start.5
  0.6 0.0 copy-start.4
  0.7 0.7 copy-done.5
  1.3 0.0 copy-done.4
  1.3 0.0 copy-start.2
  1.4 0.8 copy-done.2
  2.2 0.0 copy-start.3
  2.2 0.8 copy-done.3
  3.0 0.1 shard_map.85
  3.2 3.3 %collective-permute-start = (bf16[2,80,256]{2,1,0:T(8,128)(2,1)S(1)}, bf16[2,80,256]{2,1,0:T(8,128)(2,1)S(1)}, u32[]{:S(2)}, u32[]{:S(2)}) collective-permute-start(bf16[2,80,256]{2,1,0:T(8,128)(2,1)S(1)} %get-tuple-element.86), channel_id=1, source_target_pairs={{0,8},{8,0},{128,136},{136,128},{1,9},{9,1},{129,137},{137,129},{2... | collective-permute-start | bytes 245768 | tf_op jit(solution)/shard_map/ppermute | solution.py:346
  6.5 0.9 %collective-permute-done.pair_ref = bf16[2,80,256]{2,1,0:T(8,128)(2,1)S(1)} collective-permute-done((bf16[2,80,256]{2,1,0:T(8,128)(2,1)S(1)}, bf16[2,80,256]{2,1,0:T(8,128)(2,1)S(1)}, u32[]{:S(2)}, u32[]{:S(2)}) %collective-permute-start) | collective-permute-done | bytes 81952 | tf_op jit(solution)/shard_map/ppermute | solution.py:346
  7.4 1.1 %collective-permute-start.1 = (bf16[2,80,256]{2,1,0:T(8,128)(2,1)S(1)}, bf16[2,80,256]{2,1,0:T(8,128)(2,1)S(1)}, u32[]{:S(2)}, u32[]{:S(2)}) collective-permute-start(bf16[2,80,256]{2,1,0:T(8,128)(2,1)S(1)} %pad_maximum_fusion), channel_id=1, source_target_pairs={{0,128},{8,136},{128,0},{136,8},{1,129},{9,137},{129,1},{137,9},{2... | collective-permute-start | bytes 245768 | tf_op jit(solution)/shard_map/ppermute | solution.py:346
  8.5 0.0 copy-start
  8.5 1.0 %copy-done = bf16[4,64,1024]{2,1,0:T(8,128)(2,1)S(1)} copy-done((bf16[4,64,1024]{2,1,0:T(8,128)(2,1)S(1)}, bf16[4,64,1024]{2,1,0:T(8,128)(2,1)}, u32[]{:S(2)}) %copy-start) | copy-done | bytes 524312
  9.6 0.0 copy-start.1
  9.6 1.0 %copy-done.1 = bf16[4,64,1024]{2,1,0:T(8,128)(2,1)S(1)} copy-done((bf16[4,64,1024]{2,1,0:T(8,128)(2,1)S(1)}, bf16[4,64,1024]{2,1,0:T(8,128)(2,1)}, u32[]{:S(2)}) %copy-start.1) | copy-done | bytes 524312
  10.6 1.4 %shard_map.86 = (bf16[128,1024]{1,0:T(8,128)(2,1)S(1)}, bf16[128,1024]{1,0:T(8,128)(2,1)S(1)}, bf16[128,1024]{1,0:T(8,128)(2,1)S(1)}, bf16[128,1024]{1,0:T(8,128)(2,1)S(1)}) custom-call(s32[1]{0:T(128)} %bitcast.place_ref, bf16[4,64,1024]{2,1,0:T(8,128)(2,1)S(1)} %copy-done, bf16[4,64,1024]{2,1,0:T(8,128)(2,1)S(1)} %copy-done.1), custom_call_target="tpu_custom_call" | custom-call | tf_op jit(solution)/shard_map/pallas_call | solution.py:317
  12.0 0.7 collective-permute-done.1.across_ref
  12.7 0.1 shard_map.87
  12.8 1.0 %collective-permute-start.2 = (bf16[272,256]{1,0:T(8,128)(2,1)S(1)}, bf16[272,256]{1,0:T(8,128)(2,1)S(1)}, u32[]{:S(2)}, u32[]{:S(2)}) collective-permute-start(bf16[272,256]{1,0:T(8,128)(2,1)S(1)} %get-tuple-element.95.refs_4_), channel_id=1, source_target_pairs={{0,16},{16,32},{32,48},{48,64},{64,80},{80,96},{96,112},{112,0},{1... | collective-permute-start | bytes 417800 | tf_op jit(solution)/shard_map/ppermute | solution.py:350
  13.8 4.0 %collective-permute-start.8 = (bf16[272,256]{1,0:T(8,128)(2,1)S(1)}, bf16[272,256]{1,0:T(8,128)(2,1)S(1)}, u32[]{:S(2)}, u32[]{:S(2)}) collective-permute-start(bf16[272,256]{1,0:T(8,128)(2,1)S(1)} %get-tuple-element.95.refs_4_), channel_id=1, source_target_pairs={{0,112},{16,0},{32,16},{48,32},{64,48},{80,64},{96,80},{112,96},{1... | collective-permute-start | bytes 417800 | tf_op jit(solution)/shard_map/ppermute | solution.py:350
  17.8 0.9 collective-permute-start.4
  18.7 2.2 %collective-permute-start.5 = (bf16[128,1024]{1,0:T(8,128)(2,1)S(1)}, bf16[128,1024]{1,0:T(8,128)(2,1)S(1)}, u32[]{:S(2)}, u32[]{:S(2)}) collective-permute-start(bf16[128,1024]{1,0:T(8,128)(2,1)S(1)} %get-tuple-element.97), channel_id=1, source_target_pairs={{0,128},{8,136},{128,0},{136,8},{1,129},{9,137},{129,1},{137,9},{2... | collective-permute-start | bytes 786440 | tf_op jit(solution)/shard_map/ppermute | solution.py:346
  20.9 0.2 collective-permute-done.2.refs_5_
  21.1 0.0 collective-permute-start.3
  21.1 0.0 collective-permute-done.8.refs_8_.refs_4_
  21.2 2.7 %collective-permute-start.9 = (bf16[272,256]{1,0:T(8,128)(2,1)S(1)}, bf16[272,256]{1,0:T(8,128)(2,1)S(1)}, u32[]{:S(2)}, u32[]{:S(2)}) collective-permute-start(bf16[272,256]{1,0:T(8,128)(2,1)S(1)} %collective-permute-done.8.refs_8_.refs_4_), channel_id=1, source_target_pairs={{0,112},{16,0},{32,16},{48,32},{64,48},{80,64},{96,80},{112,96},{1... | collective-permute-start | bytes 417800 | tf_op jit(solution)/shard_map/ppermute | solution.py:350
  23.8 3.3 %collective-permute-start.7 = (bf16[128,1024]{1,0:T(8,128)(2,1)S(1)}, bf16[128,1024]{1,0:T(8,128)(2,1)S(1)}, u32[]{:S(2)}, u32[]{:S(2)}) collective-permute-start(bf16[128,1024]{1,0:T(8,128)(2,1)S(1)} %get-tuple-element.102), channel_id=1, source_target_pairs={{0,136},{8,128},{128,8},{136,0},{1,137},{9,129},{129,9},{137,1},{2... | collective-permute-start | bytes 786440 | tf_op jit(solution)/shard_map/ppermute | solution.py:346
  27.1 0.0 collective-permute-done.4.refs_1_
  27.1 1.0 %collective-permute-done.5.refs_2_ = bf16[128,1024]{1,0:T(8,128)(2,1)S(1)} collective-permute-done((bf16[128,1024]{1,0:T(8,128)(2,1)S(1)}, bf16[128,1024]{1,0:T(8,128)(2,1)S(1)}, u32[]{:S(2)}, u32[]{:S(2)}) %collective-permute-start.5) | collective-permute-done | bytes 262176 | tf_op jit(solution)/shard_map/ppermute | solution.py:346
  28.1 0.0 collective-permute-done.3.refs_6_.refs_5_
  28.2 0.0 collective-permute-start.6
  28.2 0.0 collective-permute-done.9.refs_9_.refs_4_
  28.2 2.7 %collective-permute-start.10 = (bf16[272,256]{1,0:T(8,128)(2,1)S(1)}, bf16[272,256]{1,0:T(8,128)(2,1)S(1)}, u32[]{:S(2)}, u32[]{:S(2)}) collective-permute-start(bf16[272,256]{1,0:T(8,128)(2,1)S(1)} %collective-permute-done.9.refs_9_.refs_4_), channel_id=1, source_target_pairs={{0,112},{16,0},{32,16},{48,32},{64,48},{80,64},{96,80},{112,96},{1... | collective-permute-start | bytes 417800 | tf_op jit(solution)/shard_map/ppermute | solution.py:350
  30.8 2.4 %collective-permute-done.7.refs_3_ = bf16[128,1024]{1,0:T(8,128)(2,1)S(1)} collective-permute-done((bf16[128,1024]{1,0:T(8,128)(2,1)S(1)}, bf16[128,1024]{1,0:T(8,128)(2,1)S(1)}, u32[]{:S(2)}, u32[]{:S(2)}) %collective-permute-start.7) | collective-permute-done | bytes 262176 | tf_op jit(solution)/shard_map/ppermute | solution.py:346
  33.3 0.5 collective-permute-done.6.refs_7_.refs_5_
  33.8 0.0 collective-permute-start.11
  33.8 0.0 collective-permute-done.10.refs_10_.refs_4_
  33.8 6.1 %shard_map.88.state_ref = f32[8,8,256]{2,1,0:T(8,128)S(1)} custom-call(f32[1,256]{1,0:T(1,128)S(1)} %get-tuple-element.93.low_ref, f32[1,256]{1,0:T(1,128)S(1)} %get-tuple-element.94.high_ref, bf16[128,1024]{1,0:T(8,128)(2,1)S(1)} %get-tuple-element.103.refs_0_, bf16[128,1024]{1,0:T(8,128)(2,1)S(1)} %collective-permute-done.4.refs_1_, ...), custom_call_target="tpu_custom_call" | custom-call | flops 3758096384 | bytes 1048576 | tf_op jit(solution)/shard_map/pallas_call | solution.py:204
  39.9 0.0 collective-permute-done.11.refs_4_
  39.9 2.6 %shard_map.89 = (f32[8,128,256]{2,1,0:T(8,128)S(1)}, bf16[4,64,256]{2,1,0:T(8,128)(2,1)S(1)}, f32[8,8,256]{2,1,0:T(8,128)S(1)}) custom-call(s32[1]{0:T(128)} %bitcast.place_ref, f32[1,256]{1,0:T(1,128)S(1)} %get-tuple-element.93.low_ref, f32[1,256]{1,0:T(1,128)S(1)} %get-tuple-element.94.high_ref, f32[8,8,256]{2,1,0:T(8,128)S(1)} %shard_map.88.state_ref, ...), custom_call_target="tpu_custom_call" | custom-call | flops 1073741824 | bytes 2097152 | tf_op jit(solution)/shard_map/pallas_call | solution.py:230
  42.5 0.1 collective-permute-start.12
  42.6 3.1 %shard_map.90 = (f32[8,128,256]{2,1,0:T(8,128)S(1)}, bf16[4,64,256]{2,1,0:T(8,128)(2,1)S(1)}, bf16[4,64,256]{2,1,0:T(8,128)(2,1)S(1)}) custom-call(s32[1]{0:T(128)} %bitcast.place_ref, f32[1,256]{1,0:T(1,128)S(1)} %get-tuple-element.93.low_ref, f32[1,256]{1,0:T(1,128)S(1)} %get-tuple-element.94.high_ref, f32[8,8,256]{2,1,0:T(8,128)S(1)} %get-tuple-element.113.state_ref, ...), custom_call_target="tpu_custom_call" | custom-call | flops 2147483648 | bytes 2097152 | tf_op jit(solution)/shard_map/pallas_call | solution.py:230
  45.7 1.9 %collective-permute-done.12 = bf16[4,64,256]{2,1,0:T(8,128)(2,1)S(1)} collective-permute-done((bf16[4,64,256]{2,1,0:T(8,128)(2,1)S(1)}, bf16[4,64,256]{2,1,0:T(8,128)(2,1)S(1)}, u32[]{:S(2)}, u32[]{:S(2)}) %collective-permute-start.12) | collective-permute-done | bytes 131104 | tf_op jit(solution)/shard_map/ppermute | solution.py:350
  47.6 0.5 collective-permute-start.13
  48.2 2.2 %collective-permute-start.14 = (bf16[4,64,256]{2,1,0:T(8,128)(2,1)S(1)}, bf16[4,64,256]{2,1,0:T(8,128)(2,1)S(1)}, u32[]{:S(2)}, u32[]{:S(2)}) collective-permute-start(bf16[4,64,256]{2,1,0:T(8,128)(2,1)S(1)} %get-tuple-element.129), channel_id=1, source_target_pairs={{0,112},{16,0},{32,16},{48,32},{64,48},{80,64},{96,80},{112,96},{1... | collective-permute-start | bytes 393224 | tf_op jit(solution)/shard_map/ppermute | solution.py:350
  50.4 3.1 %shard_map.91 = (f32[8,128,256]{2,1,0:T(8,128)S(1)}, bf16[4,64,256]{2,1,0:T(8,128)(2,1)S(1)}, bf16[4,64,256]{2,1,0:T(8,128)(2,1)S(1)}) custom-call(s32[1]{0:T(128)} %bitcast.place_ref, f32[1,256]{1,0:T(1,128)S(1)} %get-tuple-element.93.low_ref, f32[1,256]{1,0:T(1,128)S(1)} %get-tuple-element.94.high_ref, f32[8,8,256]{2,1,0:T(8,128)S(1)} %get-tuple-element.113.state_ref, ...), custom_call_target="tpu_custom_call" | custom-call | flops 2147483648 | bytes 2097152 | tf_op jit(solution)/shard_map/pallas_call | solution.py:230
  53.5 0.0 collective-permute-done.13
  53.5 0.0 collective-permute-done.14
  53.5 0.1 add_convert_fusion.3
  53.6 1.5 %collective-permute-start.15 = (bf16[4,64,256]{2,1,0:T(8,128)(2,1)S(1)}, bf16[4,64,256]{2,1,0:T(8,128)(2,1)S(1)}, u32[]{:S(2)}, u32[]{:S(2)}) collective-permute-start(bf16[4,64,256]{2,1,0:T(8,128)(2,1)S(1)} %get-tuple-element.140), channel_id=1, source_target_pairs={{0,16},{16,32},{32,48},{48,64},{64,80},{80,96},{96,112},{112,0},{1... | collective-permute-start | bytes 393224 | tf_op jit(solution)/shard_map/ppermute | solution.py:350
  55.1 1.3 %collective-permute-start.16 = (bf16[4,64,256]{2,1,0:T(8,128)(2,1)S(1)}, bf16[4,64,256]{2,1,0:T(8,128)(2,1)S(1)}, u32[]{:S(2)}, u32[]{:S(2)}) collective-permute-start(bf16[4,64,256]{2,1,0:T(8,128)(2,1)S(1)} %get-tuple-element.141), channel_id=1, source_target_pairs={{0,112},{16,0},{32,16},{48,32},{64,48},{80,64},{96,80},{112,96},{1... | collective-permute-start | bytes 393224 | tf_op jit(solution)/shard_map/ppermute | solution.py:350
  56.3 3.1 %shard_map.92 = (f32[8,128,256]{2,1,0:T(8,128)S(1)}, bf16[4,64,256]{2,1,0:T(8,128)(2,1)S(1)}, bf16[4,64,256]{2,1,0:T(8,128)(2,1)S(1)}) custom-call(s32[1]{0:T(128)} %bitcast.place_ref, f32[1,256]{1,0:T(1,128)S(1)} %get-tuple-element.93.low_ref, f32[1,256]{1,0:T(1,128)S(1)} %get-tuple-element.94.high_ref, f32[8,8,256]{2,1,0:T(8,128)S(1)} %get-tuple-element.113.state_ref, ...), custom_call_target="tpu_custom_call" | custom-call | flops 2147483648 | bytes 2097152 | tf_op jit(solution)/shard_map/pallas_call | solution.py:230
  59.5 0.0 collective-permute-done.15
  59.5 0.0 collective-permute-done.16
  59.6 0.9 collective-permute-start.17
  60.5 1.9 %collective-permute-start.18 = (bf16[4,64,256]{2,1,0:T(8,128)(2,1)S(1)}, bf16[4,64,256]{2,1,0:T(8,128)(2,1)S(1)}, u32[]{:S(2)}, u32[]{:S(2)}) collective-permute-start(bf16[4,64,256]{2,1,0:T(8,128)(2,1)S(1)} %add_convert_fusion.1), channel_id=1, source_target_pairs={{0,112},{16,0},{32,16},{48,32},{64,48},{80,64},{96,80},{112,96},{1... | collective-permute-start | bytes 393224 | tf_op jit(solution)/shard_map/ppermute | solution.py:350
  62.3 2.0 %shard_map.93 = (bf16[4,64,1280]{2,1,0:T(8,128)(2,1)S(1)}, bf16[4,64,256]{2,1,0:T(8,128)(2,1)S(1)}) custom-call(s32[1]{0:T(128)} %bitcast.place_ref, f32[1,256]{1,0:T(1,128)S(1)} %get-tuple-element.93.low_ref, f32[1,256]{1,0:T(1,128)S(1)} %get-tuple-element.94.high_ref, f32[8,8,256]{2,1,0:T(8,128)S(1)} %get-tuple-element.113.state_ref, ...), custom_call_target="tpu_custom_call" | custom-call | flops 1073741824 | bytes 2097152 | tf_op jit(solution)/shard_map/pallas_call | solution.py:230
  64.3 0.4 collective-permute-done.17
  64.7 0.0 collective-permute-done.18
  64.7 0.1 add_convert_fusion
  64.8 25.7 %all_to_all.5 = bf16[32,8,1280]{2,1,0:T(8,128)(2,1)S(1)} all-to-all(bf16[32,8,1280]{2,1,0:T(8,128)(2,1)S(1)} %bitcast.20), channel_id=1, replica_groups=mesh['xh'=2,'z'=8,'core'=2,'y'=4,'xl'=2] {'xh','core','y','xl'}, dimensions={0} | all-to-all | bytes 1310720 | tf_op jit(solution)/shard_map/all_to_all | solution.py:414
  90.6 0.7 fusion
  91.2 0.9 slice.39
  (10 shorter events, 0.2 us)
Async XLA Ops:
  0.6 0.7 copy-start.5
  0.6 0.7 copy-start.4
  1.3 0.8 copy-start.2
  2.2 0.8 copy-start.3
  3.2 4.3 %collective-permute-start = (bf16[2,80,256]{2,1,0:T(8,128)(2,1)S(1)}, bf16[2,80,256]{2,1,0:T(8,128)(2,1)S(1)}, u32[]{:S(2)}, u32[]{:S(2)}) collective-permute-start(bf16[2,80,256]{2,1,0:T(8,128)(2,1)S(1)} %get-tuple-element.86), channel_id=1, source_target_pairs={{0,8},{8,0},{128,136},{136,128},{1,9},{9,1},{129,137},{137,129},{2... | collective-permute-start | bytes 245768 | tf_op jit(solution)/shard_map/ppermute | solution.py:346
  7.4 5.3 %collective-permute-start.1 = (bf16[2,80,256]{2,1,0:T(8,128)(2,1)S(1)}, bf16[2,80,256]{2,1,0:T(8,128)(2,1)S(1)}, u32[]{:S(2)}, u32[]{:S(2)}) collective-permute-start(bf16[2,80,256]{2,1,0:T(8,128)(2,1)S(1)} %pad_maximum_fusion), channel_id=1, source_target_pairs={{0,128},{8,136},{128,0},{136,8},{1,129},{9,137},{129,1},{137,9},{2... | collective-permute-start | bytes 245768 | tf_op jit(solution)/shard_map/ppermute | solution.py:346
  8.5 1.0 %copy-start = (bf16[4,64,1024]{2,1,0:T(8,128)(2,1)S(1)}, bf16[4,64,1024]{2,1,0:T(8,128)(2,1)}, u32[]{:S(2)}) copy-start(bf16[4,64,1024]{2,1,0:T(8,128)(2,1)} %q_ref.1) | copy-start | bytes 1572868
  9.6 1.0 %copy-start.1 = (bf16[4,64,1024]{2,1,0:T(8,128)(2,1)S(1)}, bf16[4,64,1024]{2,1,0:T(8,128)(2,1)}, u32[]{:S(2)}) copy-start(bf16[4,64,1024]{2,1,0:T(8,128)(2,1)} %do_ref.1) | copy-start | bytes 1572868
  12.8 8.4 %collective-permute-start.2 = (bf16[272,256]{1,0:T(8,128)(2,1)S(1)}, bf16[272,256]{1,0:T(8,128)(2,1)S(1)}, u32[]{:S(2)}, u32[]{:S(2)}) collective-permute-start(bf16[272,256]{1,0:T(8,128)(2,1)S(1)} %get-tuple-element.95.refs_4_), channel_id=1, source_target_pairs={{0,16},{16,32},{32,48},{48,64},{64,80},{80,96},{96,112},{112,0},{1... | collective-permute-start | bytes 417800 | tf_op jit(solution)/shard_map/ppermute | solution.py:350
  13.8 7.4 %collective-permute-start.8 = (bf16[272,256]{1,0:T(8,128)(2,1)S(1)}, bf16[272,256]{1,0:T(8,128)(2,1)S(1)}, u32[]{:S(2)}, u32[]{:S(2)}) collective-permute-start(bf16[272,256]{1,0:T(8,128)(2,1)S(1)} %get-tuple-element.95.refs_4_), channel_id=1, source_target_pairs={{0,112},{16,0},{32,16},{48,32},{64,48},{80,64},{96,80},{112,96},{1... | collective-permute-start | bytes 417800 | tf_op jit(solution)/shard_map/ppermute | solution.py:350
  17.8 9.3 %collective-permute-start.4 = (bf16[128,1024]{1,0:T(8,128)(2,1)S(1)}, bf16[128,1024]{1,0:T(8,128)(2,1)S(1)}, u32[]{:S(2)}, u32[]{:S(2)}) collective-permute-start(bf16[128,1024]{1,0:T(8,128)(2,1)S(1)} %get-tuple-element.96), channel_id=1, source_target_pairs={{0,8},{8,0},{128,136},{136,128},{1,9},{9,1},{129,137},{137,129},{2... | collective-permute-start | bytes 786440 | tf_op jit(solution)/shard_map/ppermute | solution.py:346
  18.7 9.4 %collective-permute-start.5 = (bf16[128,1024]{1,0:T(8,128)(2,1)S(1)}, bf16[128,1024]{1,0:T(8,128)(2,1)S(1)}, u32[]{:S(2)}, u32[]{:S(2)}) collective-permute-start(bf16[128,1024]{1,0:T(8,128)(2,1)S(1)} %get-tuple-element.97), channel_id=1, source_target_pairs={{0,128},{8,136},{128,0},{136,8},{1,129},{9,137},{129,1},{137,9},{2... | collective-permute-start | bytes 786440 | tf_op jit(solution)/shard_map/ppermute | solution.py:346
  21.1 7.0 %collective-permute-start.3 = (bf16[272,256]{1,0:T(8,128)(2,1)S(1)}, bf16[272,256]{1,0:T(8,128)(2,1)S(1)}, u32[]{:S(2)}, u32[]{:S(2)}) collective-permute-start(bf16[272,256]{1,0:T(8,128)(2,1)S(1)} %collective-permute-done.2.refs_5_), channel_id=1, source_target_pairs={{0,16},{16,32},{32,48},{48,64},{64,80},{80,96},{96,112},{112,0},{1... | collective-permute-start | bytes 417800 | tf_op jit(solution)/shard_map/ppermute | solution.py:350
  21.2 7.0 %collective-permute-start.9 = (bf16[272,256]{1,0:T(8,128)(2,1)S(1)}, bf16[272,256]{1,0:T(8,128)(2,1)S(1)}, u32[]{:S(2)}, u32[]{:S(2)}) collective-permute-start(bf16[272,256]{1,0:T(8,128)(2,1)S(1)} %collective-permute-done.8.refs_8_.refs_4_), channel_id=1, source_target_pairs={{0,112},{16,0},{32,16},{48,32},{64,48},{80,64},{96,80},{112,96},{1... | collective-permute-start | bytes 417800 | tf_op jit(solution)/shard_map/ppermute | solution.py:350
  23.8 9.5 %collective-permute-start.7 = (bf16[128,1024]{1,0:T(8,128)(2,1)S(1)}, bf16[128,1024]{1,0:T(8,128)(2,1)S(1)}, u32[]{:S(2)}, u32[]{:S(2)}) collective-permute-start(bf16[128,1024]{1,0:T(8,128)(2,1)S(1)} %get-tuple-element.102), channel_id=1, source_target_pairs={{0,136},{8,128},{128,8},{136,0},{1,137},{9,129},{129,9},{137,1},{2... | collective-permute-start | bytes 786440 | tf_op jit(solution)/shard_map/ppermute | solution.py:346
  28.2 5.6 %collective-permute-start.6 = (bf16[272,256]{1,0:T(8,128)(2,1)S(1)}, bf16[272,256]{1,0:T(8,128)(2,1)S(1)}, u32[]{:S(2)}, u32[]{:S(2)}) collective-permute-start(bf16[272,256]{1,0:T(8,128)(2,1)S(1)} %collective-permute-done.3.refs_6_.refs_5_), channel_id=1, source_target_pairs={{0,16},{16,32},{32,48},{48,64},{64,80},{80,96},{96,112},{112,0},{1... | collective-permute-start | bytes 417800 | tf_op jit(solution)/shard_map/ppermute | solution.py:350
  28.2 5.6 %collective-permute-start.10 = (bf16[272,256]{1,0:T(8,128)(2,1)S(1)}, bf16[272,256]{1,0:T(8,128)(2,1)S(1)}, u32[]{:S(2)}, u32[]{:S(2)}) collective-permute-start(bf16[272,256]{1,0:T(8,128)(2,1)S(1)} %collective-permute-done.9.refs_9_.refs_4_), channel_id=1, source_target_pairs={{0,112},{16,0},{32,16},{48,32},{64,48},{80,64},{96,80},{112,96},{1... | collective-permute-start | bytes 417800 | tf_op jit(solution)/shard_map/ppermute | solution.py:350
  33.8 6.1 %collective-permute-start.11 = (bf16[272,256]{1,0:T(8,128)(2,1)S(1)}, bf16[272,256]{1,0:T(8,128)(2,1)S(1)}, u32[]{:S(2)}, u32[]{:S(2)}) collective-permute-start(bf16[272,256]{1,0:T(8,128)(2,1)S(1)} %collective-permute-done.6.refs_7_.refs_5_), channel_id=1, source_target_pairs={{0,16},{16,32},{32,48},{48,64},{64,80},{80,96},{96,112},{112,0},{1... | collective-permute-start | bytes 417800 | tf_op jit(solution)/shard_map/ppermute | solution.py:350
  42.5 5.1 %collective-permute-start.12 = (bf16[4,64,256]{2,1,0:T(8,128)(2,1)S(1)}, bf16[4,64,256]{2,1,0:T(8,128)(2,1)S(1)}, u32[]{:S(2)}, u32[]{:S(2)}) collective-permute-start(bf16[4,64,256]{2,1,0:T(8,128)(2,1)S(1)} %get-tuple-element.118), channel_id=1, source_target_pairs={{0,16},{16,32},{32,48},{48,64},{64,80},{80,96},{96,112},{112,0},{1... | collective-permute-start | bytes 393224 | tf_op jit(solution)/shard_map/ppermute | solution.py:350
  47.6 5.9 %collective-permute-start.13 = (bf16[4,64,256]{2,1,0:T(8,128)(2,1)S(1)}, bf16[4,64,256]{2,1,0:T(8,128)(2,1)S(1)}, u32[]{:S(2)}, u32[]{:S(2)}) collective-permute-start(bf16[4,64,256]{2,1,0:T(8,128)(2,1)S(1)} %add_convert_fusion.5), channel_id=1, source_target_pairs={{0,16},{16,32},{32,48},{48,64},{64,80},{80,96},{96,112},{112,0},{1... | collective-permute-start | bytes 393224 | tf_op jit(solution)/shard_map/ppermute | solution.py:350
  48.2 5.3 %collective-permute-start.14 = (bf16[4,64,256]{2,1,0:T(8,128)(2,1)S(1)}, bf16[4,64,256]{2,1,0:T(8,128)(2,1)S(1)}, u32[]{:S(2)}, u32[]{:S(2)}) collective-permute-start(bf16[4,64,256]{2,1,0:T(8,128)(2,1)S(1)} %get-tuple-element.129), channel_id=1, source_target_pairs={{0,112},{16,0},{32,16},{48,32},{64,48},{80,64},{96,80},{112,96},{1... | collective-permute-start | bytes 393224 | tf_op jit(solution)/shard_map/ppermute | solution.py:350
  53.6 5.9 %collective-permute-start.15 = (bf16[4,64,256]{2,1,0:T(8,128)(2,1)S(1)}, bf16[4,64,256]{2,1,0:T(8,128)(2,1)S(1)}, u32[]{:S(2)}, u32[]{:S(2)}) collective-permute-start(bf16[4,64,256]{2,1,0:T(8,128)(2,1)S(1)} %get-tuple-element.140), channel_id=1, source_target_pairs={{0,16},{16,32},{32,48},{48,64},{64,80},{80,96},{96,112},{112,0},{1... | collective-permute-start | bytes 393224 | tf_op jit(solution)/shard_map/ppermute | solution.py:350
  55.1 4.4 %collective-permute-start.16 = (bf16[4,64,256]{2,1,0:T(8,128)(2,1)S(1)}, bf16[4,64,256]{2,1,0:T(8,128)(2,1)S(1)}, u32[]{:S(2)}, u32[]{:S(2)}) collective-permute-start(bf16[4,64,256]{2,1,0:T(8,128)(2,1)S(1)} %get-tuple-element.141), channel_id=1, source_target_pairs={{0,112},{16,0},{32,16},{48,32},{64,48},{80,64},{96,80},{112,96},{1... | collective-permute-start | bytes 393224 | tf_op jit(solution)/shard_map/ppermute | solution.py:350
  59.6 5.1 %collective-permute-start.17 = (bf16[4,64,256]{2,1,0:T(8,128)(2,1)S(1)}, bf16[4,64,256]{2,1,0:T(8,128)(2,1)S(1)}, u32[]{:S(2)}, u32[]{:S(2)}) collective-permute-start(bf16[4,64,256]{2,1,0:T(8,128)(2,1)S(1)} %add_convert_fusion.2), channel_id=1, source_target_pairs={{0,16},{16,32},{32,48},{48,64},{64,80},{80,96},{96,112},{112,0},{1... | collective-permute-start | bytes 393224 | tf_op jit(solution)/shard_map/ppermute | solution.py:350
  60.5 4.2 %collective-permute-start.18 = (bf16[4,64,256]{2,1,0:T(8,128)(2,1)S(1)}, bf16[4,64,256]{2,1,0:T(8,128)(2,1)S(1)}, u32[]{:S(2)}, u32[]{:S(2)}) collective-permute-start(bf16[4,64,256]{2,1,0:T(8,128)(2,1)S(1)} %add_convert_fusion.1), channel_id=1, source_target_pairs={{0,112},{16,0},{32,16},{48,32},{64,48},{80,64},{96,80},{112,96},{1... | collective-permute-start | bytes 393224 | tf_op jit(solution)/shard_map/ppermute | solution.py:350
